TPU v7x, 32 devices: a whole 2x2x4 slice. The times are simulated.
32 devices in a mesh: tm: 4 (over x, core), space: 8 (over z, y).
Axes of the slice: x: 2, y: 2, z: 4, core: 2. Of those that a mesh axis runs over, the one named last changes fastest.
Arguments:
- enthalpy: float32 [4, 64, 512, 128], P('tm', 'space'), may hold values from -4 to 4
- solute: float32 [4, 64, 512, 128], P('tm', 'space'), may hold values from 0.5 to 1.5
- material: int32 [64, 512, 128], P('space'), may hold values from 0 to 3
- phase_flag: int32 [64, 512, 128], P('space'), may hold values from 0 to 2
- heat_capacity: float32 [4], replicated, may hold values from 0.8 to 2
- latent: float32 [4], replicated, may hold values from 0.5 to 2
- solidus: float32 [4], replicated, may hold values from -0.5 to 0.5
- partition: float32 [4], replicated, may hold values from 0.3 to 0.6
- back_diffusion: float32 [4], replicated, may hold values from 0.1 to 1
- heat_rate: float32 [4], replicated, may hold values from 0.06 to 0.16
- solute_rate: float32 [3], replicated, may hold values from 0.005 to 0.045
Outputs:
- end_enthalpy: float32 [4, 64, 512, 128], P('tm', 'space')
- end_solute: float32 [4, 64, 512, 128], P('tm', 'space')
All inputs are finite; a program needn't handle non-finite values.
Results may differ from a plain program's by a relative error of at most 0.00002.
Values sent between devices are 32-bit elements; how exact they have to be, the bound alone decides.
No kernel may reach another device: no remote copies, remote signals or barrier semaphores. Data moves between devices by JAX's collectives and lax.ppermute only.
A program may use at most 128 MiB of HBM per device.

v0:
```python
import functools

import jax
import jax.numpy as jnp
from jax import lax
from jax.experimental import pallas as pl
from jax.experimental.pallas import tpu as pltpu
from jax.sharding import PartitionSpec as P

STEPS = 4
CHUNK = 256
MIB = 1024 * 1024
SMEM = pl.BlockSpec(memory_space=pltpu.SMEM)
VMEM = pl.BlockSpec(memory_space=pltpu.VMEM)
ANY = pl.BlockSpec(memory_space=pl.ANY)


class Tables:
    def __init__(self, prm):
        def raw(first, count):
            return [jnp.full((8, 128), prm[first + m], jnp.float32) for m in range(count)]

        cap, self.lat, self.hs = raw(0, 4), raw(4, 4), raw(8, 4)
        kp, bd, xr = raw(12, 4), raw(16, 4), raw(20, 4)
        self.sg = raw(24, 3)
        q = [(1.0 - k) / (1.0 + b) for k, b in zip(kp, bd)]
        self.icap = [1.0 / c for c in cap]
        self.den0 = [1.0 - v for v in q]
        self.den1 = [v / t for v, t in zip(q, self.lat)]
        self.hg = [x * c for x, c in zip(xr, cap)]
        self.gh = [4.0 / (1.0 + 18.0 * x) for x in xr]
        self.crh = [h * g for h, g in zip(self.hg, self.gh)]
        self.kp18 = [18.0 / k for k in kp]


class Cells:
    def __init__(self, tab, ids):
        self.tab, self.shape = tab, ids.shape
        self.b0 = (ids & 1) != 0
        self.b1 = (ids & 2) != 0
        self.p1 = (ids & 4) != 0
        self.p2 = (ids & 8) != 0

    def wide(self, tile):
        reps = self.shape[0] // 8
        return jnp.broadcast_to(tile[None], (reps, 8, 128)).reshape(self.shape)

    def alloy(self, name):
        t = [self.wide(v) for v in getattr(self.tab, name)]
        return jnp.where(self.b1, jnp.where(self.b0, t[3], t[2]), jnp.where(self.b0, t[1], t[0]))

    def solute_gain(self):
        t = [self.wide(v) for v in self.tab.sg]
        return jnp.where(self.p2, t[2], jnp.where(self.p1, t[1], t[0]))

    def fine(self):
        return self.alloy("hg"), self.solute_gain()

    def ratio(self):
        sg = self.solute_gain()
        return self.alloy("gh"), 4.0 / (1.0 + sg * self.alloy("kp18"))

    def coarse(self):
        sg = self.solute_gain()
        return self.alloy("crh"), 4.0 * sg / (1.0 + sg * self.alloy("kp18"))

    def melt(self, h, c):
        sensible = h - self.alloy("hs")
        held = jnp.minimum(jnp.maximum(sensible, 0.0), self.alloy("lat"))
        t = (h - held) * self.alloy("icap")
        return t, c / (self.alloy("den0") + self.alloy("den1") * held)


F2 = range(2)


class Fields:
    def __init__(self, *refs):
        self.refs = refs
        self.shape = (2,) + tuple(refs[0].shape)

    def __getitem__(self, key):
        return self.refs[key[0]][key[1:]]

    def __setitem__(self, key, value):
        self.refs[key[0]][key[1:]] = value


class Tile:
    def __init__(self, y, n):
        self.y, self.n = y, n
        self.at = pl.ds(y, n)

    def pad(self, by=0):
        return pl.ds(self.y + (8 + by), self.n)


def tiles(count, ny, body):
    n = CHUNK if ny % CHUNK == 0 else ny
    per = ny // n

    def run(k, carry):
        body(k // per, Tile(pl.multiple_of((k % per) * n, n), n))
        return carry

    lax.fori_loop(0, count * per, run, 0)


def clear_rims(pad):
    rows, long = pad.shape[1], pad.shape[2]
    for f in F2:
        for r in range(rows):
            pad[f, r, 0:8, :] = jnp.zeros((8, 128), jnp.float32)
            pad[f, r, long - 8 : long, :] = jnp.zeros((8, 128), jnp.float32)


def clear_ends(pad):
    def body(i, t):
        for f in F2:
            pad[f, i * (pad.shape[1] - 1), t.pad(), :] = jnp.zeros((t.n, 128), jnp.float32)

    tiles(2, pad.shape[2] - 16, body)


def put_melt(tab, pad, r, t, ids, h, c):
    values = Cells(tab, ids).melt(h, c)
    for f in F2:
        pad[f, r, t.pad(), :] = values[f]


def lap(pad, f, r, t):
    mid = pad[f, r, t.pad(), :]
    lane = lax.broadcasted_iota(jnp.int32, mid.shape, 1)
    total = pad[f, r, t.pad(-1), :] + pad[f, r, t.pad(1), :]
    total = total + jnp.where(lane == 0, 0.0, pltpu.roll(mid, 1, 1))
    total = total + jnp.where(lane == 127, 0.0, pltpu.roll(mid, 127, 1))
    return total - 6.0 * mid + pad[f, r - 1, t.pad(), :] + pad[f, r + 1, t.pad(), :]


def fine(tab, pad, r, t, ids, now):
    rate = Cells(tab, ids).fine()
    return [now[f] + rate[f] * lap(pad, f, r, t) for f in F2]


def coarse(tab, pad, r, t, ids, now):
    rate = Cells(tab, ids).coarse()
    return [now[f] + rate[f] * lap(pad, f, r, t) for f in F2]


class Parts:
    def __init__(self, mid):
        self.mid, self.rows = mid, mid + 4

    def each(self, ny, body, which="mnx"):
        if "x" in which:
            tiles(2, ny, lambda i, t: body("x", i, i * (self.rows - 1), t))
        if "n" in which:
            tiles(2, ny, lambda i, t: body("n", i, 1 + i * (self.rows - 3), t))
        if "m" in which:
            tiles(self.mid, ny, lambda i, t: body("m", i, i + 2, t))


def first_edges_kernel(prm, h, c, mat, tl0, tl7):
    tab = Tables(prm)
    side = pl.program_id(0)

    def body(i, t):
        values = Cells(tab, mat[0, t.at, :]).melt(h[0, t.at, :], c[0, t.at, :])

        @pl.when(side == 0)
        def _():
            for f in F2:
                tl0[f, t.at, :] = values[f]

        @pl.when(side == 1)
        def _():
            for f in F2:
                tl7[f, t.at, :] = values[f]

    tiles(1, h.shape[1], body)


def first_step_kernel(prm, h, c, mat, ph, sm, sn, part, ids, ide, pad):
    tab = Tables(prm)
    rows, ny = h.shape[0], h.shape[1]
    outs = {"m": sm, "n": sn, "x": part}
    clear_rims(pad)
    clear_ends(pad)

    def melt(r, t):
        cell = mat[r, t.at, :] + 4 * ph[r, t.at, :]
        ids[r, t.at, :] = cell
        put_melt(tab, pad, r + 1, t, cell, h[r, t.at, :], c[r, t.at, :])

    def update(part_name, i, r, t):
        new = fine(tab, pad, r + 1, t, ids[r, t.at, :], (h[r, t.at, :], c[r, t.at, :]))
        for f in F2:
            outs[part_name][f, i, t.at, :] = new[f]

    tiles(rows, ny, melt)
    ide[0] = ids[0]
    ide[1] = ids[rows - 1]
    Parts(rows - 4).each(ny, update)


def step_body(prm, sm, sn, sx, ids, outs, pad):
    tab = Tables(prm)
    ny = sm.shape[2]
    now = {"m": sm, "n": sn, "x": sx}
    block = Parts(sm.shape[1])
    clear_rims(pad)
    clear_ends(pad)

    def at(name, i, t):
        return [now[name][f, i, t.at, :] for f in F2]

    def melt(name, i, r, t):
        put_melt(tab, pad, r + 1, t, ids[r, t.at, :], *at(name, i, t))

    def update(name, i, r, t):
        new = fine(tab, pad, r + 1, t, ids[r, t.at, :], at(name, i, t))
        for f in F2:
            outs[name][f, i, t.at, :] = new[f]

    block.each(ny, melt)
    block.each(ny, update, outs)


def step_kernel(prm, sm, sn, sx, ids, nm, nn, part, pad):
    step_body(prm, sm, sn, sx, ids, {"x": part, "n": nn, "m": nm}, pad)


def step_apart_kernel(prm, sm, sn, sx, ids, mh, mc, nn, part, pad):
    step_body(prm, sm, sn, sx, ids, {"x": part, "n": nn, "m": Fields(mh, mc)}, pad)


def step_joined_kernel(prm, mh, mc, sn, sx, ids, nm, nn, part, pad):
    step_body(prm, Fields(mh, mc), sn, sx, ids, {"x": part, "n": nn, "m": nm}, pad)


def replay_kernel(own, prm, mh, mc, sn, sx, ids, nm, nn, pad):
    @pl.when(own[0] != 0)
    def _():
        step_body(prm, Fields(mh, mc), sn, sx, ids, {"n": nn, "m": nm}, pad)


def edges_body(prm, gains, part, low, high, ide, edge, tl0, tl7):
    tab = Tables(prm)
    for e, (halo, tl) in enumerate(((low, tl0), (high, tl7))):

        def body(i, t, e=e, halo=halo, tl=tl):
            cells = Cells(tab, ide[e, t.at, :])
            rate = getattr(cells, gains)()
            new = [part[f, e, t.at, :] + rate[f] * halo[f, t.at, :] for f in F2]
            values = cells.melt(*new)
            for f in F2:
                edge[f, e, t.at, :] = new[f]
                tl[f, t.at, :] = values[f]

        tiles(1, part.shape[2], body)


def edges_kernel(prm, part, low, high, ide, edge, tl0, tl7):
    edges_body(prm, "fine", part, low, high, ide, edge, tl0, tl7)


def coarse_edges_kernel(own, prm, part, low, high, ide, old, *refs):
    edge, tl0, tl7 = refs[-3:]

    @pl.when(own[0] != 0)
    def _():
        edges_body(prm, "coarse", part, low, high, ide, edge, tl0, tl7)

    @pl.when(own[0] == 0)
    def _():
        edge[...] = old[...]


def base_kernel(prm, h, c, sm, sn, sx, ids, km, kn, kx):
    tab = Tables(prm)
    first = {"m": sm, "n": sn, "x": sx}
    outs = {"m": km, "n": kn, "x": kx}

    def body(name, i, r, t):
        ratio = Cells(tab, ids[r, t.at, :]).ratio()
        for f, u in enumerate((h[r, t.at, :], c[r, t.at, :])):
            outs[name][f, i, t.at, :] = u + ratio[f] * (first[name][f, i, t.at, :] - u)

    Parts(sm.shape[1]).each(h.shape[1], body)


def coarse_body(prm, arrived, base, old, ids, put, which, pad, edge_less):
    tab = Tables(prm)
    mid, ny = arrived["m"].shape[1], arrived["m"].shape[2]
    block = Parts(mid)
    clear_rims(pad)
    if edge_less:
        clear_ends(pad)

    def at(ref, i, t):
        return [ref[f, i, t.at, :] for f in F2]

    def melt(name, i, r, t):
        put_melt(tab, pad, r + 1, t, ids[r, t.at, :], *at(arrived[name], i, t))

    def update(name, i, r, t):
        new = coarse(tab, pad, r + 1, t, ids[r, t.at, :], at(arrived[name], i, t))
        end, start = at(old[name], i, t), at(base[name], i, t)
        for f in F2:
            put(name, f, i, r, t, new[f] + (end[f] - start[f]))

    block.each(ny, melt, arrived)
    block.each(ny, update, which)


def into(outs):
    def put(name, f, i, r, t, value):
        outs[name][f, i, t.at, :] = value

    return put


def coarse_mid_kernel(own, prm, am, an, km, ids, om, nm, pad):
    @pl.when(own[0] != 0)
    def _():
        coarse_body(
            prm, {"n": an, "m": am}, {"m": km}, {"m": om}, ids, into({"m": nm}), "m", pad, False
        )

    @pl.when(own[0] == 0)
    def _():
        nm[...] = om[...]


def coarse_rim_kernel(own, prm, am, an, ax, kn, kx, ids, on, ox, nn, part, pad):
    @pl.when(own[0] != 0)
    def _():
        coarse_body(
            prm,
            {"x": ax, "n": an, "m": am},
            {"n": kn, "x": kx},
            {"n": on, "x": ox},
            ids,
            into({"n": nn, "x": part}),
            "xn",
            pad,
            True,
        )

    @pl.when(own[0] == 0)
    def _():
        nn[...] = on[...]


def coarse_inner_kernel(own, prm, am, an, ax, km, kn, kx, ids, om, on, ox, nm, nn, part, pad):
    @pl.when(own[0] != 0)
    def _():
        coarse_body(
            prm,
            {"x": ax, "n": an, "m": am},
            {"m": km, "n": kn, "x": kx},
            {"m": om, "n": on, "x": ox},
            ids,
            into({"m": nm, "n": nn, "x": part}),
            "mnx",
            pad,
            True,
        )

    @pl.when(own[0] == 0)
    def _():
        nm[...] = om[...]
        nn[...] = on[...]


def last_rows_kernel(own, prm, am, an, ax, km, kn, kx, ids, om, on, ox, oh, oc, pad):
    out = (oh, oc)

    @pl.when(own[0] != 0)
    def _():
        def put(name, f, i, r, t, value):
            out[f][0, r, t.at, :] = value

        coarse_body(
            prm,
            {"x": ax, "n": an, "m": am},
            {"m": km, "n": kn, "x": kx},
            {"m": om, "n": on, "x": ox},
            ids,
            put,
            "mnx",
            pad,
            True,
        )

    @pl.when(own[0] == 0)
    def _():
        old = {"m": om, "n": on, "x": ox}

        def body(name, i, r, t):
            for f in F2:
                out[f][0, r, t.at, :] = old[name][f, i, t.at, :]

        Parts(om.shape[1]).each(om.shape[2], body)


def last_edges_kernel(own, prm, low, high, ide, oh, oc, nh, nc):
    first = pl.program_id(0) == 0

    @pl.when(own[0] != 0)
    def _():
        tab = Tables(prm)

        def body(i, t):
            rate = Cells(tab, ide[0, t.at, :]).coarse()
            for f, (old, new) in enumerate(((oh, nh), (oc, nc))):
                halo = jnp.where(first, low[f, t.at, :], high[f, t.at, :])
                new[0, 0, t.at, :] = old[0, 0, t.at, :] + rate[f] * halo

        tiles(1, ide.shape[1], body)

    @pl.when(own[0] == 0)
    def _():
        nh[...] = oh[...]
        nc[...] = oc[...]


def f32(*shape):
    return jax.ShapeDtypeStruct(shape, jnp.float32)


def i32(*shape):
    return jax.ShapeDtypeStruct(shape, jnp.int32)


TINY = pl.CostEstimate(flops=1000, bytes_accessed=1000, transcendentals=0)


def call(kernel, outs, args, smem, name, scratch=(), limit=8, after=(), through=()):
    after = (*after, *through)
    first = len(args) + len(after) - len(through)
    run = kernel
    if after:
        count = len(args)

        def run(*refs):
            kernel(*refs[:count], *refs[count + len(after) + len(through) :])

    return pl.pallas_call(
        run,
        out_shape=[f32(*x.shape) for x in through] + list(outs),
        in_specs=[SMEM] * smem + [VMEM] * (len(args) - smem) + [ANY] * len(after),
        out_specs=[ANY] * len(through) + [VMEM] * len(outs),
        input_output_aliases={first + i: i for i in range(len(through))},
        scratch_shapes=scratch,
        compiler_params=pltpu.CompilerParams(vmem_limit_bytes=limit * MIB),
        cost_estimate=TINY,
        name=name,
    )(*args, *after)


def per_device(slices, parts, enthalpy, solute, material, phase_flag, *params):
    rows, ny, nz = material.shape
    mid = rows - 4
    h0 = enthalpy.reshape(rows, ny, nz)
    c0 = solute.reshape(rows, ny, nz)
    prm = jnp.concatenate(params)
    slot = lax.axis_index("tm")
    pair, tall = f32(2, 2, ny, nz), f32(2, mid, ny, nz)
    halo = f32(2, ny, nz)
    pad = [pltpu.VMEM((2, rows + 2, ny + 16, nz), jnp.float32)]

    def move(x, tms, up, by):
        pairs = [
            (t * parts + s, (t + up) * parts + s + by)
            for t in tms
            for s in range(parts)
            if 0 <= s + by < parts
        ]
        return lax.ppermute(x, ("tm", "space"), pairs)

    def halos(tl0, tl7, tms, up):
        return move(tl7, tms, up, 1), move(tl0, tms, up, -1)

    def send(x, n):
        return move(x, (n - 1,), 1, 0)

    def own(n):
        return (slot == n).astype(jnp.int32).reshape(1)

    def gridded(kernel, steps, outs, out_specs, in_specs, args, name, aliases={}):
        return pl.pallas_call(
            kernel,
            grid=(steps,),
            out_shape=outs,
            in_specs=in_specs,
            out_specs=out_specs,
            input_output_aliases=aliases,
            compiler_params=pltpu.CompilerParams(vmem_limit_bytes=8 * MIB),
            cost_estimate=TINY,
            name=name,
        )(*args)

    edge_row = pl.BlockSpec((1, ny, nz), lambda i: ((rows - 1) * i, 0, 0))
    whole = pl.BlockSpec((2, ny, nz), lambda i: (0, 0, 0))
    far = [pltpu.with_memory_space_constraint(x, pltpu.HBM) for x in (h0, c0, material)]
    tl0, tl7 = gridded(
        first_edges_kernel,
        2,
        [halo] * 2,
        [whole] * 2,
        [SMEM] + [edge_row] * 3,
        (prm, *far),
        "first_edges",
    )
    every = range(slices)
    low, high = halos(tl0, tl7, every, 0)
    sm, sn, part, ids, ide = call(
        first_step_kernel,
        [tall, pair, pair, i32(rows, ny, nz), i32(2, ny, nz)],
        (prm, h0, c0, material, phase_flag),
        1,
        "first_step",
        pad,
        26,
    )

    def fine_edges(part, low, high, after=()):
        return call(
            edges_kernel, [pair, halo, halo], (prm, part, low, high, ide), 1, "edges", after=after
        )

    base = ()
    for k in range(STEPS - 1):
        sx, tl0, tl7 = fine_edges(part, low, high, base)
        low, high = halos(tl0, tl7, every, 0)
        if k == 0:
            base = call(
                base_kernel,
                [tall, pair, pair],
                (prm, h0, c0, sm, sn, sx, ids),
                1,
                "base",
                limit=16,
            )
        if k == STEPS - 3:
            *sm, sn, part = call(
                step_apart_kernel,
                [f32(mid, ny, nz)] * 2 + [pair, pair],
                (prm, sm, sn, sx, ids),
                1,
                "step_apart",
                pad,
                18,
            )
        elif k == STEPS - 2:
            last = (*sm, sn, sx)
            sm, sn, part = call(
                step_joined_kernel,
                [tall, pair, pair],
                (prm, *sm, sn, sx, ids),
                1,
                "step_joined",
                pad,
                18,
            )
        else:
            sm, sn, part = call(
                step_kernel, [tall, pair, pair], (prm, sm, sn, sx, ids), 1, "step", pad, 18
            )
    km, kn, kx = base

    am, an = call(
        replay_kernel,
        [tall, pair],
        (own(1), prm, *(send(x, 1) for x in last), ids),
        2,
        "replay",
        pad,
        18,
    )
    vm, vn = (
        call(
            coarse_mid_kernel,
            [tall],
            (own(1), prm, am, an, km, ids, sm),
            2,
            "coarse_mid",
            pad,
            18,
        )[0],
        sn,
    )
    vx, tl0, tl7 = fine_edges(part, low, high, (vm,))
    for n in range(1, slices):
        low, high = halos(tl0, tl7, (n - 1,), 1)
        ax = send(vx, n)
        if n > 1:
            am, an = send(vm, n), send(vn, n)
        if n == slices - 1:
            break
        if n == 1:
            vn, part = call(
                coarse_rim_kernel,
                [pair, pair],
                (own(n), prm, am, an, ax, kn, kx, ids, vn, vx),
                2,
                "coarse_rim",
                pad,
                20,
            )
        else:
            vm, vn, part = call(
                coarse_inner_kernel,
                [tall, pair, pair],
                (own(n), prm, am, an, ax, km, kn, kx, ids, vm, vn, vx),
                2,
                "coarse_inner",
                pad,
                26,
            )
        *passed, vx, tl0, tl7 = call(
            coarse_edges_kernel,
            [pair, halo, halo],
            (own(n), prm, part, low, high, ide, vx),
            2,
            "coarse_edges",
            through=(vm, vn) if n > 1 else (),
        )
        if n > 1:
            vm, vn = passed

    out = f32(1, rows, ny, nz)
    last_own = own(slices - 1)
    oh, oc = call(
        last_rows_kernel,
        [out, out],
        (last_own, prm, am, an, ax, km, kn, kx, ids, vm, vn, vx),
        2,
        "last_rows",
        pad,
        28,
    )
    out_row = pl.BlockSpec((1, 1, ny, nz), lambda i: (0, (rows - 1) * i, 0, 0))
    one = pl.BlockSpec((1, ny, nz), lambda i: (i, 0, 0))
    return tuple(
        gridded(
            last_edges_kernel,
            2,
            [out, out],
            [out_row] * 2,
            [SMEM, SMEM, whole, whole, one, out_row, out_row],
            (last_own, prm, low, high, ide, oh, oc),
            "last_edges",
            {5: 0, 6: 1},
        )
    )


def solution(mesh):
    body = functools.partial(per_device, mesh.shape["tm"], mesh.shape["space"])
    return jax.shard_map(
        body,
        mesh=mesh,
        in_specs=(
            P("tm", "space", None, None),
            P("tm", "space", None, None),
            P("space", None, None),
            P("space", None, None),
        )
        + (P(),) * 7,
        out_specs=(P("tm", "space", None, None), P("tm", "space", None, None)),
        check_vma=False,
    )
```

profile of v0, /device:TPU:11, one launch (start us, length us, event | category | flops | bytes accessed | tf_op | source)
XLA Modules:
  0.0 228.4 jit_solution(17669076658030261446)
XLA Ops:
  1.5 2.3 %first_edges.1 = (f32[2,512,128]{2,1,0:T(8,128)S(1)}, f32[2,512,128]{2,1,0:T(8,128)S(1)}) custom-call(f32[27]{0:T(128)S(1)} %concatenate.3.prm.refs_0_.refs_1_, f32[8,512,128]{2,1,0:T(8,128)} %bitcast.5, f32[8,512,128]{2,1,0:T(8,128)} %bitcast.8, s32[8,512,128]{2,1,0:T(8,128)} %mat.3), custom_call_target="tpu_custom_call" | custom-call | flops 1000 | bytes 1000 | tf_op jit(solution)/shard_map/first_edges/pallas_call | solution.py:492
  3.8 3.1 %collective-permute-start = (f32[2,512,128]{2,1,0:T(8,128)S(1)}, f32[2,512,128]{2,1,0:T(8,128)S(1)}, u32[]{:S(2)}, u32[]{:S(2)}) collective-permute-start(f32[2,512,128]{2,1,0:T(8,128)S(1)} %get-tuple-element.54), channel_id=1, source_target_pairs={{0,1},{1,2},{2,3},{3,4},{4,5},{5,6},{6,7},{8,9},{9,10},{10,11},{11... | collective-permute-start | bytes 1572872 | tf_op jit(solution)/shard_map/ppermute | solution.py:480
  7.0 3.0 %collective-permute-start.1 = (f32[2,512,128]{2,1,0:T(8,128)S(1)}, f32[2,512,128]{2,1,0:T(8,128)S(1)}, u32[]{:S(2)}, u32[]{:S(2)}) collective-permute-start(f32[2,512,128]{2,1,0:T(8,128)S(1)} %get-tuple-element.55), channel_id=1, source_target_pairs={{1,0},{2,1},{3,2},{4,3},{5,4},{6,5},{7,6},{9,8},{10,9},{11,10},{12... | collective-permute-start | bytes 1572872 | tf_op jit(solution)/shard_map/ppermute | solution.py:480
  11.6 7.1 %first_step.1 = (f32[2,4,512,128]{3,2,1,0:T(8,128)S(1)}, f32[2,2,512,128]{3,2,1,0:T(8,128)S(1)}, f32[2,2,512,128]{3,2,1,0:T(8,128)S(1)}, s32[8,512,128]{2,1,0:T(8,128)S(1)}, s32[2,512,128]{2,1,0:T(8,128)S(1)}) custom-call(f32[27]{0:T(128)S(1)} %concatenate.3.prm.refs_0_.refs_1_, f32[8,512,128]{2,1,0:T(8,128)S(1)} %bitcast.6, f32[8,512,128]{2,1,0:T(8,128)S(1)} %bitcast.9, ...), custom_call_target="tpu_custom_call" | custom-call | flops 1000 | bytes 1000 | tf_op jit(solution)/shard_map/first_step/pallas_call | solution.py:449
  18.7 10.0 %collective-permute-done.low = f32[2,512,128]{2,1,0:T(8,128)S(1)} collective-permute-done((f32[2,512,128]{2,1,0:T(8,128)S(1)}, f32[2,512,128]{2,1,0:T(8,128)S(1)}, u32[]{:S(2)}, u32[]{:S(2)}) %collective-permute-start) | collective-permute-done | bytes 524320 | tf_op jit(solution)/shard_map/ppermute | solution.py:480
  28.8 2.9 %collective-permute-done.1.high = f32[2,512,128]{2,1,0:T(8,128)S(1)} collective-permute-done((f32[2,512,128]{2,1,0:T(8,128)S(1)}, f32[2,512,128]{2,1,0:T(8,128)S(1)}, u32[]{:S(2)}, u32[]{:S(2)}) %collective-permute-start.1) | collective-permute-done | bytes 524320 | tf_op jit(solution)/shard_map/ppermute | solution.py:480
  33.0 1.9 collective-permute-start.2
  35.0 4.3 %collective-permute-start.3 = (f32[2,512,128]{2,1,0:T(8,128)S(1)}, f32[2,512,128]{2,1,0:T(8,128)S(1)}, u32[]{:S(2)}, u32[]{:S(2)}) collective-permute-start(f32[2,512,128]{2,1,0:T(8,128)S(1)} %get-tuple-element.63), channel_id=1, source_target_pairs={{1,0},{2,1},{3,2},{4,3},{5,4},{6,5},{7,6},{9,8},{10,9},{11,10},{12... | collective-permute-start | bytes 1572872 | tf_op jit(solution)/shard_map/ppermute | solution.py:480
  39.2 3.3 %base.1 = (f32[2,4,512,128]{3,2,1,0:T(8,128)S(1)}, f32[2,2,512,128]{3,2,1,0:T(8,128)S(1)}, f32[2,2,512,128]{3,2,1,0:T(8,128)S(1)}) custom-call(f32[27]{0:T(128)S(1)} %concatenate.3.prm.refs_0_.refs_1_, f32[8,512,128]{2,1,0:T(8,128)S(1)} %bitcast.7, f32[8,512,128]{2,1,0:T(8,128)S(1)} %bitcast.10, f32[2,4,512,128]{3,2,1,0:T(8,128)S(1)} %get-tuple-element.51.sm, ...), custom_call_target="tpu_custom_call" | custom-call | flops 1000 | bytes 1000 | tf_op jit(solution)/shard_map/base/pallas_call | solution.py:449
  42.5 6.9 %step.1 = (f32[2,4,512,128]{3,2,1,0:T(8,128)S(1)}, f32[2,2,512,128]{3,2,1,0:T(8,128)S(1)}, f32[2,2,512,128]{3,2,1,0:T(8,128)S(1)}) custom-call(f32[27]{0:T(128)S(1)} %concatenate.3.prm.refs_0_.refs_1_, f32[2,4,512,128]{3,2,1,0:T(8,128)S(1)} %get-tuple-element.51.sm, f32[2,2,512,128]{3,2,1,0:T(8,128)S(1)} %get-tuple-element.52.sn, ...), custom_call_target="tpu_custom_call" | custom-call | flops 1000 | bytes 1000 | tf_op jit(solution)/shard_map/step/pallas_call | solution.py:449
  49.4 7.2 %collective-permute-done.2.refs_2_ = f32[2,512,128]{2,1,0:T(8,128)S(1)} collective-permute-done((f32[2,512,128]{2,1,0:T(8,128)S(1)}, f32[2,512,128]{2,1,0:T(8,128)S(1)}, u32[]{:S(2)}, u32[]{:S(2)}) %collective-permute-start.2) | collective-permute-done | bytes 524320 | tf_op jit(solution)/shard_map/ppermute | solution.py:480
  56.6 4.3 %collective-permute-done.3.refs_3_ = f32[2,512,128]{2,1,0:T(8,128)S(1)} collective-permute-done((f32[2,512,128]{2,1,0:T(8,128)S(1)}, f32[2,512,128]{2,1,0:T(8,128)S(1)}, u32[]{:S(2)}, u32[]{:S(2)}) %collective-permute-start.3) | collective-permute-done | bytes 524320 | tf_op jit(solution)/shard_map/ppermute | solution.py:480
  64.2 4.3 %collective-permute-start.8 = (f32[2,512,128]{2,1,0:T(8,128)S(1)}, f32[2,512,128]{2,1,0:T(8,128)S(1)}, u32[]{:S(2)}, u32[]{:S(2)}) collective-permute-start(f32[2,512,128]{2,1,0:T(8,128)S(1)} %get-tuple-element.73), channel_id=1, source_target_pairs={{1,0},{2,1},{3,2},{4,3},{5,4},{6,5},{7,6},{9,8},{10,9},{11,10},{12... | collective-permute-start | bytes 1572872 | tf_op jit(solution)/shard_map/ppermute | solution.py:480
  68.5 7.9 %step_apart.1 = (f32[4,512,128]{2,1,0:T(8,128)S(1)}, f32[4,512,128]{2,1,0:T(8,128)}, f32[2,2,512,128]{3,2,1,0:T(8,128)}, f32[2,2,512,128]{3,2,1,0:T(8,128)S(1)}) custom-call(f32[27]{0:T(128)S(1)} %concatenate.3.prm.refs_0_.refs_1_, f32[2,4,512,128]{3,2,1,0:T(8,128)S(1)} %get-tuple-element.59.sm, f32[2,2,512,128]{3,2,1,0:T(8,128)S(1)} %get-tuple-element.60.sn, ...), custom_call_target="tpu_custom_call" | custom-call | flops 1000 | bytes 1000 | tf_op jit(solution)/shard_map/step_apart/pallas_call | solution.py:449
  80.5 6.1 %collective-permute-done.7.refs_2_ = f32[2,512,128]{2,1,0:T(8,128)S(1)} collective-permute-done((f32[2,512,128]{2,1,0:T(8,128)S(1)}, f32[2,512,128]{2,1,0:T(8,128)S(1)}, u32[]{:S(2)}, u32[]{:S(2)}) %collective-permute-start.7) | collective-permute-done | bytes 524320 | tf_op jit(solution)/shard_map/ppermute | solution.py:480
  86.6 3.6 %collective-permute-done.8.refs_3_ = f32[2,512,128]{2,1,0:T(8,128)S(1)} collective-permute-done((f32[2,512,128]{2,1,0:T(8,128)S(1)}, f32[2,512,128]{2,1,0:T(8,128)S(1)}, u32[]{:S(2)}, u32[]{:S(2)}) %collective-permute-start.8) | collective-permute-done | bytes 524320 | tf_op jit(solution)/shard_map/ppermute | solution.py:480
  90.2 2.5 %edges.6 = (f32[2,2,512,128]{3,2,1,0:T(8,128)}, f32[2,512,128]{2,1,0:T(8,128)}, f32[2,512,128]{2,1,0:T(8,128)}) custom-call(f32[27]{0:T(128)S(1)} %concatenate.3.prm.refs_0_.refs_1_, f32[2,2,512,128]{3,2,1,0:T(8,128)S(1)} %get-tuple-element.71.refs_1_, f32[2,512,128]{2,1,0:T(8,128)S(1)} %collective-permute-done.7.refs_2_, ...), custom_call_target="tpu_custom_call" | custom-call | flops 1000 | bytes 1000 | tf_op jit(solution)/shard_map/edges/pallas_call | solution.py:449
  97.3 4.2 %collective-permute-start.12 = (f32[2,512,128]{2,1,0:T(8,128)}, f32[2,512,128]{2,1,0:T(8,128)}, u32[]{:S(2)}, u32[]{:S(2)}) collective-permute-start(f32[2,512,128]{2,1,0:T(8,128)} %get-tuple-element.80), channel_id=1, source_target_pairs={{1,0},{2,1},{3,2},{4,3},{5,4},{6,5},{7,6},{9,8},{10,9},{11,10},{12... | collective-permute-start | bytes 1572872 | tf_op jit(solution)/shard_map/ppermute | solution.py:480
  102.8 8.1 %step_joined.1 = (f32[2,4,512,128]{3,2,1,0:T(8,128)S(1)}, f32[2,2,512,128]{3,2,1,0:T(8,128)S(1)}, f32[2,2,512,128]{3,2,1,0:T(8,128)S(1)}) custom-call(f32[27]{0:T(128)S(1)} %concatenate.3.prm.refs_0_.refs_1_, f32[4,512,128]{2,1,0:T(8,128)S(1)} %copy-done.17, f32[4,512,128]{2,1,0:T(8,128)} %get-tuple-element.69.mc, f32[2,2,512,128]{3,2,1,0:T(8,128)} %get-tuple-element.70.sn, ...), custom_call_target="tpu_custom_call" | custom-call | flops 1000 | bytes 1000 | tf_op jit(solution)/shard_map/step_joined/pallas_call | solution.py:449
  111.0 2.0 replay.1
  113.5 2.0 coarse_mid.1.refs_5_.om
  115.6 3.4 %collective-permute-done.11.refs_2_ = f32[2,512,128]{2,1,0:T(8,128)} collective-permute-done((f32[2,512,128]{2,1,0:T(8,128)}, f32[2,512,128]{2,1,0:T(8,128)}, u32[]{:S(2)}, u32[]{:S(2)}) %collective-permute-start.11) | collective-permute-done | bytes 524320 | tf_op jit(solution)/shard_map/ppermute | solution.py:480
  118.9 3.6 %collective-permute-done.12.refs_3_ = f32[2,512,128]{2,1,0:T(8,128)} collective-permute-done((f32[2,512,128]{2,1,0:T(8,128)}, f32[2,512,128]{2,1,0:T(8,128)}, u32[]{:S(2)}, u32[]{:S(2)}) %collective-permute-start.12) | collective-permute-done | bytes 524320 | tf_op jit(solution)/shard_map/ppermute | solution.py:480
  122.5 2.1 edges.7
  125.4 2.0 collective-permute-start.10
  130.7 2.0 coarse_edges.2
  141.6 5.4 %coarse_inner.1 = (f32[2,4,512,128]{3,2,1,0:T(8,128)}, f32[2,2,512,128]{3,2,1,0:T(8,128)}, f32[2,2,512,128]{3,2,1,0:T(8,128)S(1)}) custom-call(s32[1]{0:T(128)} %bitcast.1.own.refs_0_, f32[27]{0:T(128)S(1)} %concatenate.3.prm.refs_0_.refs_1_, f32[2,4,512,128]{3,2,1,0:T(8,128)} %collective-permute-done.10.am, f32[2,2,512,128]{3,2,1,0:T(8,128)} %collective-permute-done.14.an, ...), custom_call_target="tpu_custom_call" | custom-call | flops 1000 | bytes 1000 | tf_op jit(solution)/shard_map/coarse_inner/pallas_call | solution.py:449
  147.1 3.0 %coarse_edges.3 = (f32[2,4,512,128]{3,2,1,0:T(8,128)}, f32[2,2,512,128]{3,2,1,0:T(8,128)}, f32[2,2,512,128]{3,2,1,0:T(8,128)}, f32[2,512,128]{2,1,0:T(8,128)}, f32[2,512,128]{2,1,0:T(8,128)}) custom-call(s32[1]{0:T(128)} %bitcast.1.own.refs_0_, f32[27]{0:T(128)S(1)} %concatenate.3.prm.refs_0_.refs_1_, ...), custom_call_target="tpu_custom_call", output_to_operand_aliasing={{0}: (7, {}), {1}: (8, {})} | custom-call | flops 1000 | bytes 1000 | tf_op jit(solution)/shard_map/coarse_edges/pallas_call | solution.py:449
  156.5 51.4 %collective-permute-done.23.an = f32[2,2,512,128]{3,2,1,0:T(8,128)} collective-permute-done((f32[2,2,512,128]{3,2,1,0:T(8,128)}, f32[2,2,512,128]{3,2,1,0:T(8,128)}, u32[]{:S(2)}, u32[]{:S(2)}) %collective-permute-start.23) | collective-permute-done | bytes 1048608 | tf_op jit(solution)/shard_map/ppermute | solution.py:480
  207.9 1.9 collective-permute-done.24.ax
  212.7 12.7 %last_rows.1 = (f32[1,8,512,128]{3,2,1,0:T(8,128)}, f32[1,8,512,128]{3,2,1,0:T(8,128)}) custom-call(s32[1]{0:T(128)} %bitcast.own, f32[27]{0:T(128)S(1)} %concatenate.3.prm.refs_0_.refs_1_, f32[2,4,512,128]{3,2,1,0:T(8,128)} %collective-permute-done.22.am, f32[2,2,512,128]{3,2,1,0:T(8,128)} %collective-permute-done.23.an, ...), custom_call_target="tpu_custom_call" | custom-call | flops 1000 | bytes 1000 | tf_op jit(solution)/shard_map/last_rows/pallas_call | solution.py:449
  225.4 2.9 %last_edges.1 = (f32[1,8,512,128]{3,2,1,0:T(8,128)}, f32[1,8,512,128]{3,2,1,0:T(8,128)}) custom-call(s32[1]{0:T(128)} %bitcast.own, f32[27]{0:T(128)S(1)} %concatenate.3.prm.refs_0_.refs_1_, f32[2,512,128]{2,1,0:T(8,128)} %collective-permute-done.20.low, f32[2,512,128]{2,1,0:T(8,128)} %collective-permute-done.21.high, ...), custom_call_target="tpu_custom_call", output_to_operand_aliasing={{0}: (5, {}), {1}: (6, {})} | custom-call | flops 1000 | bytes 1000 | tf_op jit(solution)/shard_map/last_edges/pallas_call | solution.py:492
  (77 shorter events, 39.6 us)
Async XLA Ops:
  1.5 8.6 %copy-start.14 = (s32[8,512,128]{2,1,0:T(8,128)S(1)}, s32[8,512,128]{2,1,0:T(8,128)}, u32[]{:S(2)}) copy-start(s32[8,512,128]{2,1,0:T(8,128)} %mat.3) | copy-start | bytes 6291460
  3.8 25.0 %collective-permute-start = (f32[2,512,128]{2,1,0:T(8,128)S(1)}, f32[2,512,128]{2,1,0:T(8,128)S(1)}, u32[]{:S(2)}, u32[]{:S(2)}) collective-permute-start(f32[2,512,128]{2,1,0:T(8,128)S(1)} %get-tuple-element.54), channel_id=1, source_target_pairs={{0,1},{1,2},{2,3},{3,4},{4,5},{5,6},{6,7},{8,9},{9,10},{10,11},{11... | collective-permute-start | bytes 1572872 | tf_op jit(solution)/shard_map/ppermute | solution.py:480
  7.0 24.7 %collective-permute-start.1 = (f32[2,512,128]{2,1,0:T(8,128)S(1)}, f32[2,512,128]{2,1,0:T(8,128)S(1)}, u32[]{:S(2)}, u32[]{:S(2)}) collective-permute-start(f32[2,512,128]{2,1,0:T(8,128)S(1)} %get-tuple-element.55), channel_id=1, source_target_pairs={{1,0},{2,1},{3,2},{4,3},{5,4},{6,5},{7,6},{9,8},{10,9},{11,10},{12... | collective-permute-start | bytes 1572872 | tf_op jit(solution)/shard_map/ppermute | solution.py:480
  18.7 71.5 %copy-start.8 = (s32[2,512,128]{2,1,0:T(8,128)}, s32[2,512,128]{2,1,0:T(8,128)S(1)}, u32[]{:S(2)}) copy-start(s32[2,512,128]{2,1,0:T(8,128)S(1)} %get-tuple-element.56.ide.refs_4_.refs_5_) | copy-start | bytes 1572868
  33.0 23.6 %collective-permute-start.2 = (f32[2,512,128]{2,1,0:T(8,128)S(1)}, f32[2,512,128]{2,1,0:T(8,128)S(1)}, u32[]{:S(2)}, u32[]{:S(2)}) collective-permute-start(f32[2,512,128]{2,1,0:T(8,128)S(1)} %get-tuple-element.62), channel_id=1, source_target_pairs={{0,1},{1,2},{2,3},{3,4},{4,5},{5,6},{6,7},{8,9},{9,10},{10,11},{11... | collective-permute-start | bytes 1572872 | tf_op jit(solution)/shard_map/ppermute | solution.py:480
  35.0 26.0 %collective-permute-start.3 = (f32[2,512,128]{2,1,0:T(8,128)S(1)}, f32[2,512,128]{2,1,0:T(8,128)S(1)}, u32[]{:S(2)}, u32[]{:S(2)}) collective-permute-start(f32[2,512,128]{2,1,0:T(8,128)S(1)} %get-tuple-element.63), channel_id=1, source_target_pairs={{1,0},{2,1},{3,2},{4,3},{5,4},{6,5},{7,6},{9,8},{10,9},{11,10},{12... | collective-permute-start | bytes 1572872 | tf_op jit(solution)/shard_map/ppermute | solution.py:480
  42.5 47.7 %copy-start = (f32[2,4,512,128]{3,2,1,0:T(8,128)}, f32[2,4,512,128]{3,2,1,0:T(8,128)S(1)}, u32[]{:S(2)}) copy-start(f32[2,4,512,128]{3,2,1,0:T(8,128)S(1)} %get-tuple-element.64.refs_5_.km) | copy-start | bytes 6291460
  42.5 47.7 %copy-start.4 = (f32[2,2,512,128]{3,2,1,0:T(8,128)}, f32[2,2,512,128]{3,2,1,0:T(8,128)S(1)}, u32[]{:S(2)}) copy-start(f32[2,2,512,128]{3,2,1,0:T(8,128)S(1)} %get-tuple-element.66.refs_7_.kx) | copy-start | bytes 3145732
  62.3 24.3 %collective-permute-start.7 = (f32[2,512,128]{2,1,0:T(8,128)S(1)}, f32[2,512,128]{2,1,0:T(8,128)S(1)}, u32[]{:S(2)}, u32[]{:S(2)}) collective-permute-start(f32[2,512,128]{2,1,0:T(8,128)S(1)} %get-tuple-element.72), channel_id=1, source_target_pairs={{0,1},{1,2},{2,3},{3,4},{4,5},{5,6},{6,7},{8,9},{9,10},{10,11},{11... | collective-permute-start | bytes 1572872 | tf_op jit(solution)/shard_map/ppermute | solution.py:480
  64.2 26.0 %collective-permute-start.8 = (f32[2,512,128]{2,1,0:T(8,128)S(1)}, f32[2,512,128]{2,1,0:T(8,128)S(1)}, u32[]{:S(2)}, u32[]{:S(2)}) collective-permute-start(f32[2,512,128]{2,1,0:T(8,128)S(1)} %get-tuple-element.73), channel_id=1, source_target_pairs={{1,0},{2,1},{3,2},{4,3},{5,4},{6,5},{7,6},{9,8},{10,9},{11,10},{12... | collective-permute-start | bytes 1572872 | tf_op jit(solution)/shard_map/ppermute | solution.py:480
  76.4 16.3 %copy-start.16 = (f32[4,512,128]{2,1,0:T(8,128)}, f32[4,512,128]{2,1,0:T(8,128)S(1)}, u32[]{:S(2)}) copy-start(f32[4,512,128]{2,1,0:T(8,128)S(1)} %get-tuple-element.68.mh) | copy-start | bytes 3145732
  76.4 19.9 %collective-permute-start.4 = (f32[4,512,128]{2,1,0:T(8,128)S(1)}, f32[4,512,128]{2,1,0:T(8,128)S(1)}, u32[]{:S(2)}, u32[]{:S(2)}) collective-permute-start(f32[4,512,128]{2,1,0:T(8,128)S(1)} %get-tuple-element.68.mh), channel_id=1, source_target_pairs={{0,8},{1,9},{2,10},{3,11},{4,12},{5,13},{6,14},{7,15}} | collective-permute-start | bytes 3145736 | tf_op jit(solution)/shard_map/ppermute | solution.py:480
  77.1 33.8 %collective-permute-start.5 = (f32[4,512,128]{2,1,0:T(8,128)}, f32[4,512,128]{2,1,0:T(8,128)}, u32[]{:S(2)}, u32[]{:S(2)}) collective-permute-start(f32[4,512,128]{2,1,0:T(8,128)} %get-tuple-element.69.mc), channel_id=1, source_target_pairs={{0,8},{1,9},{2,10},{3,11},{4,12},{5,13},{6,14},{7,15}} | collective-permute-start | bytes 3145736 | tf_op jit(solution)/shard_map/ppermute | solution.py:480
  78.8 32.1 %collective-permute-start.6 = (f32[2,2,512,128]{3,2,1,0:T(8,128)}, f32[2,2,512,128]{3,2,1,0:T(8,128)}, u32[]{:S(2)}, u32[]{:S(2)}) collective-permute-start(f32[2,2,512,128]{3,2,1,0:T(8,128)} %get-tuple-element.70.sn), channel_id=1, source_target_pairs={{0,8},{1,9},{2,10},{3,11},{4,12},{5,13},{6,14},{7,15}} | collective-permute-start | bytes 3145736 | tf_op jit(solution)/shard_map/ppermute | solution.py:480
  92.7 18.3 %collective-permute-start.9 = (f32[2,2,512,128]{3,2,1,0:T(8,128)}, f32[2,2,512,128]{3,2,1,0:T(8,128)}, u32[]{:S(2)}, u32[]{:S(2)}) collective-permute-start(f32[2,2,512,128]{3,2,1,0:T(8,128)} %get-tuple-element.74.sx), channel_id=1, source_target_pairs={{0,8},{1,9},{2,10},{3,11},{4,12},{5,13},{6,14},{7,15}} | collective-permute-start | bytes 3145736 | tf_op jit(solution)/shard_map/ppermute | solution.py:480
  94.4 24.6 %collective-permute-start.11 = (f32[2,512,128]{2,1,0:T(8,128)}, f32[2,512,128]{2,1,0:T(8,128)}, u32[]{:S(2)}, u32[]{:S(2)}) collective-permute-start(f32[2,512,128]{2,1,0:T(8,128)} %get-tuple-element.79), channel_id=1, source_target_pairs={{0,1},{1,2},{2,3},{3,4},{4,5},{5,6},{6,7},{8,9},{9,10},{10,11},{11... | collective-permute-start | bytes 1572872 | tf_op jit(solution)/shard_map/ppermute | solution.py:480
  97.3 25.2 %collective-permute-start.12 = (f32[2,512,128]{2,1,0:T(8,128)}, f32[2,512,128]{2,1,0:T(8,128)}, u32[]{:S(2)}, u32[]{:S(2)}) collective-permute-start(f32[2,512,128]{2,1,0:T(8,128)} %get-tuple-element.80), channel_id=1, source_target_pairs={{1,0},{2,1},{3,2},{4,3},{5,4},{6,5},{7,6},{9,8},{10,9},{11,10},{12... | collective-permute-start | bytes 1572872 | tf_op jit(solution)/shard_map/ppermute | solution.py:480
  113.5 9.0 %copy-start.9 = (s32[2,512,128]{2,1,0:T(8,128)S(1)}, s32[2,512,128]{2,1,0:T(8,128)}, u32[]{:S(2)}) copy-start(s32[2,512,128]{2,1,0:T(8,128)} %copy-done.8) | copy-start | bytes 1572868
  124.7 4.2 %collective-permute-start.13 = (f32[2,2,512,128]{3,2,1,0:T(8,128)S(1)}, f32[2,2,512,128]{3,2,1,0:T(8,128)S(1)}, u32[]{:S(2)}, u32[]{:S(2)}) collective-permute-start(f32[2,2,512,128]{3,2,1,0:T(8,128)S(1)} %get-tuple-element.81.ox.old), channel_id=1, source_target_pairs={{0,8},{1,9},{2,10},{3,11},{4,12},{5,13},{6,14},{7,15}} | collective-permute-start | bytes 3145736 | tf_op jit(solution)/shard_map/ppermute | solution.py:480
  125.4 13.4 %collective-permute-start.10 = (f32[2,4,512,128]{3,2,1,0:T(8,128)}, f32[2,4,512,128]{3,2,1,0:T(8,128)}, u32[]{:S(2)}, u32[]{:S(2)}) collective-permute-start(f32[2,4,512,128]{3,2,1,0:T(8,128)} %coarse_mid.1.refs_5_.om), channel_id=1, source_target_pairs={{8,16},{9,17},{10,18},{11,19},{12,20},{13,21},{14,22},{15,23}} | collective-permute-start | bytes 6291464 | tf_op jit(solution)/shard_map/ppermute | solution.py:480
  127.5 3.2 %collective-permute-start.15 = (f32[2,512,128]{2,1,0:T(8,128)S(1)}, f32[2,512,128]{2,1,0:T(8,128)S(1)}, u32[]{:S(2)}, u32[]{:S(2)}) collective-permute-start(f32[2,512,128]{2,1,0:T(8,128)S(1)} %get-tuple-element.85), channel_id=1, source_target_pairs={{0,9},{1,10},{2,11},{3,12},{4,13},{5,14},{6,15}} | collective-permute-start | bytes 1572872 | tf_op jit(solution)/shard_map/ppermute | solution.py:480
  128.2 2.5 %collective-permute-start.16 = (f32[2,512,128]{2,1,0:T(8,128)S(1)}, f32[2,512,128]{2,1,0:T(8,128)S(1)}, u32[]{:S(2)}, u32[]{:S(2)}) collective-permute-start(f32[2,512,128]{2,1,0:T(8,128)S(1)} %get-tuple-element.86), channel_id=1, source_target_pairs={{1,8},{2,9},{3,10},{4,11},{5,12},{6,13},{7,14}} | collective-permute-start | bytes 1572872 | tf_op jit(solution)/shard_map/ppermute | solution.py:480
  132.6 6.2 %collective-permute-start.17 = (f32[2,2,512,128]{3,2,1,0:T(8,128)}, f32[2,2,512,128]{3,2,1,0:T(8,128)}, u32[]{:S(2)}, u32[]{:S(2)}) collective-permute-start(f32[2,2,512,128]{3,2,1,0:T(8,128)} %get-tuple-element.87.ox.refs_6_), channel_id=1, source_target_pairs={{8,16},{9,17},{10,18},{11,19},{12,20},{13,21},{14,22},{15,23}} | collective-permute-start | bytes 3145736 | tf_op jit(solution)/shard_map/ppermute | solution.py:480
  134.3 4.6 %collective-permute-start.14 = (f32[2,2,512,128]{3,2,1,0:T(8,128)}, f32[2,2,512,128]{3,2,1,0:T(8,128)}, u32[]{:S(2)}, u32[]{:S(2)}) collective-permute-start(f32[2,2,512,128]{3,2,1,0:T(8,128)} %get-tuple-element.83.on), channel_id=1, source_target_pairs={{8,16},{9,17},{10,18},{11,19},{12,20},{13,21},{14,22},{15,23}} | collective-permute-start | bytes 3145736 | tf_op jit(solution)/shard_map/ppermute | solution.py:480
  135.9 11.2 %collective-permute-start.18 = (f32[2,512,128]{2,1,0:T(8,128)}, f32[2,512,128]{2,1,0:T(8,128)}, u32[]{:S(2)}, u32[]{:S(2)}) collective-permute-start(f32[2,512,128]{2,1,0:T(8,128)} %get-tuple-element.89), channel_id=1, source_target_pairs={{8,17},{9,18},{10,19},{11,20},{12,21},{13,22},{14,23}} | collective-permute-start | bytes 1572872 | tf_op jit(solution)/shard_map/ppermute | solution.py:480
  137.3 9.7 %collective-permute-start.19 = (f32[2,512,128]{2,1,0:T(8,128)}, f32[2,512,128]{2,1,0:T(8,128)}, u32[]{:S(2)}, u32[]{:S(2)}) collective-permute-start(f32[2,512,128]{2,1,0:T(8,128)} %get-tuple-element.90), channel_id=1, source_target_pairs={{9,16},{10,17},{11,18},{12,19},{13,20},{14,21},{15,22}} | collective-permute-start | bytes 1572872 | tf_op jit(solution)/shard_map/ppermute | solution.py:480
  150.0 59.8 %collective-permute-start.22 = (f32[2,4,512,128]{3,2,1,0:T(8,128)}, f32[2,4,512,128]{3,2,1,0:T(8,128)}, u32[]{:S(2)}, u32[]{:S(2)}) collective-permute-start(f32[2,4,512,128]{3,2,1,0:T(8,128)} %get-tuple-element.95.om), channel_id=1, source_target_pairs={{16,24},{17,25},{18,26},{19,27},{20,28},{21,29},{22,30},{23,31}} | collective-permute-start | bytes 6291464 | tf_op jit(solution)/shard_map/ppermute | solution.py:480
  151.3 56.6 %collective-permute-start.23 = (f32[2,2,512,128]{3,2,1,0:T(8,128)}, f32[2,2,512,128]{3,2,1,0:T(8,128)}, u32[]{:S(2)}, u32[]{:S(2)}) collective-permute-start(f32[2,2,512,128]{3,2,1,0:T(8,128)} %get-tuple-element.96.on), channel_id=1, source_target_pairs={{16,24},{17,25},{18,26},{19,27},{20,28},{21,29},{22,30},{23,31}} | collective-permute-start | bytes 3145736 | tf_op jit(solution)/shard_map/ppermute | solution.py:480
  152.6 57.2 %collective-permute-start.24 = (f32[2,2,512,128]{3,2,1,0:T(8,128)}, f32[2,2,512,128]{3,2,1,0:T(8,128)}, u32[]{:S(2)}, u32[]{:S(2)}) collective-permute-start(f32[2,2,512,128]{3,2,1,0:T(8,128)} %get-tuple-element.97.ox), channel_id=1, source_target_pairs={{16,24},{17,25},{18,26},{19,27},{20,28},{21,29},{22,30},{23,31}} | collective-permute-start | bytes 3145736 | tf_op jit(solution)/shard_map/ppermute | solution.py:480
  153.9 71.5 %collective-permute-start.20 = (f32[2,512,128]{2,1,0:T(8,128)}, f32[2,512,128]{2,1,0:T(8,128)}, u32[]{:S(2)}, u32[]{:S(2)}) collective-permute-start(f32[2,512,128]{2,1,0:T(8,128)} %get-tuple-element.93), channel_id=1, source_target_pairs={{16,25},{17,26},{18,27},{19,28},{20,29},{21,30},{22,31}} | collective-permute-start | bytes 1572872 | tf_op jit(solution)/shard_map/ppermute | solution.py:480
  155.2 70.2 %collective-permute-start.21 = (f32[2,512,128]{2,1,0:T(8,128)}, f32[2,512,128]{2,1,0:T(8,128)}, u32[]{:S(2)}, u32[]{:S(2)}) collective-permute-start(f32[2,512,128]{2,1,0:T(8,128)} %get-tuple-element.94), channel_id=1, source_target_pairs={{17,24},{18,25},{19,26},{20,27},{21,28},{22,29},{23,30}} | collective-permute-start | bytes 1572872 | tf_op jit(solution)/shard_map/ppermute | solution.py:480
  212.7 12.7 %copy-start.11 = (s32[2,512,128]{2,1,0:T(8,128)S(1)}, s32[2,512,128]{2,1,0:T(8,128)}, u32[]{:S(2)}) copy-start(s32[2,512,128]{2,1,0:T(8,128)} %copy-done.8) | copy-start | bytes 1572868
  (13 other events, 49.0 us)
where the time goes:
time: 229 us; the launch traced here: 228 us
  waiting for transfers between devices  94.5 us (41%)
  Pallas kernels  74.8 us (33%)
  starting transfers between devices  47.1 us (21%)
  local copies, waits for them, and re-layouts  10.9 us (5%)
    ppermute x25, waiting for transfers between devices, move(): return lax.ppermute(x, ('tm', 'space'), pairs)  94.5 us
    pallas_call x16, Pallas kernels, call(): pl.pallas_call(run, out_shape=[f32(*x.shape) for x in through] + list(out...  69.6 us
    ppermute x25, starting transfers between devices, move(): return lax.ppermute(x, ('tm', 'space'), pairs)  47.1 us
    unnamed x40, local copies, waits for them, and re-layouts  10 us
    pallas_call x2, Pallas kernels, gridded(): pl.pallas_call(kernel, grid=(steps,), out_shape=outs, in_specs=in_specs,...  5.23 us
  transfers between devices with their start and end apart: 25, of which 10 were waited for; matrix products, arithmetic and copies ran while one was open for 0% of the time, Pallas kernels for 27%

commit v1 on v0

--- a/solution.py
+++ b/solution.py
@@ -86,6 +86,20 @@
         self.refs[key[0]][key[1:]] = value
 
 
+class Rows:
+    def __init__(self, ref, first):
+        self.ref, self.first = ref, first
+
+    def key(self, key):
+        return (key[0], key[1] + self.first, *key[2:])
+
+    def __getitem__(self, key):
+        return self.ref[self.key(key)]
+
+    def __setitem__(self, key, value):
+        self.ref[self.key(key)] = value
+
+
 class Tile:
     def __init__(self, y, n):
         self.y, self.n = y, n
@@ -238,10 +252,17 @@
     step_body(prm, Fields(mh, mc), sn, sx, ids, {"x": part, "n": nn, "m": nm}, pad)
 
 
-def replay_kernel(own, prm, mh, mc, sn, sx, ids, nm, nn, pad):
+def replay_kernel(own, prm, mh, mc, sn, sx, ids, km, om, am, an, nm, pad):
     @pl.when(own[0] != 0)
     def _():
-        step_body(prm, Fields(mh, mc), sn, sx, ids, {"n": nn, "m": nm}, pad)
+        step_body(prm, Fields(mh, mc), sn, sx, ids, {"n": an, "m": am}, pad)
+        coarse_body(
+            prm, {"n": an, "m": am}, {"m": km}, {"m": om}, ids, into({"m": nm}), "m", pad, False
+        )
+
+    @pl.when(own[0] == 0)
+    def _():
+        nm[...] = om[...]
 
 
 def edges_body(prm, gains, part, low, high, ide, edge, tl0, tl7):
@@ -265,7 +286,7 @@
 
 
 def coarse_edges_kernel(own, prm, part, low, high, ide, old, *refs):
-    edge, tl0, tl7 = refs[-3:]
+    edge, tl0, tl7 = refs
 
     @pl.when(own[0] != 0)
     def _():
@@ -309,7 +330,11 @@
         for f in F2:
             put(name, f, i, r, t, new[f] + (end[f] - start[f]))
 
-    block.each(ny, melt, arrived)
+    if "m" in which:
+        block.each(ny, melt, arrived)
+    else:
+        block.each(ny, melt, "nx")
+        tiles(2, ny, lambda i, t: melt("m", i * (mid - 1), 2 + i * (mid - 1), t))
     block.each(ny, update, which)
 
 
@@ -352,29 +377,38 @@
         nn[...] = on[...]
 
 
-def coarse_inner_kernel(own, prm, am, an, ax, km, kn, kx, ids, om, on, ox, nm, nn, part, pad):
+def coarse_outer_kernel(
+    own, prm, am, an, ax, low, high, kn, kx, ids, ide, on, ox, *refs
+):
+    rim, tl0, tl7, part, pad = refs[-5:]
+    edge, beside = Rows(rim, 0), Rows(rim, 2)
+
     @pl.when(own[0] != 0)
     def _():
         coarse_body(
             prm,
             {"x": ax, "n": an, "m": am},
-            {"m": km, "n": kn, "x": kx},
-            {"m": om, "n": on, "x": ox},
+            {"n": kn, "x": kx},
+            {"n": on, "x": ox},
             ids,
-            into({"m": nm, "n": nn, "x": part}),
-            "mnx",
+            into({"n": beside, "x": part}),
+            "xn",
             pad,
             True,
         )
+        edges_body(prm, "coarse", part, low, high, ide, edge, tl0, tl7)
 
     @pl.when(own[0] == 0)
     def _():
-        nm[...] = om[...]
-        nn[...] = on[...]
-
-
-def last_rows_kernel(own, prm, am, an, ax, km, kn, kx, ids, om, on, ox, oh, oc, pad):
+        for f in F2:
+            for e in range(2):
+                edge[f, e] = ox[f, e]
+                beside[f, e] = on[f, e]
+
+
+def last_rows_kernel(own, prm, am, ar, km, kn, kx, ids, om, rim, oh, oc, pad):
     out = (oh, oc)
+    ax, an, ox, on = Rows(ar, 0), Rows(ar, 2), Rows(rim, 0), Rows(rim, 2)
 
     @pl.when(own[0] != 0)
     def _():
@@ -570,72 +604,71 @@
             )
     km, kn, kx = base
 
-    am, an = call(
+    am, an, vm = call(
         replay_kernel,
-        [tall, pair],
-        (own(1), prm, *(send(x, 1) for x in last), ids),
+        [tall, pair, tall],
+        (own(1), prm, *(send(x, 1) for x in last), ids, km, sm),
         2,
         "replay",
         pad,
-        18,
+        24,
     )
-    vm, vn = (
-        call(
+    vn = sn
+    vx, tl0, tl7 = fine_edges(part, low, high, (vm,))
+    low, high = halos(tl0, tl7, (0,), 1)
+    ax = send(vx, 1)
+    vn, part = call(
+        coarse_rim_kernel,
+        [pair, pair],
+        (own(1), prm, am, an, ax, kn, kx, ids, vn, vx),
+        2,
+        "coarse_rim",
+        pad,
+        20,
+    )
+    vx, tl0, tl7 = call(
+        coarse_edges_kernel,
+        [pair, halo, halo],
+        (own(1), prm, part, low, high, ide, vx),
+        2,
+        "coarse_edges",
+    )
+    rim = None
+    for n in range(2, slices):
+        low, high = halos(tl0, tl7, (n - 1,), 1)
+        am = send(vm, n)
+        if n == 2:
+            an, ax = send(vn, n), send(vx, n)
+        else:
+            ar = send(rim, n)
+        if n == slices - 1:
+            break
+        vm = call(
             coarse_mid_kernel,
             [tall],
-            (own(1), prm, am, an, km, ids, sm),
+            (own(n), prm, am, an, km, ids, vm),
             2,
             "coarse_mid",
             pad,
             18,
-        )[0],
-        sn,
-    )
-    vx, tl0, tl7 = fine_edges(part, low, high, (vm,))
-    for n in range(1, slices):
-        low, high = halos(tl0, tl7, (n - 1,), 1)
-        ax = send(vx, n)
-        if n > 1:
-            am, an = send(vm, n), send(vn, n)
-        if n == slices - 1:
-            break
-        if n == 1:
-            vn, part = call(
-                coarse_rim_kernel,
-                [pair, pair],
-                (own(n), prm, am, an, ax, kn, kx, ids, vn, vx),
-                2,
-                "coarse_rim",
-                pad,
-                20,
-            )
-        else:
-            vm, vn, part = call(
-                coarse_inner_kernel,
-                [tall, pair, pair],
-                (own(n), prm, am, an, ax, km, kn, kx, ids, vm, vn, vx),
-                2,
-                "coarse_inner",
-                pad,
-                26,
-            )
-        *passed, vx, tl0, tl7 = call(
-            coarse_edges_kernel,
-            [pair, halo, halo],
-            (own(n), prm, part, low, high, ide, vx),
+        )[0]
+        vm, rim, tl0, tl7 = call(
+            coarse_outer_kernel,
+            [f32(2, 4, ny, nz), halo, halo],
+            (own(n), prm, am, an, ax, low, high, kn, kx, ids, ide, vn, vx),
             2,
-            "coarse_edges",
-            through=(vm, vn) if n > 1 else (),
-        )
-        if n > 1:
-            vm, vn = passed
+            "coarse_outer",
+            [pltpu.VMEM((2, 2, ny, nz), jnp.float32), *pad],
+            26,
+            through=(vm,),
+        )
 
     out = f32(1, rows, ny, nz)
     last_own = own(slices - 1)
     oh, oc = call(
         last_rows_kernel,
         [out, out],
-        (last_own, prm, am, an, ax, km, kn, kx, ids, vm, vn, vx),
+        (last_own, prm, am, ar, km, kn, kx, ids, vm, rim),
         2,
         "last_rows",
         pad,

time: 229 us -> 225 us (0.983)
    ppermute x25 -> x24, waiting for transfers between devices: 94.5 us -> 92.4 us  [move(): return lax.ppermute(x, ('tm', 'space'), pairs)]
    ppermute x25 -> x24, starting transfers between devices: 47.1 us -> 45.9 us  [move(): return lax.ppermute(x, ('tm', 'space'), pairs)]
    pallas_call x16 -> x15, Pallas kernels: 69.6 us -> 69.9 us  [call(): pl.pallas_call(run, out_shape=[f32(*x.shape) for x in through] + list(out...]
  transfers between devices with their start and end apart: 25 -> 24, of which waited for: 10 -> 10; matrix products, arithmetic and copies ran while one was open for 0% -> 0% of each run, Pallas kernels for 27% -> 27%
where the time goes in v1:
time: 225 us; the launch traced here: 223 us
  waiting for transfers between devices  92.4 us (41%)
  Pallas kernels  75.1 us (33%)
  starting transfers between devices  45.9 us (20%)
  local copies, waits for them, and re-layouts  9.08 us (4%)
    ppermute x24, waiting for transfers between devices, move(): return lax.ppermute(x, ('tm', 'space'), pairs)  92.4 us
    pallas_call x15, Pallas kernels, call(): pl.pallas_call(run, out_shape=[f32(*x.shape) for x in through] + list(out...  69.9 us
    ppermute x24, starting transfers between devices, move(): return lax.ppermute(x, ('tm', 'space'), pairs)  45.9 us
    unnamed x40, local copies, waits for them, and re-layouts  8.25 us
    pallas_call x2, Pallas kernels, gridded(): pl.pallas_call(kernel, grid=(steps,), out_shape=outs, in_specs=in_specs,...  5.23 us
  transfers between devices with their start and end apart: 24, of which 10 were waited for; matrix products, arithmetic and copies ran while one was open for 0% of the time, Pallas kernels for 27%

profile of v1, /device:TPU:11, one launch (start us, length us, event | category | flops | bytes accessed | tf_op | source)
XLA Modules:
  0.0 223.5 jit_solution(14269987501480724313)
XLA Ops:
  1.5 2.3 %first_edges.1 = (f32[2,512,128]{2,1,0:T(8,128)S(1)}, f32[2,512,128]{2,1,0:T(8,128)S(1)}) custom-call(f32[27]{0:T(128)S(1)} %concatenate.3.prm.refs_0_.refs_1_, f32[8,512,128]{2,1,0:T(8,128)} %bitcast.5, f32[8,512,128]{2,1,0:T(8,128)} %bitcast.8, s32[8,512,128]{2,1,0:T(8,128)} %mat.3), custom_call_target="tpu_custom_call" | custom-call | flops 1000 | bytes 1000 | tf_op jit(solution)/shard_map/first_edges/pallas_call | solution.py:526
  3.8 3.1 %collective-permute-start = (f32[2,512,128]{2,1,0:T(8,128)S(1)}, f32[2,512,128]{2,1,0:T(8,128)S(1)}, u32[]{:S(2)}, u32[]{:S(2)}) collective-permute-start(f32[2,512,128]{2,1,0:T(8,128)S(1)} %get-tuple-element.51), channel_id=1, source_target_pairs={{0,1},{1,2},{2,3},{3,4},{4,5},{5,6},{6,7},{8,9},{9,10},{10,11},{11... | collective-permute-start | bytes 1572872 | tf_op jit(solution)/shard_map/ppermute | solution.py:514
  7.0 3.0 %collective-permute-start.1 = (f32[2,512,128]{2,1,0:T(8,128)S(1)}, f32[2,512,128]{2,1,0:T(8,128)S(1)}, u32[]{:S(2)}, u32[]{:S(2)}) collective-permute-start(f32[2,512,128]{2,1,0:T(8,128)S(1)} %get-tuple-element.52), channel_id=1, source_target_pairs={{1,0},{2,1},{3,2},{4,3},{5,4},{6,5},{7,6},{9,8},{10,9},{11,10},{12... | collective-permute-start | bytes 1572872 | tf_op jit(solution)/shard_map/ppermute | solution.py:514
  11.6 7.1 %first_step.1 = (f32[2,4,512,128]{3,2,1,0:T(8,128)S(1)}, f32[2,2,512,128]{3,2,1,0:T(8,128)S(1)}, f32[2,2,512,128]{3,2,1,0:T(8,128)S(1)}, s32[8,512,128]{2,1,0:T(8,128)S(1)}, s32[2,512,128]{2,1,0:T(8,128)S(1)}) custom-call(f32[27]{0:T(128)S(1)} %concatenate.3.prm.refs_0_.refs_1_, f32[8,512,128]{2,1,0:T(8,128)S(1)} %bitcast.6, f32[8,512,128]{2,1,0:T(8,128)S(1)} %bitcast.9, ...), custom_call_target="tpu_custom_call" | custom-call | flops 1000 | bytes 1000 | tf_op jit(solution)/shard_map/first_step/pallas_call | solution.py:483
  18.7 10.0 %collective-permute-done.low = f32[2,512,128]{2,1,0:T(8,128)S(1)} collective-permute-done((f32[2,512,128]{2,1,0:T(8,128)S(1)}, f32[2,512,128]{2,1,0:T(8,128)S(1)}, u32[]{:S(2)}, u32[]{:S(2)}) %collective-permute-start) | collective-permute-done | bytes 524320 | tf_op jit(solution)/shard_map/ppermute | solution.py:514
  28.8 2.9 %collective-permute-done.1.high = f32[2,512,128]{2,1,0:T(8,128)S(1)} collective-permute-done((f32[2,512,128]{2,1,0:T(8,128)S(1)}, f32[2,512,128]{2,1,0:T(8,128)S(1)}, u32[]{:S(2)}, u32[]{:S(2)}) %collective-permute-start.1) | collective-permute-done | bytes 524320 | tf_op jit(solution)/shard_map/ppermute | solution.py:514
  33.0 1.9 collective-permute-start.2
  35.0 4.3 %collective-permute-start.3 = (f32[2,512,128]{2,1,0:T(8,128)S(1)}, f32[2,512,128]{2,1,0:T(8,128)S(1)}, u32[]{:S(2)}, u32[]{:S(2)}) collective-permute-start(f32[2,512,128]{2,1,0:T(8,128)S(1)} %get-tuple-element.60), channel_id=1, source_target_pairs={{1,0},{2,1},{3,2},{4,3},{5,4},{6,5},{7,6},{9,8},{10,9},{11,10},{12... | collective-permute-start | bytes 1572872 | tf_op jit(solution)/shard_map/ppermute | solution.py:514
  39.2 3.3 %base.1 = (f32[2,4,512,128]{3,2,1,0:T(8,128)S(1)}, f32[2,2,512,128]{3,2,1,0:T(8,128)S(1)}, f32[2,2,512,128]{3,2,1,0:T(8,128)S(1)}) custom-call(f32[27]{0:T(128)S(1)} %concatenate.3.prm.refs_0_.refs_1_, f32[8,512,128]{2,1,0:T(8,128)S(1)} %bitcast.7, f32[8,512,128]{2,1,0:T(8,128)S(1)} %bitcast.10, f32[2,4,512,128]{3,2,1,0:T(8,128)S(1)} %get-tuple-element.48.sm, ...), custom_call_target="tpu_custom_call" | custom-call | flops 1000 | bytes 1000 | tf_op jit(solution)/shard_map/base/pallas_call | solution.py:483
  42.5 6.9 %step.1 = (f32[2,4,512,128]{3,2,1,0:T(8,128)S(1)}, f32[2,2,512,128]{3,2,1,0:T(8,128)S(1)}, f32[2,2,512,128]{3,2,1,0:T(8,128)S(1)}) custom-call(f32[27]{0:T(128)S(1)} %concatenate.3.prm.refs_0_.refs_1_, f32[2,4,512,128]{3,2,1,0:T(8,128)S(1)} %get-tuple-element.48.sm, f32[2,2,512,128]{3,2,1,0:T(8,128)S(1)} %get-tuple-element.49.sn, ...), custom_call_target="tpu_custom_call" | custom-call | flops 1000 | bytes 1000 | tf_op jit(solution)/shard_map/step/pallas_call | solution.py:483
  49.4 7.2 %collective-permute-done.2.refs_2_ = f32[2,512,128]{2,1,0:T(8,128)S(1)} collective-permute-done((f32[2,512,128]{2,1,0:T(8,128)S(1)}, f32[2,512,128]{2,1,0:T(8,128)S(1)}, u32[]{:S(2)}, u32[]{:S(2)}) %collective-permute-start.2) | collective-permute-done | bytes 524320 | tf_op jit(solution)/shard_map/ppermute | solution.py:514
  56.6 4.3 %collective-permute-done.3.refs_3_ = f32[2,512,128]{2,1,0:T(8,128)S(1)} collective-permute-done((f32[2,512,128]{2,1,0:T(8,128)S(1)}, f32[2,512,128]{2,1,0:T(8,128)S(1)}, u32[]{:S(2)}, u32[]{:S(2)}) %collective-permute-start.3) | collective-permute-done | bytes 524320 | tf_op jit(solution)/shard_map/ppermute | solution.py:514
  62.3 1.9 collective-permute-start.7
  64.2 4.3 %collective-permute-start.8 = (f32[2,512,128]{2,1,0:T(8,128)S(1)}, f32[2,512,128]{2,1,0:T(8,128)S(1)}, u32[]{:S(2)}, u32[]{:S(2)}) collective-permute-start(f32[2,512,128]{2,1,0:T(8,128)S(1)} %get-tuple-element.70), channel_id=1, source_target_pairs={{1,0},{2,1},{3,2},{4,3},{5,4},{6,5},{7,6},{9,8},{10,9},{11,10},{12... | collective-permute-start | bytes 1572872 | tf_op jit(solution)/shard_map/ppermute | solution.py:514
  68.5 7.9 %step_apart.1 = (f32[4,512,128]{2,1,0:T(8,128)S(1)}, f32[4,512,128]{2,1,0:T(8,128)}, f32[2,2,512,128]{3,2,1,0:T(8,128)}, f32[2,2,512,128]{3,2,1,0:T(8,128)S(1)}) custom-call(f32[27]{0:T(128)S(1)} %concatenate.3.prm.refs_0_.refs_1_, f32[2,4,512,128]{3,2,1,0:T(8,128)S(1)} %get-tuple-element.56.sm, f32[2,2,512,128]{3,2,1,0:T(8,128)S(1)} %get-tuple-element.57.sn, ...), custom_call_target="tpu_custom_call" | custom-call | flops 1000 | bytes 1000 | tf_op jit(solution)/shard_map/step_apart/pallas_call | solution.py:483
  80.5 6.1 %collective-permute-done.7.refs_2_ = f32[2,512,128]{2,1,0:T(8,128)S(1)} collective-permute-done((f32[2,512,128]{2,1,0:T(8,128)S(1)}, f32[2,512,128]{2,1,0:T(8,128)S(1)}, u32[]{:S(2)}, u32[]{:S(2)}) %collective-permute-start.7) | collective-permute-done | bytes 524320 | tf_op jit(solution)/shard_map/ppermute | solution.py:514
  86.6 3.6 %collective-permute-done.8.refs_3_ = f32[2,512,128]{2,1,0:T(8,128)S(1)} collective-permute-done((f32[2,512,128]{2,1,0:T(8,128)S(1)}, f32[2,512,128]{2,1,0:T(8,128)S(1)}, u32[]{:S(2)}, u32[]{:S(2)}) %collective-permute-start.8) | collective-permute-done | bytes 524320 | tf_op jit(solution)/shard_map/ppermute | solution.py:514
  90.2 2.6 %edges.6 = (f32[2,2,512,128]{3,2,1,0:T(8,128)}, f32[2,512,128]{2,1,0:T(8,128)}, f32[2,512,128]{2,1,0:T(8,128)}) custom-call(f32[27]{0:T(128)S(1)} %concatenate.3.prm.refs_0_.refs_1_, f32[2,2,512,128]{3,2,1,0:T(8,128)S(1)} %get-tuple-element.68.refs_1_, f32[2,512,128]{2,1,0:T(8,128)S(1)} %collective-permute-done.7.refs_2_, ...), custom_call_target="tpu_custom_call" | custom-call | flops 1000 | bytes 1000 | tf_op jit(solution)/shard_map/edges/pallas_call | solution.py:483
  97.3 4.2 %collective-permute-start.12 = (f32[2,512,128]{2,1,0:T(8,128)}, f32[2,512,128]{2,1,0:T(8,128)}, u32[]{:S(2)}, u32[]{:S(2)}) collective-permute-start(f32[2,512,128]{2,1,0:T(8,128)} %get-tuple-element.78), channel_id=1, source_target_pairs={{1,0},{2,1},{3,2},{4,3},{5,4},{6,5},{7,6},{9,8},{10,9},{11,10},{12... | collective-permute-start | bytes 1572872 | tf_op jit(solution)/shard_map/ppermute | solution.py:514
  102.8 8.2 %step_joined.1 = (f32[2,4,512,128]{3,2,1,0:T(8,128)S(1)}, f32[2,2,512,128]{3,2,1,0:T(8,128)S(1)}, f32[2,2,512,128]{3,2,1,0:T(8,128)S(1)}) custom-call(f32[27]{0:T(128)S(1)} %concatenate.3.prm.refs_0_.refs_1_, f32[4,512,128]{2,1,0:T(8,128)S(1)} %copy-done.17, f32[4,512,128]{2,1,0:T(8,128)} %get-tuple-element.66.mc, f32[2,2,512,128]{3,2,1,0:T(8,128)} %get-tuple-element.67.sn, ...), custom_call_target="tpu_custom_call" | custom-call | flops 1000 | bytes 1000 | tf_op jit(solution)/shard_map/step_joined/pallas_call | solution.py:483
  111.1 3.4 %replay.1 = (f32[2,4,512,128]{3,2,1,0:T(8,128)S(1)}, f32[2,2,512,128]{3,2,1,0:T(8,128)S(1)}, f32[2,4,512,128]{3,2,1,0:T(8,128)}) custom-call(s32[1]{0:T(128)} %bitcast.2.own, f32[27]{0:T(128)S(1)} %concatenate.3.prm.refs_0_.refs_1_, f32[4,512,128]{2,1,0:T(8,128)S(1)} %copy-done.19, f32[4,512,128]{2,1,0:T(8,128)} %collective-permute-done.5.mc, ...), custom_call_target="tpu_custom_call" | custom-call | flops 1000 | bytes 1000 | tf_op jit(solution)/shard_map/replay/pallas_call | solution.py:483
  114.5 4.5 %collective-permute-done.11.refs_2_ = f32[2,512,128]{2,1,0:T(8,128)} collective-permute-done((f32[2,512,128]{2,1,0:T(8,128)}, f32[2,512,128]{2,1,0:T(8,128)}, u32[]{:S(2)}, u32[]{:S(2)}) %collective-permute-start.11) | collective-permute-done | bytes 524320 | tf_op jit(solution)/shard_map/ppermute | solution.py:514
  119.0 3.6 %collective-permute-done.12.refs_3_ = f32[2,512,128]{2,1,0:T(8,128)} collective-permute-done((f32[2,512,128]{2,1,0:T(8,128)}, f32[2,512,128]{2,1,0:T(8,128)}, u32[]{:S(2)}, u32[]{:S(2)}) %collective-permute-start.12) | collective-permute-done | bytes 524320 | tf_op jit(solution)/shard_map/ppermute | solution.py:514
  122.6 2.1 edges.7
  125.5 2.0 collective-permute-start.10
  132.4 1.9 coarse_edges.1
  140.5 4.2 %coarse_mid.1.refs_13_ = f32[2,4,512,128]{3,2,1,0:T(8,128)} custom-call(s32[1]{0:T(128)} %bitcast.1.own.refs_0_, f32[27]{0:T(128)S(1)} %concatenate.3.prm.refs_0_.refs_1_, f32[2,4,512,128]{3,2,1,0:T(8,128)} %collective-permute-done.10.am.refs_2_, f32[2,2,512,128]{3,2,1,0:T(8,128)} %collective-permute-done.14.an.refs_3_, f32[2,4,512,128]{3,2,1,0:T(8,128)S(1)} %copy-done.2, ...), custom_call_target="tpu_custom_call" | custom-call | flops 1000 | bytes 1000 | tf_op jit(solution)/shard_map/coarse_mid/pallas_call | solution.py:483
  144.7 5.0 %coarse_outer.1 = (f32[2,4,512,128]{3,2,1,0:T(8,128)}, f32[2,4,512,128]{3,2,1,0:T(8,128)}, f32[2,512,128]{2,1,0:T(8,128)}, f32[2,512,128]{2,1,0:T(8,128)}) custom-call(s32[1]{0:T(128)} %bitcast.1.own.refs_0_, f32[27]{0:T(128)S(1)} %concatenate.3.prm.refs_0_.refs_1_, ...), custom_call_target="tpu_custom_call", output_to_operand_aliasing={{0}: (13, {})} | custom-call | flops 1000 | bytes 1000 | tf_op jit(solution)/shard_map/coarse_outer/pallas_call | solution.py:483
  154.9 47.0 %collective-permute-done.22.am = f32[2,4,512,128]{3,2,1,0:T(8,128)} collective-permute-done((f32[2,4,512,128]{3,2,1,0:T(8,128)}, f32[2,4,512,128]{3,2,1,0:T(8,128)}, u32[]{:S(2)}, u32[]{:S(2)}) %collective-permute-start.22) | collective-permute-done | bytes 2097184 | tf_op jit(solution)/shard_map/ppermute | solution.py:514
  201.9 3.0 %collective-permute-done.23.ar = f32[2,4,512,128]{3,2,1,0:T(8,128)} collective-permute-done((f32[2,4,512,128]{3,2,1,0:T(8,128)}, f32[2,4,512,128]{3,2,1,0:T(8,128)}, u32[]{:S(2)}, u32[]{:S(2)}) %collective-permute-start.23) | collective-permute-done | bytes 2097184 | tf_op jit(solution)/shard_map/ppermute | solution.py:514
  207.7 12.8 %last_rows.1 = (f32[1,8,512,128]{3,2,1,0:T(8,128)}, f32[1,8,512,128]{3,2,1,0:T(8,128)}) custom-call(s32[1]{0:T(128)} %bitcast.own, f32[27]{0:T(128)S(1)} %concatenate.3.prm.refs_0_.refs_1_, f32[2,4,512,128]{3,2,1,0:T(8,128)} %collective-permute-done.22.am, f32[2,4,512,128]{3,2,1,0:T(8,128)} %collective-permute-done.23.ar, f32[2,4,512,128]{3,2,1,0:T(8,128)S(1)} %copy-done.3, ...), custom_call_target="tpu_custom_call" | custom-call | flops 1000 | bytes 1000 | tf_op jit(solution)/shard_map/last_rows/pallas_call | solution.py:483
  220.6 2.9 %last_edges.1 = (f32[1,8,512,128]{3,2,1,0:T(8,128)}, f32[1,8,512,128]{3,2,1,0:T(8,128)}) custom-call(s32[1]{0:T(128)} %bitcast.own, f32[27]{0:T(128)S(1)} %concatenate.3.prm.refs_0_.refs_1_, f32[2,512,128]{2,1,0:T(8,128)} %collective-permute-done.20.low, f32[2,512,128]{2,1,0:T(8,128)} %collective-permute-done.21.high, ...), custom_call_target="tpu_custom_call", output_to_operand_aliasing={{0}: (5, {}), {1}: (6, {})} | custom-call | flops 1000 | bytes 1000 | tf_op jit(solution)/shard_map/last_edges/pallas_call | solution.py:526
  (74 shorter events, 34.7 us)
Async XLA Ops:
  1.5 8.5 %copy-start.13 = (f32[1,8,512,128]{3,2,1,0:T(8,128)S(1)}, f32[1,8,512,128]{3,2,1,0:T(8,128)}, u32[]{:S(2)}) copy-start(f32[1,8,512,128]{3,2,1,0:T(8,128)} %param.12) | copy-start | bytes 6291460
  1.5 8.6 %copy-start.14 = (s32[8,512,128]{2,1,0:T(8,128)S(1)}, s32[8,512,128]{2,1,0:T(8,128)}, u32[]{:S(2)}) copy-start(s32[8,512,128]{2,1,0:T(8,128)} %mat.3) | copy-start | bytes 6291460
  3.8 25.0 %collective-permute-start = (f32[2,512,128]{2,1,0:T(8,128)S(1)}, f32[2,512,128]{2,1,0:T(8,128)S(1)}, u32[]{:S(2)}, u32[]{:S(2)}) collective-permute-start(f32[2,512,128]{2,1,0:T(8,128)S(1)} %get-tuple-element.51), channel_id=1, source_target_pairs={{0,1},{1,2},{2,3},{3,4},{4,5},{5,6},{6,7},{8,9},{9,10},{10,11},{11... | collective-permute-start | bytes 1572872 | tf_op jit(solution)/shard_map/ppermute | solution.py:514
  7.0 24.7 %collective-permute-start.1 = (f32[2,512,128]{2,1,0:T(8,128)S(1)}, f32[2,512,128]{2,1,0:T(8,128)S(1)}, u32[]{:S(2)}, u32[]{:S(2)}) collective-permute-start(f32[2,512,128]{2,1,0:T(8,128)S(1)} %get-tuple-element.52), channel_id=1, source_target_pairs={{1,0},{2,1},{3,2},{4,3},{5,4},{6,5},{7,6},{9,8},{10,9},{11,10},{12... | collective-permute-start | bytes 1572872 | tf_op jit(solution)/shard_map/ppermute | solution.py:514
  18.7 71.5 %copy-start.8 = (s32[2,512,128]{2,1,0:T(8,128)}, s32[2,512,128]{2,1,0:T(8,128)S(1)}, u32[]{:S(2)}) copy-start(s32[2,512,128]{2,1,0:T(8,128)S(1)} %get-tuple-element.53.ide.refs_4_.refs_10_) | copy-start | bytes 1572868
  33.0 23.6 %collective-permute-start.2 = (f32[2,512,128]{2,1,0:T(8,128)S(1)}, f32[2,512,128]{2,1,0:T(8,128)S(1)}, u32[]{:S(2)}, u32[]{:S(2)}) collective-permute-start(f32[2,512,128]{2,1,0:T(8,128)S(1)} %get-tuple-element.59), channel_id=1, source_target_pairs={{0,1},{1,2},{2,3},{3,4},{4,5},{5,6},{6,7},{8,9},{9,10},{10,11},{11... | collective-permute-start | bytes 1572872 | tf_op jit(solution)/shard_map/ppermute | solution.py:514
  35.0 26.0 %collective-permute-start.3 = (f32[2,512,128]{2,1,0:T(8,128)S(1)}, f32[2,512,128]{2,1,0:T(8,128)S(1)}, u32[]{:S(2)}, u32[]{:S(2)}) collective-permute-start(f32[2,512,128]{2,1,0:T(8,128)S(1)} %get-tuple-element.60), channel_id=1, source_target_pairs={{1,0},{2,1},{3,2},{4,3},{5,4},{6,5},{7,6},{9,8},{10,9},{11,10},{12... | collective-permute-start | bytes 1572872 | tf_op jit(solution)/shard_map/ppermute | solution.py:514
  42.5 47.7 %copy-start = (f32[2,4,512,128]{3,2,1,0:T(8,128)}, f32[2,4,512,128]{3,2,1,0:T(8,128)S(1)}, u32[]{:S(2)}) copy-start(f32[2,4,512,128]{3,2,1,0:T(8,128)S(1)} %get-tuple-element.61.refs_5_.km) | copy-start | bytes 6291460
  42.5 47.7 %copy-start.4 = (f32[2,2,512,128]{3,2,1,0:T(8,128)}, f32[2,2,512,128]{3,2,1,0:T(8,128)S(1)}, u32[]{:S(2)}) copy-start(f32[2,2,512,128]{3,2,1,0:T(8,128)S(1)} %get-tuple-element.63.refs_7_.kx.refs_8_) | copy-start | bytes 3145732
  62.3 24.3 %collective-permute-start.7 = (f32[2,512,128]{2,1,0:T(8,128)S(1)}, f32[2,512,128]{2,1,0:T(8,128)S(1)}, u32[]{:S(2)}, u32[]{:S(2)}) collective-permute-start(f32[2,512,128]{2,1,0:T(8,128)S(1)} %get-tuple-element.69), channel_id=1, source_target_pairs={{0,1},{1,2},{2,3},{3,4},{4,5},{5,6},{6,7},{8,9},{9,10},{10,11},{11... | collective-permute-start | bytes 1572872 | tf_op jit(solution)/shard_map/ppermute | solution.py:514
  64.2 26.0 %collective-permute-start.8 = (f32[2,512,128]{2,1,0:T(8,128)S(1)}, f32[2,512,128]{2,1,0:T(8,128)S(1)}, u32[]{:S(2)}, u32[]{:S(2)}) collective-permute-start(f32[2,512,128]{2,1,0:T(8,128)S(1)} %get-tuple-element.70), channel_id=1, source_target_pairs={{1,0},{2,1},{3,2},{4,3},{5,4},{6,5},{7,6},{9,8},{10,9},{11,10},{12... | collective-permute-start | bytes 1572872 | tf_op jit(solution)/shard_map/ppermute | solution.py:514
  76.4 16.4 %copy-start.16 = (f32[4,512,128]{2,1,0:T(8,128)}, f32[4,512,128]{2,1,0:T(8,128)S(1)}, u32[]{:S(2)}) copy-start(f32[4,512,128]{2,1,0:T(8,128)S(1)} %get-tuple-element.65.mh) | copy-start | bytes 3145732
  76.4 19.9 %collective-permute-start.4 = (f32[4,512,128]{2,1,0:T(8,128)S(1)}, f32[4,512,128]{2,1,0:T(8,128)S(1)}, u32[]{:S(2)}, u32[]{:S(2)}) collective-permute-start(f32[4,512,128]{2,1,0:T(8,128)S(1)} %get-tuple-element.65.mh), channel_id=1, source_target_pairs={{0,8},{1,9},{2,10},{3,11},{4,12},{5,13},{6,14},{7,15}} | collective-permute-start | bytes 3145736 | tf_op jit(solution)/shard_map/ppermute | solution.py:514
  77.1 33.9 %collective-permute-start.5 = (f32[4,512,128]{2,1,0:T(8,128)}, f32[4,512,128]{2,1,0:T(8,128)}, u32[]{:S(2)}, u32[]{:S(2)}) collective-permute-start(f32[4,512,128]{2,1,0:T(8,128)} %get-tuple-element.66.mc), channel_id=1, source_target_pairs={{0,8},{1,9},{2,10},{3,11},{4,12},{5,13},{6,14},{7,15}} | collective-permute-start | bytes 3145736 | tf_op jit(solution)/shard_map/ppermute | solution.py:514
  78.8 32.2 %collective-permute-start.6 = (f32[2,2,512,128]{3,2,1,0:T(8,128)}, f32[2,2,512,128]{3,2,1,0:T(8,128)}, u32[]{:S(2)}, u32[]{:S(2)}) collective-permute-start(f32[2,2,512,128]{3,2,1,0:T(8,128)} %get-tuple-element.67.sn), channel_id=1, source_target_pairs={{0,8},{1,9},{2,10},{3,11},{4,12},{5,13},{6,14},{7,15}} | collective-permute-start | bytes 3145736 | tf_op jit(solution)/shard_map/ppermute | solution.py:514
  92.8 18.3 %collective-permute-start.9 = (f32[2,2,512,128]{3,2,1,0:T(8,128)}, f32[2,2,512,128]{3,2,1,0:T(8,128)}, u32[]{:S(2)}, u32[]{:S(2)}) collective-permute-start(f32[2,2,512,128]{3,2,1,0:T(8,128)} %get-tuple-element.71.sx), channel_id=1, source_target_pairs={{0,8},{1,9},{2,10},{3,11},{4,12},{5,13},{6,14},{7,15}} | collective-permute-start | bytes 3145736 | tf_op jit(solution)/shard_map/ppermute | solution.py:514
  94.4 24.6 %collective-permute-start.11 = (f32[2,512,128]{2,1,0:T(8,128)}, f32[2,512,128]{2,1,0:T(8,128)}, u32[]{:S(2)}, u32[]{:S(2)}) collective-permute-start(f32[2,512,128]{2,1,0:T(8,128)} %get-tuple-element.77), channel_id=1, source_target_pairs={{0,1},{1,2},{2,3},{3,4},{4,5},{5,6},{6,7},{8,9},{9,10},{10,11},{11... | collective-permute-start | bytes 1572872 | tf_op jit(solution)/shard_map/ppermute | solution.py:514
  97.3 25.3 %collective-permute-start.12 = (f32[2,512,128]{2,1,0:T(8,128)}, f32[2,512,128]{2,1,0:T(8,128)}, u32[]{:S(2)}, u32[]{:S(2)}) collective-permute-start(f32[2,512,128]{2,1,0:T(8,128)} %get-tuple-element.78), channel_id=1, source_target_pairs={{1,0},{2,1},{3,2},{4,3},{5,4},{6,5},{7,6},{9,8},{10,9},{11,10},{12... | collective-permute-start | bytes 1572872 | tf_op jit(solution)/shard_map/ppermute | solution.py:514
  111.1 11.5 %copy-start.9 = (s32[2,512,128]{2,1,0:T(8,128)S(1)}, s32[2,512,128]{2,1,0:T(8,128)}, u32[]{:S(2)}) copy-start(s32[2,512,128]{2,1,0:T(8,128)} %copy-done.8) | copy-start | bytes 1572868
  124.8 4.2 %collective-permute-start.13 = (f32[2,2,512,128]{3,2,1,0:T(8,128)S(1)}, f32[2,2,512,128]{3,2,1,0:T(8,128)S(1)}, u32[]{:S(2)}, u32[]{:S(2)}) collective-permute-start(f32[2,2,512,128]{3,2,1,0:T(8,128)S(1)} %get-tuple-element.79.ox.old), channel_id=1, source_target_pairs={{0,8},{1,9},{2,10},{3,11},{4,12},{5,13},{6,14},{7,15}} | collective-permute-start | bytes 3145736 | tf_op jit(solution)/shard_map/ppermute | solution.py:514
  125.5 13.4 %collective-permute-start.10 = (f32[2,4,512,128]{3,2,1,0:T(8,128)}, f32[2,4,512,128]{3,2,1,0:T(8,128)}, u32[]{:S(2)}, u32[]{:S(2)}) collective-permute-start(f32[2,4,512,128]{3,2,1,0:T(8,128)} %get-tuple-element.73.refs_5_.om), channel_id=1, source_target_pairs={{8,16},{9,17},{10,18},{11,19},{12,20},{13,21},{14,22},{15,23}} | collective-permute-start | bytes 6291464 | tf_op jit(solution)/shard_map/ppermute | solution.py:514
  127.5 4.9 %collective-permute-start.15 = (f32[2,512,128]{2,1,0:T(8,128)S(1)}, f32[2,512,128]{2,1,0:T(8,128)S(1)}, u32[]{:S(2)}, u32[]{:S(2)}) collective-permute-start(f32[2,512,128]{2,1,0:T(8,128)S(1)} %get-tuple-element.83), channel_id=1, source_target_pairs={{0,9},{1,10},{2,11},{3,12},{4,13},{5,14},{6,15}} | collective-permute-start | bytes 1572872 | tf_op jit(solution)/shard_map/ppermute | solution.py:514
  128.2 4.2 %collective-permute-start.16 = (f32[2,512,128]{2,1,0:T(8,128)S(1)}, f32[2,512,128]{2,1,0:T(8,128)S(1)}, u32[]{:S(2)}, u32[]{:S(2)}) collective-permute-start(f32[2,512,128]{2,1,0:T(8,128)S(1)} %get-tuple-element.84), channel_id=1, source_target_pairs={{1,8},{2,9},{3,10},{4,11},{5,12},{6,13},{7,14}} | collective-permute-start | bytes 1572872 | tf_op jit(solution)/shard_map/ppermute | solution.py:514
  130.7 8.2 %collective-permute-start.14 = (f32[2,2,512,128]{3,2,1,0:T(8,128)}, f32[2,2,512,128]{3,2,1,0:T(8,128)}, u32[]{:S(2)}, u32[]{:S(2)}) collective-permute-start(f32[2,2,512,128]{3,2,1,0:T(8,128)} %get-tuple-element.81.refs_11_), channel_id=1, source_target_pairs={{8,16},{9,17},{10,18},{11,19},{12,20},{13,21},{14,22},{15,23}} | collective-permute-start | bytes 3145736 | tf_op jit(solution)/shard_map/ppermute | solution.py:514
  134.4 10.3 %collective-permute-start.17 = (f32[2,2,512,128]{3,2,1,0:T(8,128)}, f32[2,2,512,128]{3,2,1,0:T(8,128)}, u32[]{:S(2)}, u32[]{:S(2)}) collective-permute-start(f32[2,2,512,128]{3,2,1,0:T(8,128)} %get-tuple-element.85.refs_12_), channel_id=1, source_target_pairs={{8,16},{9,17},{10,18},{11,19},{12,20},{13,21},{14,22},{15,23}} | collective-permute-start | bytes 3145736 | tf_op jit(solution)/shard_map/ppermute | solution.py:514
  136.0 8.7 %collective-permute-start.18 = (f32[2,512,128]{2,1,0:T(8,128)}, f32[2,512,128]{2,1,0:T(8,128)}, u32[]{:S(2)}, u32[]{:S(2)}) collective-permute-start(f32[2,512,128]{2,1,0:T(8,128)} %get-tuple-element.86), channel_id=1, source_target_pairs={{8,17},{9,18},{10,19},{11,20},{12,21},{13,22},{14,23}} | collective-permute-start | bytes 1572872 | tf_op jit(solution)/shard_map/ppermute | solution.py:514
  137.5 7.2 %collective-permute-start.19 = (f32[2,512,128]{2,1,0:T(8,128)}, f32[2,512,128]{2,1,0:T(8,128)}, u32[]{:S(2)}, u32[]{:S(2)}) collective-permute-start(f32[2,512,128]{2,1,0:T(8,128)} %get-tuple-element.87), channel_id=1, source_target_pairs={{9,16},{10,17},{11,18},{12,19},{13,20},{14,21},{15,22}} | collective-permute-start | bytes 1572872 | tf_op jit(solution)/shard_map/ppermute | solution.py:514
  149.7 52.2 %collective-permute-start.22 = (f32[2,4,512,128]{3,2,1,0:T(8,128)}, f32[2,4,512,128]{3,2,1,0:T(8,128)}, u32[]{:S(2)}, u32[]{:S(2)}) collective-permute-start(f32[2,4,512,128]{3,2,1,0:T(8,128)} %get-tuple-element.90.om), channel_id=1, source_target_pairs={{16,24},{17,25},{18,26},{19,27},{20,28},{21,29},{22,30},{23,31}} | collective-permute-start | bytes 6291464 | tf_op jit(solution)/shard_map/ppermute | solution.py:514
  151.0 53.9 %collective-permute-start.23 = (f32[2,4,512,128]{3,2,1,0:T(8,128)}, f32[2,4,512,128]{3,2,1,0:T(8,128)}, u32[]{:S(2)}, u32[]{:S(2)}) collective-permute-start(f32[2,4,512,128]{3,2,1,0:T(8,128)} %get-tuple-element.91.rim), channel_id=1, source_target_pairs={{16,24},{17,25},{18,26},{19,27},{20,28},{21,29},{22,30},{23,31}} | collective-permute-start | bytes 6291464 | tf_op jit(solution)/shard_map/ppermute | solution.py:514
  152.3 68.2 %collective-permute-start.20 = (f32[2,512,128]{2,1,0:T(8,128)}, f32[2,512,128]{2,1,0:T(8,128)}, u32[]{:S(2)}, u32[]{:S(2)}) collective-permute-start(f32[2,512,128]{2,1,0:T(8,128)} %get-tuple-element.88), channel_id=1, source_target_pairs={{16,25},{17,26},{18,27},{19,28},{20,29},{21,30},{22,31}} | collective-permute-start | bytes 1572872 | tf_op jit(solution)/shard_map/ppermute | solution.py:514
  153.6 66.9 %collective-permute-start.21 = (f32[2,512,128]{2,1,0:T(8,128)}, f32[2,512,128]{2,1,0:T(8,128)}, u32[]{:S(2)}, u32[]{:S(2)}) collective-permute-start(f32[2,512,128]{2,1,0:T(8,128)} %get-tuple-element.89), channel_id=1, source_target_pairs={{17,24},{18,25},{19,26},{20,27},{21,28},{22,29},{23,30}} | collective-permute-start | bytes 1572872 | tf_op jit(solution)/shard_map/ppermute | solution.py:514
  207.7 12.8 %copy-start.11 = (s32[2,512,128]{2,1,0:T(8,128)S(1)}, s32[2,512,128]{2,1,0:T(8,128)}, u32[]{:S(2)}) copy-start(s32[2,512,128]{2,1,0:T(8,128)} %copy-done.8) | copy-start | bytes 1572868
  (12 other events, 47.9 us)

commit v2 on v1

--- a/solution.py
+++ b/solution.py
@@ -174,7 +174,7 @@
             tiles(self.mid, ny, lambda i, t: body("m", i, i + 2, t))
 
 
-def first_edges_kernel(prm, h, c, mat, tl0, tl7):
+def first_edges_kernel(prm, h, c, mat, tl0, tl7, later0, later7):
     tab = Tables(prm)
     side = pl.program_id(0)
 
@@ -185,11 +185,13 @@
         def _():
             for f in F2:
                 tl0[f, t.at, :] = values[f]
+                later0[f, t.at, :] = values[f]
 
         @pl.when(side == 1)
         def _():
             for f in F2:
                 tl7[f, t.at, :] = values[f]
+                later7[f, t.at, :] = values[f]
 
     tiles(1, h.shape[1], body)
 
@@ -281,8 +283,24 @@
         tiles(1, part.shape[2], body)
 
 
+class Sum:
+    def __init__(self, one, other):
+        self.one, self.other = one, other
+
+    def __getitem__(self, key):
+        return self.one[key] + self.other[key]
+
+
+def nothing_kernel():
+    pass
+
+
 def edges_kernel(prm, part, low, high, ide, edge, tl0, tl7):
     edges_body(prm, "fine", part, low, high, ide, edge, tl0, tl7)
+
+
+def edges_kernel_of_two(prm, part, low, high, low2, high2, ide, edge, tl0, tl7):
+    edges_body(prm, "fine", part, Sum(low, low2), Sum(high, high2), ide, edge, tl0, tl7)
 
 
 def coarse_edges_kernel(own, prm, part, low, high, ide, old, *refs):
@@ -470,7 +488,7 @@
 TINY = pl.CostEstimate(flops=1000, bytes_accessed=1000, transcendentals=0)
 
 
-def call(kernel, outs, args, smem, name, scratch=(), limit=8, after=(), through=()):
+def call(kernel, outs, args, smem, name, scratch=(), limit=8, after=(), through=(), flops=1000):
     after = (*after, *through)
     first = len(args) + len(after) - len(through)
     run = kernel
@@ -488,7 +506,7 @@
         input_output_aliases={first + i: i for i in range(len(through))},
         scratch_shapes=scratch,
         compiler_params=pltpu.CompilerParams(vmem_limit_bytes=limit * MIB),
-        cost_estimate=TINY,
+        cost_estimate=pl.CostEstimate(flops=flops, bytes_accessed=1000, transcendentals=0),
         name=name,
     )(*args, *after)
 
@@ -538,18 +556,18 @@
     edge_row = pl.BlockSpec((1, ny, nz), lambda i: ((rows - 1) * i, 0, 0))
     whole = pl.BlockSpec((2, ny, nz), lambda i: (0, 0, 0))
     far = [pltpu.with_memory_space_constraint(x, pltpu.HBM) for x in (h0, c0, material)]
-    tl0, tl7 = gridded(
+    tl0, tl7, later0, later7 = gridded(
         first_edges_kernel,
         2,
-        [halo] * 2,
-        [whole] * 2,
+        [halo] * 4,
+        [whole] * 4,
         [SMEM] + [edge_row] * 3,
         (prm, *far),
         "first_edges",
     )
     every = range(slices)
-    low, high = halos(tl0, tl7, every, 0)
-    sm, sn, part, ids, ide = call(
+    even = halos(tl0, tl7, every[::2], 0)
+    later0, later7, sm, sn, part, ids, ide = call(
         first_step_kernel,
         [tall, pair, pair, i32(rows, ny, nz), i32(2, ny, nz)],
         (prm, h0, c0, material, phase_flag),
@@ -557,17 +575,26 @@
         "first_step",
         pad,
         26,
+        through=(later0, later7),
     )
-
-    def fine_edges(part, low, high, after=()):
+    odd = halos(later0, later7, every[1::2], 0)
+    even = call(nothing_kernel, [], (), 0, "even_arrived", through=even, flops=10**11)
+
+    def fine_edges(part, sides, after=()):
         return call(
-            edges_kernel, [pair, halo, halo], (prm, part, low, high, ide), 1, "edges", after=after
+            edges_kernel if len(sides) == 2 else edges_kernel_of_two,
+            [pair, halo, halo],
+            (prm, part, *sides, ide),
+            1,
+            "edges",
+            after=after,
         )
 
     base = ()
+    sides = (*even, *odd)
     for k in range(STEPS - 1):
-        sx, tl0, tl7 = fine_edges(part, low, high, base)
-        low, high = halos(tl0, tl7, every, 0)
+        sx, tl0, tl7 = fine_edges(part, sides, base)
+        sides = halos(tl0, tl7, every, 0)
         if k == 0:
             base = call(
                 base_kernel,
@@ -614,7 +641,7 @@
         24,
     )
     vn = sn
-    vx, tl0, tl7 = fine_edges(part, low, high, (vm,))
+    vx, tl0, tl7 = fine_edges(part, sides, (vm,))
     low, high = halos(tl0, tl7, (0,), 1)
     ax = send(vx, 1)
     vn, part = call(

time: 225 us -> 223 us (level)
  waiting for transfers between devices: 92.4 us -> 88.8 us
    ppermute x24 -> x26, waiting for transfers between devices: 92.4 us -> 88.8 us  [move(): return lax.ppermute(x, ('tm', 'space'), pairs)]
    ppermute x24 -> x26, starting transfers between devices: 45.9 us -> 47.8 us  [move(): return lax.ppermute(x, ('tm', 'space'), pairs)]
    pallas_call x15 -> x16, Pallas kernels: 69.9 us -> 69.9 us  [call(): pl.pallas_call(run, out_shape=[f32(*x.shape) for x in through] + list(out...]
  transfers between devices with their start and end apart: 24 -> 26, of which waited for: 10 -> 9; matrix products, arithmetic and copies ran while one was open for 0% -> 0% of each run, Pallas kernels for 27% -> 27%
where the time goes in v2:
time: 223 us; the launch traced here: 222 us
  waiting for transfers between devices  88.8 us (40%)
  Pallas kernels  75.2 us (34%)
  starting transfers between devices  47.8 us (21%)
  local copies, waits for them, and re-layouts  9.07 us (4%)
    ppermute x26, waiting for transfers between devices, move(): return lax.ppermute(x, ('tm', 'space'), pairs)  88.8 us
    pallas_call x16, Pallas kernels, call(): pl.pallas_call(run, out_shape=[f32(*x.shape) for x in through] + list(out...  69.9 us
    ppermute x26, starting transfers between devices, move(): return lax.ppermute(x, ('tm', 'space'), pairs)  47.8 us
    unnamed x40, local copies, waits for them, and re-layouts  8.24 us
    pallas_call x2, Pallas kernels, gridded(): pl.pallas_call(kernel, grid=(steps,), out_shape=outs, in_specs=in_specs,...  5.3 us
  transfers between devices with their start and end apart: 26, of which 9 were waited for; matrix products, arithmetic and copies ran while one was open for 0% of the time, Pallas kernels for 27%

profile of v2, /device:TPU:11, one launch (start us, length us, event | category | flops | bytes accessed | tf_op | source)
XLA Modules:
  0.0 221.9 jit_solution(4968450333835466935)
XLA Ops:
  1.5 2.4 %first_edges.1 = (f32[2,512,128]{2,1,0:T(8,128)S(1)}, f32[2,512,128]{2,1,0:T(8,128)S(1)}, f32[2,512,128]{2,1,0:T(8,128)S(1)}, f32[2,512,128]{2,1,0:T(8,128)S(1)}) custom-call(f32[27]{0:T(128)S(1)} %concatenate.3.prm.refs_0_.refs_1_, f32[8,512,128]{2,1,0:T(8,128)} %bitcast.5, f32[8,512,128]{2,1,0:T(8,128)} %bitcast.8, s32[8,512,128]{2,1,0:T(8,128)} %refs_3_.1), custom_call_target="tpu_custom_call" | custom-call | flops 1000 | bytes 1000 | tf_op jit(solution)/shard_map/first_edges/pallas_call | solution.py:544
  6.9 7.1 %first_step.1 = (f32[2,512,128]{2,1,0:T(8,128)S(1)}, f32[2,512,128]{2,1,0:T(8,128)S(1)}, f32[2,4,512,128]{3,2,1,0:T(8,128)S(1)}, f32[2,2,512,128]{3,2,1,0:T(8,12...) custom-call(f32[27]{0:T(128)S(1)} %concatenate.3.prm.refs_0_.refs_1_, ...), custom_call_target="tpu_custom_call", output_to_operand_aliasing={{0}: (5, {}), {1}: (6, {})} | custom-call | flops 1000 | bytes 1000 | tf_op jit(solution)/shard_map/first_step/pallas_call | solution.py:501
  14.0 3.1 %collective-permute-start.2 = (f32[2,512,128]{2,1,0:T(8,128)S(1)}, f32[2,512,128]{2,1,0:T(8,128)S(1)}, u32[]{:S(2)}, u32[]{:S(2)}) collective-permute-start(f32[2,512,128]{2,1,0:T(8,128)S(1)} %get-tuple-element.63), channel_id=1, source_target_pairs={{8,9},{9,10},{10,11},{11,12},{12,13},{13,14},{14,15},{24,25},{25,2... | collective-permute-start | bytes 1572872 | tf_op jit(solution)/shard_map/ppermute | solution.py:532
  17.1 3.0 %collective-permute-start.3 = (f32[2,512,128]{2,1,0:T(8,128)S(1)}, f32[2,512,128]{2,1,0:T(8,128)S(1)}, u32[]{:S(2)}, u32[]{:S(2)}) collective-permute-start(f32[2,512,128]{2,1,0:T(8,128)S(1)} %get-tuple-element.64), channel_id=1, source_target_pairs={{9,8},{10,9},{11,10},{12,11},{13,12},{14,13},{15,14},{25,24},{26,2... | collective-permute-start | bytes 1572872 | tf_op jit(solution)/shard_map/ppermute | solution.py:532
  20.2 10.9 %collective-permute-done.2.low2 = f32[2,512,128]{2,1,0:T(8,128)S(1)} collective-permute-done((f32[2,512,128]{2,1,0:T(8,128)S(1)}, f32[2,512,128]{2,1,0:T(8,128)S(1)}, u32[]{:S(2)}, u32[]{:S(2)}) %collective-permute-start.2) | collective-permute-done | bytes 524320 | tf_op jit(solution)/shard_map/ppermute | solution.py:532
  34.1 2.3 %collective-permute-start.4 = (f32[2,512,128]{2,1,0:T(8,128)S(1)}, f32[2,512,128]{2,1,0:T(8,128)S(1)}, u32[]{:S(2)}, u32[]{:S(2)}) collective-permute-start(f32[2,512,128]{2,1,0:T(8,128)S(1)} %get-tuple-element.71), channel_id=1, source_target_pairs={{0,1},{1,2},{2,3},{3,4},{4,5},{5,6},{6,7},{8,9},{9,10},{10,11},{11... | collective-permute-start | bytes 1572872 | tf_op jit(solution)/shard_map/ppermute | solution.py:532
  36.3 5.3 %collective-permute-start.5 = (f32[2,512,128]{2,1,0:T(8,128)S(1)}, f32[2,512,128]{2,1,0:T(8,128)S(1)}, u32[]{:S(2)}, u32[]{:S(2)}) collective-permute-start(f32[2,512,128]{2,1,0:T(8,128)S(1)} %get-tuple-element.72), channel_id=1, source_target_pairs={{1,0},{2,1},{3,2},{4,3},{5,4},{6,5},{7,6},{9,8},{10,9},{11,10},{12... | collective-permute-start | bytes 1572872 | tf_op jit(solution)/shard_map/ppermute | solution.py:532
  41.6 3.3 %base.1 = (f32[2,4,512,128]{3,2,1,0:T(8,128)S(1)}, f32[2,2,512,128]{3,2,1,0:T(8,128)S(1)}, f32[2,2,512,128]{3,2,1,0:T(8,128)S(1)}) custom-call(f32[27]{0:T(128)S(1)} %concatenate.3.prm.refs_0_.refs_1_, f32[8,512,128]{2,1,0:T(8,128)S(1)} %bitcast.7, f32[8,512,128]{2,1,0:T(8,128)S(1)} %bitcast.10, f32[2,4,512,128]{3,2,1,0:T(8,128)S(1)} %get-tuple-element.56.sm, ...), custom_call_target="tpu_custom_call" | custom-call | flops 1000 | bytes 1000 | tf_op jit(solution)/shard_map/base/pallas_call | solution.py:501
  44.9 6.9 %step.1 = (f32[2,4,512,128]{3,2,1,0:T(8,128)S(1)}, f32[2,2,512,128]{3,2,1,0:T(8,128)S(1)}, f32[2,2,512,128]{3,2,1,0:T(8,128)S(1)}) custom-call(f32[27]{0:T(128)S(1)} %concatenate.3.prm.refs_0_.refs_1_, f32[2,4,512,128]{3,2,1,0:T(8,128)S(1)} %get-tuple-element.56.sm, f32[2,2,512,128]{3,2,1,0:T(8,128)S(1)} %get-tuple-element.57.sn, ...), custom_call_target="tpu_custom_call" | custom-call | flops 1000 | bytes 1000 | tf_op jit(solution)/shard_map/step/pallas_call | solution.py:501
  51.8 4.5 %collective-permute-done.4.refs_2_ = f32[2,512,128]{2,1,0:T(8,128)S(1)} collective-permute-done((f32[2,512,128]{2,1,0:T(8,128)S(1)}, f32[2,512,128]{2,1,0:T(8,128)S(1)}, u32[]{:S(2)}, u32[]{:S(2)}) %collective-permute-start.4) | collective-permute-done | bytes 524320 | tf_op jit(solution)/shard_map/ppermute | solution.py:532
  56.3 3.3 %collective-permute-done.5.refs_3_ = f32[2,512,128]{2,1,0:T(8,128)S(1)} collective-permute-done((f32[2,512,128]{2,1,0:T(8,128)S(1)}, f32[2,512,128]{2,1,0:T(8,128)S(1)}, u32[]{:S(2)}, u32[]{:S(2)}) %collective-permute-start.5) | collective-permute-done | bytes 524320 | tf_op jit(solution)/shard_map/ppermute | solution.py:532
  61.0 1.9 collective-permute-start.10
  62.9 3.4 %collective-permute-start.9 = (f32[2,512,128]{2,1,0:T(8,128)S(1)}, f32[2,512,128]{2,1,0:T(8,128)S(1)}, u32[]{:S(2)}, u32[]{:S(2)}) collective-permute-start(f32[2,512,128]{2,1,0:T(8,128)S(1)} %get-tuple-element.81), channel_id=1, source_target_pairs={{0,1},{1,2},{2,3},{3,4},{4,5},{5,6},{6,7},{8,9},{9,10},{10,11},{11... | collective-permute-start | bytes 1572872 | tf_op jit(solution)/shard_map/ppermute | solution.py:532
  66.3 7.9 %step_apart.1 = (f32[4,512,128]{2,1,0:T(8,128)S(1)}, f32[4,512,128]{2,1,0:T(8,128)}, f32[2,2,512,128]{3,2,1,0:T(8,128)}, f32[2,2,512,128]{3,2,1,0:T(8,128)S(1)}) custom-call(f32[27]{0:T(128)S(1)} %concatenate.3.prm.refs_0_.refs_1_, f32[2,4,512,128]{3,2,1,0:T(8,128)S(1)} %get-tuple-element.68.sm, f32[2,2,512,128]{3,2,1,0:T(8,128)S(1)} %get-tuple-element.69.sn, ...), custom_call_target="tpu_custom_call" | custom-call | flops 1000 | bytes 1000 | tf_op jit(solution)/shard_map/step_apart/pallas_call | solution.py:501
  78.3 9.0 %collective-permute-done.10.refs_3_ = f32[2,512,128]{2,1,0:T(8,128)S(1)} collective-permute-done((f32[2,512,128]{2,1,0:T(8,128)S(1)}, f32[2,512,128]{2,1,0:T(8,128)S(1)}, u32[]{:S(2)}, u32[]{:S(2)}) %collective-permute-start.10) | collective-permute-done | bytes 524320 | tf_op jit(solution)/shard_map/ppermute | solution.py:532
  87.2 2.6 %edges.6 = (f32[2,2,512,128]{3,2,1,0:T(8,128)}, f32[2,512,128]{2,1,0:T(8,128)}, f32[2,512,128]{2,1,0:T(8,128)}) custom-call(f32[27]{0:T(128)S(1)} %concatenate.3.prm.refs_0_.refs_1_, f32[2,2,512,128]{3,2,1,0:T(8,128)S(1)} %get-tuple-element.80.refs_1_, f32[2,512,128]{2,1,0:T(8,128)S(1)} %collective-permute-done.9.refs_2_, ...), custom_call_target="tpu_custom_call" | custom-call | flops 1000 | bytes 1000 | tf_op jit(solution)/shard_map/edges/pallas_call | solution.py:501
  91.5 3.6 %collective-permute-start.13 = (f32[2,512,128]{2,1,0:T(8,128)}, f32[2,512,128]{2,1,0:T(8,128)}, u32[]{:S(2)}, u32[]{:S(2)}) collective-permute-start(f32[2,512,128]{2,1,0:T(8,128)} %get-tuple-element.89), channel_id=1, source_target_pairs={{0,1},{1,2},{2,3},{3,4},{4,5},{5,6},{6,7},{8,9},{9,10},{10,11},{11... | collective-permute-start | bytes 1572872 | tf_op jit(solution)/shard_map/ppermute | solution.py:532
  96.1 2.5 %collective-permute-start.14 = (f32[2,512,128]{2,1,0:T(8,128)}, f32[2,512,128]{2,1,0:T(8,128)}, u32[]{:S(2)}, u32[]{:S(2)}) collective-permute-start(f32[2,512,128]{2,1,0:T(8,128)} %get-tuple-element.90), channel_id=1, source_target_pairs={{1,0},{2,1},{3,2},{4,3},{5,4},{6,5},{7,6},{9,8},{10,9},{11,10},{12... | collective-permute-start | bytes 1572872 | tf_op jit(solution)/shard_map/ppermute | solution.py:532
  99.9 8.2 %step_joined.1 = (f32[2,4,512,128]{3,2,1,0:T(8,128)S(1)}, f32[2,2,512,128]{3,2,1,0:T(8,128)S(1)}, f32[2,2,512,128]{3,2,1,0:T(8,128)S(1)}) custom-call(f32[27]{0:T(128)S(1)} %concatenate.3.prm.refs_0_.refs_1_, f32[4,512,128]{2,1,0:T(8,128)S(1)} %copy-done.17, f32[4,512,128]{2,1,0:T(8,128)} %get-tuple-element.78.mc, f32[2,2,512,128]{3,2,1,0:T(8,128)} %get-tuple-element.79.sn, ...), custom_call_target="tpu_custom_call" | custom-call | flops 1000 | bytes 1000 | tf_op jit(solution)/shard_map/step_joined/pallas_call | solution.py:501
  108.1 3.4 %replay.1 = (f32[2,4,512,128]{3,2,1,0:T(8,128)S(1)}, f32[2,2,512,128]{3,2,1,0:T(8,128)S(1)}, f32[2,4,512,128]{3,2,1,0:T(8,128)}) custom-call(s32[1]{0:T(128)} %bitcast.2.own, f32[27]{0:T(128)S(1)} %concatenate.3.prm.refs_0_.refs_1_, f32[4,512,128]{2,1,0:T(8,128)S(1)} %copy-done.19, f32[4,512,128]{2,1,0:T(8,128)} %collective-permute-done.7.mc, ...), custom_call_target="tpu_custom_call" | custom-call | flops 1000 | bytes 1000 | tf_op jit(solution)/shard_map/replay/pallas_call | solution.py:501
  111.5 5.9 %collective-permute-done.13.refs_2_ = f32[2,512,128]{2,1,0:T(8,128)} collective-permute-done((f32[2,512,128]{2,1,0:T(8,128)}, f32[2,512,128]{2,1,0:T(8,128)}, u32[]{:S(2)}, u32[]{:S(2)}) %collective-permute-start.13) | collective-permute-done | bytes 524320 | tf_op jit(solution)/shard_map/ppermute | solution.py:532
  117.4 2.2 collective-permute-done.14.refs_3_
  119.6 2.1 edges.7
  122.5 2.0 collective-permute-start.12
  126.0 1.8 coarse_rim.1
  129.5 1.9 coarse_edges.1
  137.6 4.2 %coarse_mid.1.refs_13_ = f32[2,4,512,128]{3,2,1,0:T(8,128)} custom-call(s32[1]{0:T(128)} %bitcast.1.own.refs_0_, f32[27]{0:T(128)S(1)} %concatenate.3.prm.refs_0_.refs_1_, f32[2,4,512,128]{3,2,1,0:T(8,128)} %collective-permute-done.12.am.refs_2_, f32[2,2,512,128]{3,2,1,0:T(8,128)} %collective-permute-done.16.an.refs_3_, f32[2,4,512,128]{3,2,1,0:T(8,128)S(1)} %copy-done.2, ...), custom_call_target="tpu_custom_call" | custom-call | flops 1000 | bytes 1000 | tf_op jit(solution)/shard_map/coarse_mid/pallas_call | solution.py:501
  141.8 5.0 %coarse_outer.1 = (f32[2,4,512,128]{3,2,1,0:T(8,128)}, f32[2,4,512,128]{3,2,1,0:T(8,128)}, f32[2,512,128]{2,1,0:T(8,128)}, f32[2,512,128]{2,1,0:T(8,128)}) custom-call(s32[1]{0:T(128)} %bitcast.1.own.refs_0_, f32[27]{0:T(128)S(1)} %concatenate.3.prm.refs_0_.refs_1_, ...), custom_call_target="tpu_custom_call", output_to_operand_aliasing={{0}: (13, {})} | custom-call | flops 1000 | bytes 1000 | tf_op jit(solution)/shard_map/coarse_outer/pallas_call | solution.py:501
  152.0 48.4 %collective-permute-done.24.am = f32[2,4,512,128]{3,2,1,0:T(8,128)} collective-permute-done((f32[2,4,512,128]{3,2,1,0:T(8,128)}, f32[2,4,512,128]{3,2,1,0:T(8,128)}, u32[]{:S(2)}, u32[]{:S(2)}) %collective-permute-start.24) | collective-permute-done | bytes 2097184 | tf_op jit(solution)/shard_map/ppermute | solution.py:532
  200.4 3.0 %collective-permute-done.25.ar = f32[2,4,512,128]{3,2,1,0:T(8,128)} collective-permute-done((f32[2,4,512,128]{3,2,1,0:T(8,128)}, f32[2,4,512,128]{3,2,1,0:T(8,128)}, u32[]{:S(2)}, u32[]{:S(2)}) %collective-permute-start.25) | collective-permute-done | bytes 2097184 | tf_op jit(solution)/shard_map/ppermute | solution.py:532
  206.2 12.8 %last_rows.1 = (f32[1,8,512,128]{3,2,1,0:T(8,128)}, f32[1,8,512,128]{3,2,1,0:T(8,128)}) custom-call(s32[1]{0:T(128)} %bitcast.own, f32[27]{0:T(128)S(1)} %concatenate.3.prm.refs_0_.refs_1_, f32[2,4,512,128]{3,2,1,0:T(8,128)} %collective-permute-done.24.am, f32[2,4,512,128]{3,2,1,0:T(8,128)} %collective-permute-done.25.ar, f32[2,4,512,128]{3,2,1,0:T(8,128)S(1)} %copy-done.3, ...), custom_call_target="tpu_custom_call" | custom-call | flops 1000 | bytes 1000 | tf_op jit(solution)/shard_map/last_rows/pallas_call | solution.py:501
  219.0 2.9 %last_edges.1 = (f32[1,8,512,128]{3,2,1,0:T(8,128)}, f32[1,8,512,128]{3,2,1,0:T(8,128)}) custom-call(s32[1]{0:T(128)} %bitcast.own, f32[27]{0:T(128)S(1)} %concatenate.3.prm.refs_0_.refs_1_, f32[2,512,128]{2,1,0:T(8,128)} %collective-permute-done.22.low, f32[2,512,128]{2,1,0:T(8,128)} %collective-permute-done.23.high, ...), custom_call_target="tpu_custom_call", output_to_operand_aliasing={{0}: (5, {}), {1}: (6, {})} | custom-call | flops 1000 | bytes 1000 | tf_op jit(solution)/shard_map/last_edges/pallas_call | solution.py:544
  (79 shorter events, 34.1 us)
Async XLA Ops:
  3.9 16.3 %collective-permute-start = (f32[2,512,128]{2,1,0:T(8,128)S(1)}, f32[2,512,128]{2,1,0:T(8,128)S(1)}, u32[]{:S(2)}, u32[]{:S(2)}) collective-permute-start(f32[2,512,128]{2,1,0:T(8,128)S(1)} %get-tuple-element.59), channel_id=1, source_target_pairs={{0,1},{1,2},{2,3},{3,4},{4,5},{5,6},{6,7},{16,17},{17,18},{18,19},... | collective-permute-start | bytes 1572872 | tf_op jit(solution)/shard_map/ppermute | solution.py:532
  4.6 15.6 %collective-permute-start.1 = (f32[2,512,128]{2,1,0:T(8,128)S(1)}, f32[2,512,128]{2,1,0:T(8,128)S(1)}, u32[]{:S(2)}, u32[]{:S(2)}) collective-permute-start(f32[2,512,128]{2,1,0:T(8,128)S(1)} %get-tuple-element.60), channel_id=1, source_target_pairs={{1,0},{2,1},{3,2},{4,3},{5,4},{6,5},{7,6},{17,16},{18,17},{19,18},... | collective-permute-start | bytes 1572872 | tf_op jit(solution)/shard_map/ppermute | solution.py:532
  14.0 73.2 %copy-start.8 = (s32[2,512,128]{2,1,0:T(8,128)}, s32[2,512,128]{2,1,0:T(8,128)S(1)}, u32[]{:S(2)}) copy-start(s32[2,512,128]{2,1,0:T(8,128)S(1)} %get-tuple-element.65.ide.refs_4_.refs_10_) | copy-start | bytes 1572868
  14.0 17.1 %collective-permute-start.2 = (f32[2,512,128]{2,1,0:T(8,128)S(1)}, f32[2,512,128]{2,1,0:T(8,128)S(1)}, u32[]{:S(2)}, u32[]{:S(2)}) collective-permute-start(f32[2,512,128]{2,1,0:T(8,128)S(1)} %get-tuple-element.63), channel_id=1, source_target_pairs={{8,9},{9,10},{10,11},{11,12},{12,13},{13,14},{14,15},{24,25},{25,2... | collective-permute-start | bytes 1572872 | tf_op jit(solution)/shard_map/ppermute | solution.py:532
  17.1 15.5 %collective-permute-start.3 = (f32[2,512,128]{2,1,0:T(8,128)S(1)}, f32[2,512,128]{2,1,0:T(8,128)S(1)}, u32[]{:S(2)}, u32[]{:S(2)}) collective-permute-start(f32[2,512,128]{2,1,0:T(8,128)S(1)} %get-tuple-element.64), channel_id=1, source_target_pairs={{9,8},{10,9},{11,10},{12,11},{13,12},{14,13},{15,14},{25,24},{26,2... | collective-permute-start | bytes 1572872 | tf_op jit(solution)/shard_map/ppermute | solution.py:532
  34.1 22.2 %collective-permute-start.4 = (f32[2,512,128]{2,1,0:T(8,128)S(1)}, f32[2,512,128]{2,1,0:T(8,128)S(1)}, u32[]{:S(2)}, u32[]{:S(2)}) collective-permute-start(f32[2,512,128]{2,1,0:T(8,128)S(1)} %get-tuple-element.71), channel_id=1, source_target_pairs={{0,1},{1,2},{2,3},{3,4},{4,5},{5,6},{6,7},{8,9},{9,10},{10,11},{11... | collective-permute-start | bytes 1572872 | tf_op jit(solution)/shard_map/ppermute | solution.py:532
  36.3 23.2 %collective-permute-start.5 = (f32[2,512,128]{2,1,0:T(8,128)S(1)}, f32[2,512,128]{2,1,0:T(8,128)S(1)}, u32[]{:S(2)}, u32[]{:S(2)}) collective-permute-start(f32[2,512,128]{2,1,0:T(8,128)S(1)} %get-tuple-element.72), channel_id=1, source_target_pairs={{1,0},{2,1},{3,2},{4,3},{5,4},{6,5},{7,6},{9,8},{10,9},{11,10},{12... | collective-permute-start | bytes 1572872 | tf_op jit(solution)/shard_map/ppermute | solution.py:532
  44.9 42.3 %copy-start = (f32[2,4,512,128]{3,2,1,0:T(8,128)}, f32[2,4,512,128]{3,2,1,0:T(8,128)S(1)}, u32[]{:S(2)}) copy-start(f32[2,4,512,128]{3,2,1,0:T(8,128)S(1)} %get-tuple-element.73.refs_5_.km) | copy-start | bytes 6291460
  44.9 42.3 %copy-start.4 = (f32[2,2,512,128]{3,2,1,0:T(8,128)}, f32[2,2,512,128]{3,2,1,0:T(8,128)S(1)}, u32[]{:S(2)}) copy-start(f32[2,2,512,128]{3,2,1,0:T(8,128)S(1)} %get-tuple-element.75.refs_7_.kx.refs_8_) | copy-start | bytes 3145732
  61.0 26.2 %collective-permute-start.10 = (f32[2,512,128]{2,1,0:T(8,128)S(1)}, f32[2,512,128]{2,1,0:T(8,128)S(1)}, u32[]{:S(2)}, u32[]{:S(2)}) collective-permute-start(f32[2,512,128]{2,1,0:T(8,128)S(1)} %get-tuple-element.82), channel_id=1, source_target_pairs={{1,0},{2,1},{3,2},{4,3},{5,4},{6,5},{7,6},{9,8},{10,9},{11,10},{12... | collective-permute-start | bytes 1572872 | tf_op jit(solution)/shard_map/ppermute | solution.py:532
  62.9 24.3 %collective-permute-start.9 = (f32[2,512,128]{2,1,0:T(8,128)S(1)}, f32[2,512,128]{2,1,0:T(8,128)S(1)}, u32[]{:S(2)}, u32[]{:S(2)}) collective-permute-start(f32[2,512,128]{2,1,0:T(8,128)S(1)} %get-tuple-element.81), channel_id=1, source_target_pairs={{0,1},{1,2},{2,3},{3,4},{4,5},{5,6},{6,7},{8,9},{9,10},{10,11},{11... | collective-permute-start | bytes 1572872 | tf_op jit(solution)/shard_map/ppermute | solution.py:532
  74.2 15.7 %copy-start.16 = (f32[4,512,128]{2,1,0:T(8,128)}, f32[4,512,128]{2,1,0:T(8,128)S(1)}, u32[]{:S(2)}) copy-start(f32[4,512,128]{2,1,0:T(8,128)S(1)} %get-tuple-element.77.mh) | copy-start | bytes 3145732
  74.2 20.9 %collective-permute-start.6 = (f32[4,512,128]{2,1,0:T(8,128)S(1)}, f32[4,512,128]{2,1,0:T(8,128)S(1)}, u32[]{:S(2)}, u32[]{:S(2)}) collective-permute-start(f32[4,512,128]{2,1,0:T(8,128)S(1)} %get-tuple-element.77.mh), channel_id=1, source_target_pairs={{0,8},{1,9},{2,10},{3,11},{4,12},{5,13},{6,14},{7,15}} | collective-permute-start | bytes 3145736 | tf_op jit(solution)/shard_map/ppermute | solution.py:532
  74.9 33.2 %collective-permute-start.7 = (f32[4,512,128]{2,1,0:T(8,128)}, f32[4,512,128]{2,1,0:T(8,128)}, u32[]{:S(2)}, u32[]{:S(2)}) collective-permute-start(f32[4,512,128]{2,1,0:T(8,128)} %get-tuple-element.78.mc), channel_id=1, source_target_pairs={{0,8},{1,9},{2,10},{3,11},{4,12},{5,13},{6,14},{7,15}} | collective-permute-start | bytes 3145736 | tf_op jit(solution)/shard_map/ppermute | solution.py:532
  76.6 31.5 %collective-permute-start.8 = (f32[2,2,512,128]{3,2,1,0:T(8,128)}, f32[2,2,512,128]{3,2,1,0:T(8,128)}, u32[]{:S(2)}, u32[]{:S(2)}) collective-permute-start(f32[2,2,512,128]{3,2,1,0:T(8,128)} %get-tuple-element.79.sn), channel_id=1, source_target_pairs={{0,8},{1,9},{2,10},{3,11},{4,12},{5,13},{6,14},{7,15}} | collective-permute-start | bytes 3145736 | tf_op jit(solution)/shard_map/ppermute | solution.py:532
  89.8 18.2 %collective-permute-start.11 = (f32[2,2,512,128]{3,2,1,0:T(8,128)}, f32[2,2,512,128]{3,2,1,0:T(8,128)}, u32[]{:S(2)}, u32[]{:S(2)}) collective-permute-start(f32[2,2,512,128]{3,2,1,0:T(8,128)} %get-tuple-element.83.sx), channel_id=1, source_target_pairs={{0,8},{1,9},{2,10},{3,11},{4,12},{5,13},{6,14},{7,15}} | collective-permute-start | bytes 3145736 | tf_op jit(solution)/shard_map/ppermute | solution.py:532
  91.5 26.0 %collective-permute-start.13 = (f32[2,512,128]{2,1,0:T(8,128)}, f32[2,512,128]{2,1,0:T(8,128)}, u32[]{:S(2)}, u32[]{:S(2)}) collective-permute-start(f32[2,512,128]{2,1,0:T(8,128)} %get-tuple-element.89), channel_id=1, source_target_pairs={{0,1},{1,2},{2,3},{3,4},{4,5},{5,6},{6,7},{8,9},{9,10},{10,11},{11... | collective-permute-start | bytes 1572872 | tf_op jit(solution)/shard_map/ppermute | solution.py:532
  96.1 23.5 %collective-permute-start.14 = (f32[2,512,128]{2,1,0:T(8,128)}, f32[2,512,128]{2,1,0:T(8,128)}, u32[]{:S(2)}, u32[]{:S(2)}) collective-permute-start(f32[2,512,128]{2,1,0:T(8,128)} %get-tuple-element.90), channel_id=1, source_target_pairs={{1,0},{2,1},{3,2},{4,3},{5,4},{6,5},{7,6},{9,8},{10,9},{11,10},{12... | collective-permute-start | bytes 1572872 | tf_op jit(solution)/shard_map/ppermute | solution.py:532
  108.1 11.5 %copy-start.9 = (s32[2,512,128]{2,1,0:T(8,128)S(1)}, s32[2,512,128]{2,1,0:T(8,128)}, u32[]{:S(2)}) copy-start(s32[2,512,128]{2,1,0:T(8,128)} %copy-done.8) | copy-start | bytes 1572868
  121.8 4.2 %collective-permute-start.15 = (f32[2,2,512,128]{3,2,1,0:T(8,128)S(1)}, f32[2,2,512,128]{3,2,1,0:T(8,128)S(1)}, u32[]{:S(2)}, u32[]{:S(2)}) collective-permute-start(f32[2,2,512,128]{3,2,1,0:T(8,128)S(1)} %get-tuple-element.91.ox.old), channel_id=1, source_target_pairs={{0,8},{1,9},{2,10},{3,11},{4,12},{5,13},{6,14},{7,15}} | collective-permute-start | bytes 3145736 | tf_op jit(solution)/shard_map/ppermute | solution.py:532
  122.5 13.4 %collective-permute-start.12 = (f32[2,4,512,128]{3,2,1,0:T(8,128)}, f32[2,4,512,128]{3,2,1,0:T(8,128)}, u32[]{:S(2)}, u32[]{:S(2)}) collective-permute-start(f32[2,4,512,128]{3,2,1,0:T(8,128)} %get-tuple-element.85.refs_5_.om), channel_id=1, source_target_pairs={{8,16},{9,17},{10,18},{11,19},{12,20},{13,21},{14,22},{15,23}} | collective-permute-start | bytes 6291464 | tf_op jit(solution)/shard_map/ppermute | solution.py:532
  124.6 4.9 %collective-permute-start.17 = (f32[2,512,128]{2,1,0:T(8,128)S(1)}, f32[2,512,128]{2,1,0:T(8,128)S(1)}, u32[]{:S(2)}, u32[]{:S(2)}) collective-permute-start(f32[2,512,128]{2,1,0:T(8,128)S(1)} %get-tuple-element.95), channel_id=1, source_target_pairs={{0,9},{1,10},{2,11},{3,12},{4,13},{5,14},{6,15}} | collective-permute-start | bytes 1572872 | tf_op jit(solution)/shard_map/ppermute | solution.py:532
  125.3 4.2 %collective-permute-start.18 = (f32[2,512,128]{2,1,0:T(8,128)S(1)}, f32[2,512,128]{2,1,0:T(8,128)S(1)}, u32[]{:S(2)}, u32[]{:S(2)}) collective-permute-start(f32[2,512,128]{2,1,0:T(8,128)S(1)} %get-tuple-element.96), channel_id=1, source_target_pairs={{1,8},{2,9},{3,10},{4,11},{5,12},{6,13},{7,14}} | collective-permute-start | bytes 1572872 | tf_op jit(solution)/shard_map/ppermute | solution.py:532
  127.8 8.2 %collective-permute-start.16 = (f32[2,2,512,128]{3,2,1,0:T(8,128)}, f32[2,2,512,128]{3,2,1,0:T(8,128)}, u32[]{:S(2)}, u32[]{:S(2)}) collective-permute-start(f32[2,2,512,128]{3,2,1,0:T(8,128)} %get-tuple-element.93.refs_11_), channel_id=1, source_target_pairs={{8,16},{9,17},{10,18},{11,19},{12,20},{13,21},{14,22},{15,23}} | collective-permute-start | bytes 3145736 | tf_op jit(solution)/shard_map/ppermute | solution.py:532
  131.4 10.3 %collective-permute-start.19 = (f32[2,2,512,128]{3,2,1,0:T(8,128)}, f32[2,2,512,128]{3,2,1,0:T(8,128)}, u32[]{:S(2)}, u32[]{:S(2)}) collective-permute-start(f32[2,2,512,128]{3,2,1,0:T(8,128)} %get-tuple-element.97.refs_12_), channel_id=1, source_target_pairs={{8,16},{9,17},{10,18},{11,19},{12,20},{13,21},{14,22},{15,23}} | collective-permute-start | bytes 3145736 | tf_op jit(solution)/shard_map/ppermute | solution.py:532
  133.0 8.7 %collective-permute-start.20 = (f32[2,512,128]{2,1,0:T(8,128)}, f32[2,512,128]{2,1,0:T(8,128)}, u32[]{:S(2)}, u32[]{:S(2)}) collective-permute-start(f32[2,512,128]{2,1,0:T(8,128)} %get-tuple-element.98), channel_id=1, source_target_pairs={{8,17},{9,18},{10,19},{11,20},{12,21},{13,22},{14,23}} | collective-permute-start | bytes 1572872 | tf_op jit(solution)/shard_map/ppermute | solution.py:532
  134.5 7.2 %collective-permute-start.21 = (f32[2,512,128]{2,1,0:T(8,128)}, f32[2,512,128]{2,1,0:T(8,128)}, u32[]{:S(2)}, u32[]{:S(2)}) collective-permute-start(f32[2,512,128]{2,1,0:T(8,128)} %get-tuple-element.99), channel_id=1, source_target_pairs={{9,16},{10,17},{11,18},{12,19},{13,20},{14,21},{15,22}} | collective-permute-start | bytes 1572872 | tf_op jit(solution)/shard_map/ppermute | solution.py:532
  146.8 53.6 %collective-permute-start.24 = (f32[2,4,512,128]{3,2,1,0:T(8,128)}, f32[2,4,512,128]{3,2,1,0:T(8,128)}, u32[]{:S(2)}, u32[]{:S(2)}) collective-permute-start(f32[2,4,512,128]{3,2,1,0:T(8,128)} %get-tuple-element.102.om), channel_id=1, source_target_pairs={{16,24},{17,25},{18,26},{19,27},{20,28},{21,29},{22,30},{23,31}} | collective-permute-start | bytes 6291464 | tf_op jit(solution)/shard_map/ppermute | solution.py:532
  148.1 55.3 %collective-permute-start.25 = (f32[2,4,512,128]{3,2,1,0:T(8,128)}, f32[2,4,512,128]{3,2,1,0:T(8,128)}, u32[]{:S(2)}, u32[]{:S(2)}) collective-permute-start(f32[2,4,512,128]{3,2,1,0:T(8,128)} %get-tuple-element.103.rim), channel_id=1, source_target_pairs={{16,24},{17,25},{18,26},{19,27},{20,28},{21,29},{22,30},{23,31}} | collective-permute-start | bytes 6291464 | tf_op jit(solution)/shard_map/ppermute | solution.py:532
  149.4 69.6 %collective-permute-start.22 = (f32[2,512,128]{2,1,0:T(8,128)}, f32[2,512,128]{2,1,0:T(8,128)}, u32[]{:S(2)}, u32[]{:S(2)}) collective-permute-start(f32[2,512,128]{2,1,0:T(8,128)} %get-tuple-element.100), channel_id=1, source_target_pairs={{16,25},{17,26},{18,27},{19,28},{20,29},{21,30},{22,31}} | collective-permute-start | bytes 1572872 | tf_op jit(solution)/shard_map/ppermute | solution.py:532
  150.7 68.4 %collective-permute-start.23 = (f32[2,512,128]{2,1,0:T(8,128)}, f32[2,512,128]{2,1,0:T(8,128)}, u32[]{:S(2)}, u32[]{:S(2)}) collective-permute-start(f32[2,512,128]{2,1,0:T(8,128)} %get-tuple-element.101), channel_id=1, source_target_pairs={{17,24},{18,25},{19,26},{20,27},{21,28},{22,29},{23,30}} | collective-permute-start | bytes 1572872 | tf_op jit(solution)/shard_map/ppermute | solution.py:532
  206.2 12.8 %copy-start.11 = (s32[2,512,128]{2,1,0:T(8,128)S(1)}, s32[2,512,128]{2,1,0:T(8,128)}, u32[]{:S(2)}) copy-start(s32[2,512,128]{2,1,0:T(8,128)} %copy-done.8) | copy-start | bytes 1572868
  (14 other events, 50.8 us)

commit v3 on v2

--- a/solution.py
+++ b/solution.py
@@ -344,9 +344,11 @@
 
     def update(name, i, r, t):
         new = coarse(tab, pad, r + 1, t, ids[r, t.at, :], at(arrived[name], i, t))
-        end, start = at(old[name], i, t), at(base[name], i, t)
+        change = at(old[name], i, t)
+        if base is not None:
+            change = [v - w for v, w in zip(change, at(base[name], i, t))]
         for f in F2:
-            put(name, f, i, r, t, new[f] + (end[f] - start[f]))
+            put(name, f, i, r, t, new[f] + change[f])
 
     if "m" in which:
         block.each(ny, melt, arrived)
@@ -395,86 +397,107 @@
         nn[...] = on[...]
 
 
-def coarse_outer_kernel(
-    own, prm, am, an, ax, low, high, kn, kx, ids, ide, on, ox, *refs
-):
-    rim, tl0, tl7, part, pad = refs[-5:]
-    edge, beside = Rows(rim, 0), Rows(rim, 2)
-
+def drift_kernel(prm, on, ox, kn, kx, d):
+    def body(i, t):
+        for f in F2:
+            d[f, i, t.at, :] = ox[f, i, t.at, :] - kx[f, i, t.at, :]
+            d[f, 2 + i, t.at, :] = on[f, i, t.at, :] - kn[f, i, t.at, :]
+
+    tiles(2, on.shape[2], body)
+
+
+def next_rim_kernel(own, prm, vm, vn, vx, d, ids, nn, part, pad):
     @pl.when(own[0] != 0)
     def _():
         coarse_body(
             prm,
-            {"x": ax, "n": an, "m": am},
-            {"n": kn, "x": kx},
-            {"n": on, "x": ox},
+            {"x": vx, "n": vn, "m": vm},
+            None,
+            {"n": Rows(d, 2), "x": Rows(d, 0)},
             ids,
-            into({"n": beside, "x": part}),
+            into({"n": nn, "x": part}),
             "xn",
             pad,
             True,
         )
+
+
+def next_edges_kernel(own, prm, part, low, high, ide, edge, tl0, tl7):
+    @pl.when(own[0] != 0)
+    def _():
         edges_body(prm, "coarse", part, low, high, ide, edge, tl0, tl7)
 
-    @pl.when(own[0] == 0)
-    def _():
-        for f in F2:
-            for e in range(2):
-                edge[f, e] = ox[f, e]
-                beside[f, e] = on[f, e]
-
-
-def last_rows_kernel(own, prm, am, ar, km, kn, kx, ids, om, rim, oh, oc, pad):
+
+def last_mid_kernel(own, prm, am, an, km, ids, om, oh, oc, pad):
     out = (oh, oc)
-    ax, an, ox, on = Rows(ar, 0), Rows(ar, 2), Rows(rim, 0), Rows(rim, 2)
 
     @pl.when(own[0] != 0)
     def _():
         def put(name, f, i, r, t, value):
             out[f][0, r, t.at, :] = value
 
-        coarse_body(
-            prm,
-            {"x": ax, "n": an, "m": am},
-            {"m": km, "n": kn, "x": kx},
-            {"m": om, "n": on, "x": ox},
-            ids,
-            put,
-            "mnx",
-            pad,
-            True,
-        )
+        coarse_body(prm, {"n": an, "m": am}, {"m": km}, {"m": om}, ids, put, "m", pad, False)
 
     @pl.when(own[0] == 0)
     def _():
-        old = {"m": om, "n": on, "x": ox}
-
-        def body(name, i, r, t):
+        def body(i, t):
             for f in F2:
-                out[f][0, r, t.at, :] = old[name][f, i, t.at, :]
-
-        Parts(om.shape[1]).each(om.shape[2], body)
-
-
-def last_edges_kernel(own, prm, low, high, ide, oh, oc, nh, nc):
-    first = pl.program_id(0) == 0
-
-    @pl.when(own[0] != 0)
+                out[f][0, i + 2, t.at, :] = om[f, i, t.at, :]
+
+        tiles(om.shape[1], om.shape[2], body)
+
+
+def last_outer_kernel(
+    role, prm, am, an, ax, low, high, kn, kx, on, ox, gn, gx, idm, idn, idx, oh, oc, nh, nc, pad
+):
+    e = pl.program_id(0)
+    ny = ax.shape[2]
+    out = (nh, nc)
+
+    @pl.when(role[0] == 2)
     def _():
         tab = Tables(prm)
-
-        def body(i, t):
-            rate = Cells(tab, ide[0, t.at, :]).coarse()
-            for f, (old, new) in enumerate(((oh, nh), (oc, nc))):
-                halo = jnp.where(first, low[f, t.at, :], high[f, t.at, :])
-                new[0, 0, t.at, :] = old[0, 0, t.at, :] + rate[f] * halo
-
-        tiles(1, ide.shape[1], body)
-
-    @pl.when(own[0] == 0)
-    def _():
-        nh[...] = oh[...]
-        nc[...] = oc[...]
+        clear_rims(pad)
+        first = e == 0
+
+        def zero(i, t):
+            for f in F2:
+                pad[f, 0, t.pad(), :] = jnp.zeros((t.n, 128), jnp.float32)
+
+        tiles(1, ny, zero)
+        for k, (now, ids) in enumerate(((ax, idx), (an, idn), (am, idm))):
+
+            def melt(i, t, k=k, now=now, ids=ids):
+                values = [now[f, 0, t.at, :] for f in F2]
+                put_melt(tab, pad, k + 1, t, ids[0, t.at, :], *values)
+
+            tiles(1, ny, melt)
+        for k, (now, ids, end, start) in enumerate(((ax, idx, ox, kx), (an, idn, on, kn))):
+
+            def update(i, t, k=k, now=now, ids=ids, end=end, start=start):
+                rate = Cells(tab, ids[0, t.at, :]).coarse()
+                for f in F2:
+                    total = lap(pad, f, k + 1, t)
+                    if k == 0:
+                        total = total + jnp.where(first, low[f, t.at, :], high[f, t.at, :])
+                    new = now[f, 0, t.at, :] + rate[f] * total
+                    new = new + (end[f, 0, t.at, :] - start[f, 0, t.at, :])
+                    out[f][0, e if k == 0 else 1 - e, t.at, :] = new
+
+            tiles(1, ny, update)
+
+    def keep(n, x):
+        for f in F2:
+            out[f][0, e] = x[f, 0]
+            out[f][0, 1 - e] = n[f, 0]
+
+    @pl.when(role[0] == 1)
+    def _():
+        keep(gn, gx)
+
+    @pl.when(role[0] == 0)
+    def _():
+        keep(on, ox)
 
 
 def f32(*shape):
@@ -644,6 +667,12 @@
     vx, tl0, tl7 = fine_edges(part, sides, (vm,))
     low, high = halos(tl0, tl7, (0,), 1)
     ax = send(vx, 1)
+    d = move(
+        call(drift_kernel, [f32(2, 4, ny, nz)], (prm, vn, vx, kn, kx), 1, "drift", limit=12)[0],
+        (2,),
+        -1,
+        0,
+    )
     vn, part = call(
         coarse_rim_kernel,
         [pair, pair],
@@ -660,60 +689,77 @@
         2,
         "coarse_edges",
     )
-    rim = None
-    for n in range(2, slices):
-        low, high = halos(tl0, tl7, (n - 1,), 1)
-        am = send(vm, n)
-        if n == 2:
-            an, ax = send(vn, n), send(vx, n)
-        else:
-            ar = send(rim, n)
-        if n == slices - 1:
-            break
-        vm = call(
-            coarse_mid_kernel,
-            [tall],
-            (own(n), prm, am, an, km, ids, vm),
-            2,
-            "coarse_mid",
-            pad,
-            18,
-        )[0]
-        vm, rim, tl0, tl7 = call(
-            coarse_outer_kernel,
-            [f32(2, 4, ny, nz), halo, halo],
-            (own(n), prm, am, an, ax, low, high, kn, kx, ids, ide, vn, vx),
-            2,
-            "coarse_outer",
-            [pltpu.VMEM((2, 2, ny, nz), jnp.float32), *pad],
-            26,
-            through=(vm,),
-        )
+    vn0, vx0 = vn, vx
+    am, an = send(vm, 2), send(vn, 2)
+
+    low, high = halos(tl0, tl7, (1,), 0)
+    n2, part = call(
+        next_rim_kernel,
+        [pair, pair],
+        (own(1), prm, vm, vn, vx, d, ids),
+        2,
+        "next_rim",
+        pad,
+        20,
+    )
+    x2, tl0, tl7 = call(
+        next_edges_kernel,
+        [pair, halo, halo],
+        (own(1), prm, part, low, high, ide),
+        2,
+        "next_edges",
+    )
+    vm = call(
+        coarse_mid_kernel,
+        [tall],
+        (own(2), prm, am, an, km, ids, vm),
+        2,
+        "coarse_mid",
+        pad,
+        18,
+        after=(x2,),
+    )[0]
+    low, high = halos(tl0, tl7, (1,), 2)
+    ax, an, am = move(x2, (1,), 2, 0), move(n2, (1,), 2, 0), send(vm, 3)
 
     out = f32(1, rows, ny, nz)
-    last_own = own(slices - 1)
     oh, oc = call(
-        last_rows_kernel,
+        last_mid_kernel,
         [out, out],
-        (last_own, prm, am, ar, km, kn, kx, ids, vm, rim),
+        (own(3), prm, am, an, km, ids, vm),
         2,
-        "last_rows",
+        "last_mid",
         pad,
-        28,
-    )
-    out_row = pl.BlockSpec((1, 1, ny, nz), lambda i: (0, (rows - 1) * i, 0, 0))
-    one = pl.BlockSpec((1, ny, nz), lambda i: (i, 0, 0))
+        24,
+    )
+    far_oh = pltpu.with_memory_space_constraint(oh, pltpu.HBM)
+    low, high = call(
+        nothing_kernel, [], (), 0, "last_arrived", after=(far_oh,), through=(low, high), flops=10**11
+    )
+    gx, gn = move(ax, (3,), -1, 0), move(an, (3,), -1, 0)
+    outer = pl.BlockSpec((1, 2, ny, nz), lambda i: (0, (rows // 2 - 1) * i, 0, 0))
+    side = pl.BlockSpec((2, 1, ny, nz), lambda i: (0, i, 0, 0))
+    inside = pl.BlockSpec((2, 1, ny, nz), lambda i: (0, (mid - 1) * i, 0, 0))
+
+    def id_row(k):
+        return pl.BlockSpec((1, ny, nz), lambda i: (k + (rows - 1 - 2 * k) * i, 0, 0))
+
+    role = jnp.where(slot == 3, 2, jnp.where(slot == 2, 1, 0)).astype(jnp.int32).reshape(1)
     return tuple(
-        gridded(
-            last_edges_kernel,
-            2,
-            [out, out],
-            [out_row] * 2,
-            [SMEM, SMEM, whole, whole, one, out_row, out_row],
-            (last_own, prm, low, high, ide, oh, oc),
-            "last_edges",
-            {5: 0, 6: 1},
-        )
+        pl.pallas_call(
+            last_outer_kernel,
+            grid=(2,),
+            out_shape=[out, out],
+            in_specs=[SMEM, SMEM, inside, side, side, whole, whole]
+            + [side] * 6
+            + [id_row(2), id_row(1), id_row(0), ANY, ANY],
+            out_specs=[outer] * 2,
+            scratch_shapes=[pltpu.VMEM((2, 5, ny + 16, nz), jnp.float32)],
+            input_output_aliases={16: 0, 17: 1},
+            compiler_params=pltpu.CompilerParams(vmem_limit_bytes=26 * MIB),
+            cost_estimate=TINY,
+            name="last_outer",
+        )(role, prm, am, an, ax, low, high, kn, kx, vn0, vx0, gn, gx, ids, ids, ids, oh, oc)
     )
 
 

time: 223 us -> 233 us (1.045)
  starting transfers between devices: 47.8 us -> 52 us
  Pallas kernels: 75.2 us -> 78.5 us
    pallas_call x0 -> x1, Pallas kernels: none -> 7.06 us  [per_device(): pl.pallas_call(last_outer_kernel, grid=(2,), out_shape=[out, out], in_spe...]
    ppermute x26 -> x29, starting transfers between devices: 47.8 us -> 52 us  [move(): return lax.ppermute(x, ('tm', 'space'), pairs)]
    pallas_call x2 -> x1, Pallas kernels: 5.3 us -> 2.38 us  [gridded(): pl.pallas_call(kernel, grid=(steps,), out_shape=outs, in_specs=in_specs,...]
    ppermute x26 -> x29, waiting for transfers between devices: 88.8 us -> 90.7 us  [move(): return lax.ppermute(x, ('tm', 'space'), pairs)]
    unnamed x40 -> x42, local copies, waits for them, and re-layouts: 8.24 us -> 9.16 us
    pallas_call x16 -> x19, Pallas kernels: 69.9 us -> 69.1 us  [call(): pl.pallas_call(run, out_shape=[f32(*x.shape) for x in through] + list(out...]
  transfers between devices with their start and end apart: 26 -> 29, of which waited for: 9 -> 9; matrix products, arithmetic and copies ran while one was open for 0% -> 0% of each run, Pallas kernels for 27% -> 25%
where the time goes in v3:
time: 233 us; the launch traced here: 232 us
  waiting for transfers between devices  90.7 us (39%)
  Pallas kernels  78.5 us (34%)
  starting transfers between devices  52 us (22%)
  local copies, waits for them, and re-layouts  9.99 us (4%)
    ppermute x29, waiting for transfers between devices, move(): return lax.ppermute(x, ('tm', 'space'), pairs)  90.7 us
    pallas_call x19, Pallas kernels, call(): pl.pallas_call(run, out_shape=[f32(*x.shape) for x in through] + list(out...  69.1 us
    ppermute x29, starting transfers between devices, move(): return lax.ppermute(x, ('tm', 'space'), pairs)  52 us
    unnamed x42, local copies, waits for them, and re-layouts  9.16 us
    pallas_call x1, Pallas kernels, per_device(): pl.pallas_call(last_outer_kernel, grid=(2,), out_shape=[out, out], in_spe...  7.06 us
  transfers between devices with their start and end apart: 29, of which 9 were waited for; matrix products, arithmetic and copies ran while one was open for 0% of the time, Pallas kernels for 25%

profile of v3, /device:TPU:11, one launch (start us, length us, event | category | flops | bytes accessed | tf_op | source)
XLA Modules:
  0.0 232.3 jit_solution(5808189782158786373)
XLA Ops:
  1.5 2.4 %first_edges.1 = (f32[2,512,128]{2,1,0:T(8,128)S(1)}, f32[2,512,128]{2,1,0:T(8,128)S(1)}, f32[2,512,128]{2,1,0:T(8,128)S(1)}, f32[2,512,128]{2,1,0:T(8,128)S(1)}) custom-call(f32[27]{0:T(128)S(1)} %concatenate.3.prm.refs_0_.refs_1_, f32[8,512,128]{2,1,0:T(8,128)} %bitcast.6, f32[8,512,128]{2,1,0:T(8,128)} %bitcast.9, s32[8,512,128]{2,1,0:T(8,128)} %refs_3_.1), custom_call_target="tpu_custom_call" | custom-call | flops 1000 | bytes 1000 | tf_op jit(solution)/shard_map/first_edges/pallas_call | solution.py:567
  6.9 7.1 %first_step.1 = (f32[2,512,128]{2,1,0:T(8,128)S(1)}, f32[2,512,128]{2,1,0:T(8,128)S(1)}, f32[2,4,512,128]{3,2,1,0:T(8,128)S(1)}, f32[2,2,512,128]{3,2,1,0:T(8,12...) custom-call(f32[27]{0:T(128)S(1)} %concatenate.3.prm.refs_0_.refs_1_, ...), custom_call_target="tpu_custom_call", output_to_operand_aliasing={{0}: (5, {}), {1}: (6, {})} | custom-call | flops 1000 | bytes 1000 | tf_op jit(solution)/shard_map/first_step/pallas_call | solution.py:524
  14.0 3.1 %collective-permute-start.2 = (f32[2,512,128]{2,1,0:T(8,128)S(1)}, f32[2,512,128]{2,1,0:T(8,128)S(1)}, u32[]{:S(2)}, u32[]{:S(2)}) collective-permute-start(f32[2,512,128]{2,1,0:T(8,128)S(1)} %get-tuple-element.66), channel_id=1, source_target_pairs={{8,9},{9,10},{10,11},{11,12},{12,13},{13,14},{14,15},{24,25},{25,2... | collective-permute-start | bytes 1572872 | tf_op jit(solution)/shard_map/ppermute | solution.py:555
  17.1 3.0 %collective-permute-start.3 = (f32[2,512,128]{2,1,0:T(8,128)S(1)}, f32[2,512,128]{2,1,0:T(8,128)S(1)}, u32[]{:S(2)}, u32[]{:S(2)}) collective-permute-start(f32[2,512,128]{2,1,0:T(8,128)S(1)} %get-tuple-element.67), channel_id=1, source_target_pairs={{9,8},{10,9},{11,10},{12,11},{13,12},{14,13},{15,14},{25,24},{26,2... | collective-permute-start | bytes 1572872 | tf_op jit(solution)/shard_map/ppermute | solution.py:555
  20.2 10.9 %collective-permute-done.2.low2 = f32[2,512,128]{2,1,0:T(8,128)S(1)} collective-permute-done((f32[2,512,128]{2,1,0:T(8,128)S(1)}, f32[2,512,128]{2,1,0:T(8,128)S(1)}, u32[]{:S(2)}, u32[]{:S(2)}) %collective-permute-start.2) | collective-permute-done | bytes 524320 | tf_op jit(solution)/shard_map/ppermute | solution.py:555
  34.1 2.3 collective-permute-start.4
  36.3 5.3 %collective-permute-start.5 = (f32[2,512,128]{2,1,0:T(8,128)S(1)}, f32[2,512,128]{2,1,0:T(8,128)S(1)}, u32[]{:S(2)}, u32[]{:S(2)}) collective-permute-start(f32[2,512,128]{2,1,0:T(8,128)S(1)} %get-tuple-element.75), channel_id=1, source_target_pairs={{1,0},{2,1},{3,2},{4,3},{5,4},{6,5},{7,6},{9,8},{10,9},{11,10},{12... | collective-permute-start | bytes 1572872 | tf_op jit(solution)/shard_map/ppermute | solution.py:555
  41.6 3.3 %base.1 = (f32[2,4,512,128]{3,2,1,0:T(8,128)S(1)}, f32[2,2,512,128]{3,2,1,0:T(8,128)S(1)}, f32[2,2,512,128]{3,2,1,0:T(8,128)S(1)}) custom-call(f32[27]{0:T(128)S(1)} %concatenate.3.prm.refs_0_.refs_1_, f32[8,512,128]{2,1,0:T(8,128)S(1)} %bitcast.8, f32[8,512,128]{2,1,0:T(8,128)S(1)} %bitcast.11, f32[2,4,512,128]{3,2,1,0:T(8,128)S(1)} %get-tuple-element.59.sm, ...), custom_call_target="tpu_custom_call" | custom-call | flops 1000 | bytes 1000 | tf_op jit(solution)/shard_map/base/pallas_call | solution.py:524
  44.9 6.9 %step.1 = (f32[2,4,512,128]{3,2,1,0:T(8,128)S(1)}, f32[2,2,512,128]{3,2,1,0:T(8,128)S(1)}, f32[2,2,512,128]{3,2,1,0:T(8,128)S(1)}) custom-call(f32[27]{0:T(128)S(1)} %concatenate.3.prm.refs_0_.refs_1_, f32[2,4,512,128]{3,2,1,0:T(8,128)S(1)} %get-tuple-element.59.sm, f32[2,2,512,128]{3,2,1,0:T(8,128)S(1)} %get-tuple-element.60.sn, ...), custom_call_target="tpu_custom_call" | custom-call | flops 1000 | bytes 1000 | tf_op jit(solution)/shard_map/step/pallas_call | solution.py:524
  51.8 4.5 %collective-permute-done.4.refs_2_ = f32[2,512,128]{2,1,0:T(8,128)S(1)} collective-permute-done((f32[2,512,128]{2,1,0:T(8,128)S(1)}, f32[2,512,128]{2,1,0:T(8,128)S(1)}, u32[]{:S(2)}, u32[]{:S(2)}) %collective-permute-start.4) | collective-permute-done | bytes 524320 | tf_op jit(solution)/shard_map/ppermute | solution.py:555
  56.3 3.3 %collective-permute-done.5.refs_3_ = f32[2,512,128]{2,1,0:T(8,128)S(1)} collective-permute-done((f32[2,512,128]{2,1,0:T(8,128)S(1)}, f32[2,512,128]{2,1,0:T(8,128)S(1)}, u32[]{:S(2)}, u32[]{:S(2)}) %collective-permute-start.5) | collective-permute-done | bytes 524320 | tf_op jit(solution)/shard_map/ppermute | solution.py:555
  62.9 3.4 %collective-permute-start.9 = (f32[2,512,128]{2,1,0:T(8,128)S(1)}, f32[2,512,128]{2,1,0:T(8,128)S(1)}, u32[]{:S(2)}, u32[]{:S(2)}) collective-permute-start(f32[2,512,128]{2,1,0:T(8,128)S(1)} %get-tuple-element.84), channel_id=1, source_target_pairs={{0,1},{1,2},{2,3},{3,4},{4,5},{5,6},{6,7},{8,9},{9,10},{10,11},{11... | collective-permute-start | bytes 1572872 | tf_op jit(solution)/shard_map/ppermute | solution.py:555
  66.3 7.9 %step_apart.1 = (f32[4,512,128]{2,1,0:T(8,128)S(1)}, f32[4,512,128]{2,1,0:T(8,128)}, f32[2,2,512,128]{3,2,1,0:T(8,128)}, f32[2,2,512,128]{3,2,1,0:T(8,128)S(1)}) custom-call(f32[27]{0:T(128)S(1)} %concatenate.3.prm.refs_0_.refs_1_, f32[2,4,512,128]{3,2,1,0:T(8,128)S(1)} %get-tuple-element.71.sm, f32[2,2,512,128]{3,2,1,0:T(8,128)S(1)} %get-tuple-element.72.sn, ...), custom_call_target="tpu_custom_call" | custom-call | flops 1000 | bytes 1000 | tf_op jit(solution)/shard_map/step_apart/pallas_call | solution.py:524
  78.2 9.0 %collective-permute-done.10.refs_3_ = f32[2,512,128]{2,1,0:T(8,128)S(1)} collective-permute-done((f32[2,512,128]{2,1,0:T(8,128)S(1)}, f32[2,512,128]{2,1,0:T(8,128)S(1)}, u32[]{:S(2)}, u32[]{:S(2)}) %collective-permute-start.10) | collective-permute-done | bytes 524320 | tf_op jit(solution)/shard_map/ppermute | solution.py:555
  87.2 2.6 %edges.6 = (f32[2,2,512,128]{3,2,1,0:T(8,128)}, f32[2,512,128]{2,1,0:T(8,128)}, f32[2,512,128]{2,1,0:T(8,128)}) custom-call(f32[27]{0:T(128)S(1)} %concatenate.3.prm.refs_0_.refs_1_, f32[2,2,512,128]{3,2,1,0:T(8,128)S(1)} %get-tuple-element.83.refs_1_, f32[2,512,128]{2,1,0:T(8,128)S(1)} %collective-permute-done.9.refs_2_, ...), custom_call_target="tpu_custom_call" | custom-call | flops 1000 | bytes 1000 | tf_op jit(solution)/shard_map/edges/pallas_call | solution.py:524
  91.4 3.6 %collective-permute-start.13 = (f32[2,512,128]{2,1,0:T(8,128)}, f32[2,512,128]{2,1,0:T(8,128)}, u32[]{:S(2)}, u32[]{:S(2)}) collective-permute-start(f32[2,512,128]{2,1,0:T(8,128)} %get-tuple-element.92), channel_id=1, source_target_pairs={{0,1},{1,2},{2,3},{3,4},{4,5},{5,6},{6,7},{8,9},{9,10},{10,11},{11... | collective-permute-start | bytes 1572872 | tf_op jit(solution)/shard_map/ppermute | solution.py:555
  96.1 2.5 %collective-permute-start.14 = (f32[2,512,128]{2,1,0:T(8,128)}, f32[2,512,128]{2,1,0:T(8,128)}, u32[]{:S(2)}, u32[]{:S(2)}) collective-permute-start(f32[2,512,128]{2,1,0:T(8,128)} %get-tuple-element.93), channel_id=1, source_target_pairs={{1,0},{2,1},{3,2},{4,3},{5,4},{6,5},{7,6},{9,8},{10,9},{11,10},{12... | collective-permute-start | bytes 1572872 | tf_op jit(solution)/shard_map/ppermute | solution.py:555
  99.9 8.2 %step_joined.1 = (f32[2,4,512,128]{3,2,1,0:T(8,128)S(1)}, f32[2,2,512,128]{3,2,1,0:T(8,128)S(1)}, f32[2,2,512,128]{3,2,1,0:T(8,128)S(1)}) custom-call(f32[27]{0:T(128)S(1)} %concatenate.3.prm.refs_0_.refs_1_, f32[4,512,128]{2,1,0:T(8,128)S(1)} %copy-done.18, f32[4,512,128]{2,1,0:T(8,128)} %get-tuple-element.81.mc, f32[2,2,512,128]{3,2,1,0:T(8,128)} %get-tuple-element.82.sn, ...), custom_call_target="tpu_custom_call" | custom-call | flops 1000 | bytes 1000 | tf_op jit(solution)/shard_map/step_joined/pallas_call | solution.py:524
  108.2 3.4 %replay.1 = (f32[2,4,512,128]{3,2,1,0:T(8,128)S(1)}, f32[2,2,512,128]{3,2,1,0:T(8,128)S(1)}, f32[2,4,512,128]{3,2,1,0:T(8,128)}) custom-call(s32[1]{0:T(128)} %bitcast.2.own, f32[27]{0:T(128)S(1)} %concatenate.3.prm.refs_0_.refs_1_, f32[4,512,128]{2,1,0:T(8,128)S(1)} %copy-done.20, f32[4,512,128]{2,1,0:T(8,128)} %collective-permute-done.7.mc, ...), custom_call_target="tpu_custom_call" | custom-call | flops 1000 | bytes 1000 | tf_op jit(solution)/shard_map/replay/pallas_call | solution.py:524
  111.5 5.9 %collective-permute-done.13.refs_2_ = f32[2,512,128]{2,1,0:T(8,128)} collective-permute-done((f32[2,512,128]{2,1,0:T(8,128)}, f32[2,512,128]{2,1,0:T(8,128)}, u32[]{:S(2)}, u32[]{:S(2)}) %collective-permute-start.13) | collective-permute-done | bytes 524320 | tf_op jit(solution)/shard_map/ppermute | solution.py:555
  117.4 2.2 collective-permute-done.14.refs_3_
  119.6 2.2 edges.7
  121.8 2.2 drift.1
  124.0 2.0 collective-permute-start.19
  126.7 2.0 collective-permute-start.12
  140.3 3.6 %next_rim.1 = (f32[2,2,512,128]{3,2,1,0:T(8,128)}, f32[2,2,512,128]{3,2,1,0:T(8,128)S(1)}) custom-call(s32[1]{0:T(128)} %bitcast.2.own, f32[27]{0:T(128)S(1)} %concatenate.3.prm.refs_0_.refs_1_, f32[2,4,512,128]{3,2,1,0:T(8,128)} %get-tuple-element.88.refs_5_.vm.refs_6_, f32[2,2,512,128]{3,2,1,0:T(8,128)} %get-tuple-element.96.vn.on, ...), custom_call_target="tpu_custom_call" | custom-call | flops 1000 | bytes 1000 | tf_op jit(solution)/shard_map/next_rim/pallas_call | solution.py:524
  143.9 2.8 %next_edges.1 = (f32[2,2,512,128]{3,2,1,0:T(8,128)}, f32[2,512,128]{2,1,0:T(8,128)}, f32[2,512,128]{2,1,0:T(8,128)}) custom-call(s32[1]{0:T(128)} %bitcast.2.own, f32[27]{0:T(128)S(1)} %concatenate.3.prm.refs_0_.refs_1_, f32[2,2,512,128]{3,2,1,0:T(8,128)S(1)} %get-tuple-element.101.part, f32[2,512,128]{2,1,0:T(8,128)} %collective-permute-done.20.low, ...), custom_call_target="tpu_custom_call" | custom-call | flops 1000 | bytes 1000 | tf_op jit(solution)/shard_map/next_edges/pallas_call | solution.py:524
  146.7 4.1 %coarse_mid.1.om = f32[2,4,512,128]{3,2,1,0:T(8,128)} custom-call(s32[1]{0:T(128)} %bitcast.1.refs_0_, f32[27]{0:T(128)S(1)} %concatenate.3.prm.refs_0_.refs_1_, f32[2,4,512,128]{3,2,1,0:T(8,128)} %collective-permute-done.12.refs_2_, f32[2,2,512,128]{3,2,1,0:T(8,128)} %collective-permute-done.16.refs_3_, f32[2,4,512,128]{3,2,1,0:T(8,128)S(1)} %copy-done.2, ...), custom_call_target="tpu_custom_call" | custom-call | flops 1000 | bytes 1000 | tf_op jit(solution)/shard_map/coarse_mid/pallas_call | solution.py:524
  157.3 43.5 %collective-permute-done.24.ax = f32[2,2,512,128]{3,2,1,0:T(8,128)} collective-permute-done((f32[2,2,512,128]{3,2,1,0:T(8,128)}, f32[2,2,512,128]{3,2,1,0:T(8,128)}, u32[]{:S(2)}, u32[]{:S(2)}) %collective-permute-start.24) | collective-permute-done | bytes 1048608 | tf_op jit(solution)/shard_map/ppermute | solution.py:555
  202.1 9.9 %collective-permute-done.23.an = f32[2,2,512,128]{3,2,1,0:T(8,128)} collective-permute-done((f32[2,2,512,128]{3,2,1,0:T(8,128)}, f32[2,2,512,128]{3,2,1,0:T(8,128)}, u32[]{:S(2)}, u32[]{:S(2)}) %collective-permute-start.23) | collective-permute-done | bytes 1048608 | tf_op jit(solution)/shard_map/ppermute | solution.py:555
  214.9 8.7 %last_mid.1 = (f32[1,8,512,128]{3,2,1,0:T(8,128)}, f32[1,8,512,128]{3,2,1,0:T(8,128)}) custom-call(s32[1]{0:T(128)} %bitcast.5.own, f32[27]{0:T(128)S(1)} %concatenate.3.prm.refs_0_.refs_1_, f32[2,4,512,128]{3,2,1,0:T(8,128)} %collective-permute-done.22.am, f32[2,2,512,128]{3,2,1,0:T(8,128)} %collective-permute-done.23.an, f32[2,4,512,128]{3,2,1,0:T(8,128)S(1)} %copy-done.3, ...), custom_call_target="tpu_custom_call" | custom-call | flops 1000 | bytes 1000 | tf_op jit(solution)/shard_map/last_mid/pallas_call | solution.py:524
  225.2 7.1 %last_outer.1 = (f32[1,8,512,128]{3,2,1,0:T(8,128)}, f32[1,8,512,128]{3,2,1,0:T(8,128)}) custom-call(s32[1]{0:T(128)} %bitcast.role, f32[27]{0:T(128)S(1)} %concatenate.3.prm.refs_0_.refs_1_, f32[2,4,512,128]{3,2,1,0:T(8,128)} %collective-permute-done.22.am, ...), custom_call_target="tpu_custom_call", output_to_operand_aliasing={{0}: (16, {}), {1}: (17, {})} | custom-call | flops 1000 | bytes 1000 | tf_op jit(solution)/shard_map/last_outer/pallas_call | solution.py:749
  (90 shorter events, 42.6 us)
Async XLA Ops:
  3.9 16.3 %collective-permute-start = (f32[2,512,128]{2,1,0:T(8,128)S(1)}, f32[2,512,128]{2,1,0:T(8,128)S(1)}, u32[]{:S(2)}, u32[]{:S(2)}) collective-permute-start(f32[2,512,128]{2,1,0:T(8,128)S(1)} %get-tuple-element.62), channel_id=1, source_target_pairs={{0,1},{1,2},{2,3},{3,4},{4,5},{5,6},{6,7},{16,17},{17,18},{18,19},... | collective-permute-start | bytes 1572872 | tf_op jit(solution)/shard_map/ppermute | solution.py:555
  4.6 15.6 %collective-permute-start.1 = (f32[2,512,128]{2,1,0:T(8,128)S(1)}, f32[2,512,128]{2,1,0:T(8,128)S(1)}, u32[]{:S(2)}, u32[]{:S(2)}) collective-permute-start(f32[2,512,128]{2,1,0:T(8,128)S(1)} %get-tuple-element.63), channel_id=1, source_target_pairs={{1,0},{2,1},{3,2},{4,3},{5,4},{6,5},{7,6},{17,16},{18,17},{19,18},... | collective-permute-start | bytes 1572872 | tf_op jit(solution)/shard_map/ppermute | solution.py:555
  14.0 73.2 %copy-start.9 = (s32[2,512,128]{2,1,0:T(8,128)}, s32[2,512,128]{2,1,0:T(8,128)S(1)}, u32[]{:S(2)}) copy-start(s32[2,512,128]{2,1,0:T(8,128)S(1)} %get-tuple-element.68.ide.refs_4_) | copy-start | bytes 1572868
  14.0 17.1 %collective-permute-start.2 = (f32[2,512,128]{2,1,0:T(8,128)S(1)}, f32[2,512,128]{2,1,0:T(8,128)S(1)}, u32[]{:S(2)}, u32[]{:S(2)}) collective-permute-start(f32[2,512,128]{2,1,0:T(8,128)S(1)} %get-tuple-element.66), channel_id=1, source_target_pairs={{8,9},{9,10},{10,11},{11,12},{12,13},{13,14},{14,15},{24,25},{25,2... | collective-permute-start | bytes 1572872 | tf_op jit(solution)/shard_map/ppermute | solution.py:555
  17.1 15.5 %collective-permute-start.3 = (f32[2,512,128]{2,1,0:T(8,128)S(1)}, f32[2,512,128]{2,1,0:T(8,128)S(1)}, u32[]{:S(2)}, u32[]{:S(2)}) collective-permute-start(f32[2,512,128]{2,1,0:T(8,128)S(1)} %get-tuple-element.67), channel_id=1, source_target_pairs={{9,8},{10,9},{11,10},{12,11},{13,12},{14,13},{15,14},{25,24},{26,2... | collective-permute-start | bytes 1572872 | tf_op jit(solution)/shard_map/ppermute | solution.py:555
  34.1 22.2 %collective-permute-start.4 = (f32[2,512,128]{2,1,0:T(8,128)S(1)}, f32[2,512,128]{2,1,0:T(8,128)S(1)}, u32[]{:S(2)}, u32[]{:S(2)}) collective-permute-start(f32[2,512,128]{2,1,0:T(8,128)S(1)} %get-tuple-element.74), channel_id=1, source_target_pairs={{0,1},{1,2},{2,3},{3,4},{4,5},{5,6},{6,7},{8,9},{9,10},{10,11},{11... | collective-permute-start | bytes 1572872 | tf_op jit(solution)/shard_map/ppermute | solution.py:555
  36.3 23.2 %collective-permute-start.5 = (f32[2,512,128]{2,1,0:T(8,128)S(1)}, f32[2,512,128]{2,1,0:T(8,128)S(1)}, u32[]{:S(2)}, u32[]{:S(2)}) collective-permute-start(f32[2,512,128]{2,1,0:T(8,128)S(1)} %get-tuple-element.75), channel_id=1, source_target_pairs={{1,0},{2,1},{3,2},{4,3},{5,4},{6,5},{7,6},{9,8},{10,9},{11,10},{12... | collective-permute-start | bytes 1572872 | tf_op jit(solution)/shard_map/ppermute | solution.py:555
  44.9 42.3 %copy-start = (f32[2,4,512,128]{3,2,1,0:T(8,128)}, f32[2,4,512,128]{3,2,1,0:T(8,128)S(1)}, u32[]{:S(2)}) copy-start(f32[2,4,512,128]{3,2,1,0:T(8,128)S(1)} %get-tuple-element.76.refs_5_.km.refs_4_) | copy-start | bytes 6291460
  44.9 42.3 %copy-start.4 = (f32[2,2,512,128]{3,2,1,0:T(8,128)}, f32[2,2,512,128]{3,2,1,0:T(8,128)S(1)}, u32[]{:S(2)}) copy-start(f32[2,2,512,128]{3,2,1,0:T(8,128)S(1)} %get-tuple-element.78.refs_7_.kx) | copy-start | bytes 3145732
  61.0 26.2 %collective-permute-start.10 = (f32[2,512,128]{2,1,0:T(8,128)S(1)}, f32[2,512,128]{2,1,0:T(8,128)S(1)}, u32[]{:S(2)}, u32[]{:S(2)}) collective-permute-start(f32[2,512,128]{2,1,0:T(8,128)S(1)} %get-tuple-element.85), channel_id=1, source_target_pairs={{1,0},{2,1},{3,2},{4,3},{5,4},{6,5},{7,6},{9,8},{10,9},{11,10},{12... | collective-permute-start | bytes 1572872 | tf_op jit(solution)/shard_map/ppermute | solution.py:555
  62.9 24.3 %collective-permute-start.9 = (f32[2,512,128]{2,1,0:T(8,128)S(1)}, f32[2,512,128]{2,1,0:T(8,128)S(1)}, u32[]{:S(2)}, u32[]{:S(2)}) collective-permute-start(f32[2,512,128]{2,1,0:T(8,128)S(1)} %get-tuple-element.84), channel_id=1, source_target_pairs={{0,1},{1,2},{2,3},{3,4},{4,5},{5,6},{6,7},{8,9},{9,10},{10,11},{11... | collective-permute-start | bytes 1572872 | tf_op jit(solution)/shard_map/ppermute | solution.py:555
  74.2 20.9 %collective-permute-start.6 = (f32[4,512,128]{2,1,0:T(8,128)S(1)}, f32[4,512,128]{2,1,0:T(8,128)S(1)}, u32[]{:S(2)}, u32[]{:S(2)}) collective-permute-start(f32[4,512,128]{2,1,0:T(8,128)S(1)} %get-tuple-element.80.mh), channel_id=1, source_target_pairs={{0,8},{1,9},{2,10},{3,11},{4,12},{5,13},{6,14},{7,15}} | collective-permute-start | bytes 3145736 | tf_op jit(solution)/shard_map/ppermute | solution.py:555
  74.9 33.2 %collective-permute-start.7 = (f32[4,512,128]{2,1,0:T(8,128)}, f32[4,512,128]{2,1,0:T(8,128)}, u32[]{:S(2)}, u32[]{:S(2)}) collective-permute-start(f32[4,512,128]{2,1,0:T(8,128)} %get-tuple-element.81.mc), channel_id=1, source_target_pairs={{0,8},{1,9},{2,10},{3,11},{4,12},{5,13},{6,14},{7,15}} | collective-permute-start | bytes 3145736 | tf_op jit(solution)/shard_map/ppermute | solution.py:555
  76.6 31.5 %collective-permute-start.8 = (f32[2,2,512,128]{3,2,1,0:T(8,128)}, f32[2,2,512,128]{3,2,1,0:T(8,128)}, u32[]{:S(2)}, u32[]{:S(2)}) collective-permute-start(f32[2,2,512,128]{3,2,1,0:T(8,128)} %get-tuple-element.82.sn), channel_id=1, source_target_pairs={{0,8},{1,9},{2,10},{3,11},{4,12},{5,13},{6,14},{7,15}} | collective-permute-start | bytes 3145736 | tf_op jit(solution)/shard_map/ppermute | solution.py:555
  89.8 18.3 %collective-permute-start.11 = (f32[2,2,512,128]{3,2,1,0:T(8,128)}, f32[2,2,512,128]{3,2,1,0:T(8,128)}, u32[]{:S(2)}, u32[]{:S(2)}) collective-permute-start(f32[2,2,512,128]{3,2,1,0:T(8,128)} %get-tuple-element.86.sx), channel_id=1, source_target_pairs={{0,8},{1,9},{2,10},{3,11},{4,12},{5,13},{6,14},{7,15}} | collective-permute-start | bytes 3145736 | tf_op jit(solution)/shard_map/ppermute | solution.py:555
  91.4 26.0 %collective-permute-start.13 = (f32[2,512,128]{2,1,0:T(8,128)}, f32[2,512,128]{2,1,0:T(8,128)}, u32[]{:S(2)}, u32[]{:S(2)}) collective-permute-start(f32[2,512,128]{2,1,0:T(8,128)} %get-tuple-element.92), channel_id=1, source_target_pairs={{0,1},{1,2},{2,3},{3,4},{4,5},{5,6},{6,7},{8,9},{9,10},{10,11},{11... | collective-permute-start | bytes 1572872 | tf_op jit(solution)/shard_map/ppermute | solution.py:555
  96.1 23.5 %collective-permute-start.14 = (f32[2,512,128]{2,1,0:T(8,128)}, f32[2,512,128]{2,1,0:T(8,128)}, u32[]{:S(2)}, u32[]{:S(2)}) collective-permute-start(f32[2,512,128]{2,1,0:T(8,128)} %get-tuple-element.93), channel_id=1, source_target_pairs={{1,0},{2,1},{3,2},{4,3},{5,4},{6,5},{7,6},{9,8},{10,9},{11,10},{12... | collective-permute-start | bytes 1572872 | tf_op jit(solution)/shard_map/ppermute | solution.py:555
  124.0 15.1 %collective-permute-start.19 = (f32[2,4,512,128]{3,2,1,0:T(8,128)}, f32[2,4,512,128]{3,2,1,0:T(8,128)}, u32[]{:S(2)}, u32[]{:S(2)}) collective-permute-start(f32[2,4,512,128]{3,2,1,0:T(8,128)} %drift.1), channel_id=1, source_target_pairs={{16,8},{17,9},{18,10},{19,11},{20,12},{21,13},{22,14},{23,15}} | collective-permute-start | bytes 6291464 | tf_op jit(solution)/shard_map/ppermute | solution.py:555
  126.0 4.1 %collective-permute-start.15 = (f32[2,2,512,128]{3,2,1,0:T(8,128)S(1)}, f32[2,2,512,128]{3,2,1,0:T(8,128)S(1)}, u32[]{:S(2)}, u32[]{:S(2)}) collective-permute-start(f32[2,2,512,128]{3,2,1,0:T(8,128)S(1)} %get-tuple-element.94.ox.old), channel_id=1, source_target_pairs={{0,8},{1,9},{2,10},{3,11},{4,12},{5,13},{6,14},{7,15}} | collective-permute-start | bytes 3145736 | tf_op jit(solution)/shard_map/ppermute | solution.py:555
  126.7 20.0 %collective-permute-start.12 = (f32[2,4,512,128]{3,2,1,0:T(8,128)}, f32[2,4,512,128]{3,2,1,0:T(8,128)}, u32[]{:S(2)}, u32[]{:S(2)}) collective-permute-start(f32[2,4,512,128]{3,2,1,0:T(8,128)} %get-tuple-element.88.refs_5_.vm.refs_6_), channel_id=1, source_target_pairs={{8,16},{9,17},{10,18},{11,19},{12,20},{13,21},{14,22},{15,23}} | collective-permute-start | bytes 6291464 | tf_op jit(solution)/shard_map/ppermute | solution.py:555
  128.7 4.9 %collective-permute-start.17 = (f32[2,512,128]{2,1,0:T(8,128)S(1)}, f32[2,512,128]{2,1,0:T(8,128)S(1)}, u32[]{:S(2)}, u32[]{:S(2)}) collective-permute-start(f32[2,512,128]{2,1,0:T(8,128)S(1)} %get-tuple-element.98), channel_id=1, source_target_pairs={{0,9},{1,10},{2,11},{3,12},{4,13},{5,14},{6,15}} | collective-permute-start | bytes 1572872 | tf_op jit(solution)/shard_map/ppermute | solution.py:555
  129.4 4.2 %collective-permute-start.18 = (f32[2,512,128]{2,1,0:T(8,128)S(1)}, f32[2,512,128]{2,1,0:T(8,128)S(1)}, u32[]{:S(2)}, u32[]{:S(2)}) collective-permute-start(f32[2,512,128]{2,1,0:T(8,128)S(1)} %get-tuple-element.99), channel_id=1, source_target_pairs={{1,8},{2,9},{3,10},{4,11},{5,12},{6,13},{7,14}} | collective-permute-start | bytes 1572872 | tf_op jit(solution)/shard_map/ppermute | solution.py:555
  132.0 14.7 %collective-permute-start.16 = (f32[2,2,512,128]{3,2,1,0:T(8,128)}, f32[2,2,512,128]{3,2,1,0:T(8,128)}, u32[]{:S(2)}, u32[]{:S(2)}) collective-permute-start(f32[2,2,512,128]{3,2,1,0:T(8,128)} %get-tuple-element.96.vn.on), channel_id=1, source_target_pairs={{8,16},{9,17},{10,18},{11,19},{12,20},{13,21},{14,22},{15,23}} | collective-permute-start | bytes 3145736 | tf_op jit(solution)/shard_map/ppermute | solution.py:555
  136.2 7.7 %collective-permute-start.20 = (f32[2,512,128]{2,1,0:T(8,128)}, f32[2,512,128]{2,1,0:T(8,128)}, u32[]{:S(2)}, u32[]{:S(2)}) collective-permute-start(f32[2,512,128]{2,1,0:T(8,128)} %get-tuple-element.102), channel_id=1, source_target_pairs={{8,9},{9,10},{10,11},{11,12},{12,13},{13,14},{14,15}} | collective-permute-start | bytes 1572872 | tf_op jit(solution)/shard_map/ppermute | solution.py:555
  137.6 6.3 %collective-permute-start.21 = (f32[2,512,128]{2,1,0:T(8,128)}, f32[2,512,128]{2,1,0:T(8,128)}, u32[]{:S(2)}, u32[]{:S(2)}) collective-permute-start(f32[2,512,128]{2,1,0:T(8,128)} %get-tuple-element.103), channel_id=1, source_target_pairs={{9,8},{10,9},{11,10},{12,11},{13,12},{14,13},{15,14}} | collective-permute-start | bytes 1572872 | tf_op jit(solution)/shard_map/ppermute | solution.py:555
  150.8 62.5 %collective-permute-start.22 = (f32[2,4,512,128]{3,2,1,0:T(8,128)}, f32[2,4,512,128]{3,2,1,0:T(8,128)}, u32[]{:S(2)}, u32[]{:S(2)}) collective-permute-start(f32[2,4,512,128]{3,2,1,0:T(8,128)} %coarse_mid.1.om), channel_id=1, source_target_pairs={{16,24},{17,25},{18,26},{19,27},{20,28},{21,29},{22,30},{23,31}} | collective-permute-start | bytes 6291464 | tf_op jit(solution)/shard_map/ppermute | solution.py:555
  152.1 48.7 %collective-permute-start.24 = (f32[2,2,512,128]{3,2,1,0:T(8,128)}, f32[2,2,512,128]{3,2,1,0:T(8,128)}, u32[]{:S(2)}, u32[]{:S(2)}) collective-permute-start(f32[2,2,512,128]{3,2,1,0:T(8,128)} %get-tuple-element.104.refs_7_), channel_id=1, source_target_pairs={{8,24},{9,25},{10,26},{11,27},{12,28},{13,29},{14,30},{15,31}} | collective-permute-start | bytes 3145736 | tf_op jit(solution)/shard_map/ppermute | solution.py:555
  153.4 58.6 %collective-permute-start.23 = (f32[2,2,512,128]{3,2,1,0:T(8,128)}, f32[2,2,512,128]{3,2,1,0:T(8,128)}, u32[]{:S(2)}, u32[]{:S(2)}) collective-permute-start(f32[2,2,512,128]{3,2,1,0:T(8,128)} %get-tuple-element.105), channel_id=1, source_target_pairs={{8,24},{9,25},{10,26},{11,27},{12,28},{13,29},{14,30},{15,31}} | collective-permute-start | bytes 3145736 | tf_op jit(solution)/shard_map/ppermute | solution.py:555
  154.7 69.0 %collective-permute-start.25 = (f32[2,512,128]{2,1,0:T(8,128)}, f32[2,512,128]{2,1,0:T(8,128)}, u32[]{:S(2)}, u32[]{:S(2)}) collective-permute-start(f32[2,512,128]{2,1,0:T(8,128)} %get-tuple-element.107), channel_id=1, source_target_pairs={{8,25},{9,26},{10,27},{11,28},{12,29},{13,30},{14,31}} | collective-permute-start | bytes 1572872 | tf_op jit(solution)/shard_map/ppermute | solution.py:555
  156.0 67.7 %collective-permute-start.26 = (f32[2,512,128]{2,1,0:T(8,128)}, f32[2,512,128]{2,1,0:T(8,128)}, u32[]{:S(2)}, u32[]{:S(2)}) collective-permute-start(f32[2,512,128]{2,1,0:T(8,128)} %get-tuple-element.108), channel_id=1, source_target_pairs={{9,24},{10,25},{11,26},{12,27},{13,28},{14,29},{15,30}} | collective-permute-start | bytes 1572872 | tf_op jit(solution)/shard_map/ppermute | solution.py:555
  200.8 23.0 %collective-permute-start.28 = (f32[2,2,512,128]{3,2,1,0:T(8,128)}, f32[2,2,512,128]{3,2,1,0:T(8,128)S(1)}, u32[]{:S(2)}, u32[]{:S(2)}) collective-permute-start(f32[2,2,512,128]{3,2,1,0:T(8,128)} %collective-permute-done.24.ax), channel_id=1, source_target_pairs={{24,16},{25,17},{26,18},{27,19},{28,20},{29,21},{30,22},{31,23}} | collective-permute-start | bytes 3145736 | tf_op jit(solution)/shard_map/ppermute | solution.py:555
  212.0 11.7 %collective-permute-start.27 = (f32[2,2,512,128]{3,2,1,0:T(8,128)}, f32[2,2,512,128]{3,2,1,0:T(8,128)S(1)}, u32[]{:S(2)}, u32[]{:S(2)}) collective-permute-start(f32[2,2,512,128]{3,2,1,0:T(8,128)} %collective-permute-done.23.an), channel_id=1, source_target_pairs={{24,16},{25,17},{26,18},{27,19},{28,20},{29,21},{30,22},{31,23}} | collective-permute-start | bytes 3145736 | tf_op jit(solution)/shard_map/ppermute | solution.py:555
  (18 other events, 74.0 us)

commit v4 on v2

--- a/solution.py
+++ b/solution.py
@@ -8,7 +8,7 @@
 from jax.sharding import PartitionSpec as P
 
 STEPS = 4
-CHUNK = 256
+TILE = [256]
 MIB = 1024 * 1024
 SMEM = pl.BlockSpec(memory_space=pltpu.SMEM)
 VMEM = pl.BlockSpec(memory_space=pltpu.VMEM)
@@ -87,11 +87,11 @@
 
 
 class Rows:
-    def __init__(self, ref, first):
-        self.ref, self.first = ref, first
+    def __init__(self, ref, first, by=1):
+        self.ref, self.first, self.by = ref, first, by
 
     def key(self, key):
-        return (key[0], key[1] + self.first, *key[2:])
+        return (key[0], self.first + self.by * key[1], *key[2:])
 
     def __getitem__(self, key):
         return self.ref[self.key(key)]
@@ -110,7 +110,7 @@
 
 
 def tiles(count, ny, body):
-    n = CHUNK if ny % CHUNK == 0 else ny
+    n = TILE[-1] if ny % TILE[-1] == 0 else ny
     per = ny // n
 
     def run(k, carry):
@@ -395,38 +395,66 @@
         nn[...] = on[...]
 
 
-def coarse_outer_kernel(
-    own, prm, am, an, ax, low, high, kn, kx, ids, ide, on, ox, *refs
-):
-    rim, tl0, tl7, part, pad = refs[-5:]
-    edge, beside = Rows(rim, 0), Rows(rim, 2)
+def coarse_outer_kernel(own, prm, am, an, ax, low, high, kn, kx, on, ox, idm, idn, idx, *refs):
+    rim, tl0, tl7, pad = refs[-4:]
+    e = pl.program_id(0)
+    ny = ax.shape[2]
 
     @pl.when(own[0] != 0)
     def _():
-        coarse_body(
-            prm,
-            {"x": ax, "n": an, "m": am},
-            {"n": kn, "x": kx},
-            {"n": on, "x": ox},
-            ids,
-            into({"n": beside, "x": part}),
-            "xn",
-            pad,
-            True,
-        )
-        edges_body(prm, "coarse", part, low, high, ide, edge, tl0, tl7)
+        tab = Tables(prm)
+        clear_rims(pad)
+
+        def zero(i, t):
+            for f in F2:
+                pad[f, 0, t.pad(), :] = jnp.zeros((t.n, 128), jnp.float32)
+
+        tiles(1, ny, zero)
+        for k, (now, ids) in enumerate(((ax, idx), (an, idn), (am, idm))):
+
+            def melt(i, t, k=k, now=now, ids=ids):
+                values = [now[f, 0, t.at, :] for f in F2]
+                put_melt(tab, pad, k + 1, t, ids[0, t.at, :], *values)
+
+            tiles(1, ny, melt)
+        for k, (now, ids, end, start) in enumerate(((ax, idx, ox, kx), (an, idn, on, kn))):
+
+            def update(i, t, k=k, now=now, ids=ids, end=end, start=start):
+                cells = Cells(tab, ids[0, t.at, :])
+                rate = cells.coarse()
+                new = []
+                for f in F2:
+                    total = lap(pad, f, k + 1, t)
+                    if k == 0:
+                        total = total + jnp.where(e == 0, low[f, t.at, :], high[f, t.at, :])
+                    value = now[f, 0, t.at, :] + rate[f] * total
+                    new.append(value + (end[f, 0, t.at, :] - start[f, 0, t.at, :]))
+                    rim[f, k, t.at, :] = new[f]
+                if k == 0:
+                    values = cells.melt(*new)
+
+                    @pl.when(e == 0)
+                    def _():
+                        for f in F2:
+                            tl0[f, t.at, :] = values[f]
+
+                    @pl.when(e == 1)
+                    def _():
+                        for f in F2:
+                            tl7[f, t.at, :] = values[f]
+
+            tiles(1, ny, update)
 
     @pl.when(own[0] == 0)
     def _():
         for f in F2:
-            for e in range(2):
-                edge[f, e] = ox[f, e]
-                beside[f, e] = on[f, e]
+            rim[f, 0] = ox[f, 0]
+            rim[f, 1] = on[f, 0]
 
 
 def last_rows_kernel(own, prm, am, ar, km, kn, kx, ids, om, rim, oh, oc, pad):
     out = (oh, oc)
-    ax, an, ox, on = Rows(ar, 0), Rows(ar, 2), Rows(rim, 0), Rows(rim, 2)
+    ax, an, ox, on = Rows(ar, 0, 2), Rows(ar, 1, 2), Rows(rim, 0, 2), Rows(rim, 1, 2)
 
     @pl.when(own[0] != 0)
     def _():
@@ -488,15 +516,15 @@
 TINY = pl.CostEstimate(flops=1000, bytes_accessed=1000, transcendentals=0)
 
 
-def call(kernel, outs, args, smem, name, scratch=(), limit=8, after=(), through=(), flops=1000):
+def call(kernel, outs, args, smem, name, scratch=(), limit=8, after=(), through=(), flops=1000, tile=256):
     after = (*after, *through)
     first = len(args) + len(after) - len(through)
-    run = kernel
-    if after:
-        count = len(args)
-
-        def run(*refs):
-            kernel(*refs[:count], *refs[count + len(after) + len(through) :])
+    count = len(args)
+
+    def run(*refs):
+        TILE.append(tile)
+        kernel(*refs[:count], *refs[count + len(after) + len(through) :])
+        TILE.pop()
 
     return pl.pallas_call(
         run,
@@ -575,6 +603,7 @@
         "first_step",
         pad,
         26,
+        tile=128,
         through=(later0, later7),
     )
     odd = halos(later0, later7, every[1::2], 0)
@@ -603,6 +632,7 @@
                 1,
                 "base",
                 limit=16,
+                tile=128,
             )
         if k == STEPS - 3:
             *sm, sn, part = call(
@@ -613,6 +643,7 @@
                 "step_apart",
                 pad,
                 18,
+                tile=128,
             )
         elif k == STEPS - 2:
             last = (*sm, sn, sx)
@@ -624,10 +655,11 @@
                 "step_joined",
                 pad,
                 18,
+                tile=512,
             )
         else:
             sm, sn, part = call(
-                step_kernel, [tall, pair, pair], (prm, sm, sn, sx, ids), 1, "step", pad, 18
+                step_kernel, [tall, pair, pair], (prm, sm, sn, sx, ids), 1, "step", pad, 18, tile=128
             )
     km, kn, kx = base
 
@@ -639,6 +671,7 @@
         "replay",
         pad,
         24,
+        tile=512,
     )
     vn = sn
     vx, tl0, tl7 = fine_edges(part, sides, (vm,))
@@ -652,6 +685,7 @@
         "coarse_rim",
         pad,
         20,
+        tile=512,
     )
     vx, tl0, tl7 = call(
         coarse_edges_kernel,
@@ -660,6 +694,13 @@
         2,
         "coarse_edges",
     )
+    side = pl.BlockSpec((2, 1, ny, nz), lambda i: (0, i, 0, 0))
+    two = pl.BlockSpec((2, 2, ny, nz), lambda i: (0, i, 0, 0))
+    inside = pl.BlockSpec((2, 1, ny, nz), lambda i: (0, (mid - 1) * i, 0, 0))
+
+    def id_row(k):
+        return pl.BlockSpec((1, ny, nz), lambda i: (k + (rows - 1 - 2 * k) * i, 0, 0))
+
     rim = None
     for n in range(2, slices):
         low, high = halos(tl0, tl7, (n - 1,), 1)
@@ -679,16 +720,20 @@
             pad,
             18,
         )[0]
-        vm, rim, tl0, tl7 = call(
+        vm, rim, tl0, tl7 = pl.pallas_call(
             coarse_outer_kernel,
-            [f32(2, 4, ny, nz), halo, halo],
-            (own(n), prm, am, an, ax, low, high, kn, kx, ids, ide, vn, vx),
-            2,
-            "coarse_outer",
-            [pltpu.VMEM((2, 2, ny, nz), jnp.float32), *pad],
-            26,
-            through=(vm,),
-        )
+            grid=(2,),
+            out_shape=[tall, f32(2, 4, ny, nz), halo, halo],
+            in_specs=[SMEM, SMEM, inside, side, side, whole, whole]
+            + [side] * 4
+            + [id_row(2), id_row(1), id_row(0), ANY],
+            out_specs=[ANY, two, whole, whole],
+            scratch_shapes=[pltpu.VMEM((2, 5, ny + 16, nz), jnp.float32)],
+            input_output_aliases={14: 0},
+            compiler_params=pltpu.CompilerParams(vmem_limit_bytes=26 * MIB),
+            cost_estimate=TINY,
+            name="coarse_outer",
+        )(own(n), prm, am, an, ax, low, high, kn, kx, vn, vx, ids, ids, ids, vm)
 
     out = f32(1, rows, ny, nz)
     last_own = own(slices - 1)

time: 223 us -> 219 us (0.982)
  waiting for transfers between devices: 88.8 us -> 83.3 us
  Pallas kernels: 75.2 us -> 78.3 us
    ppermute x26, waiting for transfers between devices: 88.8 us -> 83.3 us  [move(): return lax.ppermute(x, ('tm', 'space'), pairs)]
    pallas_call x0 -> x1, Pallas kernels: none -> 4.4 us  [per_device(): pl.pallas_call(coarse_outer_kernel, grid=(2,), out_shape=[tall, f32(2, 4,...]
    pallas_call x16 -> x15, Pallas kernels: 69.9 us -> 68.6 us  [call(): pl.pallas_call(run, out_shape=[f32(*x.shape) for x in through] + list(out...]
    unnamed x40 -> x38, local copies, waits for them, and re-layouts: 8.24 us -> 8.24 us
  transfers between devices with their start and end apart: 26 -> 26, of which waited for: 9 -> 9; matrix products, arithmetic and copies ran while one was open for 0% -> 0% of each run, Pallas kernels for 27% -> 29%
where the time goes in v4:
time: 219 us
  waiting for transfers between devices  83.3 us (38%)
  Pallas kernels  78.3 us (36%)
  starting transfers between devices  46.8 us (21%)
  local copies, waits for them, and re-layouts  9.07 us (4%)
    ppermute x26, waiting for transfers between devices, move(): return lax.ppermute(x, ('tm', 'space'), pairs)  83.3 us
    pallas_call x15, Pallas kernels, call(): pl.pallas_call(run, out_shape=[f32(*x.shape) for x in through] + list(out...  68.6 us
    ppermute x26, starting transfers between devices, move(): return lax.ppermute(x, ('tm', 'space'), pairs)  46.8 us
    unnamed x38, local copies, waits for them, and re-layouts  8.24 us
    pallas_call x2, Pallas kernels, gridded(): pl.pallas_call(kernel, grid=(steps,), out_shape=outs, in_specs=in_specs,...  5.3 us
    pallas_call x1, Pallas kernels, per_device(): pl.pallas_call(coarse_outer_kernel, grid=(2,), out_shape=[tall, f32(2, 4,...  4.4 us
  transfers between devices with their start and end apart: 26, of which 9 were waited for; matrix products, arithmetic and copies ran while one was open for 0% of the time, Pallas kernels for 29%

profile of v4, /device:TPU:11, one launch (start us, length us, event | category | flops | bytes accessed | tf_op | source)
XLA Modules:
  0.0 218.5 jit_solution(4041479962153670219)
XLA Ops:
  1.5 2.4 %first_edges.1 = (f32[2,512,128]{2,1,0:T(8,128)S(1)}, f32[2,512,128]{2,1,0:T(8,128)S(1)}, f32[2,512,128]{2,1,0:T(8,128)S(1)}, f32[2,512,128]{2,1,0:T(8,128)S(1)}) custom-call(f32[27]{0:T(128)S(1)} %concatenate.3.prm.refs_0_.refs_1_, f32[8,512,128]{2,1,0:T(8,128)} %bitcast.5, f32[8,512,128]{2,1,0:T(8,128)} %bitcast.8, s32[8,512,128]{2,1,0:T(8,128)} %refs_3_.1), custom_call_target="tpu_custom_call" | custom-call | flops 1000 | bytes 1000 | tf_op jit(solution)/shard_map/first_edges/pallas_call | solution.py:572
  6.9 8.5 %first_step.1 = (f32[2,512,128]{2,1,0:T(8,128)S(1)}, f32[2,512,128]{2,1,0:T(8,128)S(1)}, f32[2,4,512,128]{3,2,1,0:T(8,128)S(1)}, f32[2,2,512,128]{3,2,1,0:T(8,12...) custom-call(f32[27]{0:T(128)S(1)} %concatenate.3.prm.refs_0_.refs_1_, ...), custom_call_target="tpu_custom_call", output_to_operand_aliasing={{0}: (5, {}), {1}: (6, {})} | custom-call | flops 1000 | bytes 1000 | tf_op jit(solution)/shard_map/first_step/pallas_call | solution.py:529
  15.4 3.1 %collective-permute-start.2 = (f32[2,512,128]{2,1,0:T(8,128)S(1)}, f32[2,512,128]{2,1,0:T(8,128)S(1)}, u32[]{:S(2)}, u32[]{:S(2)}) collective-permute-start(f32[2,512,128]{2,1,0:T(8,128)S(1)} %get-tuple-element.63), channel_id=1, source_target_pairs={{8,9},{9,10},{10,11},{11,12},{12,13},{13,14},{14,15},{24,25},{25,2... | collective-permute-start | bytes 1572872 | tf_op jit(solution)/shard_map/ppermute | solution.py:560
  18.6 3.0 %collective-permute-start.3 = (f32[2,512,128]{2,1,0:T(8,128)S(1)}, f32[2,512,128]{2,1,0:T(8,128)S(1)}, u32[]{:S(2)}, u32[]{:S(2)}) collective-permute-start(f32[2,512,128]{2,1,0:T(8,128)S(1)} %get-tuple-element.64), channel_id=1, source_target_pairs={{9,8},{10,9},{11,10},{12,11},{13,12},{14,13},{15,14},{25,24},{26,2... | collective-permute-start | bytes 1572872 | tf_op jit(solution)/shard_map/ppermute | solution.py:560
  21.7 9.5 %collective-permute-done.2.refs_4_ = f32[2,512,128]{2,1,0:T(8,128)S(1)} collective-permute-done((f32[2,512,128]{2,1,0:T(8,128)S(1)}, f32[2,512,128]{2,1,0:T(8,128)S(1)}, u32[]{:S(2)}, u32[]{:S(2)}) %collective-permute-start.2) | collective-permute-done | bytes 524320 | tf_op jit(solution)/shard_map/ppermute | solution.py:560
  34.1 2.3 %collective-permute-start.4 = (f32[2,512,128]{2,1,0:T(8,128)S(1)}, f32[2,512,128]{2,1,0:T(8,128)S(1)}, u32[]{:S(2)}, u32[]{:S(2)}) collective-permute-start(f32[2,512,128]{2,1,0:T(8,128)S(1)} %get-tuple-element.71), channel_id=1, source_target_pairs={{0,1},{1,2},{2,3},{3,4},{4,5},{5,6},{6,7},{8,9},{9,10},{10,11},{11... | collective-permute-start | bytes 1572872 | tf_op jit(solution)/shard_map/ppermute | solution.py:560
  36.3 4.3 %collective-permute-start.5 = (f32[2,512,128]{2,1,0:T(8,128)S(1)}, f32[2,512,128]{2,1,0:T(8,128)S(1)}, u32[]{:S(2)}, u32[]{:S(2)}) collective-permute-start(f32[2,512,128]{2,1,0:T(8,128)S(1)} %get-tuple-element.72), channel_id=1, source_target_pairs={{1,0},{2,1},{3,2},{4,3},{5,4},{6,5},{7,6},{9,8},{10,9},{11,10},{12... | collective-permute-start | bytes 1572872 | tf_op jit(solution)/shard_map/ppermute | solution.py:560
  40.7 3.3 %base.1 = (f32[2,4,512,128]{3,2,1,0:T(8,128)S(1)}, f32[2,2,512,128]{3,2,1,0:T(8,128)S(1)}, f32[2,2,512,128]{3,2,1,0:T(8,128)S(1)}) custom-call(f32[27]{0:T(128)S(1)} %concatenate.3.prm.refs_0_.refs_1_, f32[8,512,128]{2,1,0:T(8,128)S(1)} %bitcast.7, f32[8,512,128]{2,1,0:T(8,128)S(1)} %bitcast.10, f32[2,4,512,128]{3,2,1,0:T(8,128)S(1)} %get-tuple-element.56.refs_1_.refs_3_, ...), custom_call_target="tpu_custom_call" | custom-call | flops 1000 | bytes 1000 | tf_op jit(solution)/shard_map/base/pallas_call | solution.py:529
  44.0 8.2 %step.1 = (f32[2,4,512,128]{3,2,1,0:T(8,128)S(1)}, f32[2,2,512,128]{3,2,1,0:T(8,128)S(1)}, f32[2,2,512,128]{3,2,1,0:T(8,128)S(1)}) custom-call(f32[27]{0:T(128)S(1)} %concatenate.3.prm.refs_0_.refs_1_, f32[2,4,512,128]{3,2,1,0:T(8,128)S(1)} %get-tuple-element.56.refs_1_.refs_3_, f32[2,2,512,128]{3,2,1,0:T(8,128)S(1)} %get-tuple-element.57.refs_2_.refs_4_, ...), custom_call_target="tpu_custom_call" | custom-call | flops 1000 | bytes 1000 | tf_op jit(solution)/shard_map/step/pallas_call | solution.py:529
  52.2 2.7 %collective-permute-done.4.refs_2_ = f32[2,512,128]{2,1,0:T(8,128)S(1)} collective-permute-done((f32[2,512,128]{2,1,0:T(8,128)S(1)}, f32[2,512,128]{2,1,0:T(8,128)S(1)}, u32[]{:S(2)}, u32[]{:S(2)}) %collective-permute-start.4) | collective-permute-done | bytes 524320 | tf_op jit(solution)/shard_map/ppermute | solution.py:560
  54.9 3.3 %collective-permute-done.5.refs_3_ = f32[2,512,128]{2,1,0:T(8,128)S(1)} collective-permute-done((f32[2,512,128]{2,1,0:T(8,128)S(1)}, f32[2,512,128]{2,1,0:T(8,128)S(1)}, u32[]{:S(2)}, u32[]{:S(2)}) %collective-permute-start.5) | collective-permute-done | bytes 524320 | tf_op jit(solution)/shard_map/ppermute | solution.py:560
  59.5 1.9 collective-permute-start.10
  61.5 3.4 %collective-permute-start.9 = (f32[2,512,128]{2,1,0:T(8,128)S(1)}, f32[2,512,128]{2,1,0:T(8,128)S(1)}, u32[]{:S(2)}, u32[]{:S(2)}) collective-permute-start(f32[2,512,128]{2,1,0:T(8,128)S(1)} %get-tuple-element.81), channel_id=1, source_target_pairs={{0,1},{1,2},{2,3},{3,4},{4,5},{5,6},{6,7},{8,9},{9,10},{10,11},{11... | collective-permute-start | bytes 1572872 | tf_op jit(solution)/shard_map/ppermute | solution.py:560
  64.8 9.4 %step_apart.1 = (f32[4,512,128]{2,1,0:T(8,128)S(1)}, f32[4,512,128]{2,1,0:T(8,128)}, f32[2,2,512,128]{3,2,1,0:T(8,128)}, f32[2,2,512,128]{3,2,1,0:T(8,128)S(1)}) custom-call(f32[27]{0:T(128)S(1)} %concatenate.3.prm.refs_0_.refs_1_, f32[2,4,512,128]{3,2,1,0:T(8,128)S(1)} %get-tuple-element.68.refs_1_, f32[2,2,512,128]{3,2,1,0:T(8,128)S(1)} %get-tuple-element.69.refs_2_, ...), custom_call_target="tpu_custom_call" | custom-call | flops 1000 | bytes 1000 | tf_op jit(solution)/shard_map/step_apart/pallas_call | solution.py:529
  78.3 7.5 %collective-permute-done.10.refs_3_ = f32[2,512,128]{2,1,0:T(8,128)S(1)} collective-permute-done((f32[2,512,128]{2,1,0:T(8,128)S(1)}, f32[2,512,128]{2,1,0:T(8,128)S(1)}, u32[]{:S(2)}, u32[]{:S(2)}) %collective-permute-start.10) | collective-permute-done | bytes 524320 | tf_op jit(solution)/shard_map/ppermute | solution.py:560
  85.8 2.6 %edges.6 = (f32[2,2,512,128]{3,2,1,0:T(8,128)}, f32[2,512,128]{2,1,0:T(8,128)}, f32[2,512,128]{2,1,0:T(8,128)}) custom-call(f32[27]{0:T(128)S(1)} %concatenate.3.prm.refs_0_.refs_1_, f32[2,2,512,128]{3,2,1,0:T(8,128)S(1)} %get-tuple-element.80.refs_1_, f32[2,512,128]{2,1,0:T(8,128)S(1)} %collective-permute-done.9.refs_2_, ...), custom_call_target="tpu_custom_call" | custom-call | flops 1000 | bytes 1000 | tf_op jit(solution)/shard_map/edges/pallas_call | solution.py:529
  90.0 3.6 %collective-permute-start.13 = (f32[2,512,128]{2,1,0:T(8,128)}, f32[2,512,128]{2,1,0:T(8,128)}, u32[]{:S(2)}, u32[]{:S(2)}) collective-permute-start(f32[2,512,128]{2,1,0:T(8,128)} %get-tuple-element.89), channel_id=1, source_target_pairs={{0,1},{1,2},{2,3},{3,4},{4,5},{5,6},{6,7},{8,9},{9,10},{10,11},{11... | collective-permute-start | bytes 1572872 | tf_op jit(solution)/shard_map/ppermute | solution.py:560
  94.7 2.5 %collective-permute-start.14 = (f32[2,512,128]{2,1,0:T(8,128)}, f32[2,512,128]{2,1,0:T(8,128)}, u32[]{:S(2)}, u32[]{:S(2)}) collective-permute-start(f32[2,512,128]{2,1,0:T(8,128)} %get-tuple-element.90), channel_id=1, source_target_pairs={{1,0},{2,1},{3,2},{4,3},{5,4},{6,5},{7,6},{9,8},{10,9},{11,10},{12... | collective-permute-start | bytes 1572872 | tf_op jit(solution)/shard_map/ppermute | solution.py:560
  98.4 7.6 %step_joined.1 = (f32[2,4,512,128]{3,2,1,0:T(8,128)S(1)}, f32[2,2,512,128]{3,2,1,0:T(8,128)S(1)}, f32[2,2,512,128]{3,2,1,0:T(8,128)S(1)}) custom-call(f32[27]{0:T(128)S(1)} %concatenate.3.prm.refs_0_.refs_1_, f32[4,512,128]{2,1,0:T(8,128)S(1)} %copy-done.16, f32[4,512,128]{2,1,0:T(8,128)} %get-tuple-element.78.refs_2_, ...), custom_call_target="tpu_custom_call" | custom-call | flops 1000 | bytes 1000 | tf_op jit(solution)/shard_map/step_joined/pallas_call | solution.py:529
  106.1 3.4 %replay.1 = (f32[2,4,512,128]{3,2,1,0:T(8,128)S(1)}, f32[2,2,512,128]{3,2,1,0:T(8,128)S(1)}, f32[2,4,512,128]{3,2,1,0:T(8,128)}) custom-call(s32[1]{0:T(128)} %bitcast.2.refs_0_, f32[27]{0:T(128)S(1)} %concatenate.3.prm.refs_0_.refs_1_, f32[4,512,128]{2,1,0:T(8,128)S(1)} %copy-done.18, f32[4,512,128]{2,1,0:T(8,128)} %collective-permute-done.7.refs_3_, ...), custom_call_target="tpu_custom_call" | custom-call | flops 1000 | bytes 1000 | tf_op jit(solution)/shard_map/replay/pallas_call | solution.py:529
  109.5 6.5 %collective-permute-done.13.refs_2_ = f32[2,512,128]{2,1,0:T(8,128)} collective-permute-done((f32[2,512,128]{2,1,0:T(8,128)}, f32[2,512,128]{2,1,0:T(8,128)}, u32[]{:S(2)}, u32[]{:S(2)}) %collective-permute-start.13) | collective-permute-done | bytes 524320 | tf_op jit(solution)/shard_map/ppermute | solution.py:560
  116.0 2.2 %collective-permute-done.14.refs_3_ = f32[2,512,128]{2,1,0:T(8,128)} collective-permute-done((f32[2,512,128]{2,1,0:T(8,128)}, f32[2,512,128]{2,1,0:T(8,128)}, u32[]{:S(2)}, u32[]{:S(2)}) %collective-permute-start.14) | collective-permute-done | bytes 524320 | tf_op jit(solution)/shard_map/ppermute | solution.py:560
  118.2 2.1 edges.7
  121.1 2.0 collective-permute-start.12
  124.5 1.8 coarse_rim.1
  128.0 1.9 coarse_edges.1
  136.1 4.1 %coarse_mid.1.refs_0_ = f32[2,4,512,128]{3,2,1,0:T(8,128)} custom-call(s32[1]{0:T(128)} %bitcast.1.refs_0_.own, f32[27]{0:T(128)S(1)} %concatenate.3.prm.refs_0_.refs_1_, f32[2,4,512,128]{3,2,1,0:T(8,128)} %collective-permute-done.12.refs_2_.am, f32[2,2,512,128]{3,2,1,0:T(8,128)} %collective-permute-done.16.refs_3_.an, f32[2,4,512,128]{3,2,1,0:T(8,128)S(1)} %copy-done.2, ...), custom_call_target="tpu_custom_call" | custom-call | flops 1000 | bytes 1000 | tf_op jit(solution)/shard_map/coarse_mid/pallas_call | solution.py:529
  140.3 4.4 %coarse_outer.1 = (f32[2,4,512,128]{3,2,1,0:T(8,128)}, f32[2,4,512,128]{3,2,1,0:T(8,128)}, f32[2,512,128]{2,1,0:T(8,128)}, f32[2,512,128]{2,1,0:T(8,128)}) custom-call(s32[1]{0:T(128)} %bitcast.1.refs_0_.own, f32[27]{0:T(128)S(1)} %concatenate.3.prm.refs_0_.refs_1_, ...), custom_call_target="tpu_custom_call", output_to_operand_aliasing={{0}: (14, {})} | custom-call | flops 1000 | bytes 1000 | tf_op jit(solution)/shard_map/coarse_outer/pallas_call | solution.py:723
  149.9 47.1 %collective-permute-done.24.refs_2_ = f32[2,4,512,128]{3,2,1,0:T(8,128)} collective-permute-done((f32[2,4,512,128]{3,2,1,0:T(8,128)}, f32[2,4,512,128]{3,2,1,0:T(8,128)}, u32[]{:S(2)}, u32[]{:S(2)}) %collective-permute-start.24) | collective-permute-done | bytes 2097184 | tf_op jit(solution)/shard_map/ppermute | solution.py:560
  196.9 3.0 %collective-permute-done.25.refs_3_ = f32[2,4,512,128]{3,2,1,0:T(8,128)} collective-permute-done((f32[2,4,512,128]{3,2,1,0:T(8,128)}, f32[2,4,512,128]{3,2,1,0:T(8,128)}, u32[]{:S(2)}, u32[]{:S(2)}) %collective-permute-start.25) | collective-permute-done | bytes 2097184 | tf_op jit(solution)/shard_map/ppermute | solution.py:560
  202.8 12.8 %last_rows.1 = (f32[1,8,512,128]{3,2,1,0:T(8,128)}, f32[1,8,512,128]{3,2,1,0:T(8,128)}) custom-call(s32[1]{0:T(128)} %bitcast.refs_0_.own, f32[27]{0:T(128)S(1)} %concatenate.3.prm.refs_0_.refs_1_, f32[2,4,512,128]{3,2,1,0:T(8,128)} %collective-permute-done.24.refs_2_, f32[2,4,512,128]{3,2,1,0:T(8,128)} %collective-permute-done.25.refs_3_, ...), custom_call_target="tpu_custom_call" | custom-call | flops 1000 | bytes 1000 | tf_op jit(solution)/shard_map/last_rows/pallas_call | solution.py:529
  215.6 2.9 %last_edges.1 = (f32[1,8,512,128]{3,2,1,0:T(8,128)}, f32[1,8,512,128]{3,2,1,0:T(8,128)}) custom-call(s32[1]{0:T(128)} %bitcast.refs_0_.own, f32[27]{0:T(128)S(1)} %concatenate.3.prm.refs_0_.refs_1_, f32[2,512,128]{2,1,0:T(8,128)} %collective-permute-done.22.low, ...), custom_call_target="tpu_custom_call", output_to_operand_aliasing={{0}: (5, {}), {1}: (6, {})} | custom-call | flops 1000 | bytes 1000 | tf_op jit(solution)/shard_map/last_edges/pallas_call | solution.py:572
  (77 shorter events, 34.0 us)
Async XLA Ops:
  3.9 17.8 %collective-permute-start = (f32[2,512,128]{2,1,0:T(8,128)S(1)}, f32[2,512,128]{2,1,0:T(8,128)S(1)}, u32[]{:S(2)}, u32[]{:S(2)}) collective-permute-start(f32[2,512,128]{2,1,0:T(8,128)S(1)} %get-tuple-element.59), channel_id=1, source_target_pairs={{0,1},{1,2},{2,3},{3,4},{4,5},{5,6},{6,7},{16,17},{17,18},{18,19},... | collective-permute-start | bytes 1572872 | tf_op jit(solution)/shard_map/ppermute | solution.py:560
  4.6 17.1 %collective-permute-start.1 = (f32[2,512,128]{2,1,0:T(8,128)S(1)}, f32[2,512,128]{2,1,0:T(8,128)S(1)}, u32[]{:S(2)}, u32[]{:S(2)}) collective-permute-start(f32[2,512,128]{2,1,0:T(8,128)S(1)} %get-tuple-element.60), channel_id=1, source_target_pairs={{1,0},{2,1},{3,2},{4,3},{5,4},{6,5},{7,6},{17,16},{18,17},{19,18},... | collective-permute-start | bytes 1572872 | tf_op jit(solution)/shard_map/ppermute | solution.py:560
  15.4 70.4 %copy-start.10 = (s32[2,512,128]{2,1,0:T(8,128)}, s32[2,512,128]{2,1,0:T(8,128)S(1)}, u32[]{:S(2)}) copy-start(s32[2,512,128]{2,1,0:T(8,128)S(1)} %get-tuple-element.65.refs_6_.refs_4_.refs_5_.ide) | copy-start | bytes 1572868
  15.4 15.7 %collective-permute-start.2 = (f32[2,512,128]{2,1,0:T(8,128)S(1)}, f32[2,512,128]{2,1,0:T(8,128)S(1)}, u32[]{:S(2)}, u32[]{:S(2)}) collective-permute-start(f32[2,512,128]{2,1,0:T(8,128)S(1)} %get-tuple-element.63), channel_id=1, source_target_pairs={{8,9},{9,10},{10,11},{11,12},{12,13},{13,14},{14,15},{24,25},{25,2... | collective-permute-start | bytes 1572872 | tf_op jit(solution)/shard_map/ppermute | solution.py:560
  18.6 14.1 %collective-permute-start.3 = (f32[2,512,128]{2,1,0:T(8,128)S(1)}, f32[2,512,128]{2,1,0:T(8,128)S(1)}, u32[]{:S(2)}, u32[]{:S(2)}) collective-permute-start(f32[2,512,128]{2,1,0:T(8,128)S(1)} %get-tuple-element.64), channel_id=1, source_target_pairs={{9,8},{10,9},{11,10},{12,11},{13,12},{14,13},{15,14},{25,24},{26,2... | collective-permute-start | bytes 1572872 | tf_op jit(solution)/shard_map/ppermute | solution.py:560
  34.1 20.8 %collective-permute-start.4 = (f32[2,512,128]{2,1,0:T(8,128)S(1)}, f32[2,512,128]{2,1,0:T(8,128)S(1)}, u32[]{:S(2)}, u32[]{:S(2)}) collective-permute-start(f32[2,512,128]{2,1,0:T(8,128)S(1)} %get-tuple-element.71), channel_id=1, source_target_pairs={{0,1},{1,2},{2,3},{3,4},{4,5},{5,6},{6,7},{8,9},{9,10},{10,11},{11... | collective-permute-start | bytes 1572872 | tf_op jit(solution)/shard_map/ppermute | solution.py:560
  36.3 21.8 %collective-permute-start.5 = (f32[2,512,128]{2,1,0:T(8,128)S(1)}, f32[2,512,128]{2,1,0:T(8,128)S(1)}, u32[]{:S(2)}, u32[]{:S(2)}) collective-permute-start(f32[2,512,128]{2,1,0:T(8,128)S(1)} %get-tuple-element.72), channel_id=1, source_target_pairs={{1,0},{2,1},{3,2},{4,3},{5,4},{6,5},{7,6},{9,8},{10,9},{11,10},{12... | collective-permute-start | bytes 1572872 | tf_op jit(solution)/shard_map/ppermute | solution.py:560
  44.0 41.8 %copy-start = (f32[2,4,512,128]{3,2,1,0:T(8,128)}, f32[2,4,512,128]{3,2,1,0:T(8,128)S(1)}, u32[]{:S(2)}) copy-start(f32[2,4,512,128]{3,2,1,0:T(8,128)S(1)} %get-tuple-element.73.refs_5_.refs_7_.refs_4_) | copy-start | bytes 6291460
  44.0 41.8 %copy-start.4 = (f32[2,2,512,128]{3,2,1,0:T(8,128)}, f32[2,2,512,128]{3,2,1,0:T(8,128)S(1)}, u32[]{:S(2)}) copy-start(f32[2,2,512,128]{3,2,1,0:T(8,128)S(1)} %get-tuple-element.75.refs_7_.refs_6_.kx) | copy-start | bytes 3145732
  59.5 26.2 %collective-permute-start.10 = (f32[2,512,128]{2,1,0:T(8,128)S(1)}, f32[2,512,128]{2,1,0:T(8,128)S(1)}, u32[]{:S(2)}, u32[]{:S(2)}) collective-permute-start(f32[2,512,128]{2,1,0:T(8,128)S(1)} %get-tuple-element.82), channel_id=1, source_target_pairs={{1,0},{2,1},{3,2},{4,3},{5,4},{6,5},{7,6},{9,8},{10,9},{11,10},{12... | collective-permute-start | bytes 1572872 | tf_op jit(solution)/shard_map/ppermute | solution.py:560
  61.5 24.3 %collective-permute-start.9 = (f32[2,512,128]{2,1,0:T(8,128)S(1)}, f32[2,512,128]{2,1,0:T(8,128)S(1)}, u32[]{:S(2)}, u32[]{:S(2)}) collective-permute-start(f32[2,512,128]{2,1,0:T(8,128)S(1)} %get-tuple-element.81), channel_id=1, source_target_pairs={{0,1},{1,2},{2,3},{3,4},{4,5},{5,6},{6,7},{8,9},{9,10},{10,11},{11... | collective-permute-start | bytes 1572872 | tf_op jit(solution)/shard_map/ppermute | solution.py:560
  74.3 14.1 %copy-start.15 = (f32[4,512,128]{2,1,0:T(8,128)}, f32[4,512,128]{2,1,0:T(8,128)S(1)}, u32[]{:S(2)}) copy-start(f32[4,512,128]{2,1,0:T(8,128)S(1)} %get-tuple-element.77.refs_1_) | copy-start | bytes 3145732
  74.3 19.4 %collective-permute-start.6 = (f32[4,512,128]{2,1,0:T(8,128)S(1)}, f32[4,512,128]{2,1,0:T(8,128)S(1)}, u32[]{:S(2)}, u32[]{:S(2)}) collective-permute-start(f32[4,512,128]{2,1,0:T(8,128)S(1)} %get-tuple-element.77.refs_1_), channel_id=1, source_target_pairs={{0,8},{1,9},{2,10},{3,11},{4,12},{5,13},{6,14},{7,15}} | collective-permute-start | bytes 3145736 | tf_op jit(solution)/shard_map/ppermute | solution.py:560
  75.0 31.0 %collective-permute-start.7 = (f32[4,512,128]{2,1,0:T(8,128)}, f32[4,512,128]{2,1,0:T(8,128)}, u32[]{:S(2)}, u32[]{:S(2)}) collective-permute-start(f32[4,512,128]{2,1,0:T(8,128)} %get-tuple-element.78.refs_2_), channel_id=1, source_target_pairs={{0,8},{1,9},{2,10},{3,11},{4,12},{5,13},{6,14},{7,15}} | collective-permute-start | bytes 3145736 | tf_op jit(solution)/shard_map/ppermute | solution.py:560
  76.7 29.3 %collective-permute-start.8 = (f32[2,2,512,128]{3,2,1,0:T(8,128)}, f32[2,2,512,128]{3,2,1,0:T(8,128)}, u32[]{:S(2)}, u32[]{:S(2)}) collective-permute-start(f32[2,2,512,128]{3,2,1,0:T(8,128)} %get-tuple-element.79.refs_3_), channel_id=1, source_target_pairs={{0,8},{1,9},{2,10},{3,11},{4,12},{5,13},{6,14},{7,15}} | collective-permute-start | bytes 3145736 | tf_op jit(solution)/shard_map/ppermute | solution.py:560
  88.4 17.6 %collective-permute-start.11 = (f32[2,2,512,128]{3,2,1,0:T(8,128)}, f32[2,2,512,128]{3,2,1,0:T(8,128)}, u32[]{:S(2)}, u32[]{:S(2)}) collective-permute-start(f32[2,2,512,128]{3,2,1,0:T(8,128)} %get-tuple-element.83.refs_4_), channel_id=1, source_target_pairs={{0,8},{1,9},{2,10},{3,11},{4,12},{5,13},{6,14},{7,15}} | collective-permute-start | bytes 3145736 | tf_op jit(solution)/shard_map/ppermute | solution.py:560
  90.0 26.0 %collective-permute-start.13 = (f32[2,512,128]{2,1,0:T(8,128)}, f32[2,512,128]{2,1,0:T(8,128)}, u32[]{:S(2)}, u32[]{:S(2)}) collective-permute-start(f32[2,512,128]{2,1,0:T(8,128)} %get-tuple-element.89), channel_id=1, source_target_pairs={{0,1},{1,2},{2,3},{3,4},{4,5},{5,6},{6,7},{8,9},{9,10},{10,11},{11... | collective-permute-start | bytes 1572872 | tf_op jit(solution)/shard_map/ppermute | solution.py:560
  94.7 23.5 %collective-permute-start.14 = (f32[2,512,128]{2,1,0:T(8,128)}, f32[2,512,128]{2,1,0:T(8,128)}, u32[]{:S(2)}, u32[]{:S(2)}) collective-permute-start(f32[2,512,128]{2,1,0:T(8,128)} %get-tuple-element.90), channel_id=1, source_target_pairs={{1,0},{2,1},{3,2},{4,3},{5,4},{6,5},{7,6},{9,8},{10,9},{11,10},{12... | collective-permute-start | bytes 1572872 | tf_op jit(solution)/shard_map/ppermute | solution.py:560
  106.0 12.2 %copy-start.11 = (s32[2,512,128]{2,1,0:T(8,128)S(1)}, s32[2,512,128]{2,1,0:T(8,128)}, u32[]{:S(2)}) copy-start(s32[2,512,128]{2,1,0:T(8,128)} %copy-done.10) | copy-start | bytes 1572868
  120.3 4.2 %collective-permute-start.15 = (f32[2,2,512,128]{3,2,1,0:T(8,128)S(1)}, f32[2,2,512,128]{3,2,1,0:T(8,128)S(1)}, u32[]{:S(2)}, u32[]{:S(2)}) collective-permute-start(f32[2,2,512,128]{3,2,1,0:T(8,128)S(1)} %get-tuple-element.91.refs_9_.refs_6_), channel_id=1, source_target_pairs={{0,8},{1,9},{2,10},{3,11},{4,12},{5,13},{6,14},{7,15}} | collective-permute-start | bytes 3145736 | tf_op jit(solution)/shard_map/ppermute | solution.py:560
  121.1 13.4 %collective-permute-start.12 = (f32[2,4,512,128]{3,2,1,0:T(8,128)}, f32[2,4,512,128]{3,2,1,0:T(8,128)}, u32[]{:S(2)}, u32[]{:S(2)}) collective-permute-start(f32[2,4,512,128]{3,2,1,0:T(8,128)} %get-tuple-element.85.refs_5_.refs_6_), channel_id=1, source_target_pairs={{8,16},{9,17},{10,18},{11,19},{12,20},{13,21},{14,22},{15,23}} | collective-permute-start | bytes 6291464 | tf_op jit(solution)/shard_map/ppermute | solution.py:560
  123.1 4.9 %collective-permute-start.17 = (f32[2,512,128]{2,1,0:T(8,128)S(1)}, f32[2,512,128]{2,1,0:T(8,128)S(1)}, u32[]{:S(2)}, u32[]{:S(2)}) collective-permute-start(f32[2,512,128]{2,1,0:T(8,128)S(1)} %get-tuple-element.95), channel_id=1, source_target_pairs={{0,9},{1,10},{2,11},{3,12},{4,13},{5,14},{6,15}} | collective-permute-start | bytes 1572872 | tf_op jit(solution)/shard_map/ppermute | solution.py:560
  123.8 4.2 %collective-permute-start.18 = (f32[2,512,128]{2,1,0:T(8,128)S(1)}, f32[2,512,128]{2,1,0:T(8,128)S(1)}, u32[]{:S(2)}, u32[]{:S(2)}) collective-permute-start(f32[2,512,128]{2,1,0:T(8,128)S(1)} %get-tuple-element.96), channel_id=1, source_target_pairs={{1,8},{2,9},{3,10},{4,11},{5,12},{6,13},{7,14}} | collective-permute-start | bytes 1572872 | tf_op jit(solution)/shard_map/ppermute | solution.py:560
  126.3 8.2 %collective-permute-start.16 = (f32[2,2,512,128]{3,2,1,0:T(8,128)}, f32[2,2,512,128]{3,2,1,0:T(8,128)}, u32[]{:S(2)}, u32[]{:S(2)}) collective-permute-start(f32[2,2,512,128]{3,2,1,0:T(8,128)} %get-tuple-element.93.on), channel_id=1, source_target_pairs={{8,16},{9,17},{10,18},{11,19},{12,20},{13,21},{14,22},{15,23}} | collective-permute-start | bytes 3145736 | tf_op jit(solution)/shard_map/ppermute | solution.py:560
  130.0 10.3 %collective-permute-start.19 = (f32[2,2,512,128]{3,2,1,0:T(8,128)}, f32[2,2,512,128]{3,2,1,0:T(8,128)}, u32[]{:S(2)}, u32[]{:S(2)}) collective-permute-start(f32[2,2,512,128]{3,2,1,0:T(8,128)} %get-tuple-element.97.ox), channel_id=1, source_target_pairs={{8,16},{9,17},{10,18},{11,19},{12,20},{13,21},{14,22},{15,23}} | collective-permute-start | bytes 3145736 | tf_op jit(solution)/shard_map/ppermute | solution.py:560
  131.6 8.7 %collective-permute-start.20 = (f32[2,512,128]{2,1,0:T(8,128)}, f32[2,512,128]{2,1,0:T(8,128)}, u32[]{:S(2)}, u32[]{:S(2)}) collective-permute-start(f32[2,512,128]{2,1,0:T(8,128)} %get-tuple-element.98), channel_id=1, source_target_pairs={{8,17},{9,18},{10,19},{11,20},{12,21},{13,22},{14,23}} | collective-permute-start | bytes 1572872 | tf_op jit(solution)/shard_map/ppermute | solution.py:560
  133.0 7.2 %collective-permute-start.21 = (f32[2,512,128]{2,1,0:T(8,128)}, f32[2,512,128]{2,1,0:T(8,128)}, u32[]{:S(2)}, u32[]{:S(2)}) collective-permute-start(f32[2,512,128]{2,1,0:T(8,128)} %get-tuple-element.99), channel_id=1, source_target_pairs={{9,16},{10,17},{11,18},{12,19},{13,20},{14,21},{15,22}} | collective-permute-start | bytes 1572872 | tf_op jit(solution)/shard_map/ppermute | solution.py:560
  144.7 52.3 %collective-permute-start.24 = (f32[2,4,512,128]{3,2,1,0:T(8,128)}, f32[2,4,512,128]{3,2,1,0:T(8,128)}, u32[]{:S(2)}, u32[]{:S(2)}) collective-permute-start(f32[2,4,512,128]{3,2,1,0:T(8,128)} %get-tuple-element.102.refs_8_), channel_id=1, source_target_pairs={{16,24},{17,25},{18,26},{19,27},{20,28},{21,29},{22,30},{23,31}} | collective-permute-start | bytes 6291464 | tf_op jit(solution)/shard_map/ppermute | solution.py:560
  146.0 54.0 %collective-permute-start.25 = (f32[2,4,512,128]{3,2,1,0:T(8,128)}, f32[2,4,512,128]{3,2,1,0:T(8,128)}, u32[]{:S(2)}, u32[]{:S(2)}) collective-permute-start(f32[2,4,512,128]{3,2,1,0:T(8,128)} %get-tuple-element.103.refs_9_), channel_id=1, source_target_pairs={{16,24},{17,25},{18,26},{19,27},{20,28},{21,29},{22,30},{23,31}} | collective-permute-start | bytes 6291464 | tf_op jit(solution)/shard_map/ppermute | solution.py:560
  147.3 68.3 %collective-permute-start.22 = (f32[2,512,128]{2,1,0:T(8,128)}, f32[2,512,128]{2,1,0:T(8,128)}, u32[]{:S(2)}, u32[]{:S(2)}) collective-permute-start(f32[2,512,128]{2,1,0:T(8,128)} %get-tuple-element.100), channel_id=1, source_target_pairs={{16,25},{17,26},{18,27},{19,28},{20,29},{21,30},{22,31}} | collective-permute-start | bytes 1572872 | tf_op jit(solution)/shard_map/ppermute | solution.py:560
  148.6 67.0 %collective-permute-start.23 = (f32[2,512,128]{2,1,0:T(8,128)}, f32[2,512,128]{2,1,0:T(8,128)}, u32[]{:S(2)}, u32[]{:S(2)}) collective-permute-start(f32[2,512,128]{2,1,0:T(8,128)} %get-tuple-element.101), channel_id=1, source_target_pairs={{17,24},{18,25},{19,26},{20,27},{21,28},{22,29},{23,30}} | collective-permute-start | bytes 1572872 | tf_op jit(solution)/shard_map/ppermute | solution.py:560
  202.8 12.8 %copy-start.12 = (s32[2,512,128]{2,1,0:T(8,128)S(1)}, s32[2,512,128]{2,1,0:T(8,128)}, u32[]{:S(2)}) copy-start(s32[2,512,128]{2,1,0:T(8,128)} %copy-done.10) | copy-start | bytes 1572868
  (13 other events, 45.4 us)

commit v5 on v4

--- a/solution.py
+++ b/solution.py
@@ -452,36 +452,63 @@
             rim[f, 1] = on[f, 0]
 
 
-def last_rows_kernel(own, prm, am, ar, km, kn, kx, ids, om, rim, oh, oc, pad):
+def last_rows_kernel(own, prm, am, aq, ar, km, kn, kx, ids, idq, om, rim, oh, oc, pad):
     out = (oh, oc)
-    ax, an, ox, on = Rows(ar, 0, 2), Rows(ar, 1, 2), Rows(rim, 0, 2), Rows(rim, 1, 2)
+    e = pl.program_id(0)
+    half, ny = am.shape[1], am.shape[2]
+    count = half + 2
+
+    def place(k):
+        return jnp.where(e == 0, k, count - 1 - k)
+
+    def inner(j):
+        return jnp.where(e == 0, j, half - 1 - j)
+
+    def each(body):
+        tiles(1, ny, lambda i, t: body(0, t, 0, "x"))
+        tiles(1, ny, lambda i, t: body(1, t, 0, "n"))
+        tiles(half, ny, lambda j, t: body(j + 2, t, inner(j), "m"))
+
+    def at(ref, i, t):
+        return [ref[f, i, t.at, :] for f in F2]
+
+    arrived = {"x": Rows(ar, 0), "n": Rows(ar, 1), "m": am}
+    old = {"x": Rows(rim, 0), "n": Rows(rim, 1), "m": om}
+    base = {"x": kx, "n": kn, "m": km}
 
     @pl.when(own[0] != 0)
     def _():
-        def put(name, f, i, r, t, value):
-            out[f][0, r, t.at, :] = value
-
-        coarse_body(
-            prm,
-            {"x": ax, "n": an, "m": am},
-            {"m": km, "n": kn, "x": kx},
-            {"m": om, "n": on, "x": ox},
-            ids,
-            put,
-            "mnx",
-            pad,
-            True,
-        )
+        tab = Tables(prm)
+        clear_rims(pad)
+
+        def zero(i, t):
+            for f in F2:
+                pad[f, 0, t.pad(), :] = jnp.zeros((t.n, 128), jnp.float32)
+
+        def melt(k, t, i, name):
+            put_melt(tab, pad, k + 1, t, ids[place(k), t.at, :], *at(arrived[name], i, t))
+
+        def beyond(i, t):
+            put_melt(tab, pad, count + 1, t, idq[0, t.at, :], *at(aq, 0, t))
+
+        def update(k, t, i, name):
+            new = coarse(tab, pad, k + 1, t, ids[place(k), t.at, :], at(arrived[name], i, t))
+            end, start = at(old[name], i, t), at(base[name], i, t)
+            for f in F2:
+                out[f][0, place(k), t.at, :] = new[f] + (end[f] - start[f])
+
+        tiles(1, ny, zero)
+        each(melt)
+        tiles(1, ny, beyond)
+        each(update)
 
     @pl.when(own[0] == 0)
     def _():
-        old = {"m": om, "n": on, "x": ox}
-
-        def body(name, i, r, t):
+        def keep(k, t, i, name):
             for f in F2:
-                out[f][0, r, t.at, :] = old[name][f, i, t.at, :]
-
-        Parts(om.shape[1]).each(om.shape[2], body)
+                out[f][0, place(k), t.at, :] = old[name][f, i, t.at, :]
+
+        each(keep)
 
 
 def last_edges_kernel(own, prm, low, high, ide, oh, oc, nh, nc):
@@ -561,6 +588,9 @@
 
     def halos(tl0, tl7, tms, up):
         return move(tl7, tms, up, 1), move(tl0, tms, up, -1)
+
+    def hbm(x):
+        return pltpu.with_memory_space_constraint(x, pltpu.HBM)
 
     def send(x, n):
         return move(x, (n - 1,), 1, 0)
@@ -646,6 +676,7 @@
                 tile=128,
             )
         elif k == STEPS - 2:
+            sm = [hbm(x) for x in sm]
             last = (*sm, sn, sx)
             sm, sn, part = call(
                 step_joined_kernel,
@@ -666,7 +697,7 @@
     am, an, vm = call(
         replay_kernel,
         [tall, pair, tall],
-        (own(1), prm, *(send(x, 1) for x in last), ids, km, sm),
+        (own(1), prm, *(hbm(send(x, 1)) for x in last), ids, hbm(km), sm),
         2,
         "replay",
         pad,
@@ -737,15 +768,21 @@
 
     out = f32(1, rows, ny, nz)
     last_own = own(slices - 1)
-    oh, oc = call(
+    half = pl.BlockSpec((2, mid // 2, ny, nz), lambda i: (0, i, 0, 0))
+    beyond = pl.BlockSpec((2, 1, ny, nz), lambda i: (0, mid // 2 - i, 0, 0))
+    id_half = pl.BlockSpec((rows // 2, ny, nz), lambda i: (i, 0, 0))
+    id_beyond = pl.BlockSpec((1, ny, nz), lambda i: (rows // 2 - i, 0, 0))
+    oh, oc = pl.pallas_call(
         last_rows_kernel,
-        [out, out],
-        (last_own, prm, am, ar, km, kn, kx, ids, vm, rim),
-        2,
-        "last_rows",
-        pad,
-        28,
-    )
+        grid=(2,),
+        out_shape=[out, out],
+        in_specs=[SMEM, SMEM, half, beyond, two, half, side, side, id_half, id_beyond, half, two],
+        out_specs=[pl.BlockSpec((1, rows // 2, ny, nz), lambda i: (0, i, 0, 0))] * 2,
+        scratch_shapes=[pltpu.VMEM((2, rows // 2 + 2, ny + 16, nz), jnp.float32)],
+        compiler_params=pltpu.CompilerParams(vmem_limit_bytes=30 * MIB),
+        cost_estimate=TINY,
+        name="last_rows",
+    )(last_own, prm, am, am, ar, hbm(km), hbm(kn), hbm(kx), ids, ids, vm, rim)
     out_row = pl.BlockSpec((1, 1, ny, nz), lambda i: (0, (rows - 1) * i, 0, 0))
     one = pl.BlockSpec((1, ny, nz), lambda i: (i, 0, 0))
     return tuple(

time: 219 us -> 215 us (0.982)
  local copies, waits for them, and re-layouts: 9.07 us -> 5.1 us
    pallas_call x0 -> x1, Pallas kernels: none -> 12 us  [per_device(): pl.pallas_call(last_rows_kernel, grid=(2,), out_shape=[out, out], in_spec...]
    pallas_call x15 -> x14, Pallas kernels: 68.6 us -> 57 us  [call(): pl.pallas_call(run, out_shape=[f32(*x.shape) for x in through] + list(out...]
    unnamed x38 -> x30, local copies, waits for them, and re-layouts: 8.24 us -> 4.27 us
  transfers between devices with their start and end apart: 26 -> 26, of which waited for: 9 -> 9; matrix products, arithmetic and copies ran while one was open for 0% -> 0% of each run, Pallas kernels for 29% -> 30%
where the time goes in v5:
time: 215 us; the launch traced here: 214 us
  waiting for transfers between devices  83.4 us (39%)
  Pallas kernels  78.2 us (36%)
  starting transfers between devices  46.7 us (22%)
  local copies, waits for them, and re-layouts  5.1 us (2%)
    ppermute x26, waiting for transfers between devices, move(): return lax.ppermute(x, ('tm', 'space'), pairs)  83.4 us
    pallas_call x14, Pallas kernels, call(): pl.pallas_call(run, out_shape=[f32(*x.shape) for x in through] + list(out...  57 us
    ppermute x26, starting transfers between devices, move(): return lax.ppermute(x, ('tm', 'space'), pairs)  46.7 us
    pallas_call x1, Pallas kernels, per_device(): pl.pallas_call(last_rows_kernel, grid=(2,), out_shape=[out, out], in_spec...  12 us
    pallas_call x2, Pallas kernels, gridded(): pl.pallas_call(kernel, grid=(steps,), out_shape=outs, in_specs=in_specs,...  4.94 us
    pallas_call x1, Pallas kernels, per_device(): pl.pallas_call(coarse_outer_kernel, grid=(2,), out_shape=[tall, f32(2, 4,...  4.35 us
  transfers between devices with their start and end apart: 26, of which 9 were waited for; matrix products, arithmetic and copies ran while one was open for 0% of the time, Pallas kernels for 30%

profile of v5, /device:TPU:11, one launch (start us, length us, event | category | flops | bytes accessed | tf_op | source)
XLA Modules:
  0.0 214.4 jit_solution(10322103051799740554)
XLA Ops:
  1.5 2.4 %first_edges.1 = (f32[2,512,128]{2,1,0:T(8,128)S(1)}, f32[2,512,128]{2,1,0:T(8,128)S(1)}, f32[2,512,128]{2,1,0:T(8,128)S(1)}, f32[2,512,128]{2,1,0:T(8,128)S(1)}) custom-call(f32[27]{0:T(128)S(1)} %concatenate.3.prm.refs_0_.refs_1_, f32[8,512,128]{2,1,0:T(8,128)} %bitcast.5, f32[8,512,128]{2,1,0:T(8,128)} %bitcast.8, s32[8,512,128]{2,1,0:T(8,128)} %refs_3_.1), custom_call_target="tpu_custom_call" | custom-call | flops 1000 | bytes 1000 | tf_op jit(solution)/shard_map/first_edges/pallas_call | solution.py:602
  6.9 8.5 %first_step.1 = (f32[2,512,128]{2,1,0:T(8,128)S(1)}, f32[2,512,128]{2,1,0:T(8,128)S(1)}, f32[2,4,512,128]{3,2,1,0:T(8,128)S(1)}, f32[2,2,512,128]{3,2,1,0:T(8,12...) custom-call(f32[27]{0:T(128)S(1)} %concatenate.3.prm.refs_0_.refs_1_, ...), custom_call_target="tpu_custom_call", output_to_operand_aliasing={{0}: (5, {}), {1}: (6, {})} | custom-call | flops 1000 | bytes 1000 | tf_op jit(solution)/shard_map/first_step/pallas_call | solution.py:556
  15.4 3.1 %collective-permute-start.2 = (f32[2,512,128]{2,1,0:T(8,128)S(1)}, f32[2,512,128]{2,1,0:T(8,128)S(1)}, u32[]{:S(2)}, u32[]{:S(2)}) collective-permute-start(f32[2,512,128]{2,1,0:T(8,128)S(1)} %get-tuple-element.63), channel_id=1, source_target_pairs={{8,9},{9,10},{10,11},{11,12},{12,13},{13,14},{14,15},{24,25},{25,2... | collective-permute-start | bytes 1572872 | tf_op jit(solution)/shard_map/ppermute | solution.py:587
  18.6 3.0 %collective-permute-start.3 = (f32[2,512,128]{2,1,0:T(8,128)S(1)}, f32[2,512,128]{2,1,0:T(8,128)S(1)}, u32[]{:S(2)}, u32[]{:S(2)}) collective-permute-start(f32[2,512,128]{2,1,0:T(8,128)S(1)} %get-tuple-element.64), channel_id=1, source_target_pairs={{9,8},{10,9},{11,10},{12,11},{13,12},{14,13},{15,14},{25,24},{26,2... | collective-permute-start | bytes 1572872 | tf_op jit(solution)/shard_map/ppermute | solution.py:587
  21.7 9.5 %collective-permute-done.2.refs_4_ = f32[2,512,128]{2,1,0:T(8,128)S(1)} collective-permute-done((f32[2,512,128]{2,1,0:T(8,128)S(1)}, f32[2,512,128]{2,1,0:T(8,128)S(1)}, u32[]{:S(2)}, u32[]{:S(2)}) %collective-permute-start.2) | collective-permute-done | bytes 524320 | tf_op jit(solution)/shard_map/ppermute | solution.py:587
  34.1 2.3 %collective-permute-start.4 = (f32[2,512,128]{2,1,0:T(8,128)S(1)}, f32[2,512,128]{2,1,0:T(8,128)S(1)}, u32[]{:S(2)}, u32[]{:S(2)}) collective-permute-start(f32[2,512,128]{2,1,0:T(8,128)S(1)} %get-tuple-element.71), channel_id=1, source_target_pairs={{0,1},{1,2},{2,3},{3,4},{4,5},{5,6},{6,7},{8,9},{9,10},{10,11},{11... | collective-permute-start | bytes 1572872 | tf_op jit(solution)/shard_map/ppermute | solution.py:587
  36.3 4.3 %collective-permute-start.5 = (f32[2,512,128]{2,1,0:T(8,128)S(1)}, f32[2,512,128]{2,1,0:T(8,128)S(1)}, u32[]{:S(2)}, u32[]{:S(2)}) collective-permute-start(f32[2,512,128]{2,1,0:T(8,128)S(1)} %get-tuple-element.72), channel_id=1, source_target_pairs={{1,0},{2,1},{3,2},{4,3},{5,4},{6,5},{7,6},{9,8},{10,9},{11,10},{12... | collective-permute-start | bytes 1572872 | tf_op jit(solution)/shard_map/ppermute | solution.py:587
  40.7 3.3 %base.1 = (f32[2,4,512,128]{3,2,1,0:T(8,128)S(1)}, f32[2,2,512,128]{3,2,1,0:T(8,128)S(1)}, f32[2,2,512,128]{3,2,1,0:T(8,128)S(1)}) custom-call(f32[27]{0:T(128)S(1)} %concatenate.3.prm.refs_0_.refs_1_, f32[8,512,128]{2,1,0:T(8,128)S(1)} %bitcast.7, f32[8,512,128]{2,1,0:T(8,128)S(1)} %bitcast.10, f32[2,4,512,128]{3,2,1,0:T(8,128)S(1)} %get-tuple-element.56.refs_1_.refs_3_, ...), custom_call_target="tpu_custom_call" | custom-call | flops 1000 | bytes 1000 | tf_op jit(solution)/shard_map/base/pallas_call | solution.py:556
  44.0 8.2 %step.1 = (f32[2,4,512,128]{3,2,1,0:T(8,128)S(1)}, f32[2,2,512,128]{3,2,1,0:T(8,128)S(1)}, f32[2,2,512,128]{3,2,1,0:T(8,128)S(1)}) custom-call(f32[27]{0:T(128)S(1)} %concatenate.3.prm.refs_0_.refs_1_, f32[2,4,512,128]{3,2,1,0:T(8,128)S(1)} %get-tuple-element.56.refs_1_.refs_3_, f32[2,2,512,128]{3,2,1,0:T(8,128)S(1)} %get-tuple-element.57.refs_2_.refs_4_, ...), custom_call_target="tpu_custom_call" | custom-call | flops 1000 | bytes 1000 | tf_op jit(solution)/shard_map/step/pallas_call | solution.py:556
  52.2 2.6 %collective-permute-done.4.refs_2_ = f32[2,512,128]{2,1,0:T(8,128)S(1)} collective-permute-done((f32[2,512,128]{2,1,0:T(8,128)S(1)}, f32[2,512,128]{2,1,0:T(8,128)S(1)}, u32[]{:S(2)}, u32[]{:S(2)}) %collective-permute-start.4) | collective-permute-done | bytes 524320 | tf_op jit(solution)/shard_map/ppermute | solution.py:587
  54.9 3.3 %collective-permute-done.5.refs_3_ = f32[2,512,128]{2,1,0:T(8,128)S(1)} collective-permute-done((f32[2,512,128]{2,1,0:T(8,128)S(1)}, f32[2,512,128]{2,1,0:T(8,128)S(1)}, u32[]{:S(2)}, u32[]{:S(2)}) %collective-permute-start.5) | collective-permute-done | bytes 524320 | tf_op jit(solution)/shard_map/ppermute | solution.py:587
  59.5 1.9 collective-permute-start.10
  61.5 3.4 %collective-permute-start.9 = (f32[2,512,128]{2,1,0:T(8,128)S(1)}, f32[2,512,128]{2,1,0:T(8,128)S(1)}, u32[]{:S(2)}, u32[]{:S(2)}) collective-permute-start(f32[2,512,128]{2,1,0:T(8,128)S(1)} %get-tuple-element.81), channel_id=1, source_target_pairs={{0,1},{1,2},{2,3},{3,4},{4,5},{5,6},{6,7},{8,9},{9,10},{10,11},{11... | collective-permute-start | bytes 1572872 | tf_op jit(solution)/shard_map/ppermute | solution.py:587
  64.8 9.4 %step_apart.1 = (f32[4,512,128]{2,1,0:T(8,128)S(1)}, f32[4,512,128]{2,1,0:T(8,128)}, f32[2,2,512,128]{3,2,1,0:T(8,128)}, f32[2,2,512,128]{3,2,1,0:T(8,128)S(1)}) custom-call(f32[27]{0:T(128)S(1)} %concatenate.3.prm.refs_0_.refs_1_, f32[2,4,512,128]{3,2,1,0:T(8,128)S(1)} %get-tuple-element.68.refs_1_, f32[2,2,512,128]{3,2,1,0:T(8,128)S(1)} %get-tuple-element.69.refs_2_, ...), custom_call_target="tpu_custom_call" | custom-call | flops 1000 | bytes 1000 | tf_op jit(solution)/shard_map/step_apart/pallas_call | solution.py:556
  78.3 7.5 %collective-permute-done.10.refs_3_ = f32[2,512,128]{2,1,0:T(8,128)S(1)} collective-permute-done((f32[2,512,128]{2,1,0:T(8,128)S(1)}, f32[2,512,128]{2,1,0:T(8,128)S(1)}, u32[]{:S(2)}, u32[]{:S(2)}) %collective-permute-start.10) | collective-permute-done | bytes 524320 | tf_op jit(solution)/shard_map/ppermute | solution.py:587
  85.8 2.5 %edges.6 = (f32[2,2,512,128]{3,2,1,0:T(8,128)}, f32[2,512,128]{2,1,0:T(8,128)}, f32[2,512,128]{2,1,0:T(8,128)}) custom-call(f32[27]{0:T(128)S(1)} %concatenate.3.prm.refs_0_.refs_1_, f32[2,2,512,128]{3,2,1,0:T(8,128)S(1)} %get-tuple-element.80.refs_1_, f32[2,512,128]{2,1,0:T(8,128)S(1)} %collective-permute-done.9.refs_2_, ...), custom_call_target="tpu_custom_call" | custom-call | flops 1000 | bytes 1000 | tf_op jit(solution)/shard_map/edges/pallas_call | solution.py:556
  90.0 3.6 %collective-permute-start.13 = (f32[2,512,128]{2,1,0:T(8,128)}, f32[2,512,128]{2,1,0:T(8,128)}, u32[]{:S(2)}, u32[]{:S(2)}) collective-permute-start(f32[2,512,128]{2,1,0:T(8,128)} %get-tuple-element.89), channel_id=1, source_target_pairs={{0,1},{1,2},{2,3},{3,4},{4,5},{5,6},{6,7},{8,9},{9,10},{10,11},{11... | collective-permute-start | bytes 1572872 | tf_op jit(solution)/shard_map/ppermute | solution.py:587
  94.7 2.5 %collective-permute-start.14 = (f32[2,512,128]{2,1,0:T(8,128)}, f32[2,512,128]{2,1,0:T(8,128)}, u32[]{:S(2)}, u32[]{:S(2)}) collective-permute-start(f32[2,512,128]{2,1,0:T(8,128)} %get-tuple-element.90), channel_id=1, source_target_pairs={{1,0},{2,1},{3,2},{4,3},{5,4},{6,5},{7,6},{9,8},{10,9},{11,10},{12... | collective-permute-start | bytes 1572872 | tf_op jit(solution)/shard_map/ppermute | solution.py:587
  97.2 7.7 %step_joined.1 = (f32[2,4,512,128]{3,2,1,0:T(8,128)S(1)}, f32[2,2,512,128]{3,2,1,0:T(8,128)S(1)}, f32[2,2,512,128]{3,2,1,0:T(8,128)S(1)}) custom-call(f32[27]{0:T(128)S(1)} %concatenate.3.prm.refs_0_.refs_1_, f32[4,512,128]{2,1,0:T(8,128)} %copy-done.13, f32[4,512,128]{2,1,0:T(8,128)} %get-tuple-element.78.refs_2_, ...), custom_call_target="tpu_custom_call" | custom-call | flops 1000 | bytes 1000 | tf_op jit(solution)/shard_map/step_joined/pallas_call | solution.py:556
  104.9 4.4 %replay.1 = (f32[2,4,512,128]{3,2,1,0:T(8,128)S(1)}, f32[2,2,512,128]{3,2,1,0:T(8,128)S(1)}, f32[2,4,512,128]{3,2,1,0:T(8,128)}) custom-call(s32[1]{0:T(128)} %bitcast.2.refs_0_, f32[27]{0:T(128)S(1)} %concatenate.3.prm.refs_0_.refs_1_, f32[4,512,128]{2,1,0:T(8,128)} %copy-done.14, f32[4,512,128]{2,1,0:T(8,128)} %collective-permute-done.7.refs_3_, ...), custom_call_target="tpu_custom_call" | custom-call | flops 1000 | bytes 1000 | tf_op jit(solution)/shard_map/replay/pallas_call | solution.py:556
  109.3 6.6 %collective-permute-done.13.refs_2_ = f32[2,512,128]{2,1,0:T(8,128)} collective-permute-done((f32[2,512,128]{2,1,0:T(8,128)}, f32[2,512,128]{2,1,0:T(8,128)}, u32[]{:S(2)}, u32[]{:S(2)}) %collective-permute-start.13) | collective-permute-done | bytes 524320 | tf_op jit(solution)/shard_map/ppermute | solution.py:587
  115.9 2.2 %collective-permute-done.14.refs_3_ = f32[2,512,128]{2,1,0:T(8,128)} collective-permute-done((f32[2,512,128]{2,1,0:T(8,128)}, f32[2,512,128]{2,1,0:T(8,128)}, u32[]{:S(2)}, u32[]{:S(2)}) %collective-permute-start.14) | collective-permute-done | bytes 524320 | tf_op jit(solution)/shard_map/ppermute | solution.py:587
  118.1 2.2 %edges.7 = (f32[2,2,512,128]{3,2,1,0:T(8,128)S(1)}, f32[2,512,128]{2,1,0:T(8,128)S(1)}, f32[2,512,128]{2,1,0:T(8,128)S(1)}) custom-call(f32[27]{0:T(128)S(1)} %concatenate.3.prm.refs_0_.refs_1_, f32[2,2,512,128]{3,2,1,0:T(8,128)S(1)} %get-tuple-element.88.refs_1_, f32[2,512,128]{2,1,0:T(8,128)} %collective-permute-done.13.refs_2_, ...), custom_call_target="tpu_custom_call" | custom-call | flops 1000 | bytes 1000 | tf_op jit(solution)/shard_map/edges/pallas_call | solution.py:556
  121.1 2.0 collective-permute-start.12
  124.5 1.8 coarse_rim.1
  127.9 2.0 coarse_edges.1
  136.0 4.2 %coarse_mid.1.refs_0_ = f32[2,4,512,128]{3,2,1,0:T(8,128)} custom-call(s32[1]{0:T(128)} %bitcast.1.refs_0_.own, f32[27]{0:T(128)S(1)} %concatenate.3.prm.refs_0_.refs_1_, f32[2,4,512,128]{3,2,1,0:T(8,128)} %collective-permute-done.12.refs_2_.am, f32[2,2,512,128]{3,2,1,0:T(8,128)} %collective-permute-done.16.refs_3_.an, f32[2,4,512,128]{3,2,1,0:T(8,128)S(1)} %copy-done.1, ...), custom_call_target="tpu_custom_call" | custom-call | flops 1000 | bytes 1000 | tf_op jit(solution)/shard_map/coarse_mid/pallas_call | solution.py:556
  140.2 4.3 %coarse_outer.1 = (f32[2,4,512,128]{3,2,1,0:T(8,128)}, f32[2,4,512,128]{3,2,1,0:T(8,128)}, f32[2,512,128]{2,1,0:T(8,128)}, f32[2,512,128]{2,1,0:T(8,128)}) custom-call(s32[1]{0:T(128)} %bitcast.1.refs_0_.own, f32[27]{0:T(128)S(1)} %concatenate.3.prm.refs_0_.refs_1_, ...), custom_call_target="tpu_custom_call", output_to_operand_aliasing={{0}: (14, {})} | custom-call | flops 1000 | bytes 1000 | tf_op jit(solution)/shard_map/coarse_outer/pallas_call | solution.py:754
  149.8 47.1 %collective-permute-done.24.am.aq = f32[2,4,512,128]{3,2,1,0:T(8,128)} collective-permute-done((f32[2,4,512,128]{3,2,1,0:T(8,128)}, f32[2,4,512,128]{3,2,1,0:T(8,128)}, u32[]{:S(2)}, u32[]{:S(2)}) %collective-permute-start.24) | collective-permute-done | bytes 2097184 | tf_op jit(solution)/shard_map/ppermute | solution.py:587
  196.9 3.0 %collective-permute-done.25.ar = f32[2,4,512,128]{3,2,1,0:T(8,128)} collective-permute-done((f32[2,4,512,128]{3,2,1,0:T(8,128)}, f32[2,4,512,128]{3,2,1,0:T(8,128)}, u32[]{:S(2)}, u32[]{:S(2)}) %collective-permute-start.25) | collective-permute-done | bytes 2097184 | tf_op jit(solution)/shard_map/ppermute | solution.py:587
  199.9 12.0 %last_rows.1 = (f32[1,8,512,128]{3,2,1,0:T(8,128)}, f32[1,8,512,128]{3,2,1,0:T(8,128)}) custom-call(s32[1]{0:T(128)} %bitcast.own, f32[27]{0:T(128)S(1)} %concatenate.3.prm.refs_0_.refs_1_, f32[2,4,512,128]{3,2,1,0:T(8,128)} %collective-permute-done.24.am.aq, f32[2,4,512,128]{3,2,1,0:T(8,128)} %collective-permute-done.24.am.aq, ...), custom_call_target="tpu_custom_call" | custom-call | flops 1000 | bytes 1000 | tf_op jit(solution)/shard_map/last_rows/pallas_call | solution.py:775
  211.9 2.6 %last_edges.1 = (f32[1,8,512,128]{3,2,1,0:T(8,128)}, f32[1,8,512,128]{3,2,1,0:T(8,128)}) custom-call(s32[1]{0:T(128)} %bitcast.own, f32[27]{0:T(128)S(1)} %concatenate.3.prm.refs_0_.refs_1_, f32[2,512,128]{2,1,0:T(8,128)S(1)} %collective-permute-done.22.low, ...), custom_call_target="tpu_custom_call", output_to_operand_aliasing={{0}: (5, {}), {1}: (6, {})} | custom-call | flops 1000 | bytes 1000 | tf_op jit(solution)/shard_map/last_edges/pallas_call | solution.py:602
  (69 shorter events, 29.9 us)
Async XLA Ops:
  3.9 17.8 %collective-permute-start = (f32[2,512,128]{2,1,0:T(8,128)S(1)}, f32[2,512,128]{2,1,0:T(8,128)S(1)}, u32[]{:S(2)}, u32[]{:S(2)}) collective-permute-start(f32[2,512,128]{2,1,0:T(8,128)S(1)} %get-tuple-element.59), channel_id=1, source_target_pairs={{0,1},{1,2},{2,3},{3,4},{4,5},{5,6},{6,7},{16,17},{17,18},{18,19},... | collective-permute-start | bytes 1572872 | tf_op jit(solution)/shard_map/ppermute | solution.py:587
  4.6 17.1 %collective-permute-start.1 = (f32[2,512,128]{2,1,0:T(8,128)S(1)}, f32[2,512,128]{2,1,0:T(8,128)S(1)}, u32[]{:S(2)}, u32[]{:S(2)}) collective-permute-start(f32[2,512,128]{2,1,0:T(8,128)S(1)} %get-tuple-element.60), channel_id=1, source_target_pairs={{1,0},{2,1},{3,2},{4,3},{5,4},{6,5},{7,6},{17,16},{18,17},{19,18},... | collective-permute-start | bytes 1572872 | tf_op jit(solution)/shard_map/ppermute | solution.py:587
  15.4 70.4 %copy-start.8 = (s32[2,512,128]{2,1,0:T(8,128)}, s32[2,512,128]{2,1,0:T(8,128)S(1)}, u32[]{:S(2)}) copy-start(s32[2,512,128]{2,1,0:T(8,128)S(1)} %get-tuple-element.65.refs_6_.refs_4_.refs_5_.ide) | copy-start | bytes 1572868
  15.4 15.7 %collective-permute-start.2 = (f32[2,512,128]{2,1,0:T(8,128)S(1)}, f32[2,512,128]{2,1,0:T(8,128)S(1)}, u32[]{:S(2)}, u32[]{:S(2)}) collective-permute-start(f32[2,512,128]{2,1,0:T(8,128)S(1)} %get-tuple-element.63), channel_id=1, source_target_pairs={{8,9},{9,10},{10,11},{11,12},{12,13},{13,14},{14,15},{24,25},{25,2... | collective-permute-start | bytes 1572872 | tf_op jit(solution)/shard_map/ppermute | solution.py:587
  18.6 14.1 %collective-permute-start.3 = (f32[2,512,128]{2,1,0:T(8,128)S(1)}, f32[2,512,128]{2,1,0:T(8,128)S(1)}, u32[]{:S(2)}, u32[]{:S(2)}) collective-permute-start(f32[2,512,128]{2,1,0:T(8,128)S(1)} %get-tuple-element.64), channel_id=1, source_target_pairs={{9,8},{10,9},{11,10},{12,11},{13,12},{14,13},{15,14},{25,24},{26,2... | collective-permute-start | bytes 1572872 | tf_op jit(solution)/shard_map/ppermute | solution.py:587
  34.1 20.8 %collective-permute-start.4 = (f32[2,512,128]{2,1,0:T(8,128)S(1)}, f32[2,512,128]{2,1,0:T(8,128)S(1)}, u32[]{:S(2)}, u32[]{:S(2)}) collective-permute-start(f32[2,512,128]{2,1,0:T(8,128)S(1)} %get-tuple-element.71), channel_id=1, source_target_pairs={{0,1},{1,2},{2,3},{3,4},{4,5},{5,6},{6,7},{8,9},{9,10},{10,11},{11... | collective-permute-start | bytes 1572872 | tf_op jit(solution)/shard_map/ppermute | solution.py:587
  36.3 21.8 %collective-permute-start.5 = (f32[2,512,128]{2,1,0:T(8,128)S(1)}, f32[2,512,128]{2,1,0:T(8,128)S(1)}, u32[]{:S(2)}, u32[]{:S(2)}) collective-permute-start(f32[2,512,128]{2,1,0:T(8,128)S(1)} %get-tuple-element.72), channel_id=1, source_target_pairs={{1,0},{2,1},{3,2},{4,3},{5,4},{6,5},{7,6},{9,8},{10,9},{11,10},{12... | collective-permute-start | bytes 1572872 | tf_op jit(solution)/shard_map/ppermute | solution.py:587
  44.0 41.8 %copy-start = (f32[2,4,512,128]{3,2,1,0:T(8,128)}, f32[2,4,512,128]{3,2,1,0:T(8,128)S(1)}, u32[]{:S(2)}) copy-start(f32[2,4,512,128]{3,2,1,0:T(8,128)S(1)} %get-tuple-element.73.refs_5_.refs_7_.refs_4_.km) | copy-start | bytes 6291460
  44.0 41.8 %copy-start.3 = (f32[2,2,512,128]{3,2,1,0:T(8,128)}, f32[2,2,512,128]{3,2,1,0:T(8,128)S(1)}, u32[]{:S(2)}) copy-start(f32[2,2,512,128]{3,2,1,0:T(8,128)S(1)} %get-tuple-element.75.refs_7_.refs_6_.kx) | copy-start | bytes 3145732
  44.0 96.2 %copy-start.2 = (f32[2,2,512,128]{3,2,1,0:T(8,128)}, f32[2,2,512,128]{3,2,1,0:T(8,128)S(1)}, u32[]{:S(2)}) copy-start(f32[2,2,512,128]{3,2,1,0:T(8,128)S(1)} %get-tuple-element.74.refs_6_.refs_5_.kn) | copy-start | bytes 3145732
  59.5 26.2 %collective-permute-start.10 = (f32[2,512,128]{2,1,0:T(8,128)S(1)}, f32[2,512,128]{2,1,0:T(8,128)S(1)}, u32[]{:S(2)}, u32[]{:S(2)}) collective-permute-start(f32[2,512,128]{2,1,0:T(8,128)S(1)} %get-tuple-element.82), channel_id=1, source_target_pairs={{1,0},{2,1},{3,2},{4,3},{5,4},{6,5},{7,6},{9,8},{10,9},{11,10},{12... | collective-permute-start | bytes 1572872 | tf_op jit(solution)/shard_map/ppermute | solution.py:587
  61.5 24.3 %collective-permute-start.9 = (f32[2,512,128]{2,1,0:T(8,128)S(1)}, f32[2,512,128]{2,1,0:T(8,128)S(1)}, u32[]{:S(2)}, u32[]{:S(2)}) collective-permute-start(f32[2,512,128]{2,1,0:T(8,128)S(1)} %get-tuple-element.81), channel_id=1, source_target_pairs={{0,1},{1,2},{2,3},{3,4},{4,5},{5,6},{6,7},{8,9},{9,10},{10,11},{11... | collective-permute-start | bytes 1572872 | tf_op jit(solution)/shard_map/ppermute | solution.py:587
  74.3 14.1 %copy-start.13 = (f32[4,512,128]{2,1,0:T(8,128)}, f32[4,512,128]{2,1,0:T(8,128)S(1)}, u32[]{:S(2)}) copy-start(f32[4,512,128]{2,1,0:T(8,128)S(1)} %get-tuple-element.77.refs_1_) | copy-start | bytes 3145732
  74.3 19.3 %collective-permute-start.6 = (f32[4,512,128]{2,1,0:T(8,128)S(1)}, f32[4,512,128]{2,1,0:T(8,128)S(1)}, u32[]{:S(2)}, u32[]{:S(2)}) collective-permute-start(f32[4,512,128]{2,1,0:T(8,128)S(1)} %get-tuple-element.77.refs_1_), channel_id=1, source_target_pairs={{0,8},{1,9},{2,10},{3,11},{4,12},{5,13},{6,14},{7,15}} | collective-permute-start | bytes 3145736 | tf_op jit(solution)/shard_map/ppermute | solution.py:587
  75.0 29.9 %collective-permute-start.7 = (f32[4,512,128]{2,1,0:T(8,128)}, f32[4,512,128]{2,1,0:T(8,128)}, u32[]{:S(2)}, u32[]{:S(2)}) collective-permute-start(f32[4,512,128]{2,1,0:T(8,128)} %get-tuple-element.78.refs_2_), channel_id=1, source_target_pairs={{0,8},{1,9},{2,10},{3,11},{4,12},{5,13},{6,14},{7,15}} | collective-permute-start | bytes 3145736 | tf_op jit(solution)/shard_map/ppermute | solution.py:587
  76.6 28.3 %collective-permute-start.8 = (f32[2,2,512,128]{3,2,1,0:T(8,128)}, f32[2,2,512,128]{3,2,1,0:T(8,128)}, u32[]{:S(2)}, u32[]{:S(2)}) collective-permute-start(f32[2,2,512,128]{3,2,1,0:T(8,128)} %get-tuple-element.79.refs_3_), channel_id=1, source_target_pairs={{0,8},{1,9},{2,10},{3,11},{4,12},{5,13},{6,14},{7,15}} | collective-permute-start | bytes 3145736 | tf_op jit(solution)/shard_map/ppermute | solution.py:587
  88.3 16.6 %collective-permute-start.11 = (f32[2,2,512,128]{3,2,1,0:T(8,128)}, f32[2,2,512,128]{3,2,1,0:T(8,128)}, u32[]{:S(2)}, u32[]{:S(2)}) collective-permute-start(f32[2,2,512,128]{3,2,1,0:T(8,128)} %get-tuple-element.83.refs_4_), channel_id=1, source_target_pairs={{0,8},{1,9},{2,10},{3,11},{4,12},{5,13},{6,14},{7,15}} | collective-permute-start | bytes 3145736 | tf_op jit(solution)/shard_map/ppermute | solution.py:587
  90.0 26.0 %collective-permute-start.13 = (f32[2,512,128]{2,1,0:T(8,128)}, f32[2,512,128]{2,1,0:T(8,128)}, u32[]{:S(2)}, u32[]{:S(2)}) collective-permute-start(f32[2,512,128]{2,1,0:T(8,128)} %get-tuple-element.89), channel_id=1, source_target_pairs={{0,1},{1,2},{2,3},{3,4},{4,5},{5,6},{6,7},{8,9},{9,10},{10,11},{11... | collective-permute-start | bytes 1572872 | tf_op jit(solution)/shard_map/ppermute | solution.py:587
  94.7 23.5 %collective-permute-start.14 = (f32[2,512,128]{2,1,0:T(8,128)}, f32[2,512,128]{2,1,0:T(8,128)}, u32[]{:S(2)}, u32[]{:S(2)}) collective-permute-start(f32[2,512,128]{2,1,0:T(8,128)} %get-tuple-element.90), channel_id=1, source_target_pairs={{1,0},{2,1},{3,2},{4,3},{5,4},{6,5},{7,6},{9,8},{10,9},{11,10},{12... | collective-permute-start | bytes 1572872 | tf_op jit(solution)/shard_map/ppermute | solution.py:587
  104.9 13.2 %copy-start.9 = (s32[2,512,128]{2,1,0:T(8,128)S(1)}, s32[2,512,128]{2,1,0:T(8,128)}, u32[]{:S(2)}) copy-start(s32[2,512,128]{2,1,0:T(8,128)} %copy-done.8) | copy-start | bytes 1572868
  120.3 4.2 %collective-permute-start.15 = (f32[2,2,512,128]{3,2,1,0:T(8,128)S(1)}, f32[2,2,512,128]{3,2,1,0:T(8,128)S(1)}, u32[]{:S(2)}, u32[]{:S(2)}) collective-permute-start(f32[2,2,512,128]{3,2,1,0:T(8,128)S(1)} %get-tuple-element.91.refs_9_.refs_6_), channel_id=1, source_target_pairs={{0,8},{1,9},{2,10},{3,11},{4,12},{5,13},{6,14},{7,15}} | collective-permute-start | bytes 3145736 | tf_op jit(solution)/shard_map/ppermute | solution.py:587
  121.1 13.3 %collective-permute-start.12 = (f32[2,4,512,128]{3,2,1,0:T(8,128)}, f32[2,4,512,128]{3,2,1,0:T(8,128)}, u32[]{:S(2)}, u32[]{:S(2)}) collective-permute-start(f32[2,4,512,128]{3,2,1,0:T(8,128)} %get-tuple-element.85.refs_5_.refs_6_), channel_id=1, source_target_pairs={{8,16},{9,17},{10,18},{11,19},{12,20},{13,21},{14,22},{15,23}} | collective-permute-start | bytes 6291464 | tf_op jit(solution)/shard_map/ppermute | solution.py:587
  123.1 4.8 %collective-permute-start.17 = (f32[2,512,128]{2,1,0:T(8,128)S(1)}, f32[2,512,128]{2,1,0:T(8,128)S(1)}, u32[]{:S(2)}, u32[]{:S(2)}) collective-permute-start(f32[2,512,128]{2,1,0:T(8,128)S(1)} %get-tuple-element.95), channel_id=1, source_target_pairs={{0,9},{1,10},{2,11},{3,12},{4,13},{5,14},{6,15}} | collective-permute-start | bytes 1572872 | tf_op jit(solution)/shard_map/ppermute | solution.py:587
  123.8 4.1 %collective-permute-start.18 = (f32[2,512,128]{2,1,0:T(8,128)S(1)}, f32[2,512,128]{2,1,0:T(8,128)S(1)}, u32[]{:S(2)}, u32[]{:S(2)}) collective-permute-start(f32[2,512,128]{2,1,0:T(8,128)S(1)} %get-tuple-element.96), channel_id=1, source_target_pairs={{1,8},{2,9},{3,10},{4,11},{5,12},{6,13},{7,14}} | collective-permute-start | bytes 1572872 | tf_op jit(solution)/shard_map/ppermute | solution.py:587
  126.3 8.1 %collective-permute-start.16 = (f32[2,2,512,128]{3,2,1,0:T(8,128)}, f32[2,2,512,128]{3,2,1,0:T(8,128)}, u32[]{:S(2)}, u32[]{:S(2)}) collective-permute-start(f32[2,2,512,128]{3,2,1,0:T(8,128)} %get-tuple-element.93.on), channel_id=1, source_target_pairs={{8,16},{9,17},{10,18},{11,19},{12,20},{13,21},{14,22},{15,23}} | collective-permute-start | bytes 3145736 | tf_op jit(solution)/shard_map/ppermute | solution.py:587
  129.9 10.3 %collective-permute-start.19 = (f32[2,2,512,128]{3,2,1,0:T(8,128)}, f32[2,2,512,128]{3,2,1,0:T(8,128)}, u32[]{:S(2)}, u32[]{:S(2)}) collective-permute-start(f32[2,2,512,128]{3,2,1,0:T(8,128)} %get-tuple-element.97.ox), channel_id=1, source_target_pairs={{8,16},{9,17},{10,18},{11,19},{12,20},{13,21},{14,22},{15,23}} | collective-permute-start | bytes 3145736 | tf_op jit(solution)/shard_map/ppermute | solution.py:587
  131.5 8.7 %collective-permute-start.20 = (f32[2,512,128]{2,1,0:T(8,128)}, f32[2,512,128]{2,1,0:T(8,128)}, u32[]{:S(2)}, u32[]{:S(2)}) collective-permute-start(f32[2,512,128]{2,1,0:T(8,128)} %get-tuple-element.98), channel_id=1, source_target_pairs={{8,17},{9,18},{10,19},{11,20},{12,21},{13,22},{14,23}} | collective-permute-start | bytes 1572872 | tf_op jit(solution)/shard_map/ppermute | solution.py:587
  133.0 7.2 %collective-permute-start.21 = (f32[2,512,128]{2,1,0:T(8,128)}, f32[2,512,128]{2,1,0:T(8,128)}, u32[]{:S(2)}, u32[]{:S(2)}) collective-permute-start(f32[2,512,128]{2,1,0:T(8,128)} %get-tuple-element.99), channel_id=1, source_target_pairs={{9,16},{10,17},{11,18},{12,19},{13,20},{14,21},{15,22}} | collective-permute-start | bytes 1572872 | tf_op jit(solution)/shard_map/ppermute | solution.py:587
  144.5 52.3 %collective-permute-start.24 = (f32[2,4,512,128]{3,2,1,0:T(8,128)}, f32[2,4,512,128]{3,2,1,0:T(8,128)}, u32[]{:S(2)}, u32[]{:S(2)}) collective-permute-start(f32[2,4,512,128]{3,2,1,0:T(8,128)} %get-tuple-element.102.om), channel_id=1, source_target_pairs={{16,24},{17,25},{18,26},{19,27},{20,28},{21,29},{22,30},{23,31}} | collective-permute-start | bytes 6291464 | tf_op jit(solution)/shard_map/ppermute | solution.py:587
  145.8 54.0 %collective-permute-start.25 = (f32[2,4,512,128]{3,2,1,0:T(8,128)}, f32[2,4,512,128]{3,2,1,0:T(8,128)}, u32[]{:S(2)}, u32[]{:S(2)}) collective-permute-start(f32[2,4,512,128]{3,2,1,0:T(8,128)} %get-tuple-element.103.rim), channel_id=1, source_target_pairs={{16,24},{17,25},{18,26},{19,27},{20,28},{21,29},{22,30},{23,31}} | collective-permute-start | bytes 6291464 | tf_op jit(solution)/shard_map/ppermute | solution.py:587
  147.1 64.7 %collective-permute-start.22 = (f32[2,512,128]{2,1,0:T(8,128)}, f32[2,512,128]{2,1,0:T(8,128)S(1)}, u32[]{:S(2)}, u32[]{:S(2)}) collective-permute-start(f32[2,512,128]{2,1,0:T(8,128)} %get-tuple-element.100), channel_id=1, source_target_pairs={{16,25},{17,26},{18,27},{19,28},{20,29},{21,30},{22,31}} | collective-permute-start | bytes 1572872 | tf_op jit(solution)/shard_map/ppermute | solution.py:587
  148.4 63.4 %collective-permute-start.23 = (f32[2,512,128]{2,1,0:T(8,128)}, f32[2,512,128]{2,1,0:T(8,128)S(1)}, u32[]{:S(2)}, u32[]{:S(2)}) collective-permute-start(f32[2,512,128]{2,1,0:T(8,128)} %get-tuple-element.101), channel_id=1, source_target_pairs={{17,24},{18,25},{19,26},{20,27},{21,28},{22,29},{23,30}} | collective-permute-start | bytes 1572872 | tf_op jit(solution)/shard_map/ppermute | solution.py:587
  (9 other events, 38.2 us)

commit v6 on v5

--- a/solution.py
+++ b/solution.py
@@ -299,6 +299,12 @@
     edges_body(prm, "fine", part, low, high, ide, edge, tl0, tl7)
 
 
+def edges_apart_kernel(prm, part, low, high, ide, edge, tl0, tl7, eh, ec):
+    edges_body(prm, "fine", part, low, high, ide, edge, tl0, tl7)
+    eh[...] = edge[0]
+    ec[...] = edge[1]
+
+
 def edges_kernel_of_two(prm, part, low, high, low2, high2, ide, edge, tl0, tl7):
     edges_body(prm, "fine", part, Sum(low, low2), Sum(high, high2), ide, edge, tl0, tl7)
 
@@ -375,7 +381,9 @@
         nm[...] = om[...]
 
 
-def coarse_rim_kernel(own, prm, am, an, ax, kn, kx, ids, on, ox, nn, part, pad):
+def coarse_rim_kernel(own, prm, am, an, xh, xc, kn, kx, ids, on, ox, nn, part, pad):
+    ax = Fields(xh, xc)
+
     @pl.when(own[0] != 0)
     def _():
         coarse_body(
@@ -541,6 +549,15 @@
 
 
 TINY = pl.CostEstimate(flops=1000, bytes_accessed=1000, transcendentals=0)
+
+
+def tiled(kernel, tile):
+    def run(*refs):
+        TILE.append(tile)
+        kernel(*refs)
+        TILE.pop()
+
+    return run
 
 
 def call(kernel, outs, args, smem, name, scratch=(), limit=8, after=(), through=(), flops=1000, tile=256):
@@ -705,13 +722,20 @@
         tile=512,
     )
     vn = sn
-    vx, tl0, tl7 = fine_edges(part, sides, (vm,))
+    vx, tl0, tl7, *apart = call(
+        edges_apart_kernel,
+        [pair, halo, halo, halo, halo],
+        (prm, part, *sides, ide),
+        1,
+        "edges_apart",
+        after=(vm,),
+    )
     low, high = halos(tl0, tl7, (0,), 1)
-    ax = send(vx, 1)
+    ax = [send(x, 1) for x in apart]
     vn, part = call(
         coarse_rim_kernel,
         [pair, pair],
-        (own(1), prm, am, an, ax, kn, kx, ids, vn, vx),
+        (own(1), prm, am, an, *ax, kn, kx, ids, vn, vx),
         2,
         "coarse_rim",
         pad,
@@ -735,11 +759,10 @@
     rim = None
     for n in range(2, slices):
         low, high = halos(tl0, tl7, (n - 1,), 1)
-        am = send(vm, n)
         if n == 2:
-            an, ax = send(vn, n), send(vx, n)
+            am, an, ax = send(vm, n), send(vn, n), send(vx, n)
         else:
-            ar = send(rim, n)
+            am, ar = am3, send(rim, n)
         if n == slices - 1:
             break
         vm = call(
@@ -751,20 +774,24 @@
             pad,
             18,
         )[0]
-        vm, rim, tl0, tl7 = pl.pallas_call(
-            coarse_outer_kernel,
+        vm = hbm(vm)
+        am3 = hbm(send(vm, n + 1))
+        low, high = call(
+            nothing_kernel, [], (), 0, "arrived", through=(low, high), flops=10**11
+        )
+        rim, tl0, tl7 = pl.pallas_call(
+            tiled(coarse_outer_kernel, 512),
             grid=(2,),
-            out_shape=[tall, f32(2, 4, ny, nz), halo, halo],
+            out_shape=[f32(2, 4, ny, nz), halo, halo],
             in_specs=[SMEM, SMEM, inside, side, side, whole, whole]
             + [side] * 4
             + [id_row(2), id_row(1), id_row(0), ANY],
-            out_specs=[ANY, two, whole, whole],
+            out_specs=[two, whole, whole],
             scratch_shapes=[pltpu.VMEM((2, 5, ny + 16, nz), jnp.float32)],
-            input_output_aliases={14: 0},
             compiler_params=pltpu.CompilerParams(vmem_limit_bytes=26 * MIB),
             cost_estimate=TINY,
             name="coarse_outer",
-        )(own(n), prm, am, an, ax, low, high, kn, kx, vn, vx, ids, ids, ids, vm)
+        )(own(n), prm, am, an, ax, low, high, hbm(kn), hbm(kx), hbm(vn), hbm(vx), ids, ids, ids, am3)
 
     out = f32(1, rows, ny, nz)
     last_own = own(slices - 1)
@@ -773,7 +800,7 @@
     id_half = pl.BlockSpec((rows // 2, ny, nz), lambda i: (i, 0, 0))
     id_beyond = pl.BlockSpec((1, ny, nz), lambda i: (rows // 2 - i, 0, 0))
     oh, oc = pl.pallas_call(
-        last_rows_kernel,
+        tiled(last_rows_kernel, 512),
         grid=(2,),
         out_shape=[out, out],
         in_specs=[SMEM, SMEM, half, beyond, two, half, side, side, id_half, id_beyond, half, two],
@@ -782,7 +809,7 @@
         compiler_params=pltpu.CompilerParams(vmem_limit_bytes=30 * MIB),
         cost_estimate=TINY,
         name="last_rows",
-    )(last_own, prm, am, am, ar, hbm(km), hbm(kn), hbm(kx), ids, ids, vm, rim)
+    )(last_own, prm, am, am, ar, hbm(km), hbm(kn), hbm(kx), ids, ids, hbm(vm), rim)
     out_row = pl.BlockSpec((1, 1, ny, nz), lambda i: (0, (rows - 1) * i, 0, 0))
     one = pl.BlockSpec((1, ny, nz), lambda i: (i, 0, 0))
     return tuple(

time: 215 us -> 207 us (0.963)
  waiting for transfers between devices: 83.4 us -> 76.3 us
  Pallas kernels: 78.2 us -> 75.4 us
  local copies, waits for them, and re-layouts: 5.1 us -> 7.45 us
    ppermute x26 -> x27, waiting for transfers between devices: 83.4 us -> 76.3 us  [move(): return lax.ppermute(x, ('tm', 'space'), pairs)]
    pallas_call x14 -> x15, Pallas kernels: 57 us -> 54.4 us  [call(): pl.pallas_call(run, out_shape=[f32(*x.shape) for x in through] + list(out...]
    unnamed x30 -> x34, local copies, waits for them, and re-layouts: 4.27 us -> 6.63 us
    ppermute x26 -> x27, starting transfers between devices: 46.7 us -> 45.9 us  [move(): return lax.ppermute(x, ('tm', 'space'), pairs)]
  transfers between devices with their start and end apart: 26 -> 27, of which waited for: 9 -> 9; matrix products, arithmetic and copies ran while one was open for 0% -> 0% of each run, Pallas kernels for 30% -> 31%
where the time goes in v6:
time: 207 us; the launch traced here: 206 us
  waiting for transfers between devices  76.3 us (37%)
  Pallas kernels  75.4 us (36%)
  starting transfers between devices  45.9 us (22%)
  local copies, waits for them, and re-layouts  7.45 us (4%)
    ppermute x27, waiting for transfers between devices, move(): return lax.ppermute(x, ('tm', 'space'), pairs)  76.3 us
    pallas_call x15, Pallas kernels, call(): pl.pallas_call(run, out_shape=[f32(*x.shape) for x in through] + list(out...  54.4 us
    ppermute x27, starting transfers between devices, move(): return lax.ppermute(x, ('tm', 'space'), pairs)  45.9 us
    pallas_call x1, Pallas kernels, per_device(): pl.pallas_call(tiled(last_rows_kernel, 512), grid=(2,), out_shape=[out, o...  11.8 us
    unnamed x34, local copies, waits for them, and re-layouts  6.63 us
    pallas_call x2, Pallas kernels, gridded(): pl.pallas_call(kernel, grid=(steps,), out_shape=outs, in_specs=in_specs,...  4.92 us
    pallas_call x1, Pallas kernels, per_device(): pl.pallas_call(tiled(coarse_outer_kernel, 512), grid=(2,), out_shape=[f32...  4.26 us
  transfers between devices with their start and end apart: 27, of which 9 were waited for; matrix products, arithmetic and copies ran while one was open for 0% of the time, Pallas kernels for 31%

profile of v6, /device:TPU:11, one launch (start us, length us, event | category | flops | bytes accessed | tf_op | source)
XLA Modules:
  0.0 206.1 jit_solution(7763680814139130378)
XLA Ops:
  1.5 2.4 %first_edges.1 = (f32[2,512,128]{2,1,0:T(8,128)S(1)}, f32[2,512,128]{2,1,0:T(8,128)S(1)}, f32[2,512,128]{2,1,0:T(8,128)S(1)}, f32[2,512,128]{2,1,0:T(8,128)S(1)}) custom-call(f32[27]{0:T(128)S(1)} %concatenate.3.prm.refs_0_.refs_1_, f32[8,512,128]{2,1,0:T(8,128)} %bitcast.5, f32[8,512,128]{2,1,0:T(8,128)} %bitcast.8, s32[8,512,128]{2,1,0:T(8,128)} %refs_3_.1), custom_call_target="tpu_custom_call" | custom-call | flops 1000 | bytes 1000 | tf_op jit(solution)/shard_map/first_edges/pallas_call | solution.py:619
  6.9 8.4 %first_step.1 = (f32[2,512,128]{2,1,0:T(8,128)S(1)}, f32[2,512,128]{2,1,0:T(8,128)S(1)}, f32[2,4,512,128]{3,2,1,0:T(8,128)S(1)}, f32[2,2,512,128]{3,2,1,0:T(8,12...) custom-call(f32[27]{0:T(128)S(1)} %concatenate.3.prm.refs_0_.refs_1_, ...), custom_call_target="tpu_custom_call", output_to_operand_aliasing={{0}: (5, {}), {1}: (6, {})} | custom-call | flops 1000 | bytes 1000 | tf_op jit(solution)/shard_map/first_step/pallas_call | solution.py:573
  15.3 3.1 %collective-permute-start.2 = (f32[2,512,128]{2,1,0:T(8,128)S(1)}, f32[2,512,128]{2,1,0:T(8,128)S(1)}, u32[]{:S(2)}, u32[]{:S(2)}) collective-permute-start(f32[2,512,128]{2,1,0:T(8,128)S(1)} %get-tuple-element.66), channel_id=1, source_target_pairs={{8,9},{9,10},{10,11},{11,12},{12,13},{13,14},{14,15},{24,25},{25,2... | collective-permute-start | bytes 1572872 | tf_op jit(solution)/shard_map/ppermute | solution.py:604
  18.4 3.0 %collective-permute-start.3 = (f32[2,512,128]{2,1,0:T(8,128)S(1)}, f32[2,512,128]{2,1,0:T(8,128)S(1)}, u32[]{:S(2)}, u32[]{:S(2)}) collective-permute-start(f32[2,512,128]{2,1,0:T(8,128)S(1)} %get-tuple-element.67), channel_id=1, source_target_pairs={{9,8},{10,9},{11,10},{12,11},{13,12},{14,13},{15,14},{25,24},{26,2... | collective-permute-start | bytes 1572872 | tf_op jit(solution)/shard_map/ppermute | solution.py:604
  21.5 9.6 %collective-permute-done.2.refs_4_ = f32[2,512,128]{2,1,0:T(8,128)S(1)} collective-permute-done((f32[2,512,128]{2,1,0:T(8,128)S(1)}, f32[2,512,128]{2,1,0:T(8,128)S(1)}, u32[]{:S(2)}, u32[]{:S(2)}) %collective-permute-start.2) | collective-permute-done | bytes 524320 | tf_op jit(solution)/shard_map/ppermute | solution.py:604
  34.1 2.3 %collective-permute-start.4 = (f32[2,512,128]{2,1,0:T(8,128)S(1)}, f32[2,512,128]{2,1,0:T(8,128)S(1)}, u32[]{:S(2)}, u32[]{:S(2)}) collective-permute-start(f32[2,512,128]{2,1,0:T(8,128)S(1)} %get-tuple-element.74), channel_id=1, source_target_pairs={{0,1},{1,2},{2,3},{3,4},{4,5},{5,6},{6,7},{8,9},{9,10},{10,11},{11... | collective-permute-start | bytes 1572872 | tf_op jit(solution)/shard_map/ppermute | solution.py:604
  36.4 4.5 %collective-permute-start.5 = (f32[2,512,128]{2,1,0:T(8,128)S(1)}, f32[2,512,128]{2,1,0:T(8,128)S(1)}, u32[]{:S(2)}, u32[]{:S(2)}) collective-permute-start(f32[2,512,128]{2,1,0:T(8,128)S(1)} %get-tuple-element.75), channel_id=1, source_target_pairs={{1,0},{2,1},{3,2},{4,3},{5,4},{6,5},{7,6},{9,8},{10,9},{11,10},{12... | collective-permute-start | bytes 1572872 | tf_op jit(solution)/shard_map/ppermute | solution.py:604
  40.8 3.3 %base.1 = (f32[2,4,512,128]{3,2,1,0:T(8,128)S(1)}, f32[2,2,512,128]{3,2,1,0:T(8,128)S(1)}, f32[2,2,512,128]{3,2,1,0:T(8,128)S(1)}) custom-call(f32[27]{0:T(128)S(1)} %concatenate.3.prm.refs_0_.refs_1_, f32[8,512,128]{2,1,0:T(8,128)S(1)} %bitcast.7, f32[8,512,128]{2,1,0:T(8,128)S(1)} %bitcast.10, f32[2,4,512,128]{3,2,1,0:T(8,128)S(1)} %get-tuple-element.59.refs_1_.refs_3_, ...), custom_call_target="tpu_custom_call" | custom-call | flops 1000 | bytes 1000 | tf_op jit(solution)/shard_map/base/pallas_call | solution.py:573
  44.2 8.1 %step.1 = (f32[2,4,512,128]{3,2,1,0:T(8,128)S(1)}, f32[2,2,512,128]{3,2,1,0:T(8,128)S(1)}, f32[2,2,512,128]{3,2,1,0:T(8,128)S(1)}) custom-call(f32[27]{0:T(128)S(1)} %concatenate.3.prm.refs_0_.refs_1_, f32[2,4,512,128]{3,2,1,0:T(8,128)S(1)} %get-tuple-element.59.refs_1_.refs_3_, f32[2,2,512,128]{3,2,1,0:T(8,128)S(1)} %get-tuple-element.60.refs_2_.refs_4_, ...), custom_call_target="tpu_custom_call" | custom-call | flops 1000 | bytes 1000 | tf_op jit(solution)/shard_map/step/pallas_call | solution.py:573
  52.3 2.8 %collective-permute-done.4.refs_2_ = f32[2,512,128]{2,1,0:T(8,128)S(1)} collective-permute-done((f32[2,512,128]{2,1,0:T(8,128)S(1)}, f32[2,512,128]{2,1,0:T(8,128)S(1)}, u32[]{:S(2)}, u32[]{:S(2)}) %collective-permute-start.4) | collective-permute-done | bytes 524320 | tf_op jit(solution)/shard_map/ppermute | solution.py:604
  55.0 3.3 %collective-permute-done.5.refs_3_ = f32[2,512,128]{2,1,0:T(8,128)S(1)} collective-permute-done((f32[2,512,128]{2,1,0:T(8,128)S(1)}, f32[2,512,128]{2,1,0:T(8,128)S(1)}, u32[]{:S(2)}, u32[]{:S(2)}) %collective-permute-start.5) | collective-permute-done | bytes 524320 | tf_op jit(solution)/shard_map/ppermute | solution.py:604
  59.7 1.9 collective-permute-start.10
  61.6 3.4 %collective-permute-start.9 = (f32[2,512,128]{2,1,0:T(8,128)S(1)}, f32[2,512,128]{2,1,0:T(8,128)S(1)}, u32[]{:S(2)}, u32[]{:S(2)}) collective-permute-start(f32[2,512,128]{2,1,0:T(8,128)S(1)} %get-tuple-element.84), channel_id=1, source_target_pairs={{0,1},{1,2},{2,3},{3,4},{4,5},{5,6},{6,7},{8,9},{9,10},{10,11},{11... | collective-permute-start | bytes 1572872 | tf_op jit(solution)/shard_map/ppermute | solution.py:604
  65.0 9.3 %step_apart.1 = (f32[4,512,128]{2,1,0:T(8,128)S(1)}, f32[4,512,128]{2,1,0:T(8,128)}, f32[2,2,512,128]{3,2,1,0:T(8,128)}, f32[2,2,512,128]{3,2,1,0:T(8,128)S(1)}) custom-call(f32[27]{0:T(128)S(1)} %concatenate.3.prm.refs_0_.refs_1_, f32[2,4,512,128]{3,2,1,0:T(8,128)S(1)} %get-tuple-element.71.refs_1_, f32[2,2,512,128]{3,2,1,0:T(8,128)S(1)} %get-tuple-element.72.refs_2_, ...), custom_call_target="tpu_custom_call" | custom-call | flops 1000 | bytes 1000 | tf_op jit(solution)/shard_map/step_apart/pallas_call | solution.py:573
  75.0 1.6 collective-permute-start.7
  78.3 7.6 %collective-permute-done.10.refs_3_ = f32[2,512,128]{2,1,0:T(8,128)S(1)} collective-permute-done((f32[2,512,128]{2,1,0:T(8,128)S(1)}, f32[2,512,128]{2,1,0:T(8,128)S(1)}, u32[]{:S(2)}, u32[]{:S(2)}) %collective-permute-start.10) | collective-permute-done | bytes 524320 | tf_op jit(solution)/shard_map/ppermute | solution.py:604
  86.0 2.6 %edges.5 = (f32[2,2,512,128]{3,2,1,0:T(8,128)}, f32[2,512,128]{2,1,0:T(8,128)}, f32[2,512,128]{2,1,0:T(8,128)}) custom-call(f32[27]{0:T(128)S(1)} %concatenate.3.prm.refs_0_.refs_1_, f32[2,2,512,128]{3,2,1,0:T(8,128)S(1)} %get-tuple-element.83.refs_1_, f32[2,512,128]{2,1,0:T(8,128)S(1)} %collective-permute-done.9.refs_2_, ...), custom_call_target="tpu_custom_call" | custom-call | flops 1000 | bytes 1000 | tf_op jit(solution)/shard_map/edges/pallas_call | solution.py:573
  88.5 1.6 collective-permute-start.11
  90.2 3.6 %collective-permute-start.13 = (f32[2,512,128]{2,1,0:T(8,128)}, f32[2,512,128]{2,1,0:T(8,128)}, u32[]{:S(2)}, u32[]{:S(2)}) collective-permute-start(f32[2,512,128]{2,1,0:T(8,128)} %get-tuple-element.92), channel_id=1, source_target_pairs={{0,1},{1,2},{2,3},{3,4},{4,5},{5,6},{6,7},{8,9},{9,10},{10,11},{11... | collective-permute-start | bytes 1572872 | tf_op jit(solution)/shard_map/ppermute | solution.py:604
  94.9 2.5 %collective-permute-start.14 = (f32[2,512,128]{2,1,0:T(8,128)}, f32[2,512,128]{2,1,0:T(8,128)}, u32[]{:S(2)}, u32[]{:S(2)}) collective-permute-start(f32[2,512,128]{2,1,0:T(8,128)} %get-tuple-element.93), channel_id=1, source_target_pairs={{1,0},{2,1},{3,2},{4,3},{5,4},{6,5},{7,6},{9,8},{10,9},{11,10},{12... | collective-permute-start | bytes 1572872 | tf_op jit(solution)/shard_map/ppermute | solution.py:604
  97.4 7.7 %step_joined.1 = (f32[2,4,512,128]{3,2,1,0:T(8,128)S(1)}, f32[2,2,512,128]{3,2,1,0:T(8,128)S(1)}, f32[2,2,512,128]{3,2,1,0:T(8,128)S(1)}) custom-call(f32[27]{0:T(128)S(1)} %concatenate.3.prm.refs_0_.refs_1_, f32[4,512,128]{2,1,0:T(8,128)} %copy-done.13, f32[4,512,128]{2,1,0:T(8,128)} %get-tuple-element.81.refs_2_, ...), custom_call_target="tpu_custom_call" | custom-call | flops 1000 | bytes 1000 | tf_op jit(solution)/shard_map/step_joined/pallas_call | solution.py:573
  105.2 4.4 %replay.1 = (f32[2,4,512,128]{3,2,1,0:T(8,128)S(1)}, f32[2,2,512,128]{3,2,1,0:T(8,128)S(1)}, f32[2,4,512,128]{3,2,1,0:T(8,128)}) custom-call(s32[1]{0:T(128)} %bitcast.2.refs_0_, f32[27]{0:T(128)S(1)} %concatenate.3.prm.refs_0_.refs_1_, f32[4,512,128]{2,1,0:T(8,128)} %copy-done.16, f32[4,512,128]{2,1,0:T(8,128)} %collective-permute-done.7.refs_3_, ...), custom_call_target="tpu_custom_call" | custom-call | flops 1000 | bytes 1000 | tf_op jit(solution)/shard_map/replay/pallas_call | solution.py:573
  109.6 2.0 collective-permute-start.12
  111.6 4.6 %collective-permute-done.13.refs_2_ = f32[2,512,128]{2,1,0:T(8,128)} collective-permute-done((f32[2,512,128]{2,1,0:T(8,128)}, f32[2,512,128]{2,1,0:T(8,128)}, u32[]{:S(2)}, u32[]{:S(2)}) %collective-permute-start.13) | collective-permute-done | bytes 524320 | tf_op jit(solution)/shard_map/ppermute | solution.py:604
  116.2 2.2 %collective-permute-done.14.refs_3_ = f32[2,512,128]{2,1,0:T(8,128)} collective-permute-done((f32[2,512,128]{2,1,0:T(8,128)}, f32[2,512,128]{2,1,0:T(8,128)}, u32[]{:S(2)}, u32[]{:S(2)}) %collective-permute-start.14) | collective-permute-done | bytes 524320 | tf_op jit(solution)/shard_map/ppermute | solution.py:604
  118.4 2.2 %edges_apart.1 = (f32[2,2,512,128]{3,2,1,0:T(8,128)S(1)}, f32[2,512,128]{2,1,0:T(8,128)S(1)}, f32[2,512,128]{2,1,0:T(8,128)S(1)}, f32[2,512,128]{2,1,0:T(8,128)S(1)}, f32[2,512,128]{2,1,0:T(8,128)S(1)}) custom-call(f32[27]{0:T(128)S(1)} %concatenate.3.prm.refs_0_.refs_1_, f32[2,2,512,128]{3,2,1,0:T(8,128)S(1)} %get-tuple-element.91.refs_1_, ...), custom_call_target="tpu_custom_call" | custom-call | flops 1000 | bytes 1000 | tf_op jit(solution)/shard_map/edges_apart/pallas_call | solution.py:573
  133.8 2.4 %coarse_mid.1.refs_10_ = f32[2,4,512,128]{3,2,1,0:T(8,128)S(1)} custom-call(s32[1]{0:T(128)} %bitcast.1.refs_0_, f32[27]{0:T(128)S(1)} %concatenate.3.prm.refs_0_.refs_1_, f32[2,4,512,128]{3,2,1,0:T(8,128)} %collective-permute-done.12.refs_2_, f32[2,2,512,128]{3,2,1,0:T(8,128)S(1)} %collective-permute-done.17.refs_3_, f32[2,4,512,128]{3,2,1,0:T(8,128)S(1)} %copy-done.1, ...), custom_call_target="tpu_custom_call" | custom-call | flops 1000 | bytes 1000 | tf_op jit(solution)/shard_map/coarse_mid/pallas_call | solution.py:573
  137.6 35.6 %collective-permute-done.23.refs_14_.refs_2_.refs_3_ = f32[2,4,512,128]{3,2,1,0:T(8,128)S(1)} collective-permute-done((f32[2,4,512,128]{3,2,1,0:T(8,128)S(1)}, f32[2,4,512,128]{3,2,1,0:T(8,128)S(1)}, u32[]{:S(2)}, u32[]{:S(2)}) %collective-permute-start.23) | collective-permute-done | bytes 2097184 | tf_op jit(solution)/shard_map/ppermute | solution.py:604
  174.5 4.3 %coarse_outer.1 = (f32[2,4,512,128]{3,2,1,0:T(8,128)}, f32[2,512,128]{2,1,0:T(8,128)}, f32[2,512,128]{2,1,0:T(8,128)}) custom-call(s32[1]{0:T(128)} %bitcast.1.refs_0_, f32[27]{0:T(128)S(1)} %concatenate.3.prm.refs_0_.refs_1_, f32[2,4,512,128]{3,2,1,0:T(8,128)} %collective-permute-done.12.refs_2_, f32[2,2,512,128]{3,2,1,0:T(8,128)S(1)} %collective-permute-done.17.refs_3_, ...), custom_call_target="tpu_custom_call" | custom-call | flops 1000 | bytes 1000 | tf_op jit(solution)/shard_map/coarse_outer/pallas_call | solution.py:782
  182.7 9.1 %collective-permute-done.26.refs_4_ = f32[2,4,512,128]{3,2,1,0:T(8,128)} collective-permute-done((f32[2,4,512,128]{3,2,1,0:T(8,128)}, f32[2,4,512,128]{3,2,1,0:T(8,128)}, u32[]{:S(2)}, u32[]{:S(2)}) %collective-permute-start.26) | collective-permute-done | bytes 2097184 | tf_op jit(solution)/shard_map/ppermute | solution.py:604
  191.8 11.8 %last_rows.1 = (f32[1,8,512,128]{3,2,1,0:T(8,128)}, f32[1,8,512,128]{3,2,1,0:T(8,128)}) custom-call(s32[1]{0:T(128)} %bitcast.refs_0_.own, f32[27]{0:T(128)S(1)} %concatenate.3.prm.refs_0_.refs_1_, f32[2,4,512,128]{3,2,1,0:T(8,128)} %copy-done.15, f32[2,4,512,128]{3,2,1,0:T(8,128)} %copy-done.15, f32[2,4,512,128]{3,2,1,0:T(8,128)} %collective-permute-done.26.refs_4_, ...), custom_call_target="tpu_custom_call" | custom-call | flops 1000 | bytes 1000 | tf_op jit(solution)/shard_map/last_rows/pallas_call | solution.py:802
  203.6 2.5 %last_edges.1 = (f32[1,8,512,128]{3,2,1,0:T(8,128)}, f32[1,8,512,128]{3,2,1,0:T(8,128)}) custom-call(s32[1]{0:T(128)} %bitcast.refs_0_.own, f32[27]{0:T(128)S(1)} %concatenate.3.prm.refs_0_.refs_1_, f32[2,512,128]{2,1,0:T(8,128)S(1)} %collective-permute-done.24.low, ...), custom_call_target="tpu_custom_call", output_to_operand_aliasing={{0}: (5, {}), {1}: (6, {})} | custom-call | flops 1000 | bytes 1000 | tf_op jit(solution)/shard_map/last_edges/pallas_call | solution.py:619
  (76 shorter events, 31.3 us)
Async XLA Ops:
  3.9 17.6 %collective-permute-start = (f32[2,512,128]{2,1,0:T(8,128)S(1)}, f32[2,512,128]{2,1,0:T(8,128)S(1)}, u32[]{:S(2)}, u32[]{:S(2)}) collective-permute-start(f32[2,512,128]{2,1,0:T(8,128)S(1)} %get-tuple-element.62), channel_id=1, source_target_pairs={{0,1},{1,2},{2,3},{3,4},{4,5},{5,6},{6,7},{16,17},{17,18},{18,19},... | collective-permute-start | bytes 1572872 | tf_op jit(solution)/shard_map/ppermute | solution.py:604
  4.6 16.9 %collective-permute-start.1 = (f32[2,512,128]{2,1,0:T(8,128)S(1)}, f32[2,512,128]{2,1,0:T(8,128)S(1)}, u32[]{:S(2)}, u32[]{:S(2)}) collective-permute-start(f32[2,512,128]{2,1,0:T(8,128)S(1)} %get-tuple-element.63), channel_id=1, source_target_pairs={{1,0},{2,1},{3,2},{4,3},{5,4},{6,5},{7,6},{17,16},{18,17},{19,18},... | collective-permute-start | bytes 1572872 | tf_op jit(solution)/shard_map/ppermute | solution.py:604
  15.3 70.7 %copy-start.7 = (s32[2,512,128]{2,1,0:T(8,128)}, s32[2,512,128]{2,1,0:T(8,128)S(1)}, u32[]{:S(2)}) copy-start(s32[2,512,128]{2,1,0:T(8,128)S(1)} %get-tuple-element.68.refs_6_.refs_4_.refs_5_.ide) | copy-start | bytes 1572868
  15.3 15.8 %collective-permute-start.2 = (f32[2,512,128]{2,1,0:T(8,128)S(1)}, f32[2,512,128]{2,1,0:T(8,128)S(1)}, u32[]{:S(2)}, u32[]{:S(2)}) collective-permute-start(f32[2,512,128]{2,1,0:T(8,128)S(1)} %get-tuple-element.66), channel_id=1, source_target_pairs={{8,9},{9,10},{10,11},{11,12},{12,13},{13,14},{14,15},{24,25},{25,2... | collective-permute-start | bytes 1572872 | tf_op jit(solution)/shard_map/ppermute | solution.py:604
  18.4 14.2 %collective-permute-start.3 = (f32[2,512,128]{2,1,0:T(8,128)S(1)}, f32[2,512,128]{2,1,0:T(8,128)S(1)}, u32[]{:S(2)}, u32[]{:S(2)}) collective-permute-start(f32[2,512,128]{2,1,0:T(8,128)S(1)} %get-tuple-element.67), channel_id=1, source_target_pairs={{9,8},{10,9},{11,10},{12,11},{13,12},{14,13},{15,14},{25,24},{26,2... | collective-permute-start | bytes 1572872 | tf_op jit(solution)/shard_map/ppermute | solution.py:604
  34.1 20.9 %collective-permute-start.4 = (f32[2,512,128]{2,1,0:T(8,128)S(1)}, f32[2,512,128]{2,1,0:T(8,128)S(1)}, u32[]{:S(2)}, u32[]{:S(2)}) collective-permute-start(f32[2,512,128]{2,1,0:T(8,128)S(1)} %get-tuple-element.74), channel_id=1, source_target_pairs={{0,1},{1,2},{2,3},{3,4},{4,5},{5,6},{6,7},{8,9},{9,10},{10,11},{11... | collective-permute-start | bytes 1572872 | tf_op jit(solution)/shard_map/ppermute | solution.py:604
  36.4 21.9 %collective-permute-start.5 = (f32[2,512,128]{2,1,0:T(8,128)S(1)}, f32[2,512,128]{2,1,0:T(8,128)S(1)}, u32[]{:S(2)}, u32[]{:S(2)}) collective-permute-start(f32[2,512,128]{2,1,0:T(8,128)S(1)} %get-tuple-element.75), channel_id=1, source_target_pairs={{1,0},{2,1},{3,2},{4,3},{5,4},{6,5},{7,6},{9,8},{10,9},{11,10},{12... | collective-permute-start | bytes 1572872 | tf_op jit(solution)/shard_map/ppermute | solution.py:604
  44.2 41.8 %copy-start = (f32[2,4,512,128]{3,2,1,0:T(8,128)}, f32[2,4,512,128]{3,2,1,0:T(8,128)S(1)}, u32[]{:S(2)}) copy-start(f32[2,4,512,128]{3,2,1,0:T(8,128)S(1)} %get-tuple-element.76.refs_5_.refs_7_.refs_4_) | copy-start | bytes 6291460
  44.2 41.8 %copy-start.3 = (f32[2,2,512,128]{3,2,1,0:T(8,128)}, f32[2,2,512,128]{3,2,1,0:T(8,128)S(1)}, u32[]{:S(2)}) copy-start(f32[2,2,512,128]{3,2,1,0:T(8,128)S(1)} %get-tuple-element.78.refs_7_.refs_8_) | copy-start | bytes 3145732
  44.2 79.4 %copy-start.2 = (f32[2,2,512,128]{3,2,1,0:T(8,128)}, f32[2,2,512,128]{3,2,1,0:T(8,128)S(1)}, u32[]{:S(2)}) copy-start(f32[2,2,512,128]{3,2,1,0:T(8,128)S(1)} %get-tuple-element.77.refs_6_.refs_7_) | copy-start | bytes 3145732
  59.7 26.2 %collective-permute-start.10 = (f32[2,512,128]{2,1,0:T(8,128)S(1)}, f32[2,512,128]{2,1,0:T(8,128)S(1)}, u32[]{:S(2)}, u32[]{:S(2)}) collective-permute-start(f32[2,512,128]{2,1,0:T(8,128)S(1)} %get-tuple-element.85), channel_id=1, source_target_pairs={{1,0},{2,1},{3,2},{4,3},{5,4},{6,5},{7,6},{9,8},{10,9},{11,10},{12... | collective-permute-start | bytes 1572872 | tf_op jit(solution)/shard_map/ppermute | solution.py:604
  61.6 24.3 %collective-permute-start.9 = (f32[2,512,128]{2,1,0:T(8,128)S(1)}, f32[2,512,128]{2,1,0:T(8,128)S(1)}, u32[]{:S(2)}, u32[]{:S(2)}) collective-permute-start(f32[2,512,128]{2,1,0:T(8,128)S(1)} %get-tuple-element.84), channel_id=1, source_target_pairs={{0,1},{1,2},{2,3},{3,4},{4,5},{5,6},{6,7},{8,9},{9,10},{10,11},{11... | collective-permute-start | bytes 1572872 | tf_op jit(solution)/shard_map/ppermute | solution.py:604
  74.3 14.2 %copy-start.13 = (f32[4,512,128]{2,1,0:T(8,128)}, f32[4,512,128]{2,1,0:T(8,128)S(1)}, u32[]{:S(2)}) copy-start(f32[4,512,128]{2,1,0:T(8,128)S(1)} %get-tuple-element.80.refs_1_) | copy-start | bytes 3145732
  74.3 19.5 %collective-permute-start.6 = (f32[4,512,128]{2,1,0:T(8,128)S(1)}, f32[4,512,128]{2,1,0:T(8,128)S(1)}, u32[]{:S(2)}, u32[]{:S(2)}) collective-permute-start(f32[4,512,128]{2,1,0:T(8,128)S(1)} %get-tuple-element.80.refs_1_), channel_id=1, source_target_pairs={{0,8},{1,9},{2,10},{3,11},{4,12},{5,13},{6,14},{7,15}} | collective-permute-start | bytes 3145736 | tf_op jit(solution)/shard_map/ppermute | solution.py:604
  75.0 30.1 %collective-permute-start.7 = (f32[4,512,128]{2,1,0:T(8,128)}, f32[4,512,128]{2,1,0:T(8,128)}, u32[]{:S(2)}, u32[]{:S(2)}) collective-permute-start(f32[4,512,128]{2,1,0:T(8,128)} %get-tuple-element.81.refs_2_), channel_id=1, source_target_pairs={{0,8},{1,9},{2,10},{3,11},{4,12},{5,13},{6,14},{7,15}} | collective-permute-start | bytes 3145736 | tf_op jit(solution)/shard_map/ppermute | solution.py:604
  76.7 28.5 %collective-permute-start.8 = (f32[2,2,512,128]{3,2,1,0:T(8,128)}, f32[2,2,512,128]{3,2,1,0:T(8,128)}, u32[]{:S(2)}, u32[]{:S(2)}) collective-permute-start(f32[2,2,512,128]{3,2,1,0:T(8,128)} %get-tuple-element.82.refs_3_), channel_id=1, source_target_pairs={{0,8},{1,9},{2,10},{3,11},{4,12},{5,13},{6,14},{7,15}} | collective-permute-start | bytes 3145736 | tf_op jit(solution)/shard_map/ppermute | solution.py:604
  88.5 16.6 %collective-permute-start.11 = (f32[2,2,512,128]{3,2,1,0:T(8,128)}, f32[2,2,512,128]{3,2,1,0:T(8,128)}, u32[]{:S(2)}, u32[]{:S(2)}) collective-permute-start(f32[2,2,512,128]{3,2,1,0:T(8,128)} %get-tuple-element.86.refs_4_), channel_id=1, source_target_pairs={{0,8},{1,9},{2,10},{3,11},{4,12},{5,13},{6,14},{7,15}} | collective-permute-start | bytes 3145736 | tf_op jit(solution)/shard_map/ppermute | solution.py:604
  90.2 26.0 %collective-permute-start.13 = (f32[2,512,128]{2,1,0:T(8,128)}, f32[2,512,128]{2,1,0:T(8,128)}, u32[]{:S(2)}, u32[]{:S(2)}) collective-permute-start(f32[2,512,128]{2,1,0:T(8,128)} %get-tuple-element.92), channel_id=1, source_target_pairs={{0,1},{1,2},{2,3},{3,4},{4,5},{5,6},{6,7},{8,9},{9,10},{10,11},{11... | collective-permute-start | bytes 1572872 | tf_op jit(solution)/shard_map/ppermute | solution.py:604
  94.9 23.5 %collective-permute-start.14 = (f32[2,512,128]{2,1,0:T(8,128)}, f32[2,512,128]{2,1,0:T(8,128)}, u32[]{:S(2)}, u32[]{:S(2)}) collective-permute-start(f32[2,512,128]{2,1,0:T(8,128)} %get-tuple-element.93), channel_id=1, source_target_pairs={{1,0},{2,1},{3,2},{4,3},{5,4},{6,5},{7,6},{9,8},{10,9},{11,10},{12... | collective-permute-start | bytes 1572872 | tf_op jit(solution)/shard_map/ppermute | solution.py:604
  109.6 22.7 %collective-permute-start.12 = (f32[2,4,512,128]{3,2,1,0:T(8,128)}, f32[2,4,512,128]{3,2,1,0:T(8,128)}, u32[]{:S(2)}, u32[]{:S(2)}) collective-permute-start(f32[2,4,512,128]{3,2,1,0:T(8,128)} %get-tuple-element.88.refs_5_.refs_6_), channel_id=1, source_target_pairs={{8,16},{9,17},{10,18},{11,19},{12,20},{13,21},{14,22},{15,23}} | collective-permute-start | bytes 6291464 | tf_op jit(solution)/shard_map/ppermute | solution.py:604
  120.6 3.0 %collective-permute-start.15 = (f32[2,512,128]{2,1,0:T(8,128)S(1)}, f32[2,512,128]{2,1,0:T(8,128)S(1)}, u32[]{:S(2)}, u32[]{:S(2)}) collective-permute-start(f32[2,512,128]{2,1,0:T(8,128)S(1)} %get-tuple-element.94), channel_id=1, source_target_pairs={{0,8},{1,9},{2,10},{3,11},{4,12},{5,13},{6,14},{7,15}} | collective-permute-start | bytes 1572872 | tf_op jit(solution)/shard_map/ppermute | solution.py:604
  121.3 2.3 %collective-permute-start.16 = (f32[2,512,128]{2,1,0:T(8,128)S(1)}, f32[2,512,128]{2,1,0:T(8,128)S(1)}, u32[]{:S(2)}, u32[]{:S(2)}) collective-permute-start(f32[2,512,128]{2,1,0:T(8,128)S(1)} %get-tuple-element.95), channel_id=1, source_target_pairs={{0,8},{1,9},{2,10},{3,11},{4,12},{5,13},{6,14},{7,15}} | collective-permute-start | bytes 1572872 | tf_op jit(solution)/shard_map/ppermute | solution.py:604
  122.0 4.0 %collective-permute-start.18 = (f32[2,512,128]{2,1,0:T(8,128)S(1)}, f32[2,512,128]{2,1,0:T(8,128)S(1)}, u32[]{:S(2)}, u32[]{:S(2)}) collective-permute-start(f32[2,512,128]{2,1,0:T(8,128)S(1)} %get-tuple-element.100), channel_id=1, source_target_pairs={{0,9},{1,10},{2,11},{3,12},{4,13},{5,14},{6,15}} | collective-permute-start | bytes 1572872 | tf_op jit(solution)/shard_map/ppermute | solution.py:604
  122.7 3.3 %collective-permute-start.19 = (f32[2,512,128]{2,1,0:T(8,128)S(1)}, f32[2,512,128]{2,1,0:T(8,128)S(1)}, u32[]{:S(2)}, u32[]{:S(2)}) collective-permute-start(f32[2,512,128]{2,1,0:T(8,128)S(1)} %get-tuple-element.101), channel_id=1, source_target_pairs={{1,8},{2,9},{3,10},{4,11},{5,12},{6,13},{7,14}} | collective-permute-start | bytes 1572872 | tf_op jit(solution)/shard_map/ppermute | solution.py:604
  125.2 7.0 %collective-permute-start.17 = (f32[2,2,512,128]{3,2,1,0:T(8,128)}, f32[2,2,512,128]{3,2,1,0:T(8,128)S(1)}, u32[]{:S(2)}, u32[]{:S(2)}) collective-permute-start(f32[2,2,512,128]{3,2,1,0:T(8,128)} %get-tuple-element.98.refs_9_), channel_id=1, source_target_pairs={{8,16},{9,17},{10,18},{11,19},{12,20},{13,21},{14,22},{15,23}} | collective-permute-start | bytes 3145736 | tf_op jit(solution)/shard_map/ppermute | solution.py:604
  128.5 9.0 %collective-permute-start.21 = (f32[2,512,128]{2,1,0:T(8,128)}, f32[2,512,128]{2,1,0:T(8,128)}, u32[]{:S(2)}, u32[]{:S(2)}) collective-permute-start(f32[2,512,128]{2,1,0:T(8,128)} %get-tuple-element.103), channel_id=1, source_target_pairs={{8,17},{9,18},{10,19},{11,20},{12,21},{13,22},{14,23}} | collective-permute-start | bytes 1572872 | tf_op jit(solution)/shard_map/ppermute | solution.py:604
  130.0 7.5 %collective-permute-start.22 = (f32[2,512,128]{2,1,0:T(8,128)}, f32[2,512,128]{2,1,0:T(8,128)}, u32[]{:S(2)}, u32[]{:S(2)}) collective-permute-start(f32[2,512,128]{2,1,0:T(8,128)} %get-tuple-element.104), channel_id=1, source_target_pairs={{9,16},{10,17},{11,18},{12,19},{13,20},{14,21},{15,22}} | collective-permute-start | bytes 1572872 | tf_op jit(solution)/shard_map/ppermute | solution.py:604
  131.5 6.1 %collective-permute-start.20 = (f32[2,2,512,128]{3,2,1,0:T(8,128)}, f32[2,2,512,128]{3,2,1,0:T(8,128)S(1)}, u32[]{:S(2)}, u32[]{:S(2)}) collective-permute-start(f32[2,2,512,128]{3,2,1,0:T(8,128)} %copy-done.14), channel_id=1, source_target_pairs={{8,16},{9,17},{10,18},{11,19},{12,20},{13,21},{14,22},{15,23}} | collective-permute-start | bytes 3145736 | tf_op jit(solution)/shard_map/ppermute | solution.py:604
  136.2 36.9 %collective-permute-start.23 = (f32[2,4,512,128]{3,2,1,0:T(8,128)S(1)}, f32[2,4,512,128]{3,2,1,0:T(8,128)S(1)}, u32[]{:S(2)}, u32[]{:S(2)}) collective-permute-start(f32[2,4,512,128]{3,2,1,0:T(8,128)S(1)} %coarse_mid.1.refs_10_), channel_id=1, source_target_pairs={{16,24},{17,25},{18,26},{19,27},{20,28},{21,29},{22,30},{23,31}} | collective-permute-start | bytes 6291464 | tf_op jit(solution)/shard_map/ppermute | solution.py:604
  178.8 13.0 %collective-permute-start.26 = (f32[2,4,512,128]{3,2,1,0:T(8,128)}, f32[2,4,512,128]{3,2,1,0:T(8,128)}, u32[]{:S(2)}, u32[]{:S(2)}) collective-permute-start(f32[2,4,512,128]{3,2,1,0:T(8,128)} %get-tuple-element.109.refs_11_), channel_id=1, source_target_pairs={{16,24},{17,25},{18,26},{19,27},{20,28},{21,29},{22,30},{23,31}} | collective-permute-start | bytes 6291464 | tf_op jit(solution)/shard_map/ppermute | solution.py:604
  180.1 23.5 %collective-permute-start.24 = (f32[2,512,128]{2,1,0:T(8,128)}, f32[2,512,128]{2,1,0:T(8,128)S(1)}, u32[]{:S(2)}, u32[]{:S(2)}) collective-permute-start(f32[2,512,128]{2,1,0:T(8,128)} %get-tuple-element.107), channel_id=1, source_target_pairs={{16,25},{17,26},{18,27},{19,28},{20,29},{21,30},{22,31}} | collective-permute-start | bytes 1572872 | tf_op jit(solution)/shard_map/ppermute | solution.py:604
  181.4 22.2 %collective-permute-start.25 = (f32[2,512,128]{2,1,0:T(8,128)}, f32[2,512,128]{2,1,0:T(8,128)S(1)}, u32[]{:S(2)}, u32[]{:S(2)}) collective-permute-start(f32[2,512,128]{2,1,0:T(8,128)} %get-tuple-element.108), channel_id=1, source_target_pairs={{17,24},{18,25},{19,26},{20,27},{21,28},{22,29},{23,30}} | collective-permute-start | bytes 1572872 | tf_op jit(solution)/shard_map/ppermute | solution.py:604
  (12 other events, 49.7 us)

commit v7 on v6

--- a/solution.py
+++ b/solution.py
@@ -684,7 +684,7 @@
         if k == STEPS - 3:
             *sm, sn, part = call(
                 step_apart_kernel,
-                [f32(mid, ny, nz)] * 2 + [pair, pair],
+                [pltpu.HBM((mid, ny, nz), jnp.float32)] * 2 + [pair, pair],
                 (prm, sm, sn, sx, ids),
                 1,
                 "step_apart",
@@ -744,7 +744,7 @@
     )
     vx, tl0, tl7 = call(
         coarse_edges_kernel,
-        [pair, halo, halo],
+        [pltpu.HBM(pair.shape, pair.dtype), halo, halo],
         (own(1), prm, part, low, high, ide, vx),
         2,
         "coarse_edges",
@@ -767,7 +767,7 @@
             break
         vm = call(
             coarse_mid_kernel,
-            [tall],
+            [pltpu.HBM(tall.shape, tall.dtype)],
             (own(n), prm, am, an, km, ids, vm),
             2,
             "coarse_mid",

time: 207 us -> 207 us (level)
  Pallas kernels: 75.4 us -> 78.8 us
    pallas_call x15, Pallas kernels: 54.4 us -> 57.4 us  [call(): pl.pallas_call(run, out_shape=[f32(*x.shape) for x in through] + list(out...]
    unnamed x34 -> x26, local copies, waits for them, and re-layouts: 6.63 us -> 4.59 us
  transfers between devices with their start and end apart: 27 -> 27, of which waited for: 9 -> 9; matrix products, arithmetic and copies ran while one was open for 0% -> 0% of each run, Pallas kernels for 31% -> 32%
where the time goes in v7:
time: 207 us; the launch traced here: 206 us
  Pallas kernels  78.8 us (38%)
  waiting for transfers between devices  74.4 us (36%)
  starting transfers between devices  46.5 us (22%)
  local copies, waits for them, and re-layouts  5.42 us (3%)
    ppermute x27, waiting for transfers between devices, move(): return lax.ppermute(x, ('tm', 'space'), pairs)  74.4 us
    pallas_call x15, Pallas kernels, call(): pl.pallas_call(run, out_shape=[f32(*x.shape) for x in through] + list(out...  57.4 us
    ppermute x27, starting transfers between devices, move(): return lax.ppermute(x, ('tm', 'space'), pairs)  46.5 us
    pallas_call x1, Pallas kernels, per_device(): pl.pallas_call(tiled(last_rows_kernel, 512), grid=(2,), out_shape=[out, o...  12.1 us
    pallas_call x2, Pallas kernels, gridded(): pl.pallas_call(kernel, grid=(steps,), out_shape=outs, in_specs=in_specs,...  4.96 us
    unnamed x26, local copies, waits for them, and re-layouts  4.59 us
    pallas_call x1, Pallas kernels, per_device(): pl.pallas_call(tiled(coarse_outer_kernel, 512), grid=(2,), out_shape=[f32...  4.26 us
  transfers between devices with their start and end apart: 27, of which 9 were waited for; matrix products, arithmetic and copies ran while one was open for 0% of the time, Pallas kernels for 32%

profile of v7, /device:TPU:11, one launch (start us, length us, event | category | flops | bytes accessed | tf_op | source)
XLA Modules:
  0.0 206.2 jit_solution(4768390371954553597)
XLA Ops:
  1.5 2.4 %first_edges.1 = (f32[2,512,128]{2,1,0:T(8,128)S(1)}, f32[2,512,128]{2,1,0:T(8,128)S(1)}, f32[2,512,128]{2,1,0:T(8,128)S(1)}, f32[2,512,128]{2,1,0:T(8,128)S(1)}) custom-call(f32[27]{0:T(128)S(1)} %concatenate.3.prm.refs_0_.refs_1_, f32[8,512,128]{2,1,0:T(8,128)} %bitcast.5, f32[8,512,128]{2,1,0:T(8,128)} %bitcast.8, s32[8,512,128]{2,1,0:T(8,128)} %refs_3_.1), custom_call_target="tpu_custom_call" | custom-call | flops 1000 | bytes 1000 | tf_op jit(solution)/shard_map/first_edges/pallas_call | solution.py:619
  6.9 8.5 %first_step.1 = (f32[2,512,128]{2,1,0:T(8,128)S(1)}, f32[2,512,128]{2,1,0:T(8,128)S(1)}, f32[2,4,512,128]{3,2,1,0:T(8,128)S(1)}, f32[2,2,512,128]{3,2,1,0:T(8,12...) custom-call(f32[27]{0:T(128)S(1)} %concatenate.3.prm.refs_0_.refs_1_, ...), custom_call_target="tpu_custom_call", output_to_operand_aliasing={{0}: (5, {}), {1}: (6, {})} | custom-call | flops 1000 | bytes 1000 | tf_op jit(solution)/shard_map/first_step/pallas_call | solution.py:573
  15.4 3.1 %collective-permute-start.2 = (f32[2,512,128]{2,1,0:T(8,128)S(1)}, f32[2,512,128]{2,1,0:T(8,128)S(1)}, u32[]{:S(2)}, u32[]{:S(2)}) collective-permute-start(f32[2,512,128]{2,1,0:T(8,128)S(1)} %get-tuple-element.66), channel_id=1, source_target_pairs={{8,9},{9,10},{10,11},{11,12},{12,13},{13,14},{14,15},{24,25},{25,2... | collective-permute-start | bytes 1572872 | tf_op jit(solution)/shard_map/ppermute | solution.py:604
  18.6 3.0 %collective-permute-start.3 = (f32[2,512,128]{2,1,0:T(8,128)S(1)}, f32[2,512,128]{2,1,0:T(8,128)S(1)}, u32[]{:S(2)}, u32[]{:S(2)}) collective-permute-start(f32[2,512,128]{2,1,0:T(8,128)S(1)} %get-tuple-element.67), channel_id=1, source_target_pairs={{9,8},{10,9},{11,10},{12,11},{13,12},{14,13},{15,14},{25,24},{26,2... | collective-permute-start | bytes 1572872 | tf_op jit(solution)/shard_map/ppermute | solution.py:604
  21.6 9.5 %collective-permute-done.2.refs_4_ = f32[2,512,128]{2,1,0:T(8,128)S(1)} collective-permute-done((f32[2,512,128]{2,1,0:T(8,128)S(1)}, f32[2,512,128]{2,1,0:T(8,128)S(1)}, u32[]{:S(2)}, u32[]{:S(2)}) %collective-permute-start.2) | collective-permute-done | bytes 524320 | tf_op jit(solution)/shard_map/ppermute | solution.py:604
  34.1 2.3 %collective-permute-start.4 = (f32[2,512,128]{2,1,0:T(8,128)S(1)}, f32[2,512,128]{2,1,0:T(8,128)S(1)}, u32[]{:S(2)}, u32[]{:S(2)}) collective-permute-start(f32[2,512,128]{2,1,0:T(8,128)S(1)} %get-tuple-element.74), channel_id=1, source_target_pairs={{0,1},{1,2},{2,3},{3,4},{4,5},{5,6},{6,7},{8,9},{9,10},{10,11},{11... | collective-permute-start | bytes 1572872 | tf_op jit(solution)/shard_map/ppermute | solution.py:604
  36.4 4.4 %collective-permute-start.5 = (f32[2,512,128]{2,1,0:T(8,128)S(1)}, f32[2,512,128]{2,1,0:T(8,128)S(1)}, u32[]{:S(2)}, u32[]{:S(2)}) collective-permute-start(f32[2,512,128]{2,1,0:T(8,128)S(1)} %get-tuple-element.75), channel_id=1, source_target_pairs={{1,0},{2,1},{3,2},{4,3},{5,4},{6,5},{7,6},{9,8},{10,9},{11,10},{12... | collective-permute-start | bytes 1572872 | tf_op jit(solution)/shard_map/ppermute | solution.py:604
  40.7 3.3 %base.1 = (f32[2,4,512,128]{3,2,1,0:T(8,128)S(1)}, f32[2,2,512,128]{3,2,1,0:T(8,128)S(1)}, f32[2,2,512,128]{3,2,1,0:T(8,128)S(1)}) custom-call(f32[27]{0:T(128)S(1)} %concatenate.3.prm.refs_0_.refs_1_, f32[8,512,128]{2,1,0:T(8,128)S(1)} %bitcast.7, f32[8,512,128]{2,1,0:T(8,128)S(1)} %bitcast.10, f32[2,4,512,128]{3,2,1,0:T(8,128)S(1)} %get-tuple-element.59.refs_1_.refs_3_, ...), custom_call_target="tpu_custom_call" | custom-call | flops 1000 | bytes 1000 | tf_op jit(solution)/shard_map/base/pallas_call | solution.py:573
  44.1 8.2 %step.1 = (f32[2,4,512,128]{3,2,1,0:T(8,128)S(1)}, f32[2,2,512,128]{3,2,1,0:T(8,128)S(1)}, f32[2,2,512,128]{3,2,1,0:T(8,128)S(1)}) custom-call(f32[27]{0:T(128)S(1)} %concatenate.3.prm.refs_0_.refs_1_, f32[2,4,512,128]{3,2,1,0:T(8,128)S(1)} %get-tuple-element.59.refs_1_.refs_3_, f32[2,2,512,128]{3,2,1,0:T(8,128)S(1)} %get-tuple-element.60.refs_2_.refs_4_, ...), custom_call_target="tpu_custom_call" | custom-call | flops 1000 | bytes 1000 | tf_op jit(solution)/shard_map/step/pallas_call | solution.py:573
  52.3 2.6 %collective-permute-done.4.refs_2_ = f32[2,512,128]{2,1,0:T(8,128)S(1)} collective-permute-done((f32[2,512,128]{2,1,0:T(8,128)S(1)}, f32[2,512,128]{2,1,0:T(8,128)S(1)}, u32[]{:S(2)}, u32[]{:S(2)}) %collective-permute-start.4) | collective-permute-done | bytes 524320 | tf_op jit(solution)/shard_map/ppermute | solution.py:604
  55.0 3.3 %collective-permute-done.5.refs_3_ = f32[2,512,128]{2,1,0:T(8,128)S(1)} collective-permute-done((f32[2,512,128]{2,1,0:T(8,128)S(1)}, f32[2,512,128]{2,1,0:T(8,128)S(1)}, u32[]{:S(2)}, u32[]{:S(2)}) %collective-permute-start.5) | collective-permute-done | bytes 524320 | tf_op jit(solution)/shard_map/ppermute | solution.py:604
  59.6 1.9 collective-permute-start.10
  61.5 3.4 %collective-permute-start.9 = (f32[2,512,128]{2,1,0:T(8,128)S(1)}, f32[2,512,128]{2,1,0:T(8,128)S(1)}, u32[]{:S(2)}, u32[]{:S(2)}) collective-permute-start(f32[2,512,128]{2,1,0:T(8,128)S(1)} %get-tuple-element.84), channel_id=1, source_target_pairs={{0,1},{1,2},{2,3},{3,4},{4,5},{5,6},{6,7},{8,9},{9,10},{10,11},{11... | collective-permute-start | bytes 1572872 | tf_op jit(solution)/shard_map/ppermute | solution.py:604
  64.9 9.9 %step_apart.1 = (f32[4,512,128]{2,1,0:T(8,128)}, f32[4,512,128]{2,1,0:T(8,128)}, f32[2,2,512,128]{3,2,1,0:T(8,128)}, f32[2,2,512,128]{3,2,1,0:T(8,128)S(1)}) custom-call(f32[27]{0:T(128)S(1)} %concatenate.3.prm.refs_0_.refs_1_, f32[2,4,512,128]{3,2,1,0:T(8,128)S(1)} %get-tuple-element.71.refs_1_, f32[2,2,512,128]{3,2,1,0:T(8,128)S(1)} %get-tuple-element.72.refs_2_, ...), custom_call_target="tpu_custom_call" | custom-call | flops 1000 | bytes 1000 | tf_op jit(solution)/shard_map/step_apart/pallas_call | solution.py:573
  79.8 6.1 %collective-permute-done.10.refs_3_ = f32[2,512,128]{2,1,0:T(8,128)S(1)} collective-permute-done((f32[2,512,128]{2,1,0:T(8,128)S(1)}, f32[2,512,128]{2,1,0:T(8,128)S(1)}, u32[]{:S(2)}, u32[]{:S(2)}) %collective-permute-start.10) | collective-permute-done | bytes 524320 | tf_op jit(solution)/shard_map/ppermute | solution.py:604
  85.9 2.6 %edges.5 = (f32[2,2,512,128]{3,2,1,0:T(8,128)}, f32[2,512,128]{2,1,0:T(8,128)}, f32[2,512,128]{2,1,0:T(8,128)}) custom-call(f32[27]{0:T(128)S(1)} %concatenate.3.prm.refs_0_.refs_1_, f32[2,2,512,128]{3,2,1,0:T(8,128)S(1)} %get-tuple-element.83.refs_1_, f32[2,512,128]{2,1,0:T(8,128)S(1)} %collective-permute-done.9.refs_2_, ...), custom_call_target="tpu_custom_call" | custom-call | flops 1000 | bytes 1000 | tf_op jit(solution)/shard_map/edges/pallas_call | solution.py:573
  90.1 3.6 %collective-permute-start.13 = (f32[2,512,128]{2,1,0:T(8,128)}, f32[2,512,128]{2,1,0:T(8,128)}, u32[]{:S(2)}, u32[]{:S(2)}) collective-permute-start(f32[2,512,128]{2,1,0:T(8,128)} %get-tuple-element.92), channel_id=1, source_target_pairs={{0,1},{1,2},{2,3},{3,4},{4,5},{5,6},{6,7},{8,9},{9,10},{10,11},{11... | collective-permute-start | bytes 1572872 | tf_op jit(solution)/shard_map/ppermute | solution.py:604
  93.8 2.5 %collective-permute-start.14 = (f32[2,512,128]{2,1,0:T(8,128)}, f32[2,512,128]{2,1,0:T(8,128)}, u32[]{:S(2)}, u32[]{:S(2)}) collective-permute-start(f32[2,512,128]{2,1,0:T(8,128)} %get-tuple-element.93), channel_id=1, source_target_pairs={{1,0},{2,1},{3,2},{4,3},{5,4},{6,5},{7,6},{9,8},{10,9},{11,10},{12... | collective-permute-start | bytes 1572872 | tf_op jit(solution)/shard_map/ppermute | solution.py:604
  96.3 8.0 %step_joined.1 = (f32[2,4,512,128]{3,2,1,0:T(8,128)S(1)}, f32[2,2,512,128]{3,2,1,0:T(8,128)S(1)}, f32[2,2,512,128]{3,2,1,0:T(8,128)S(1)}) custom-call(f32[27]{0:T(128)S(1)} %concatenate.3.prm.refs_0_.refs_1_, f32[4,512,128]{2,1,0:T(8,128)} %get-tuple-element.80.refs_1_, f32[4,512,128]{2,1,0:T(8,128)} %get-tuple-element.81.refs_2_, ...), custom_call_target="tpu_custom_call" | custom-call | flops 1000 | bytes 1000 | tf_op jit(solution)/shard_map/step_joined/pallas_call | solution.py:573
  104.4 4.4 %replay.1 = (f32[2,4,512,128]{3,2,1,0:T(8,128)S(1)}, f32[2,2,512,128]{3,2,1,0:T(8,128)S(1)}, f32[2,4,512,128]{3,2,1,0:T(8,128)}) custom-call(s32[1]{0:T(128)} %bitcast.2.refs_0_, f32[27]{0:T(128)S(1)} %concatenate.3.prm.refs_0_.refs_1_, f32[4,512,128]{2,1,0:T(8,128)} %collective-permute-done.6.refs_2_, f32[4,512,128]{2,1,0:T(8,128)} %collective-permute-done.7.refs_3_, ...), custom_call_target="tpu_custom_call" | custom-call | flops 1000 | bytes 1000 | tf_op jit(solution)/shard_map/replay/pallas_call | solution.py:573
  108.8 2.0 collective-permute-start.12
  110.8 5.3 %collective-permute-done.13.refs_2_ = f32[2,512,128]{2,1,0:T(8,128)} collective-permute-done((f32[2,512,128]{2,1,0:T(8,128)}, f32[2,512,128]{2,1,0:T(8,128)}, u32[]{:S(2)}, u32[]{:S(2)}) %collective-permute-start.13) | collective-permute-done | bytes 524320 | tf_op jit(solution)/shard_map/ppermute | solution.py:604
  116.1 2.2 %collective-permute-done.14.refs_3_ = f32[2,512,128]{2,1,0:T(8,128)} collective-permute-done((f32[2,512,128]{2,1,0:T(8,128)}, f32[2,512,128]{2,1,0:T(8,128)}, u32[]{:S(2)}, u32[]{:S(2)}) %collective-permute-start.14) | collective-permute-done | bytes 524320 | tf_op jit(solution)/shard_map/ppermute | solution.py:604
  118.3 2.2 %edges_apart.1 = (f32[2,2,512,128]{3,2,1,0:T(8,128)S(1)}, f32[2,512,128]{2,1,0:T(8,128)S(1)}, f32[2,512,128]{2,1,0:T(8,128)S(1)}, f32[2,512,128]{2,1,0:T(8,128)S(1)}, f32[2,512,128]{2,1,0:T(8,128)S(1)}) custom-call(f32[27]{0:T(128)S(1)} %concatenate.3.prm.refs_0_.refs_1_, f32[2,2,512,128]{3,2,1,0:T(8,128)S(1)} %get-tuple-element.91.refs_1_, ...), custom_call_target="tpu_custom_call" | custom-call | flops 1000 | bytes 1000 | tf_op jit(solution)/shard_map/edges_apart/pallas_call | solution.py:573
  123.3 1.8 coarse_rim.1
  125.9 2.0 coarse_edges.1
  133.1 3.7 %coarse_mid.1.refs_10_ = f32[2,4,512,128]{3,2,1,0:T(8,128)} custom-call(s32[1]{0:T(128)} %bitcast.1.refs_0_, f32[27]{0:T(128)S(1)} %concatenate.3.prm.refs_0_.refs_1_, f32[2,4,512,128]{3,2,1,0:T(8,128)} %collective-permute-done.12.refs_2_, f32[2,2,512,128]{3,2,1,0:T(8,128)S(1)} %collective-permute-done.17.refs_3_, f32[2,4,512,128]{3,2,1,0:T(8,128)S(1)} %copy-done.1, ...), custom_call_target="tpu_custom_call" | custom-call | flops 1000 | bytes 1000 | tf_op jit(solution)/shard_map/coarse_mid/pallas_call | solution.py:573
  138.1 36.5 %collective-permute-done.23.refs_14_.refs_2_.refs_3_ = f32[2,4,512,128]{3,2,1,0:T(8,128)S(1)} collective-permute-done((f32[2,4,512,128]{3,2,1,0:T(8,128)}, f32[2,4,512,128]{3,2,1,0:T(8,128)S(1)}, u32[]{:S(2)}, u32[]{:S(2)}) %collective-permute-start.23) | collective-permute-done | bytes 2097184 | tf_op jit(solution)/shard_map/ppermute | solution.py:604
  176.0 4.3 %coarse_outer.1 = (f32[2,4,512,128]{3,2,1,0:T(8,128)}, f32[2,512,128]{2,1,0:T(8,128)}, f32[2,512,128]{2,1,0:T(8,128)}) custom-call(s32[1]{0:T(128)} %bitcast.1.refs_0_, f32[27]{0:T(128)S(1)} %concatenate.3.prm.refs_0_.refs_1_, f32[2,4,512,128]{3,2,1,0:T(8,128)} %collective-permute-done.12.refs_2_, f32[2,2,512,128]{3,2,1,0:T(8,128)S(1)} %collective-permute-done.17.refs_3_, ...), custom_call_target="tpu_custom_call" | custom-call | flops 1000 | bytes 1000 | tf_op jit(solution)/shard_map/coarse_outer/pallas_call | solution.py:782
  184.2 7.3 %collective-permute-done.26.refs_4_ = f32[2,4,512,128]{3,2,1,0:T(8,128)} collective-permute-done((f32[2,4,512,128]{3,2,1,0:T(8,128)}, f32[2,4,512,128]{3,2,1,0:T(8,128)}, u32[]{:S(2)}, u32[]{:S(2)}) %collective-permute-start.26) | collective-permute-done | bytes 2097184 | tf_op jit(solution)/shard_map/ppermute | solution.py:604
  191.5 12.1 %last_rows.1 = (f32[1,8,512,128]{3,2,1,0:T(8,128)}, f32[1,8,512,128]{3,2,1,0:T(8,128)}) custom-call(s32[1]{0:T(128)} %bitcast.refs_0_.own, f32[27]{0:T(128)S(1)} %concatenate.3.prm.refs_0_.refs_1_, f32[2,4,512,128]{3,2,1,0:T(8,128)} %copy-done.12, f32[2,4,512,128]{3,2,1,0:T(8,128)} %copy-done.12, f32[2,4,512,128]{3,2,1,0:T(8,128)} %collective-permute-done.26.refs_4_, ...), custom_call_target="tpu_custom_call" | custom-call | flops 1000 | bytes 1000 | tf_op jit(solution)/shard_map/last_rows/pallas_call | solution.py:802
  203.7 2.5 %last_edges.1 = (f32[1,8,512,128]{3,2,1,0:T(8,128)}, f32[1,8,512,128]{3,2,1,0:T(8,128)}) custom-call(s32[1]{0:T(128)} %bitcast.refs_0_.own, f32[27]{0:T(128)S(1)} %concatenate.3.prm.refs_0_.refs_1_, f32[2,512,128]{2,1,0:T(8,128)S(1)} %collective-permute-done.24.low, ...), custom_call_target="tpu_custom_call", output_to_operand_aliasing={{0}: (5, {}), {1}: (6, {})} | custom-call | flops 1000 | bytes 1000 | tf_op jit(solution)/shard_map/last_edges/pallas_call | solution.py:619
  (68 shorter events, 30.0 us)
Async XLA Ops:
  3.9 17.7 %collective-permute-start = (f32[2,512,128]{2,1,0:T(8,128)S(1)}, f32[2,512,128]{2,1,0:T(8,128)S(1)}, u32[]{:S(2)}, u32[]{:S(2)}) collective-permute-start(f32[2,512,128]{2,1,0:T(8,128)S(1)} %get-tuple-element.62), channel_id=1, source_target_pairs={{0,1},{1,2},{2,3},{3,4},{4,5},{5,6},{6,7},{16,17},{17,18},{18,19},... | collective-permute-start | bytes 1572872 | tf_op jit(solution)/shard_map/ppermute | solution.py:604
  4.6 17.0 %collective-permute-start.1 = (f32[2,512,128]{2,1,0:T(8,128)S(1)}, f32[2,512,128]{2,1,0:T(8,128)S(1)}, u32[]{:S(2)}, u32[]{:S(2)}) collective-permute-start(f32[2,512,128]{2,1,0:T(8,128)S(1)} %get-tuple-element.63), channel_id=1, source_target_pairs={{1,0},{2,1},{3,2},{4,3},{5,4},{6,5},{7,6},{17,16},{18,17},{19,18},... | collective-permute-start | bytes 1572872 | tf_op jit(solution)/shard_map/ppermute | solution.py:604
  15.4 70.5 %copy-start.7 = (s32[2,512,128]{2,1,0:T(8,128)}, s32[2,512,128]{2,1,0:T(8,128)S(1)}, u32[]{:S(2)}) copy-start(s32[2,512,128]{2,1,0:T(8,128)S(1)} %get-tuple-element.68.refs_6_.refs_4_.refs_5_.ide) | copy-start | bytes 1572868
  15.4 15.7 %collective-permute-start.2 = (f32[2,512,128]{2,1,0:T(8,128)S(1)}, f32[2,512,128]{2,1,0:T(8,128)S(1)}, u32[]{:S(2)}, u32[]{:S(2)}) collective-permute-start(f32[2,512,128]{2,1,0:T(8,128)S(1)} %get-tuple-element.66), channel_id=1, source_target_pairs={{8,9},{9,10},{10,11},{11,12},{12,13},{13,14},{14,15},{24,25},{25,2... | collective-permute-start | bytes 1572872 | tf_op jit(solution)/shard_map/ppermute | solution.py:604
  18.6 14.1 %collective-permute-start.3 = (f32[2,512,128]{2,1,0:T(8,128)S(1)}, f32[2,512,128]{2,1,0:T(8,128)S(1)}, u32[]{:S(2)}, u32[]{:S(2)}) collective-permute-start(f32[2,512,128]{2,1,0:T(8,128)S(1)} %get-tuple-element.67), channel_id=1, source_target_pairs={{9,8},{10,9},{11,10},{12,11},{13,12},{14,13},{15,14},{25,24},{26,2... | collective-permute-start | bytes 1572872 | tf_op jit(solution)/shard_map/ppermute | solution.py:604
  34.1 20.8 %collective-permute-start.4 = (f32[2,512,128]{2,1,0:T(8,128)S(1)}, f32[2,512,128]{2,1,0:T(8,128)S(1)}, u32[]{:S(2)}, u32[]{:S(2)}) collective-permute-start(f32[2,512,128]{2,1,0:T(8,128)S(1)} %get-tuple-element.74), channel_id=1, source_target_pairs={{0,1},{1,2},{2,3},{3,4},{4,5},{5,6},{6,7},{8,9},{9,10},{10,11},{11... | collective-permute-start | bytes 1572872 | tf_op jit(solution)/shard_map/ppermute | solution.py:604
  36.4 21.8 %collective-permute-start.5 = (f32[2,512,128]{2,1,0:T(8,128)S(1)}, f32[2,512,128]{2,1,0:T(8,128)S(1)}, u32[]{:S(2)}, u32[]{:S(2)}) collective-permute-start(f32[2,512,128]{2,1,0:T(8,128)S(1)} %get-tuple-element.75), channel_id=1, source_target_pairs={{1,0},{2,1},{3,2},{4,3},{5,4},{6,5},{7,6},{9,8},{10,9},{11,10},{12... | collective-permute-start | bytes 1572872 | tf_op jit(solution)/shard_map/ppermute | solution.py:604
  44.1 41.8 %copy-start = (f32[2,4,512,128]{3,2,1,0:T(8,128)}, f32[2,4,512,128]{3,2,1,0:T(8,128)S(1)}, u32[]{:S(2)}) copy-start(f32[2,4,512,128]{3,2,1,0:T(8,128)S(1)} %get-tuple-element.76.refs_5_.refs_7_.refs_4_) | copy-start | bytes 6291460
  44.1 41.8 %copy-start.3 = (f32[2,2,512,128]{3,2,1,0:T(8,128)}, f32[2,2,512,128]{3,2,1,0:T(8,128)S(1)}, u32[]{:S(2)}) copy-start(f32[2,2,512,128]{3,2,1,0:T(8,128)S(1)} %get-tuple-element.78.refs_7_.refs_8_) | copy-start | bytes 3145732
  44.1 79.2 %copy-start.2 = (f32[2,2,512,128]{3,2,1,0:T(8,128)}, f32[2,2,512,128]{3,2,1,0:T(8,128)S(1)}, u32[]{:S(2)}) copy-start(f32[2,2,512,128]{3,2,1,0:T(8,128)S(1)} %get-tuple-element.77.refs_6_.refs_7_) | copy-start | bytes 3145732
  59.6 26.2 %collective-permute-start.10 = (f32[2,512,128]{2,1,0:T(8,128)S(1)}, f32[2,512,128]{2,1,0:T(8,128)S(1)}, u32[]{:S(2)}, u32[]{:S(2)}) collective-permute-start(f32[2,512,128]{2,1,0:T(8,128)S(1)} %get-tuple-element.85), channel_id=1, source_target_pairs={{1,0},{2,1},{3,2},{4,3},{5,4},{6,5},{7,6},{9,8},{10,9},{11,10},{12... | collective-permute-start | bytes 1572872 | tf_op jit(solution)/shard_map/ppermute | solution.py:604
  61.5 24.3 %collective-permute-start.9 = (f32[2,512,128]{2,1,0:T(8,128)S(1)}, f32[2,512,128]{2,1,0:T(8,128)S(1)}, u32[]{:S(2)}, u32[]{:S(2)}) collective-permute-start(f32[2,512,128]{2,1,0:T(8,128)S(1)} %get-tuple-element.84), channel_id=1, source_target_pairs={{0,1},{1,2},{2,3},{3,4},{4,5},{5,6},{6,7},{8,9},{9,10},{10,11},{11... | collective-permute-start | bytes 1572872 | tf_op jit(solution)/shard_map/ppermute | solution.py:604
  74.8 18.9 %collective-permute-start.6 = (f32[4,512,128]{2,1,0:T(8,128)}, f32[4,512,128]{2,1,0:T(8,128)}, u32[]{:S(2)}, u32[]{:S(2)}) collective-permute-start(f32[4,512,128]{2,1,0:T(8,128)} %get-tuple-element.80.refs_1_), channel_id=1, source_target_pairs={{0,8},{1,9},{2,10},{3,11},{4,12},{5,13},{6,14},{7,15}} | collective-permute-start | bytes 3145736 | tf_op jit(solution)/shard_map/ppermute | solution.py:604
  76.5 27.9 %collective-permute-start.7 = (f32[4,512,128]{2,1,0:T(8,128)}, f32[4,512,128]{2,1,0:T(8,128)}, u32[]{:S(2)}, u32[]{:S(2)}) collective-permute-start(f32[4,512,128]{2,1,0:T(8,128)} %get-tuple-element.81.refs_2_), channel_id=1, source_target_pairs={{0,8},{1,9},{2,10},{3,11},{4,12},{5,13},{6,14},{7,15}} | collective-permute-start | bytes 3145736 | tf_op jit(solution)/shard_map/ppermute | solution.py:604
  78.1 26.2 %collective-permute-start.8 = (f32[2,2,512,128]{3,2,1,0:T(8,128)}, f32[2,2,512,128]{3,2,1,0:T(8,128)}, u32[]{:S(2)}, u32[]{:S(2)}) collective-permute-start(f32[2,2,512,128]{3,2,1,0:T(8,128)} %get-tuple-element.82.refs_3_), channel_id=1, source_target_pairs={{0,8},{1,9},{2,10},{3,11},{4,12},{5,13},{6,14},{7,15}} | collective-permute-start | bytes 3145736 | tf_op jit(solution)/shard_map/ppermute | solution.py:604
  88.5 15.9 %collective-permute-start.11 = (f32[2,2,512,128]{3,2,1,0:T(8,128)}, f32[2,2,512,128]{3,2,1,0:T(8,128)}, u32[]{:S(2)}, u32[]{:S(2)}) collective-permute-start(f32[2,2,512,128]{3,2,1,0:T(8,128)} %get-tuple-element.86.refs_4_), channel_id=1, source_target_pairs={{0,8},{1,9},{2,10},{3,11},{4,12},{5,13},{6,14},{7,15}} | collective-permute-start | bytes 3145736 | tf_op jit(solution)/shard_map/ppermute | solution.py:604
  90.1 26.0 %collective-permute-start.13 = (f32[2,512,128]{2,1,0:T(8,128)}, f32[2,512,128]{2,1,0:T(8,128)}, u32[]{:S(2)}, u32[]{:S(2)}) collective-permute-start(f32[2,512,128]{2,1,0:T(8,128)} %get-tuple-element.92), channel_id=1, source_target_pairs={{0,1},{1,2},{2,3},{3,4},{4,5},{5,6},{6,7},{8,9},{9,10},{10,11},{11... | collective-permute-start | bytes 1572872 | tf_op jit(solution)/shard_map/ppermute | solution.py:604
  93.8 24.5 %collective-permute-start.14 = (f32[2,512,128]{2,1,0:T(8,128)}, f32[2,512,128]{2,1,0:T(8,128)}, u32[]{:S(2)}, u32[]{:S(2)}) collective-permute-start(f32[2,512,128]{2,1,0:T(8,128)} %get-tuple-element.93), channel_id=1, source_target_pairs={{1,0},{2,1},{3,2},{4,3},{5,4},{6,5},{7,6},{9,8},{10,9},{11,10},{12... | collective-permute-start | bytes 1572872 | tf_op jit(solution)/shard_map/ppermute | solution.py:604
  104.4 13.9 %copy-start.8 = (s32[2,512,128]{2,1,0:T(8,128)S(1)}, s32[2,512,128]{2,1,0:T(8,128)}, u32[]{:S(2)}) copy-start(s32[2,512,128]{2,1,0:T(8,128)} %copy-done.7) | copy-start | bytes 1572868
  108.8 22.7 %collective-permute-start.12 = (f32[2,4,512,128]{3,2,1,0:T(8,128)}, f32[2,4,512,128]{3,2,1,0:T(8,128)}, u32[]{:S(2)}, u32[]{:S(2)}) collective-permute-start(f32[2,4,512,128]{3,2,1,0:T(8,128)} %get-tuple-element.88.refs_5_.refs_6_), channel_id=1, source_target_pairs={{8,16},{9,17},{10,18},{11,19},{12,20},{13,21},{14,22},{15,23}} | collective-permute-start | bytes 6291464 | tf_op jit(solution)/shard_map/ppermute | solution.py:604
  120.5 2.8 %collective-permute-start.15 = (f32[2,512,128]{2,1,0:T(8,128)S(1)}, f32[2,512,128]{2,1,0:T(8,128)S(1)}, u32[]{:S(2)}, u32[]{:S(2)}) collective-permute-start(f32[2,512,128]{2,1,0:T(8,128)S(1)} %get-tuple-element.94), channel_id=1, source_target_pairs={{0,8},{1,9},{2,10},{3,11},{4,12},{5,13},{6,14},{7,15}} | collective-permute-start | bytes 1572872 | tf_op jit(solution)/shard_map/ppermute | solution.py:604
  121.2 2.1 %collective-permute-start.16 = (f32[2,512,128]{2,1,0:T(8,128)S(1)}, f32[2,512,128]{2,1,0:T(8,128)S(1)}, u32[]{:S(2)}, u32[]{:S(2)}) collective-permute-start(f32[2,512,128]{2,1,0:T(8,128)S(1)} %get-tuple-element.95), channel_id=1, source_target_pairs={{0,8},{1,9},{2,10},{3,11},{4,12},{5,13},{6,14},{7,15}} | collective-permute-start | bytes 1572872 | tf_op jit(solution)/shard_map/ppermute | solution.py:604
  121.9 4.0 %collective-permute-start.18 = (f32[2,512,128]{2,1,0:T(8,128)S(1)}, f32[2,512,128]{2,1,0:T(8,128)S(1)}, u32[]{:S(2)}, u32[]{:S(2)}) collective-permute-start(f32[2,512,128]{2,1,0:T(8,128)S(1)} %get-tuple-element.100), channel_id=1, source_target_pairs={{0,9},{1,10},{2,11},{3,12},{4,13},{5,14},{6,15}} | collective-permute-start | bytes 1572872 | tf_op jit(solution)/shard_map/ppermute | solution.py:604
  122.6 3.3 %collective-permute-start.19 = (f32[2,512,128]{2,1,0:T(8,128)S(1)}, f32[2,512,128]{2,1,0:T(8,128)S(1)}, u32[]{:S(2)}, u32[]{:S(2)}) collective-permute-start(f32[2,512,128]{2,1,0:T(8,128)S(1)} %get-tuple-element.101), channel_id=1, source_target_pairs={{1,8},{2,9},{3,10},{4,11},{5,12},{6,13},{7,14}} | collective-permute-start | bytes 1572872 | tf_op jit(solution)/shard_map/ppermute | solution.py:604
  125.1 6.3 %collective-permute-start.17 = (f32[2,2,512,128]{3,2,1,0:T(8,128)}, f32[2,2,512,128]{3,2,1,0:T(8,128)S(1)}, u32[]{:S(2)}, u32[]{:S(2)}) collective-permute-start(f32[2,2,512,128]{3,2,1,0:T(8,128)} %get-tuple-element.98.refs_9_), channel_id=1, source_target_pairs={{8,16},{9,17},{10,18},{11,19},{12,20},{13,21},{14,22},{15,23}} | collective-permute-start | bytes 3145736 | tf_op jit(solution)/shard_map/ppermute | solution.py:604
  127.8 10.3 %collective-permute-start.21 = (f32[2,512,128]{2,1,0:T(8,128)}, f32[2,512,128]{2,1,0:T(8,128)}, u32[]{:S(2)}, u32[]{:S(2)}) collective-permute-start(f32[2,512,128]{2,1,0:T(8,128)} %get-tuple-element.103), channel_id=1, source_target_pairs={{8,17},{9,18},{10,19},{11,20},{12,21},{13,22},{14,23}} | collective-permute-start | bytes 1572872 | tf_op jit(solution)/shard_map/ppermute | solution.py:604
  129.3 8.8 %collective-permute-start.22 = (f32[2,512,128]{2,1,0:T(8,128)}, f32[2,512,128]{2,1,0:T(8,128)}, u32[]{:S(2)}, u32[]{:S(2)}) collective-permute-start(f32[2,512,128]{2,1,0:T(8,128)} %get-tuple-element.104), channel_id=1, source_target_pairs={{9,16},{10,17},{11,18},{12,19},{13,20},{14,21},{15,22}} | collective-permute-start | bytes 1572872 | tf_op jit(solution)/shard_map/ppermute | solution.py:604
  130.7 7.4 %collective-permute-start.20 = (f32[2,2,512,128]{3,2,1,0:T(8,128)}, f32[2,2,512,128]{3,2,1,0:T(8,128)S(1)}, u32[]{:S(2)}, u32[]{:S(2)}) collective-permute-start(f32[2,2,512,128]{3,2,1,0:T(8,128)} %get-tuple-element.102.refs_10_), channel_id=1, source_target_pairs={{8,16},{9,17},{10,18},{11,19},{12,20},{13,21},{14,22},{15,23}} | collective-permute-start | bytes 3145736 | tf_op jit(solution)/shard_map/ppermute | solution.py:604
  136.8 37.8 %collective-permute-start.23 = (f32[2,4,512,128]{3,2,1,0:T(8,128)}, f32[2,4,512,128]{3,2,1,0:T(8,128)S(1)}, u32[]{:S(2)}, u32[]{:S(2)}) collective-permute-start(f32[2,4,512,128]{3,2,1,0:T(8,128)} %coarse_mid.1.refs_10_), channel_id=1, source_target_pairs={{16,24},{17,25},{18,26},{19,27},{20,28},{21,29},{22,30},{23,31}} | collective-permute-start | bytes 6291464 | tf_op jit(solution)/shard_map/ppermute | solution.py:604
  180.3 11.2 %collective-permute-start.26 = (f32[2,4,512,128]{3,2,1,0:T(8,128)}, f32[2,4,512,128]{3,2,1,0:T(8,128)}, u32[]{:S(2)}, u32[]{:S(2)}) collective-permute-start(f32[2,4,512,128]{3,2,1,0:T(8,128)} %get-tuple-element.109.refs_11_), channel_id=1, source_target_pairs={{16,24},{17,25},{18,26},{19,27},{20,28},{21,29},{22,30},{23,31}} | collective-permute-start | bytes 6291464 | tf_op jit(solution)/shard_map/ppermute | solution.py:604
  181.6 22.1 %collective-permute-start.24 = (f32[2,512,128]{2,1,0:T(8,128)}, f32[2,512,128]{2,1,0:T(8,128)S(1)}, u32[]{:S(2)}, u32[]{:S(2)}) collective-permute-start(f32[2,512,128]{2,1,0:T(8,128)} %get-tuple-element.107), channel_id=1, source_target_pairs={{16,25},{17,26},{18,27},{19,28},{20,29},{21,30},{22,31}} | collective-permute-start | bytes 1572872 | tf_op jit(solution)/shard_map/ppermute | solution.py:604
  182.9 20.8 %collective-permute-start.25 = (f32[2,512,128]{2,1,0:T(8,128)}, f32[2,512,128]{2,1,0:T(8,128)S(1)}, u32[]{:S(2)}, u32[]{:S(2)}) collective-permute-start(f32[2,512,128]{2,1,0:T(8,128)} %get-tuple-element.108), channel_id=1, source_target_pairs={{17,24},{18,25},{19,26},{20,27},{21,28},{22,29},{23,30}} | collective-permute-start | bytes 1572872 | tf_op jit(solution)/shard_map/ppermute | solution.py:604
  (8 other events, 33.3 us)

commit v8 on v7

--- a/solution.py
+++ b/solution.py
@@ -664,6 +664,7 @@
             1,
             "edges",
             after=after,
+            tile=512,
         )
 
     base = ()
@@ -728,6 +729,7 @@
         (prm, part, *sides, ide),
         1,
         "edges_apart",
+        tile=512,
         after=(vm,),
     )
     low, high = halos(tl0, tl7, (0,), 1)
@@ -748,6 +750,7 @@
         (own(1), prm, part, low, high, ide, vx),
         2,
         "coarse_edges",
+        tile=512,
     )
     side = pl.BlockSpec((2, 1, ny, nz), lambda i: (0, i, 0, 0))
     two = pl.BlockSpec((2, 2, ny, nz), lambda i: (0, i, 0, 0))
@@ -773,6 +776,7 @@
             "coarse_mid",
             pad,
             18,
+            tile=128,
         )[0]
         vm = hbm(vm)
         am3 = hbm(send(vm, n + 1))

time: 207 us -> 207 us (level)
  transfers between devices with their start and end apart: 27 -> 27, of which waited for: 9 -> 9; matrix products, arithmetic and copies ran while one was open for 0% -> 0% of each run, Pallas kernels for 32% -> 33%
where the time goes in v8:
time: 207 us; the launch traced here: 206 us
  Pallas kernels  79 us (38%)
  waiting for transfers between devices  73.7 us (36%)
  starting transfers between devices  46.9 us (23%)
  local copies, waits for them, and re-layouts  5.42 us (3%)
    ppermute x27, waiting for transfers between devices, move(): return lax.ppermute(x, ('tm', 'space'), pairs)  73.7 us
    pallas_call x15, Pallas kernels, call(): pl.pallas_call(run, out_shape=[f32(*x.shape) for x in through] + list(out...  57.6 us
    ppermute x27, starting transfers between devices, move(): return lax.ppermute(x, ('tm', 'space'), pairs)  46.9 us
    pallas_call x1, Pallas kernels, per_device(): pl.pallas_call(tiled(last_rows_kernel, 512), grid=(2,), out_shape=[out, o...  12.1 us
    pallas_call x2, Pallas kernels, gridded(): pl.pallas_call(kernel, grid=(steps,), out_shape=outs, in_specs=in_specs,...  4.96 us
    unnamed x26, local copies, waits for them, and re-layouts  4.59 us
    pallas_call x1, Pallas kernels, per_device(): pl.pallas_call(tiled(coarse_outer_kernel, 512), grid=(2,), out_shape=[f32...  4.26 us
  transfers between devices with their start and end apart: 27, of which 9 were waited for; matrix products, arithmetic and copies ran while one was open for 0% of the time, Pallas kernels for 33%

profile of v8, /device:TPU:11, one launch (start us, length us, event | category | flops | bytes accessed | tf_op | source)
XLA Modules:
  0.0 206.1 jit_solution(13060490604629916627)
XLA Ops:
  1.5 2.4 %first_edges.1 = (f32[2,512,128]{2,1,0:T(8,128)S(1)}, f32[2,512,128]{2,1,0:T(8,128)S(1)}, f32[2,512,128]{2,1,0:T(8,128)S(1)}, f32[2,512,128]{2,1,0:T(8,128)S(1)}) custom-call(f32[27]{0:T(128)S(1)} %concatenate.3.prm.refs_0_.refs_1_, f32[8,512,128]{2,1,0:T(8,128)} %bitcast.5, f32[8,512,128]{2,1,0:T(8,128)} %bitcast.8, s32[8,512,128]{2,1,0:T(8,128)} %refs_3_.1), custom_call_target="tpu_custom_call" | custom-call | flops 1000 | bytes 1000 | tf_op jit(solution)/shard_map/first_edges/pallas_call | solution.py:619
  6.9 8.5 %first_step.1 = (f32[2,512,128]{2,1,0:T(8,128)S(1)}, f32[2,512,128]{2,1,0:T(8,128)S(1)}, f32[2,4,512,128]{3,2,1,0:T(8,128)S(1)}, f32[2,2,512,128]{3,2,1,0:T(8,12...) custom-call(f32[27]{0:T(128)S(1)} %concatenate.3.prm.refs_0_.refs_1_, ...), custom_call_target="tpu_custom_call", output_to_operand_aliasing={{0}: (5, {}), {1}: (6, {})} | custom-call | flops 1000 | bytes 1000 | tf_op jit(solution)/shard_map/first_step/pallas_call | solution.py:573
  15.4 3.1 %collective-permute-start.2 = (f32[2,512,128]{2,1,0:T(8,128)S(1)}, f32[2,512,128]{2,1,0:T(8,128)S(1)}, u32[]{:S(2)}, u32[]{:S(2)}) collective-permute-start(f32[2,512,128]{2,1,0:T(8,128)S(1)} %get-tuple-element.66), channel_id=1, source_target_pairs={{8,9},{9,10},{10,11},{11,12},{12,13},{13,14},{14,15},{24,25},{25,2... | collective-permute-start | bytes 1572872 | tf_op jit(solution)/shard_map/ppermute | solution.py:604
  18.6 3.0 %collective-permute-start.3 = (f32[2,512,128]{2,1,0:T(8,128)S(1)}, f32[2,512,128]{2,1,0:T(8,128)S(1)}, u32[]{:S(2)}, u32[]{:S(2)}) collective-permute-start(f32[2,512,128]{2,1,0:T(8,128)S(1)} %get-tuple-element.67), channel_id=1, source_target_pairs={{9,8},{10,9},{11,10},{12,11},{13,12},{14,13},{15,14},{25,24},{26,2... | collective-permute-start | bytes 1572872 | tf_op jit(solution)/shard_map/ppermute | solution.py:604
  21.6 9.5 %collective-permute-done.2.refs_4_ = f32[2,512,128]{2,1,0:T(8,128)S(1)} collective-permute-done((f32[2,512,128]{2,1,0:T(8,128)S(1)}, f32[2,512,128]{2,1,0:T(8,128)S(1)}, u32[]{:S(2)}, u32[]{:S(2)}) %collective-permute-start.2) | collective-permute-done | bytes 524320 | tf_op jit(solution)/shard_map/ppermute | solution.py:604
  34.1 2.3 %collective-permute-start.4 = (f32[2,512,128]{2,1,0:T(8,128)S(1)}, f32[2,512,128]{2,1,0:T(8,128)S(1)}, u32[]{:S(2)}, u32[]{:S(2)}) collective-permute-start(f32[2,512,128]{2,1,0:T(8,128)S(1)} %get-tuple-element.74), channel_id=1, source_target_pairs={{0,1},{1,2},{2,3},{3,4},{4,5},{5,6},{6,7},{8,9},{9,10},{10,11},{11... | collective-permute-start | bytes 1572872 | tf_op jit(solution)/shard_map/ppermute | solution.py:604
  36.4 4.4 %collective-permute-start.5 = (f32[2,512,128]{2,1,0:T(8,128)S(1)}, f32[2,512,128]{2,1,0:T(8,128)S(1)}, u32[]{:S(2)}, u32[]{:S(2)}) collective-permute-start(f32[2,512,128]{2,1,0:T(8,128)S(1)} %get-tuple-element.75), channel_id=1, source_target_pairs={{1,0},{2,1},{3,2},{4,3},{5,4},{6,5},{7,6},{9,8},{10,9},{11,10},{12... | collective-permute-start | bytes 1572872 | tf_op jit(solution)/shard_map/ppermute | solution.py:604
  40.7 3.3 %base.1 = (f32[2,4,512,128]{3,2,1,0:T(8,128)S(1)}, f32[2,2,512,128]{3,2,1,0:T(8,128)S(1)}, f32[2,2,512,128]{3,2,1,0:T(8,128)S(1)}) custom-call(f32[27]{0:T(128)S(1)} %concatenate.3.prm.refs_0_.refs_1_, f32[8,512,128]{2,1,0:T(8,128)S(1)} %bitcast.7, f32[8,512,128]{2,1,0:T(8,128)S(1)} %bitcast.10, f32[2,4,512,128]{3,2,1,0:T(8,128)S(1)} %get-tuple-element.59.refs_1_.refs_3_, ...), custom_call_target="tpu_custom_call" | custom-call | flops 1000 | bytes 1000 | tf_op jit(solution)/shard_map/base/pallas_call | solution.py:573
  44.1 8.2 %step.1 = (f32[2,4,512,128]{3,2,1,0:T(8,128)S(1)}, f32[2,2,512,128]{3,2,1,0:T(8,128)S(1)}, f32[2,2,512,128]{3,2,1,0:T(8,128)S(1)}) custom-call(f32[27]{0:T(128)S(1)} %concatenate.3.prm.refs_0_.refs_1_, f32[2,4,512,128]{3,2,1,0:T(8,128)S(1)} %get-tuple-element.59.refs_1_.refs_3_, f32[2,2,512,128]{3,2,1,0:T(8,128)S(1)} %get-tuple-element.60.refs_2_.refs_4_, ...), custom_call_target="tpu_custom_call" | custom-call | flops 1000 | bytes 1000 | tf_op jit(solution)/shard_map/step/pallas_call | solution.py:573
  52.3 2.6 %collective-permute-done.4.refs_2_ = f32[2,512,128]{2,1,0:T(8,128)S(1)} collective-permute-done((f32[2,512,128]{2,1,0:T(8,128)S(1)}, f32[2,512,128]{2,1,0:T(8,128)S(1)}, u32[]{:S(2)}, u32[]{:S(2)}) %collective-permute-start.4) | collective-permute-done | bytes 524320 | tf_op jit(solution)/shard_map/ppermute | solution.py:604
  54.9 3.3 %collective-permute-done.5.refs_3_ = f32[2,512,128]{2,1,0:T(8,128)S(1)} collective-permute-done((f32[2,512,128]{2,1,0:T(8,128)S(1)}, f32[2,512,128]{2,1,0:T(8,128)S(1)}, u32[]{:S(2)}, u32[]{:S(2)}) %collective-permute-start.5) | collective-permute-done | bytes 524320 | tf_op jit(solution)/shard_map/ppermute | solution.py:604
  59.6 1.9 collective-permute-start.10
  61.5 3.4 %collective-permute-start.9 = (f32[2,512,128]{2,1,0:T(8,128)S(1)}, f32[2,512,128]{2,1,0:T(8,128)S(1)}, u32[]{:S(2)}, u32[]{:S(2)}) collective-permute-start(f32[2,512,128]{2,1,0:T(8,128)S(1)} %get-tuple-element.84), channel_id=1, source_target_pairs={{0,1},{1,2},{2,3},{3,4},{4,5},{5,6},{6,7},{8,9},{9,10},{10,11},{11... | collective-permute-start | bytes 1572872 | tf_op jit(solution)/shard_map/ppermute | solution.py:604
  64.9 9.9 %step_apart.1 = (f32[4,512,128]{2,1,0:T(8,128)}, f32[4,512,128]{2,1,0:T(8,128)}, f32[2,2,512,128]{3,2,1,0:T(8,128)}, f32[2,2,512,128]{3,2,1,0:T(8,128)S(1)}) custom-call(f32[27]{0:T(128)S(1)} %concatenate.3.prm.refs_0_.refs_1_, f32[2,4,512,128]{3,2,1,0:T(8,128)S(1)} %get-tuple-element.71.refs_1_, f32[2,2,512,128]{3,2,1,0:T(8,128)S(1)} %get-tuple-element.72.refs_2_, ...), custom_call_target="tpu_custom_call" | custom-call | flops 1000 | bytes 1000 | tf_op jit(solution)/shard_map/step_apart/pallas_call | solution.py:573
  78.1 1.7 collective-permute-start.8
  79.7 6.1 %collective-permute-done.10.refs_3_ = f32[2,512,128]{2,1,0:T(8,128)S(1)} collective-permute-done((f32[2,512,128]{2,1,0:T(8,128)S(1)}, f32[2,512,128]{2,1,0:T(8,128)S(1)}, u32[]{:S(2)}, u32[]{:S(2)}) %collective-permute-start.10) | collective-permute-done | bytes 524320 | tf_op jit(solution)/shard_map/ppermute | solution.py:604
  85.8 2.5 %edges.5 = (f32[2,2,512,128]{3,2,1,0:T(8,128)}, f32[2,512,128]{2,1,0:T(8,128)}, f32[2,512,128]{2,1,0:T(8,128)}) custom-call(f32[27]{0:T(128)S(1)} %concatenate.3.prm.refs_0_.refs_1_, f32[2,2,512,128]{3,2,1,0:T(8,128)S(1)} %get-tuple-element.83.refs_1_, f32[2,512,128]{2,1,0:T(8,128)S(1)} %collective-permute-done.9.refs_2_, ...), custom_call_target="tpu_custom_call" | custom-call | flops 1000 | bytes 1000 | tf_op jit(solution)/shard_map/edges/pallas_call | solution.py:573
  90.0 3.6 %collective-permute-start.13 = (f32[2,512,128]{2,1,0:T(8,128)}, f32[2,512,128]{2,1,0:T(8,128)}, u32[]{:S(2)}, u32[]{:S(2)}) collective-permute-start(f32[2,512,128]{2,1,0:T(8,128)} %get-tuple-element.92), channel_id=1, source_target_pairs={{0,1},{1,2},{2,3},{3,4},{4,5},{5,6},{6,7},{8,9},{9,10},{10,11},{11... | collective-permute-start | bytes 1572872 | tf_op jit(solution)/shard_map/ppermute | solution.py:604
  93.6 2.5 %collective-permute-start.14 = (f32[2,512,128]{2,1,0:T(8,128)}, f32[2,512,128]{2,1,0:T(8,128)}, u32[]{:S(2)}, u32[]{:S(2)}) collective-permute-start(f32[2,512,128]{2,1,0:T(8,128)} %get-tuple-element.93), channel_id=1, source_target_pairs={{1,0},{2,1},{3,2},{4,3},{5,4},{6,5},{7,6},{9,8},{10,9},{11,10},{12... | collective-permute-start | bytes 1572872 | tf_op jit(solution)/shard_map/ppermute | solution.py:604
  96.2 8.0 %step_joined.1 = (f32[2,4,512,128]{3,2,1,0:T(8,128)S(1)}, f32[2,2,512,128]{3,2,1,0:T(8,128)S(1)}, f32[2,2,512,128]{3,2,1,0:T(8,128)S(1)}) custom-call(f32[27]{0:T(128)S(1)} %concatenate.3.prm.refs_0_.refs_1_, f32[4,512,128]{2,1,0:T(8,128)} %get-tuple-element.80.refs_1_, f32[4,512,128]{2,1,0:T(8,128)} %get-tuple-element.81.refs_2_, ...), custom_call_target="tpu_custom_call" | custom-call | flops 1000 | bytes 1000 | tf_op jit(solution)/shard_map/step_joined/pallas_call | solution.py:573
  104.3 4.4 %replay.1 = (f32[2,4,512,128]{3,2,1,0:T(8,128)S(1)}, f32[2,2,512,128]{3,2,1,0:T(8,128)S(1)}, f32[2,4,512,128]{3,2,1,0:T(8,128)}) custom-call(s32[1]{0:T(128)} %bitcast.2.refs_0_, f32[27]{0:T(128)S(1)} %concatenate.3.prm.refs_0_.refs_1_, f32[4,512,128]{2,1,0:T(8,128)} %collective-permute-done.6.refs_2_, f32[4,512,128]{2,1,0:T(8,128)} %collective-permute-done.7.refs_3_, ...), custom_call_target="tpu_custom_call" | custom-call | flops 1000 | bytes 1000 | tf_op jit(solution)/shard_map/replay/pallas_call | solution.py:573
  108.7 2.2 %collective-permute-start.12 = (f32[2,4,512,128]{3,2,1,0:T(8,128)}, f32[2,4,512,128]{3,2,1,0:T(8,128)}, u32[]{:S(2)}, u32[]{:S(2)}) collective-permute-start(f32[2,4,512,128]{3,2,1,0:T(8,128)} %get-tuple-element.88.refs_5_.refs_6_), channel_id=1, source_target_pairs={{8,16},{9,17},{10,18},{11,19},{12,20},{13,21},{14,22},{15,23}} | collective-permute-start | bytes 6291464 | tf_op jit(solution)/shard_map/ppermute | solution.py:604
  110.8 5.1 %collective-permute-done.13.refs_2_ = f32[2,512,128]{2,1,0:T(8,128)} collective-permute-done((f32[2,512,128]{2,1,0:T(8,128)}, f32[2,512,128]{2,1,0:T(8,128)}, u32[]{:S(2)}, u32[]{:S(2)}) %collective-permute-start.13) | collective-permute-done | bytes 524320 | tf_op jit(solution)/shard_map/ppermute | solution.py:604
  116.0 2.2 %collective-permute-done.14.refs_3_ = f32[2,512,128]{2,1,0:T(8,128)} collective-permute-done((f32[2,512,128]{2,1,0:T(8,128)}, f32[2,512,128]{2,1,0:T(8,128)}, u32[]{:S(2)}, u32[]{:S(2)}) %collective-permute-start.14) | collective-permute-done | bytes 524320 | tf_op jit(solution)/shard_map/ppermute | solution.py:604
  118.2 2.7 %edges_apart.1 = (f32[2,2,512,128]{3,2,1,0:T(8,128)S(1)}, f32[2,512,128]{2,1,0:T(8,128)S(1)}, f32[2,512,128]{2,1,0:T(8,128)S(1)}, f32[2,512,128]{2,1,0:T(8,128)S(1)}, f32[2,512,128]{2,1,0:T(8,128)S(1)}) custom-call(f32[27]{0:T(128)S(1)} %concatenate.3.prm.refs_0_.refs_1_, f32[2,2,512,128]{3,2,1,0:T(8,128)S(1)} %get-tuple-element.91.refs_1_, ...), custom_call_target="tpu_custom_call" | custom-call | flops 1000 | bytes 1000 | tf_op jit(solution)/shard_map/edges_apart/pallas_call | solution.py:573
  126.1 2.0 coarse_edges.1
  133.3 3.7 %coarse_mid.1.refs_10_ = f32[2,4,512,128]{3,2,1,0:T(8,128)} custom-call(s32[1]{0:T(128)} %bitcast.1.refs_0_, f32[27]{0:T(128)S(1)} %concatenate.3.prm.refs_0_.refs_1_, f32[2,4,512,128]{3,2,1,0:T(8,128)} %collective-permute-done.12.refs_2_, f32[2,2,512,128]{3,2,1,0:T(8,128)S(1)} %collective-permute-done.17.refs_3_, f32[2,4,512,128]{3,2,1,0:T(8,128)S(1)} %copy-done.1, ...), custom_call_target="tpu_custom_call" | custom-call | flops 1000 | bytes 1000 | tf_op jit(solution)/shard_map/coarse_mid/pallas_call | solution.py:573
  138.4 36.6 %collective-permute-done.23.refs_14_.refs_2_.refs_3_ = f32[2,4,512,128]{3,2,1,0:T(8,128)S(1)} collective-permute-done((f32[2,4,512,128]{3,2,1,0:T(8,128)}, f32[2,4,512,128]{3,2,1,0:T(8,128)S(1)}, u32[]{:S(2)}, u32[]{:S(2)}) %collective-permute-start.23) | collective-permute-done | bytes 2097184 | tf_op jit(solution)/shard_map/ppermute | solution.py:604
  176.3 4.3 %coarse_outer.1 = (f32[2,4,512,128]{3,2,1,0:T(8,128)}, f32[2,512,128]{2,1,0:T(8,128)}, f32[2,512,128]{2,1,0:T(8,128)}) custom-call(s32[1]{0:T(128)} %bitcast.1.refs_0_, f32[27]{0:T(128)S(1)} %concatenate.3.prm.refs_0_.refs_1_, f32[2,4,512,128]{3,2,1,0:T(8,128)} %collective-permute-done.12.refs_2_, f32[2,2,512,128]{3,2,1,0:T(8,128)S(1)} %collective-permute-done.17.refs_3_, ...), custom_call_target="tpu_custom_call" | custom-call | flops 1000 | bytes 1000 | tf_op jit(solution)/shard_map/coarse_outer/pallas_call | solution.py:786
  184.7 6.7 %collective-permute-done.26.refs_4_ = f32[2,4,512,128]{3,2,1,0:T(8,128)} collective-permute-done((f32[2,4,512,128]{3,2,1,0:T(8,128)}, f32[2,4,512,128]{3,2,1,0:T(8,128)}, u32[]{:S(2)}, u32[]{:S(2)}) %collective-permute-start.26) | collective-permute-done | bytes 2097184 | tf_op jit(solution)/shard_map/ppermute | solution.py:604
  191.4 12.1 %last_rows.1 = (f32[1,8,512,128]{3,2,1,0:T(8,128)}, f32[1,8,512,128]{3,2,1,0:T(8,128)}) custom-call(s32[1]{0:T(128)} %bitcast.refs_0_.own, f32[27]{0:T(128)S(1)} %concatenate.3.prm.refs_0_.refs_1_, f32[2,4,512,128]{3,2,1,0:T(8,128)} %copy-done.12, f32[2,4,512,128]{3,2,1,0:T(8,128)} %copy-done.12, f32[2,4,512,128]{3,2,1,0:T(8,128)} %collective-permute-done.26.refs_4_, ...), custom_call_target="tpu_custom_call" | custom-call | flops 1000 | bytes 1000 | tf_op jit(solution)/shard_map/last_rows/pallas_call | solution.py:806
  203.6 2.5 %last_edges.1 = (f32[1,8,512,128]{3,2,1,0:T(8,128)}, f32[1,8,512,128]{3,2,1,0:T(8,128)}) custom-call(s32[1]{0:T(128)} %bitcast.refs_0_.own, f32[27]{0:T(128)S(1)} %concatenate.3.prm.refs_0_.refs_1_, f32[2,512,128]{2,1,0:T(8,128)S(1)} %collective-permute-done.24.low, ...), custom_call_target="tpu_custom_call", output_to_operand_aliasing={{0}: (5, {}), {1}: (6, {})} | custom-call | flops 1000 | bytes 1000 | tf_op jit(solution)/shard_map/last_edges/pallas_call | solution.py:619
  (68 shorter events, 30.2 us)
Async XLA Ops:
  3.9 17.7 %collective-permute-start = (f32[2,512,128]{2,1,0:T(8,128)S(1)}, f32[2,512,128]{2,1,0:T(8,128)S(1)}, u32[]{:S(2)}, u32[]{:S(2)}) collective-permute-start(f32[2,512,128]{2,1,0:T(8,128)S(1)} %get-tuple-element.62), channel_id=1, source_target_pairs={{0,1},{1,2},{2,3},{3,4},{4,5},{5,6},{6,7},{16,17},{17,18},{18,19},... | collective-permute-start | bytes 1572872 | tf_op jit(solution)/shard_map/ppermute | solution.py:604
  4.6 17.0 %collective-permute-start.1 = (f32[2,512,128]{2,1,0:T(8,128)S(1)}, f32[2,512,128]{2,1,0:T(8,128)S(1)}, u32[]{:S(2)}, u32[]{:S(2)}) collective-permute-start(f32[2,512,128]{2,1,0:T(8,128)S(1)} %get-tuple-element.63), channel_id=1, source_target_pairs={{1,0},{2,1},{3,2},{4,3},{5,4},{6,5},{7,6},{17,16},{18,17},{19,18},... | collective-permute-start | bytes 1572872 | tf_op jit(solution)/shard_map/ppermute | solution.py:604
  15.4 70.4 %copy-start.7 = (s32[2,512,128]{2,1,0:T(8,128)}, s32[2,512,128]{2,1,0:T(8,128)S(1)}, u32[]{:S(2)}) copy-start(s32[2,512,128]{2,1,0:T(8,128)S(1)} %get-tuple-element.68.refs_6_.refs_4_.refs_5_.ide) | copy-start | bytes 1572868
  15.4 15.7 %collective-permute-start.2 = (f32[2,512,128]{2,1,0:T(8,128)S(1)}, f32[2,512,128]{2,1,0:T(8,128)S(1)}, u32[]{:S(2)}, u32[]{:S(2)}) collective-permute-start(f32[2,512,128]{2,1,0:T(8,128)S(1)} %get-tuple-element.66), channel_id=1, source_target_pairs={{8,9},{9,10},{10,11},{11,12},{12,13},{13,14},{14,15},{24,25},{25,2... | collective-permute-start | bytes 1572872 | tf_op jit(solution)/shard_map/ppermute | solution.py:604
  18.6 14.1 %collective-permute-start.3 = (f32[2,512,128]{2,1,0:T(8,128)S(1)}, f32[2,512,128]{2,1,0:T(8,128)S(1)}, u32[]{:S(2)}, u32[]{:S(2)}) collective-permute-start(f32[2,512,128]{2,1,0:T(8,128)S(1)} %get-tuple-element.67), channel_id=1, source_target_pairs={{9,8},{10,9},{11,10},{12,11},{13,12},{14,13},{15,14},{25,24},{26,2... | collective-permute-start | bytes 1572872 | tf_op jit(solution)/shard_map/ppermute | solution.py:604
  34.1 20.8 %collective-permute-start.4 = (f32[2,512,128]{2,1,0:T(8,128)S(1)}, f32[2,512,128]{2,1,0:T(8,128)S(1)}, u32[]{:S(2)}, u32[]{:S(2)}) collective-permute-start(f32[2,512,128]{2,1,0:T(8,128)S(1)} %get-tuple-element.74), channel_id=1, source_target_pairs={{0,1},{1,2},{2,3},{3,4},{4,5},{5,6},{6,7},{8,9},{9,10},{10,11},{11... | collective-permute-start | bytes 1572872 | tf_op jit(solution)/shard_map/ppermute | solution.py:604
  36.4 21.8 %collective-permute-start.5 = (f32[2,512,128]{2,1,0:T(8,128)S(1)}, f32[2,512,128]{2,1,0:T(8,128)S(1)}, u32[]{:S(2)}, u32[]{:S(2)}) collective-permute-start(f32[2,512,128]{2,1,0:T(8,128)S(1)} %get-tuple-element.75), channel_id=1, source_target_pairs={{1,0},{2,1},{3,2},{4,3},{5,4},{6,5},{7,6},{9,8},{10,9},{11,10},{12... | collective-permute-start | bytes 1572872 | tf_op jit(solution)/shard_map/ppermute | solution.py:604
  44.1 41.8 %copy-start = (f32[2,4,512,128]{3,2,1,0:T(8,128)}, f32[2,4,512,128]{3,2,1,0:T(8,128)S(1)}, u32[]{:S(2)}) copy-start(f32[2,4,512,128]{3,2,1,0:T(8,128)S(1)} %get-tuple-element.76.refs_5_.refs_7_.refs_4_) | copy-start | bytes 6291460
  44.1 41.8 %copy-start.3 = (f32[2,2,512,128]{3,2,1,0:T(8,128)}, f32[2,2,512,128]{3,2,1,0:T(8,128)S(1)}, u32[]{:S(2)}) copy-start(f32[2,2,512,128]{3,2,1,0:T(8,128)S(1)} %get-tuple-element.78.refs_7_.refs_8_) | copy-start | bytes 3145732
  44.1 79.6 %copy-start.2 = (f32[2,2,512,128]{3,2,1,0:T(8,128)}, f32[2,2,512,128]{3,2,1,0:T(8,128)S(1)}, u32[]{:S(2)}) copy-start(f32[2,2,512,128]{3,2,1,0:T(8,128)S(1)} %get-tuple-element.77.refs_6_.refs_7_) | copy-start | bytes 3145732
  59.6 26.2 %collective-permute-start.10 = (f32[2,512,128]{2,1,0:T(8,128)S(1)}, f32[2,512,128]{2,1,0:T(8,128)S(1)}, u32[]{:S(2)}, u32[]{:S(2)}) collective-permute-start(f32[2,512,128]{2,1,0:T(8,128)S(1)} %get-tuple-element.85), channel_id=1, source_target_pairs={{1,0},{2,1},{3,2},{4,3},{5,4},{6,5},{7,6},{9,8},{10,9},{11,10},{12... | collective-permute-start | bytes 1572872 | tf_op jit(solution)/shard_map/ppermute | solution.py:604
  61.5 24.3 %collective-permute-start.9 = (f32[2,512,128]{2,1,0:T(8,128)S(1)}, f32[2,512,128]{2,1,0:T(8,128)S(1)}, u32[]{:S(2)}, u32[]{:S(2)}) collective-permute-start(f32[2,512,128]{2,1,0:T(8,128)S(1)} %get-tuple-element.84), channel_id=1, source_target_pairs={{0,1},{1,2},{2,3},{3,4},{4,5},{5,6},{6,7},{8,9},{9,10},{10,11},{11... | collective-permute-start | bytes 1572872 | tf_op jit(solution)/shard_map/ppermute | solution.py:604
  74.8 18.9 %collective-permute-start.6 = (f32[4,512,128]{2,1,0:T(8,128)}, f32[4,512,128]{2,1,0:T(8,128)}, u32[]{:S(2)}, u32[]{:S(2)}) collective-permute-start(f32[4,512,128]{2,1,0:T(8,128)} %get-tuple-element.80.refs_1_), channel_id=1, source_target_pairs={{0,8},{1,9},{2,10},{3,11},{4,12},{5,13},{6,14},{7,15}} | collective-permute-start | bytes 3145736 | tf_op jit(solution)/shard_map/ppermute | solution.py:604
  76.4 27.8 %collective-permute-start.7 = (f32[4,512,128]{2,1,0:T(8,128)}, f32[4,512,128]{2,1,0:T(8,128)}, u32[]{:S(2)}, u32[]{:S(2)}) collective-permute-start(f32[4,512,128]{2,1,0:T(8,128)} %get-tuple-element.81.refs_2_), channel_id=1, source_target_pairs={{0,8},{1,9},{2,10},{3,11},{4,12},{5,13},{6,14},{7,15}} | collective-permute-start | bytes 3145736 | tf_op jit(solution)/shard_map/ppermute | solution.py:604
  78.1 26.2 %collective-permute-start.8 = (f32[2,2,512,128]{3,2,1,0:T(8,128)}, f32[2,2,512,128]{3,2,1,0:T(8,128)}, u32[]{:S(2)}, u32[]{:S(2)}) collective-permute-start(f32[2,2,512,128]{3,2,1,0:T(8,128)} %get-tuple-element.82.refs_3_), channel_id=1, source_target_pairs={{0,8},{1,9},{2,10},{3,11},{4,12},{5,13},{6,14},{7,15}} | collective-permute-start | bytes 3145736 | tf_op jit(solution)/shard_map/ppermute | solution.py:604
  88.4 15.9 %collective-permute-start.11 = (f32[2,2,512,128]{3,2,1,0:T(8,128)}, f32[2,2,512,128]{3,2,1,0:T(8,128)}, u32[]{:S(2)}, u32[]{:S(2)}) collective-permute-start(f32[2,2,512,128]{3,2,1,0:T(8,128)} %get-tuple-element.86.refs_4_), channel_id=1, source_target_pairs={{0,8},{1,9},{2,10},{3,11},{4,12},{5,13},{6,14},{7,15}} | collective-permute-start | bytes 3145736 | tf_op jit(solution)/shard_map/ppermute | solution.py:604
  90.0 26.0 %collective-permute-start.13 = (f32[2,512,128]{2,1,0:T(8,128)}, f32[2,512,128]{2,1,0:T(8,128)}, u32[]{:S(2)}, u32[]{:S(2)}) collective-permute-start(f32[2,512,128]{2,1,0:T(8,128)} %get-tuple-element.92), channel_id=1, source_target_pairs={{0,1},{1,2},{2,3},{3,4},{4,5},{5,6},{6,7},{8,9},{9,10},{10,11},{11... | collective-permute-start | bytes 1572872 | tf_op jit(solution)/shard_map/ppermute | solution.py:604
  93.6 24.5 %collective-permute-start.14 = (f32[2,512,128]{2,1,0:T(8,128)}, f32[2,512,128]{2,1,0:T(8,128)}, u32[]{:S(2)}, u32[]{:S(2)}) collective-permute-start(f32[2,512,128]{2,1,0:T(8,128)} %get-tuple-element.93), channel_id=1, source_target_pairs={{1,0},{2,1},{3,2},{4,3},{5,4},{6,5},{7,6},{9,8},{10,9},{11,10},{12... | collective-permute-start | bytes 1572872 | tf_op jit(solution)/shard_map/ppermute | solution.py:604
  104.2 13.9 %copy-start.8 = (s32[2,512,128]{2,1,0:T(8,128)S(1)}, s32[2,512,128]{2,1,0:T(8,128)}, u32[]{:S(2)}) copy-start(s32[2,512,128]{2,1,0:T(8,128)} %copy-done.7) | copy-start | bytes 1572868
  108.7 23.0 %collective-permute-start.12 = (f32[2,4,512,128]{3,2,1,0:T(8,128)}, f32[2,4,512,128]{3,2,1,0:T(8,128)}, u32[]{:S(2)}, u32[]{:S(2)}) collective-permute-start(f32[2,4,512,128]{3,2,1,0:T(8,128)} %get-tuple-element.88.refs_5_.refs_6_), channel_id=1, source_target_pairs={{8,16},{9,17},{10,18},{11,19},{12,20},{13,21},{14,22},{15,23}} | collective-permute-start | bytes 6291464 | tf_op jit(solution)/shard_map/ppermute | solution.py:604
  120.9 2.8 %collective-permute-start.15 = (f32[2,512,128]{2,1,0:T(8,128)S(1)}, f32[2,512,128]{2,1,0:T(8,128)S(1)}, u32[]{:S(2)}, u32[]{:S(2)}) collective-permute-start(f32[2,512,128]{2,1,0:T(8,128)S(1)} %get-tuple-element.94), channel_id=1, source_target_pairs={{0,8},{1,9},{2,10},{3,11},{4,12},{5,13},{6,14},{7,15}} | collective-permute-start | bytes 1572872 | tf_op jit(solution)/shard_map/ppermute | solution.py:604
  121.6 2.1 %collective-permute-start.16 = (f32[2,512,128]{2,1,0:T(8,128)S(1)}, f32[2,512,128]{2,1,0:T(8,128)S(1)}, u32[]{:S(2)}, u32[]{:S(2)}) collective-permute-start(f32[2,512,128]{2,1,0:T(8,128)S(1)} %get-tuple-element.95), channel_id=1, source_target_pairs={{0,8},{1,9},{2,10},{3,11},{4,12},{5,13},{6,14},{7,15}} | collective-permute-start | bytes 1572872 | tf_op jit(solution)/shard_map/ppermute | solution.py:604
  122.3 3.8 %collective-permute-start.18 = (f32[2,512,128]{2,1,0:T(8,128)S(1)}, f32[2,512,128]{2,1,0:T(8,128)S(1)}, u32[]{:S(2)}, u32[]{:S(2)}) collective-permute-start(f32[2,512,128]{2,1,0:T(8,128)S(1)} %get-tuple-element.100), channel_id=1, source_target_pairs={{0,9},{1,10},{2,11},{3,12},{4,13},{5,14},{6,15}} | collective-permute-start | bytes 1572872 | tf_op jit(solution)/shard_map/ppermute | solution.py:604
  123.0 3.1 %collective-permute-start.19 = (f32[2,512,128]{2,1,0:T(8,128)S(1)}, f32[2,512,128]{2,1,0:T(8,128)S(1)}, u32[]{:S(2)}, u32[]{:S(2)}) collective-permute-start(f32[2,512,128]{2,1,0:T(8,128)S(1)} %get-tuple-element.101), channel_id=1, source_target_pairs={{1,8},{2,9},{3,10},{4,11},{5,12},{6,13},{7,14}} | collective-permute-start | bytes 1572872 | tf_op jit(solution)/shard_map/ppermute | solution.py:604
  125.3 6.3 %collective-permute-start.17 = (f32[2,2,512,128]{3,2,1,0:T(8,128)}, f32[2,2,512,128]{3,2,1,0:T(8,128)S(1)}, u32[]{:S(2)}, u32[]{:S(2)}) collective-permute-start(f32[2,2,512,128]{3,2,1,0:T(8,128)} %get-tuple-element.98.refs_9_), channel_id=1, source_target_pairs={{8,16},{9,17},{10,18},{11,19},{12,20},{13,21},{14,22},{15,23}} | collective-permute-start | bytes 3145736 | tf_op jit(solution)/shard_map/ppermute | solution.py:604
  128.1 10.3 %collective-permute-start.21 = (f32[2,512,128]{2,1,0:T(8,128)}, f32[2,512,128]{2,1,0:T(8,128)}, u32[]{:S(2)}, u32[]{:S(2)}) collective-permute-start(f32[2,512,128]{2,1,0:T(8,128)} %get-tuple-element.103), channel_id=1, source_target_pairs={{8,17},{9,18},{10,19},{11,20},{12,21},{13,22},{14,23}} | collective-permute-start | bytes 1572872 | tf_op jit(solution)/shard_map/ppermute | solution.py:604
  129.5 8.8 %collective-permute-start.22 = (f32[2,512,128]{2,1,0:T(8,128)}, f32[2,512,128]{2,1,0:T(8,128)}, u32[]{:S(2)}, u32[]{:S(2)}) collective-permute-start(f32[2,512,128]{2,1,0:T(8,128)} %get-tuple-element.104), channel_id=1, source_target_pairs={{9,16},{10,17},{11,18},{12,19},{13,20},{14,21},{15,22}} | collective-permute-start | bytes 1572872 | tf_op jit(solution)/shard_map/ppermute | solution.py:604
  131.0 7.4 %collective-permute-start.20 = (f32[2,2,512,128]{3,2,1,0:T(8,128)}, f32[2,2,512,128]{3,2,1,0:T(8,128)S(1)}, u32[]{:S(2)}, u32[]{:S(2)}) collective-permute-start(f32[2,2,512,128]{3,2,1,0:T(8,128)} %get-tuple-element.102.refs_10_), channel_id=1, source_target_pairs={{8,16},{9,17},{10,18},{11,19},{12,20},{13,21},{14,22},{15,23}} | collective-permute-start | bytes 3145736 | tf_op jit(solution)/shard_map/ppermute | solution.py:604
  137.0 37.9 %collective-permute-start.23 = (f32[2,4,512,128]{3,2,1,0:T(8,128)}, f32[2,4,512,128]{3,2,1,0:T(8,128)S(1)}, u32[]{:S(2)}, u32[]{:S(2)}) collective-permute-start(f32[2,4,512,128]{3,2,1,0:T(8,128)} %coarse_mid.1.refs_10_), channel_id=1, source_target_pairs={{16,24},{17,25},{18,26},{19,27},{20,28},{21,29},{22,30},{23,31}} | collective-permute-start | bytes 6291464 | tf_op jit(solution)/shard_map/ppermute | solution.py:604
  180.6 10.8 %collective-permute-start.26 = (f32[2,4,512,128]{3,2,1,0:T(8,128)}, f32[2,4,512,128]{3,2,1,0:T(8,128)}, u32[]{:S(2)}, u32[]{:S(2)}) collective-permute-start(f32[2,4,512,128]{3,2,1,0:T(8,128)} %get-tuple-element.109.refs_11_), channel_id=1, source_target_pairs={{16,24},{17,25},{18,26},{19,27},{20,28},{21,29},{22,30},{23,31}} | collective-permute-start | bytes 6291464 | tf_op jit(solution)/shard_map/ppermute | solution.py:604
  181.9 21.7 %collective-permute-start.24 = (f32[2,512,128]{2,1,0:T(8,128)}, f32[2,512,128]{2,1,0:T(8,128)S(1)}, u32[]{:S(2)}, u32[]{:S(2)}) collective-permute-start(f32[2,512,128]{2,1,0:T(8,128)} %get-tuple-element.107), channel_id=1, source_target_pairs={{16,25},{17,26},{18,27},{19,28},{20,29},{21,30},{22,31}} | collective-permute-start | bytes 1572872 | tf_op jit(solution)/shard_map/ppermute | solution.py:604
  183.2 20.4 %collective-permute-start.25 = (f32[2,512,128]{2,1,0:T(8,128)}, f32[2,512,128]{2,1,0:T(8,128)S(1)}, u32[]{:S(2)}, u32[]{:S(2)}) collective-permute-start(f32[2,512,128]{2,1,0:T(8,128)} %get-tuple-element.108), channel_id=1, source_target_pairs={{17,24},{18,25},{19,26},{20,27},{21,28},{22,29},{23,30}} | collective-permute-start | bytes 1572872 | tf_op jit(solution)/shard_map/ppermute | solution.py:604
  (8 other events, 33.8 us)

commit v9 on v8

--- a/solution.py
+++ b/solution.py
@@ -33,6 +33,15 @@
         self.kp18 = [18.0 / k for k in kp]
 
 
+class Params:
+    def __init__(self, refs):
+        self.refs = refs
+
+    def __getitem__(self, i):
+        k = min(i // 4, 6)
+        return self.refs[k][i - 4 * k]
+
+
 class Cells:
     def __init__(self, tab, ids):
         self.tab, self.shape = tab, ids.shape
@@ -174,8 +183,9 @@
             tiles(self.mid, ny, lambda i, t: body("m", i, i + 2, t))
 
 
-def first_edges_kernel(prm, h, c, mat, tl0, tl7, later0, later7):
-    tab = Tables(prm)
+def first_edges_kernel(*refs):
+    h, c, mat, tl0, tl7, later0, later7 = refs[7:]
+    tab = Tables(Params(refs[:7]))
     side = pl.program_id(0)
 
     def body(i, t):
@@ -636,8 +646,8 @@
         2,
         [halo] * 4,
         [whole] * 4,
-        [SMEM] + [edge_row] * 3,
-        (prm, *far),
+        [SMEM] * 7 + [edge_row] * 3,
+        (*params, *far),
         "first_edges",
     )
     every = range(slices)

time: 207 us -> 223 us (1.077)
  local copies, waits for them, and re-layouts: 5.42 us -> 14.1 us
  waiting for transfers between devices: 73.7 us -> 78.3 us
    unnamed x26 -> x58, local copies, waits for them, and re-layouts: 4.59 us -> 14 us
    ppermute x27, waiting for transfers between devices: 73.7 us -> 78.3 us  [move(): return lax.ppermute(x, ('tm', 'space'), pairs)]
  transfers between devices with their start and end apart: 27 -> 27, of which waited for: 9 -> 8; matrix products, arithmetic and copies ran while one was open for 0% -> 0% of each run, Pallas kernels for 33% -> 30%
where the time goes in v9:
time: 223 us; the launch traced here: 222 us
  Pallas kernels  80.8 us (36%)
  waiting for transfers between devices  78.3 us (35%)
  starting transfers between devices  47.8 us (21%)
  local copies, waits for them, and re-layouts  14.1 us (6%)
    ppermute x27, waiting for transfers between devices, move(): return lax.ppermute(x, ('tm', 'space'), pairs)  78.3 us
    pallas_call x15, Pallas kernels, call(): pl.pallas_call(run, out_shape=[f32(*x.shape) for x in through] + list(out...  58.5 us
    ppermute x27, starting transfers between devices, move(): return lax.ppermute(x, ('tm', 'space'), pairs)  47.8 us
    unnamed x58, local copies, waits for them, and re-layouts  14 us
    pallas_call x1, Pallas kernels, per_device(): pl.pallas_call(tiled(last_rows_kernel, 512), grid=(2,), out_shape=[out, o...  12.1 us
    pallas_call x2, Pallas kernels, gridded(): pl.pallas_call(kernel, grid=(steps,), out_shape=outs, in_specs=in_specs,...  5.83 us
  transfers between devices with their start and end apart: 27, of which 8 were waited for; matrix products, arithmetic and copies ran while one was open for 0% of the time, Pallas kernels for 30%

profile of v9, /device:TPU:11, one launch (start us, length us, event | category | flops | bytes accessed | tf_op | source)
XLA Modules:
  0.0 222.2 jit_solution(5503131816208979329)
XLA Ops:
  5.3 3.3 %first_edges.1 = (f32[2,512,128]{2,1,0:T(8,128)}, f32[2,512,128]{2,1,0:T(8,128)}, f32[2,512,128]{2,1,0:T(8,128)S(1)}, f32[2,512,128]{2,1,0:T(8,128)S(1)}) custom-call(f32[4]{0:T(128)S(1)} %copy-done.14, f32[4]{0:T(128)S(1)} %copy-done.16, f32[4]{0:T(128)S(1)} %copy-done.18, f32[4]{0:T(128)S(1)} %copy-done.20, f32[4]{0:T(128)S(1)} %copy-done.22, ...), custom_call_target="tpu_custom_call" | custom-call | flops 1000 | bytes 1000 | tf_op jit(solution)/shard_map/first_edges/pallas_call | solution.py:629
  18.0 8.5 %first_step.1 = (f32[2,512,128]{2,1,0:T(8,128)S(1)}, f32[2,512,128]{2,1,0:T(8,128)S(1)}, f32[2,4,512,128]{3,2,1,0:T(8,128)S(1)}, f32[2,2,512,128]{3,2,1,0:T(8,12...) custom-call(f32[27]{0:T(128)S(1)} %concatenate.3.refs_0_.refs_1_.prm, ...), custom_call_target="tpu_custom_call", output_to_operand_aliasing={{0}: (5, {}), {1}: (6, {})} | custom-call | flops 1000 | bytes 1000 | tf_op jit(solution)/shard_map/first_step/pallas_call | solution.py:583
  26.4 3.1 %collective-permute-start.2 = (f32[2,512,128]{2,1,0:T(8,128)S(1)}, f32[2,512,128]{2,1,0:T(8,128)S(1)}, u32[]{:S(2)}, u32[]{:S(2)}) collective-permute-start(f32[2,512,128]{2,1,0:T(8,128)S(1)} %get-tuple-element.66), channel_id=1, source_target_pairs={{8,9},{9,10},{10,11},{11,12},{12,13},{13,14},{14,15},{24,25},{25,2... | collective-permute-start | bytes 1572872 | tf_op jit(solution)/shard_map/ppermute | solution.py:614
  29.6 3.0 %collective-permute-start.3 = (f32[2,512,128]{2,1,0:T(8,128)S(1)}, f32[2,512,128]{2,1,0:T(8,128)S(1)}, u32[]{:S(2)}, u32[]{:S(2)}) collective-permute-start(f32[2,512,128]{2,1,0:T(8,128)S(1)} %get-tuple-element.67), channel_id=1, source_target_pairs={{9,8},{10,9},{11,10},{12,11},{13,12},{14,13},{15,14},{25,24},{26,2... | collective-permute-start | bytes 1572872 | tf_op jit(solution)/shard_map/ppermute | solution.py:614
  32.7 10.0 %collective-permute-done.2.refs_4_ = f32[2,512,128]{2,1,0:T(8,128)S(1)} collective-permute-done((f32[2,512,128]{2,1,0:T(8,128)S(1)}, f32[2,512,128]{2,1,0:T(8,128)S(1)}, u32[]{:S(2)}, u32[]{:S(2)}) %collective-permute-start.2) | collective-permute-done | bytes 524320 | tf_op jit(solution)/shard_map/ppermute | solution.py:614
  42.7 8.4 %collective-permute-done.3.refs_5_ = f32[2,512,128]{2,1,0:T(8,128)S(1)} collective-permute-done((f32[2,512,128]{2,1,0:T(8,128)S(1)}, f32[2,512,128]{2,1,0:T(8,128)S(1)}, u32[]{:S(2)}, u32[]{:S(2)}) %collective-permute-start.3) | collective-permute-done | bytes 524320 | tf_op jit(solution)/shard_map/ppermute | solution.py:614
  51.1 2.1 edges.3
  53.2 1.9 collective-permute-start.4
  55.2 4.3 %collective-permute-start.5 = (f32[2,512,128]{2,1,0:T(8,128)S(1)}, f32[2,512,128]{2,1,0:T(8,128)S(1)}, u32[]{:S(2)}, u32[]{:S(2)}) collective-permute-start(f32[2,512,128]{2,1,0:T(8,128)S(1)} %get-tuple-element.75), channel_id=1, source_target_pairs={{1,0},{2,1},{3,2},{4,3},{5,4},{6,5},{7,6},{9,8},{10,9},{11,10},{12... | collective-permute-start | bytes 1572872 | tf_op jit(solution)/shard_map/ppermute | solution.py:614
  59.5 3.3 %base.1 = (f32[2,4,512,128]{3,2,1,0:T(8,128)S(1)}, f32[2,2,512,128]{3,2,1,0:T(8,128)S(1)}, f32[2,2,512,128]{3,2,1,0:T(8,128)S(1)}) custom-call(f32[27]{0:T(128)S(1)} %concatenate.3.refs_0_.refs_1_.prm, f32[8,512,128]{2,1,0:T(8,128)S(1)} %bitcast.7, f32[8,512,128]{2,1,0:T(8,128)S(1)} %bitcast.10, f32[2,4,512,128]{3,2,1,0:T(8,128)S(1)} %get-tuple-element.59.refs_1_.refs_3_, ...), custom_call_target="tpu_custom_call" | custom-call | flops 1000 | bytes 1000 | tf_op jit(solution)/shard_map/base/pallas_call | solution.py:583
  62.8 8.2 %step.1 = (f32[2,4,512,128]{3,2,1,0:T(8,128)S(1)}, f32[2,2,512,128]{3,2,1,0:T(8,128)S(1)}, f32[2,2,512,128]{3,2,1,0:T(8,128)S(1)}) custom-call(f32[27]{0:T(128)S(1)} %concatenate.3.refs_0_.refs_1_.prm, f32[2,4,512,128]{3,2,1,0:T(8,128)S(1)} %get-tuple-element.59.refs_1_.refs_3_, f32[2,2,512,128]{3,2,1,0:T(8,128)S(1)} %get-tuple-element.60.refs_2_.refs_4_, ...), custom_call_target="tpu_custom_call" | custom-call | flops 1000 | bytes 1000 | tf_op jit(solution)/shard_map/step/pallas_call | solution.py:583
  71.0 2.3 %collective-permute-done.4.refs_2_ = f32[2,512,128]{2,1,0:T(8,128)S(1)} collective-permute-done((f32[2,512,128]{2,1,0:T(8,128)S(1)}, f32[2,512,128]{2,1,0:T(8,128)S(1)}, u32[]{:S(2)}, u32[]{:S(2)}) %collective-permute-start.4) | collective-permute-done | bytes 524320 | tf_op jit(solution)/shard_map/ppermute | solution.py:614
  73.3 7.8 %collective-permute-done.5.refs_3_ = f32[2,512,128]{2,1,0:T(8,128)S(1)} collective-permute-done((f32[2,512,128]{2,1,0:T(8,128)S(1)}, f32[2,512,128]{2,1,0:T(8,128)S(1)}, u32[]{:S(2)}, u32[]{:S(2)}) %collective-permute-start.5) | collective-permute-done | bytes 524320 | tf_op jit(solution)/shard_map/ppermute | solution.py:614
  82.5 1.9 collective-permute-start.10
  84.5 3.4 %collective-permute-start.9 = (f32[2,512,128]{2,1,0:T(8,128)S(1)}, f32[2,512,128]{2,1,0:T(8,128)S(1)}, u32[]{:S(2)}, u32[]{:S(2)}) collective-permute-start(f32[2,512,128]{2,1,0:T(8,128)S(1)} %get-tuple-element.84), channel_id=1, source_target_pairs={{0,1},{1,2},{2,3},{3,4},{4,5},{5,6},{6,7},{8,9},{9,10},{10,11},{11... | collective-permute-start | bytes 1572872 | tf_op jit(solution)/shard_map/ppermute | solution.py:614
  87.8 9.9 %step_apart.1 = (f32[4,512,128]{2,1,0:T(8,128)}, f32[4,512,128]{2,1,0:T(8,128)}, f32[2,2,512,128]{3,2,1,0:T(8,128)}, f32[2,2,512,128]{3,2,1,0:T(8,128)S(1)}) custom-call(f32[27]{0:T(128)S(1)} %concatenate.3.refs_0_.refs_1_.prm, f32[2,4,512,128]{3,2,1,0:T(8,128)S(1)} %get-tuple-element.71.refs_1_, f32[2,2,512,128]{3,2,1,0:T(8,128)S(1)} %get-tuple-element.72.refs_2_, ...), custom_call_target="tpu_custom_call" | custom-call | flops 1000 | bytes 1000 | tf_op jit(solution)/shard_map/step_apart/pallas_call | solution.py:583
  102.7 4.0 %collective-permute-done.10.refs_3_ = f32[2,512,128]{2,1,0:T(8,128)S(1)} collective-permute-done((f32[2,512,128]{2,1,0:T(8,128)S(1)}, f32[2,512,128]{2,1,0:T(8,128)S(1)}, u32[]{:S(2)}, u32[]{:S(2)}) %collective-permute-start.10) | collective-permute-done | bytes 524320 | tf_op jit(solution)/shard_map/ppermute | solution.py:614
  106.7 1.7 collective-permute-done.9.refs_2_
  108.4 2.5 %edges.5 = (f32[2,2,512,128]{3,2,1,0:T(8,128)}, f32[2,512,128]{2,1,0:T(8,128)}, f32[2,512,128]{2,1,0:T(8,128)}) custom-call(f32[27]{0:T(128)S(1)} %concatenate.3.refs_0_.refs_1_.prm, f32[2,2,512,128]{3,2,1,0:T(8,128)S(1)} %get-tuple-element.83.refs_1_, f32[2,512,128]{2,1,0:T(8,128)S(1)} %collective-permute-done.9.refs_2_, ...), custom_call_target="tpu_custom_call" | custom-call | flops 1000 | bytes 1000 | tf_op jit(solution)/shard_map/edges/pallas_call | solution.py:583
  112.6 4.2 %collective-permute-start.13 = (f32[2,512,128]{2,1,0:T(8,128)}, f32[2,512,128]{2,1,0:T(8,128)}, u32[]{:S(2)}, u32[]{:S(2)}) collective-permute-start(f32[2,512,128]{2,1,0:T(8,128)} %get-tuple-element.92), channel_id=1, source_target_pairs={{0,1},{1,2},{2,3},{3,4},{4,5},{5,6},{6,7},{8,9},{9,10},{10,11},{11... | collective-permute-start | bytes 1572872 | tf_op jit(solution)/shard_map/ppermute | solution.py:614
  116.8 2.0 collective-permute-start.14
  118.8 8.0 %step_joined.1 = (f32[2,4,512,128]{3,2,1,0:T(8,128)S(1)}, f32[2,2,512,128]{3,2,1,0:T(8,128)S(1)}, f32[2,2,512,128]{3,2,1,0:T(8,128)S(1)}) custom-call(f32[27]{0:T(128)S(1)} %concatenate.3.refs_0_.refs_1_.prm, f32[4,512,128]{2,1,0:T(8,128)} %get-tuple-element.80.refs_1_, f32[4,512,128]{2,1,0:T(8,128)} %get-tuple-element.81.refs_2_, ...), custom_call_target="tpu_custom_call" | custom-call | flops 1000 | bytes 1000 | tf_op jit(solution)/shard_map/step_joined/pallas_call | solution.py:583
  126.9 4.6 %replay.1 = (f32[2,4,512,128]{3,2,1,0:T(8,128)S(1)}, f32[2,2,512,128]{3,2,1,0:T(8,128)S(1)}, f32[2,4,512,128]{3,2,1,0:T(8,128)}) custom-call(s32[1]{0:T(128)} %bitcast.2.refs_0_, f32[27]{0:T(128)S(1)} %concatenate.3.refs_0_.refs_1_.prm, f32[4,512,128]{2,1,0:T(8,128)} %collective-permute-done.6.refs_2_, f32[4,512,128]{2,1,0:T(8,128)} %collective-permute-done.7.refs_3_, ...), custom_call_target="tpu_custom_call" | custom-call | flops 1000 | bytes 1000 | tf_op jit(solution)/shard_map/replay/pallas_call | solution.py:583
  131.5 2.0 collective-permute-start.12
  133.5 2.7 %edges_apart.1 = (f32[2,2,512,128]{3,2,1,0:T(8,128)S(1)}, f32[2,512,128]{2,1,0:T(8,128)S(1)}, f32[2,512,128]{2,1,0:T(8,128)S(1)}, f32[2,512,128]{2,1,0:T(8,128)S(1)}, f32[2,512,128]{2,1,0:T(8,128)S(1)}) custom-call(f32[27]{0:T(128)S(1)} %concatenate.3.refs_0_.refs_1_.prm, f32[2,2,512,128]{3,2,1,0:T(8,128)S(1)} %get-tuple-element.91.refs_1_, ...), custom_call_target="tpu_custom_call" | custom-call | flops 1000 | bytes 1000 | tf_op jit(solution)/shard_map/edges_apart/pallas_call | solution.py:583
  141.4 2.0 coarse_edges.1
  148.6 3.7 %coarse_mid.1.refs_10_ = f32[2,4,512,128]{3,2,1,0:T(8,128)} custom-call(s32[1]{0:T(128)} %bitcast.1.refs_0_, f32[27]{0:T(128)S(1)} %concatenate.3.refs_0_.refs_1_.prm, f32[2,4,512,128]{3,2,1,0:T(8,128)} %collective-permute-done.12.refs_2_, f32[2,2,512,128]{3,2,1,0:T(8,128)S(1)} %collective-permute-done.17.refs_3_, f32[2,4,512,128]{3,2,1,0:T(8,128)S(1)} %copy-done.1, ...), custom_call_target="tpu_custom_call" | custom-call | flops 1000 | bytes 1000 | tf_op jit(solution)/shard_map/coarse_mid/pallas_call | solution.py:583
  153.7 37.3 %collective-permute-done.23.refs_14_.refs_2_.refs_3_ = f32[2,4,512,128]{3,2,1,0:T(8,128)S(1)} collective-permute-done((f32[2,4,512,128]{3,2,1,0:T(8,128)}, f32[2,4,512,128]{3,2,1,0:T(8,128)S(1)}, u32[]{:S(2)}, u32[]{:S(2)}) %collective-permute-start.23) | collective-permute-done | bytes 2097184 | tf_op jit(solution)/shard_map/ppermute | solution.py:614
  192.4 4.2 %coarse_outer.1 = (f32[2,4,512,128]{3,2,1,0:T(8,128)}, f32[2,512,128]{2,1,0:T(8,128)}, f32[2,512,128]{2,1,0:T(8,128)}) custom-call(s32[1]{0:T(128)} %bitcast.1.refs_0_, f32[27]{0:T(128)S(1)} %concatenate.3.refs_0_.refs_1_.prm, f32[2,4,512,128]{3,2,1,0:T(8,128)} %collective-permute-done.12.refs_2_, f32[2,2,512,128]{3,2,1,0:T(8,128)S(1)} %collective-permute-done.17.refs_3_, ...), custom_call_target="tpu_custom_call" | custom-call | flops 1000 | bytes 1000 | tf_op jit(solution)/shard_map/coarse_outer/pallas_call | solution.py:796
  200.8 6.7 %collective-permute-done.26.refs_4_ = f32[2,4,512,128]{3,2,1,0:T(8,128)} collective-permute-done((f32[2,4,512,128]{3,2,1,0:T(8,128)}, f32[2,4,512,128]{3,2,1,0:T(8,128)}, u32[]{:S(2)}, u32[]{:S(2)}) %collective-permute-start.26) | collective-permute-done | bytes 2097184 | tf_op jit(solution)/shard_map/ppermute | solution.py:614
  207.5 12.1 %last_rows.1 = (f32[1,8,512,128]{3,2,1,0:T(8,128)}, f32[1,8,512,128]{3,2,1,0:T(8,128)}) custom-call(s32[1]{0:T(128)} %bitcast.refs_0_.own, f32[27]{0:T(128)S(1)} %concatenate.3.refs_0_.refs_1_.prm, f32[2,4,512,128]{3,2,1,0:T(8,128)} %copy-done.28, f32[2,4,512,128]{3,2,1,0:T(8,128)} %copy-done.28, f32[2,4,512,128]{3,2,1,0:T(8,128)} %collective-permute-done.26.refs_4_, ...), custom_call_target="tpu_custom_call" | custom-call | flops 1000 | bytes 1000 | tf_op jit(solution)/shard_map/last_rows/pallas_call | solution.py:816
  219.6 2.5 %last_edges.1 = (f32[1,8,512,128]{3,2,1,0:T(8,128)}, f32[1,8,512,128]{3,2,1,0:T(8,128)}) custom-call(s32[1]{0:T(128)} %bitcast.refs_0_.own, f32[27]{0:T(128)S(1)} %concatenate.3.refs_0_.refs_1_.prm, f32[2,512,128]{2,1,0:T(8,128)S(1)} %collective-permute-done.24.low, ...), custom_call_target="tpu_custom_call", output_to_operand_aliasing={{0}: (5, {}), {1}: (6, {})} | custom-call | flops 1000 | bytes 1000 | tf_op jit(solution)/shard_map/last_edges/pallas_call | solution.py:629
  (100 shorter events, 39.1 us)
Async XLA Ops:
  8.5 24.1 %collective-permute-start = (f32[2,512,128]{2,1,0:T(8,128)}, f32[2,512,128]{2,1,0:T(8,128)}, u32[]{:S(2)}, u32[]{:S(2)}) collective-permute-start(f32[2,512,128]{2,1,0:T(8,128)} %get-tuple-element.62), channel_id=1, source_target_pairs={{0,1},{1,2},{2,3},{3,4},{4,5},{5,6},{6,7},{16,17},{17,18},{18,19},... | collective-permute-start | bytes 1572872 | tf_op jit(solution)/shard_map/ppermute | solution.py:614
  10.0 22.6 %collective-permute-start.1 = (f32[2,512,128]{2,1,0:T(8,128)}, f32[2,512,128]{2,1,0:T(8,128)}, u32[]{:S(2)}, u32[]{:S(2)}) collective-permute-start(f32[2,512,128]{2,1,0:T(8,128)} %get-tuple-element.63), channel_id=1, source_target_pairs={{1,0},{2,1},{3,2},{4,3},{5,4},{6,5},{7,6},{17,16},{18,17},{19,18},... | collective-permute-start | bytes 1572872 | tf_op jit(solution)/shard_map/ppermute | solution.py:614
  26.4 82.0 %copy-start.9 = (s32[2,512,128]{2,1,0:T(8,128)}, s32[2,512,128]{2,1,0:T(8,128)S(1)}, u32[]{:S(2)}) copy-start(s32[2,512,128]{2,1,0:T(8,128)S(1)} %get-tuple-element.68.refs_6_.refs_4_.refs_5_.ide) | copy-start | bytes 1572868
  26.4 16.3 %collective-permute-start.2 = (f32[2,512,128]{2,1,0:T(8,128)S(1)}, f32[2,512,128]{2,1,0:T(8,128)S(1)}, u32[]{:S(2)}, u32[]{:S(2)}) collective-permute-start(f32[2,512,128]{2,1,0:T(8,128)S(1)} %get-tuple-element.66), channel_id=1, source_target_pairs={{8,9},{9,10},{10,11},{11,12},{12,13},{13,14},{14,15},{24,25},{25,2... | collective-permute-start | bytes 1572872 | tf_op jit(solution)/shard_map/ppermute | solution.py:614
  29.6 21.5 %collective-permute-start.3 = (f32[2,512,128]{2,1,0:T(8,128)S(1)}, f32[2,512,128]{2,1,0:T(8,128)S(1)}, u32[]{:S(2)}, u32[]{:S(2)}) collective-permute-start(f32[2,512,128]{2,1,0:T(8,128)S(1)} %get-tuple-element.67), channel_id=1, source_target_pairs={{9,8},{10,9},{11,10},{12,11},{13,12},{14,13},{15,14},{25,24},{26,2... | collective-permute-start | bytes 1572872 | tf_op jit(solution)/shard_map/ppermute | solution.py:614
  32.7 26.8 %copy-start.8 = (f32[1,8,512,128]{3,2,1,0:T(8,128)S(1)}, f32[1,8,512,128]{3,2,1,0:T(8,128)}, u32[]{:S(2)}) copy-start(f32[1,8,512,128]{3,2,1,0:T(8,128)} %param.12) | copy-start | bytes 6291460
  53.2 20.1 %collective-permute-start.4 = (f32[2,512,128]{2,1,0:T(8,128)S(1)}, f32[2,512,128]{2,1,0:T(8,128)S(1)}, u32[]{:S(2)}, u32[]{:S(2)}) collective-permute-start(f32[2,512,128]{2,1,0:T(8,128)S(1)} %get-tuple-element.74), channel_id=1, source_target_pairs={{0,1},{1,2},{2,3},{3,4},{4,5},{5,6},{6,7},{8,9},{9,10},{10,11},{11... | collective-permute-start | bytes 1572872 | tf_op jit(solution)/shard_map/ppermute | solution.py:614
  55.2 26.0 %collective-permute-start.5 = (f32[2,512,128]{2,1,0:T(8,128)S(1)}, f32[2,512,128]{2,1,0:T(8,128)S(1)}, u32[]{:S(2)}, u32[]{:S(2)}) collective-permute-start(f32[2,512,128]{2,1,0:T(8,128)S(1)} %get-tuple-element.75), channel_id=1, source_target_pairs={{1,0},{2,1},{3,2},{4,3},{5,4},{6,5},{7,6},{9,8},{10,9},{11,10},{12... | collective-permute-start | bytes 1572872 | tf_op jit(solution)/shard_map/ppermute | solution.py:614
  62.8 45.6 %copy-start = (f32[2,4,512,128]{3,2,1,0:T(8,128)}, f32[2,4,512,128]{3,2,1,0:T(8,128)S(1)}, u32[]{:S(2)}) copy-start(f32[2,4,512,128]{3,2,1,0:T(8,128)S(1)} %get-tuple-element.76.refs_5_.refs_7_.refs_4_) | copy-start | bytes 6291460
  62.8 45.6 %copy-start.3 = (f32[2,2,512,128]{3,2,1,0:T(8,128)}, f32[2,2,512,128]{3,2,1,0:T(8,128)S(1)}, u32[]{:S(2)}) copy-start(f32[2,2,512,128]{3,2,1,0:T(8,128)S(1)} %get-tuple-element.78.refs_7_.refs_8_) | copy-start | bytes 3145732
  62.8 76.2 %copy-start.2 = (f32[2,2,512,128]{3,2,1,0:T(8,128)}, f32[2,2,512,128]{3,2,1,0:T(8,128)S(1)}, u32[]{:S(2)}) copy-start(f32[2,2,512,128]{3,2,1,0:T(8,128)S(1)} %get-tuple-element.77.refs_6_.refs_7_) | copy-start | bytes 3145732
  82.5 24.2 %collective-permute-start.10 = (f32[2,512,128]{2,1,0:T(8,128)S(1)}, f32[2,512,128]{2,1,0:T(8,128)S(1)}, u32[]{:S(2)}, u32[]{:S(2)}) collective-permute-start(f32[2,512,128]{2,1,0:T(8,128)S(1)} %get-tuple-element.85), channel_id=1, source_target_pairs={{1,0},{2,1},{3,2},{4,3},{5,4},{6,5},{7,6},{9,8},{10,9},{11,10},{12... | collective-permute-start | bytes 1572872 | tf_op jit(solution)/shard_map/ppermute | solution.py:614
  84.5 23.9 %collective-permute-start.9 = (f32[2,512,128]{2,1,0:T(8,128)S(1)}, f32[2,512,128]{2,1,0:T(8,128)S(1)}, u32[]{:S(2)}, u32[]{:S(2)}) collective-permute-start(f32[2,512,128]{2,1,0:T(8,128)S(1)} %get-tuple-element.84), channel_id=1, source_target_pairs={{0,1},{1,2},{2,3},{3,4},{4,5},{5,6},{6,7},{8,9},{9,10},{10,11},{11... | collective-permute-start | bytes 1572872 | tf_op jit(solution)/shard_map/ppermute | solution.py:614
  97.8 19.1 %collective-permute-start.6 = (f32[4,512,128]{2,1,0:T(8,128)}, f32[4,512,128]{2,1,0:T(8,128)}, u32[]{:S(2)}, u32[]{:S(2)}) collective-permute-start(f32[4,512,128]{2,1,0:T(8,128)} %get-tuple-element.80.refs_1_), channel_id=1, source_target_pairs={{0,8},{1,9},{2,10},{3,11},{4,12},{5,13},{6,14},{7,15}} | collective-permute-start | bytes 3145736 | tf_op jit(solution)/shard_map/ppermute | solution.py:614
  99.4 27.4 %collective-permute-start.7 = (f32[4,512,128]{2,1,0:T(8,128)}, f32[4,512,128]{2,1,0:T(8,128)}, u32[]{:S(2)}, u32[]{:S(2)}) collective-permute-start(f32[4,512,128]{2,1,0:T(8,128)} %get-tuple-element.81.refs_2_), channel_id=1, source_target_pairs={{0,8},{1,9},{2,10},{3,11},{4,12},{5,13},{6,14},{7,15}} | collective-permute-start | bytes 3145736 | tf_op jit(solution)/shard_map/ppermute | solution.py:614
  101.0 25.8 %collective-permute-start.8 = (f32[2,2,512,128]{3,2,1,0:T(8,128)}, f32[2,2,512,128]{3,2,1,0:T(8,128)}, u32[]{:S(2)}, u32[]{:S(2)}) collective-permute-start(f32[2,2,512,128]{3,2,1,0:T(8,128)} %get-tuple-element.82.refs_3_), channel_id=1, source_target_pairs={{0,8},{1,9},{2,10},{3,11},{4,12},{5,13},{6,14},{7,15}} | collective-permute-start | bytes 3145736 | tf_op jit(solution)/shard_map/ppermute | solution.py:614
  110.9 15.9 %collective-permute-start.11 = (f32[2,2,512,128]{3,2,1,0:T(8,128)}, f32[2,2,512,128]{3,2,1,0:T(8,128)}, u32[]{:S(2)}, u32[]{:S(2)}) collective-permute-start(f32[2,2,512,128]{3,2,1,0:T(8,128)} %get-tuple-element.86.refs_4_), channel_id=1, source_target_pairs={{0,8},{1,9},{2,10},{3,11},{4,12},{5,13},{6,14},{7,15}} | collective-permute-start | bytes 3145736 | tf_op jit(solution)/shard_map/ppermute | solution.py:614
  112.6 20.9 %collective-permute-start.13 = (f32[2,512,128]{2,1,0:T(8,128)}, f32[2,512,128]{2,1,0:T(8,128)}, u32[]{:S(2)}, u32[]{:S(2)}) collective-permute-start(f32[2,512,128]{2,1,0:T(8,128)} %get-tuple-element.92), channel_id=1, source_target_pairs={{0,1},{1,2},{2,3},{3,4},{4,5},{5,6},{6,7},{8,9},{9,10},{10,11},{11... | collective-permute-start | bytes 1572872 | tf_op jit(solution)/shard_map/ppermute | solution.py:614
  116.8 16.6 %collective-permute-start.14 = (f32[2,512,128]{2,1,0:T(8,128)}, f32[2,512,128]{2,1,0:T(8,128)}, u32[]{:S(2)}, u32[]{:S(2)}) collective-permute-start(f32[2,512,128]{2,1,0:T(8,128)} %get-tuple-element.93), channel_id=1, source_target_pairs={{1,0},{2,1},{3,2},{4,3},{5,4},{6,5},{7,6},{9,8},{10,9},{11,10},{12... | collective-permute-start | bytes 1572872 | tf_op jit(solution)/shard_map/ppermute | solution.py:614
  131.5 15.6 %collective-permute-start.12 = (f32[2,4,512,128]{3,2,1,0:T(8,128)}, f32[2,4,512,128]{3,2,1,0:T(8,128)}, u32[]{:S(2)}, u32[]{:S(2)}) collective-permute-start(f32[2,4,512,128]{3,2,1,0:T(8,128)} %get-tuple-element.88.refs_5_.refs_6_), channel_id=1, source_target_pairs={{8,16},{9,17},{10,18},{11,19},{12,20},{13,21},{14,22},{15,23}} | collective-permute-start | bytes 6291464 | tf_op jit(solution)/shard_map/ppermute | solution.py:614
  136.2 2.8 %collective-permute-start.15 = (f32[2,512,128]{2,1,0:T(8,128)S(1)}, f32[2,512,128]{2,1,0:T(8,128)S(1)}, u32[]{:S(2)}, u32[]{:S(2)}) collective-permute-start(f32[2,512,128]{2,1,0:T(8,128)S(1)} %get-tuple-element.94), channel_id=1, source_target_pairs={{0,8},{1,9},{2,10},{3,11},{4,12},{5,13},{6,14},{7,15}} | collective-permute-start | bytes 1572872 | tf_op jit(solution)/shard_map/ppermute | solution.py:614
  136.9 2.1 collective-permute-start.16
  137.6 3.8 %collective-permute-start.18 = (f32[2,512,128]{2,1,0:T(8,128)S(1)}, f32[2,512,128]{2,1,0:T(8,128)S(1)}, u32[]{:S(2)}, u32[]{:S(2)}) collective-permute-start(f32[2,512,128]{2,1,0:T(8,128)S(1)} %get-tuple-element.100), channel_id=1, source_target_pairs={{0,9},{1,10},{2,11},{3,12},{4,13},{5,14},{6,15}} | collective-permute-start | bytes 1572872 | tf_op jit(solution)/shard_map/ppermute | solution.py:614
  138.3 3.1 %collective-permute-start.19 = (f32[2,512,128]{2,1,0:T(8,128)S(1)}, f32[2,512,128]{2,1,0:T(8,128)S(1)}, u32[]{:S(2)}, u32[]{:S(2)}) collective-permute-start(f32[2,512,128]{2,1,0:T(8,128)S(1)} %get-tuple-element.101), channel_id=1, source_target_pairs={{1,8},{2,9},{3,10},{4,11},{5,12},{6,13},{7,14}} | collective-permute-start | bytes 1572872 | tf_op jit(solution)/shard_map/ppermute | solution.py:614
  140.7 6.4 %collective-permute-start.17 = (f32[2,2,512,128]{3,2,1,0:T(8,128)}, f32[2,2,512,128]{3,2,1,0:T(8,128)S(1)}, u32[]{:S(2)}, u32[]{:S(2)}) collective-permute-start(f32[2,2,512,128]{3,2,1,0:T(8,128)} %get-tuple-element.98.refs_9_), channel_id=1, source_target_pairs={{8,16},{9,17},{10,18},{11,19},{12,20},{13,21},{14,22},{15,23}} | collective-permute-start | bytes 3145736 | tf_op jit(solution)/shard_map/ppermute | solution.py:614
  143.4 10.3 %collective-permute-start.21 = (f32[2,512,128]{2,1,0:T(8,128)}, f32[2,512,128]{2,1,0:T(8,128)}, u32[]{:S(2)}, u32[]{:S(2)}) collective-permute-start(f32[2,512,128]{2,1,0:T(8,128)} %get-tuple-element.103), channel_id=1, source_target_pairs={{8,17},{9,18},{10,19},{11,20},{12,21},{13,22},{14,23}} | collective-permute-start | bytes 1572872 | tf_op jit(solution)/shard_map/ppermute | solution.py:614
  144.8 8.8 %collective-permute-start.22 = (f32[2,512,128]{2,1,0:T(8,128)}, f32[2,512,128]{2,1,0:T(8,128)}, u32[]{:S(2)}, u32[]{:S(2)}) collective-permute-start(f32[2,512,128]{2,1,0:T(8,128)} %get-tuple-element.104), channel_id=1, source_target_pairs={{9,16},{10,17},{11,18},{12,19},{13,20},{14,21},{15,22}} | collective-permute-start | bytes 1572872 | tf_op jit(solution)/shard_map/ppermute | solution.py:614
  146.3 7.4 %collective-permute-start.20 = (f32[2,2,512,128]{3,2,1,0:T(8,128)}, f32[2,2,512,128]{3,2,1,0:T(8,128)S(1)}, u32[]{:S(2)}, u32[]{:S(2)}) collective-permute-start(f32[2,2,512,128]{3,2,1,0:T(8,128)} %get-tuple-element.102.refs_10_), channel_id=1, source_target_pairs={{8,16},{9,17},{10,18},{11,19},{12,20},{13,21},{14,22},{15,23}} | collective-permute-start | bytes 3145736 | tf_op jit(solution)/shard_map/ppermute | solution.py:614
  152.4 38.6 %collective-permute-start.23 = (f32[2,4,512,128]{3,2,1,0:T(8,128)}, f32[2,4,512,128]{3,2,1,0:T(8,128)S(1)}, u32[]{:S(2)}, u32[]{:S(2)}) collective-permute-start(f32[2,4,512,128]{3,2,1,0:T(8,128)} %coarse_mid.1.refs_10_), channel_id=1, source_target_pairs={{16,24},{17,25},{18,26},{19,27},{20,28},{21,29},{22,30},{23,31}} | collective-permute-start | bytes 6291464 | tf_op jit(solution)/shard_map/ppermute | solution.py:614
  196.6 10.8 %collective-permute-start.26 = (f32[2,4,512,128]{3,2,1,0:T(8,128)}, f32[2,4,512,128]{3,2,1,0:T(8,128)}, u32[]{:S(2)}, u32[]{:S(2)}) collective-permute-start(f32[2,4,512,128]{3,2,1,0:T(8,128)} %get-tuple-element.109.refs_11_), channel_id=1, source_target_pairs={{16,24},{17,25},{18,26},{19,27},{20,28},{21,29},{22,30},{23,31}} | collective-permute-start | bytes 6291464 | tf_op jit(solution)/shard_map/ppermute | solution.py:614
  197.9 21.7 %collective-permute-start.24 = (f32[2,512,128]{2,1,0:T(8,128)}, f32[2,512,128]{2,1,0:T(8,128)S(1)}, u32[]{:S(2)}, u32[]{:S(2)}) collective-permute-start(f32[2,512,128]{2,1,0:T(8,128)} %get-tuple-element.107), channel_id=1, source_target_pairs={{16,25},{17,26},{18,27},{19,28},{20,29},{21,30},{22,31}} | collective-permute-start | bytes 1572872 | tf_op jit(solution)/shard_map/ppermute | solution.py:614
  199.2 20.4 %collective-permute-start.25 = (f32[2,512,128]{2,1,0:T(8,128)}, f32[2,512,128]{2,1,0:T(8,128)S(1)}, u32[]{:S(2)}, u32[]{:S(2)}) collective-permute-start(f32[2,512,128]{2,1,0:T(8,128)} %get-tuple-element.108), channel_id=1, source_target_pairs={{17,24},{18,25},{19,26},{20,27},{21,28},{22,29},{23,30}} | collective-permute-start | bytes 1572872 | tf_op jit(solution)/shard_map/ppermute | solution.py:614
  (24 other events, 108.8 us)

commit v10 on v8

--- a/solution.py
+++ b/solution.py
@@ -729,7 +729,6 @@
         (prm, part, *sides, ide),
         1,
         "edges_apart",
-        tile=512,
         after=(vm,),
     )
     low, high = halos(tl0, tl7, (0,), 1)
@@ -750,7 +749,6 @@
         (own(1), prm, part, low, high, ide, vx),
         2,
         "coarse_edges",
-        tile=512,
     )
     side = pl.BlockSpec((2, 1, ny, nz), lambda i: (0, i, 0, 0))
     two = pl.BlockSpec((2, 2, ny, nz), lambda i: (0, i, 0, 0))

time: 207 us -> 207 us (level)
  transfers between devices with their start and end apart: 27 -> 27, of which waited for: 9 -> 9; matrix products, arithmetic and copies ran while one was open for 0% -> 0% of each run, Pallas kernels for 33% -> 32%
where the time goes in v10:
time: 207 us; the launch traced here: 206 us
  Pallas kernels  78.5 us (38%)
  waiting for transfers between devices  74.4 us (36%)
  starting transfers between devices  46.7 us (23%)
  local copies, waits for them, and re-layouts  5.42 us (3%)
    ppermute x27, waiting for transfers between devices, move(): return lax.ppermute(x, ('tm', 'space'), pairs)  74.4 us
    pallas_call x15, Pallas kernels, call(): pl.pallas_call(run, out_shape=[f32(*x.shape) for x in through] + list(out...  57.1 us
    ppermute x27, starting transfers between devices, move(): return lax.ppermute(x, ('tm', 'space'), pairs)  46.7 us
    pallas_call x1, Pallas kernels, per_device(): pl.pallas_call(tiled(last_rows_kernel, 512), grid=(2,), out_shape=[out, o...  12.1 us
    pallas_call x2, Pallas kernels, gridded(): pl.pallas_call(kernel, grid=(steps,), out_shape=outs, in_specs=in_specs,...  4.96 us
    unnamed x26, local copies, waits for them, and re-layouts  4.59 us
    pallas_call x1, Pallas kernels, per_device(): pl.pallas_call(tiled(coarse_outer_kernel, 512), grid=(2,), out_shape=[f32...  4.26 us
  transfers between devices with their start and end apart: 27, of which 9 were waited for; matrix products, arithmetic and copies ran while one was open for 0% of the time, Pallas kernels for 32%

profile of v10, /device:TPU:11, one launch (start us, length us, event | category | flops | bytes accessed | tf_op | source)
XLA Modules:
  0.0 206.1 jit_solution(8474905067354155670)
XLA Ops:
  1.5 2.4 %first_edges.1 = (f32[2,512,128]{2,1,0:T(8,128)S(1)}, f32[2,512,128]{2,1,0:T(8,128)S(1)}, f32[2,512,128]{2,1,0:T(8,128)S(1)}, f32[2,512,128]{2,1,0:T(8,128)S(1)}) custom-call(f32[27]{0:T(128)S(1)} %concatenate.3.prm.refs_0_.refs_1_, f32[8,512,128]{2,1,0:T(8,128)} %bitcast.5, f32[8,512,128]{2,1,0:T(8,128)} %bitcast.8, s32[8,512,128]{2,1,0:T(8,128)} %refs_3_.1), custom_call_target="tpu_custom_call" | custom-call | flops 1000 | bytes 1000 | tf_op jit(solution)/shard_map/first_edges/pallas_call | solution.py:619
  6.9 8.5 %first_step.1 = (f32[2,512,128]{2,1,0:T(8,128)S(1)}, f32[2,512,128]{2,1,0:T(8,128)S(1)}, f32[2,4,512,128]{3,2,1,0:T(8,128)S(1)}, f32[2,2,512,128]{3,2,1,0:T(8,12...) custom-call(f32[27]{0:T(128)S(1)} %concatenate.3.prm.refs_0_.refs_1_, ...), custom_call_target="tpu_custom_call", output_to_operand_aliasing={{0}: (5, {}), {1}: (6, {})} | custom-call | flops 1000 | bytes 1000 | tf_op jit(solution)/shard_map/first_step/pallas_call | solution.py:573
  15.4 3.1 %collective-permute-start.2 = (f32[2,512,128]{2,1,0:T(8,128)S(1)}, f32[2,512,128]{2,1,0:T(8,128)S(1)}, u32[]{:S(2)}, u32[]{:S(2)}) collective-permute-start(f32[2,512,128]{2,1,0:T(8,128)S(1)} %get-tuple-element.66), channel_id=1, source_target_pairs={{8,9},{9,10},{10,11},{11,12},{12,13},{13,14},{14,15},{24,25},{25,2... | collective-permute-start | bytes 1572872 | tf_op jit(solution)/shard_map/ppermute | solution.py:604
  18.6 3.0 %collective-permute-start.3 = (f32[2,512,128]{2,1,0:T(8,128)S(1)}, f32[2,512,128]{2,1,0:T(8,128)S(1)}, u32[]{:S(2)}, u32[]{:S(2)}) collective-permute-start(f32[2,512,128]{2,1,0:T(8,128)S(1)} %get-tuple-element.67), channel_id=1, source_target_pairs={{9,8},{10,9},{11,10},{12,11},{13,12},{14,13},{15,14},{25,24},{26,2... | collective-permute-start | bytes 1572872 | tf_op jit(solution)/shard_map/ppermute | solution.py:604
  21.6 9.5 %collective-permute-done.2.refs_4_ = f32[2,512,128]{2,1,0:T(8,128)S(1)} collective-permute-done((f32[2,512,128]{2,1,0:T(8,128)S(1)}, f32[2,512,128]{2,1,0:T(8,128)S(1)}, u32[]{:S(2)}, u32[]{:S(2)}) %collective-permute-start.2) | collective-permute-done | bytes 524320 | tf_op jit(solution)/shard_map/ppermute | solution.py:604
  34.1 2.3 %collective-permute-start.4 = (f32[2,512,128]{2,1,0:T(8,128)S(1)}, f32[2,512,128]{2,1,0:T(8,128)S(1)}, u32[]{:S(2)}, u32[]{:S(2)}) collective-permute-start(f32[2,512,128]{2,1,0:T(8,128)S(1)} %get-tuple-element.74), channel_id=1, source_target_pairs={{0,1},{1,2},{2,3},{3,4},{4,5},{5,6},{6,7},{8,9},{9,10},{10,11},{11... | collective-permute-start | bytes 1572872 | tf_op jit(solution)/shard_map/ppermute | solution.py:604
  36.4 4.4 %collective-permute-start.5 = (f32[2,512,128]{2,1,0:T(8,128)S(1)}, f32[2,512,128]{2,1,0:T(8,128)S(1)}, u32[]{:S(2)}, u32[]{:S(2)}) collective-permute-start(f32[2,512,128]{2,1,0:T(8,128)S(1)} %get-tuple-element.75), channel_id=1, source_target_pairs={{1,0},{2,1},{3,2},{4,3},{5,4},{6,5},{7,6},{9,8},{10,9},{11,10},{12... | collective-permute-start | bytes 1572872 | tf_op jit(solution)/shard_map/ppermute | solution.py:604
  40.7 3.3 %base.1 = (f32[2,4,512,128]{3,2,1,0:T(8,128)S(1)}, f32[2,2,512,128]{3,2,1,0:T(8,128)S(1)}, f32[2,2,512,128]{3,2,1,0:T(8,128)S(1)}) custom-call(f32[27]{0:T(128)S(1)} %concatenate.3.prm.refs_0_.refs_1_, f32[8,512,128]{2,1,0:T(8,128)S(1)} %bitcast.7, f32[8,512,128]{2,1,0:T(8,128)S(1)} %bitcast.10, f32[2,4,512,128]{3,2,1,0:T(8,128)S(1)} %get-tuple-element.59.refs_1_.refs_3_, ...), custom_call_target="tpu_custom_call" | custom-call | flops 1000 | bytes 1000 | tf_op jit(solution)/shard_map/base/pallas_call | solution.py:573
  44.1 8.2 %step.1 = (f32[2,4,512,128]{3,2,1,0:T(8,128)S(1)}, f32[2,2,512,128]{3,2,1,0:T(8,128)S(1)}, f32[2,2,512,128]{3,2,1,0:T(8,128)S(1)}) custom-call(f32[27]{0:T(128)S(1)} %concatenate.3.prm.refs_0_.refs_1_, f32[2,4,512,128]{3,2,1,0:T(8,128)S(1)} %get-tuple-element.59.refs_1_.refs_3_, f32[2,2,512,128]{3,2,1,0:T(8,128)S(1)} %get-tuple-element.60.refs_2_.refs_4_, ...), custom_call_target="tpu_custom_call" | custom-call | flops 1000 | bytes 1000 | tf_op jit(solution)/shard_map/step/pallas_call | solution.py:573
  52.3 2.6 %collective-permute-done.4.refs_2_ = f32[2,512,128]{2,1,0:T(8,128)S(1)} collective-permute-done((f32[2,512,128]{2,1,0:T(8,128)S(1)}, f32[2,512,128]{2,1,0:T(8,128)S(1)}, u32[]{:S(2)}, u32[]{:S(2)}) %collective-permute-start.4) | collective-permute-done | bytes 524320 | tf_op jit(solution)/shard_map/ppermute | solution.py:604
  54.9 3.3 %collective-permute-done.5.refs_3_ = f32[2,512,128]{2,1,0:T(8,128)S(1)} collective-permute-done((f32[2,512,128]{2,1,0:T(8,128)S(1)}, f32[2,512,128]{2,1,0:T(8,128)S(1)}, u32[]{:S(2)}, u32[]{:S(2)}) %collective-permute-start.5) | collective-permute-done | bytes 524320 | tf_op jit(solution)/shard_map/ppermute | solution.py:604
  59.6 1.9 collective-permute-start.10
  61.5 3.4 %collective-permute-start.9 = (f32[2,512,128]{2,1,0:T(8,128)S(1)}, f32[2,512,128]{2,1,0:T(8,128)S(1)}, u32[]{:S(2)}, u32[]{:S(2)}) collective-permute-start(f32[2,512,128]{2,1,0:T(8,128)S(1)} %get-tuple-element.84), channel_id=1, source_target_pairs={{0,1},{1,2},{2,3},{3,4},{4,5},{5,6},{6,7},{8,9},{9,10},{10,11},{11... | collective-permute-start | bytes 1572872 | tf_op jit(solution)/shard_map/ppermute | solution.py:604
  64.9 9.9 %step_apart.1 = (f32[4,512,128]{2,1,0:T(8,128)}, f32[4,512,128]{2,1,0:T(8,128)}, f32[2,2,512,128]{3,2,1,0:T(8,128)}, f32[2,2,512,128]{3,2,1,0:T(8,128)S(1)}) custom-call(f32[27]{0:T(128)S(1)} %concatenate.3.prm.refs_0_.refs_1_, f32[2,4,512,128]{3,2,1,0:T(8,128)S(1)} %get-tuple-element.71.refs_1_, f32[2,2,512,128]{3,2,1,0:T(8,128)S(1)} %get-tuple-element.72.refs_2_, ...), custom_call_target="tpu_custom_call" | custom-call | flops 1000 | bytes 1000 | tf_op jit(solution)/shard_map/step_apart/pallas_call | solution.py:573
  78.1 1.7 collective-permute-start.8
  79.7 6.1 %collective-permute-done.10.refs_3_ = f32[2,512,128]{2,1,0:T(8,128)S(1)} collective-permute-done((f32[2,512,128]{2,1,0:T(8,128)S(1)}, f32[2,512,128]{2,1,0:T(8,128)S(1)}, u32[]{:S(2)}, u32[]{:S(2)}) %collective-permute-start.10) | collective-permute-done | bytes 524320 | tf_op jit(solution)/shard_map/ppermute | solution.py:604
  85.8 2.5 %edges.5 = (f32[2,2,512,128]{3,2,1,0:T(8,128)}, f32[2,512,128]{2,1,0:T(8,128)}, f32[2,512,128]{2,1,0:T(8,128)}) custom-call(f32[27]{0:T(128)S(1)} %concatenate.3.prm.refs_0_.refs_1_, f32[2,2,512,128]{3,2,1,0:T(8,128)S(1)} %get-tuple-element.83.refs_1_, f32[2,512,128]{2,1,0:T(8,128)S(1)} %collective-permute-done.9.refs_2_, ...), custom_call_target="tpu_custom_call" | custom-call | flops 1000 | bytes 1000 | tf_op jit(solution)/shard_map/edges/pallas_call | solution.py:573
  90.0 3.6 %collective-permute-start.13 = (f32[2,512,128]{2,1,0:T(8,128)}, f32[2,512,128]{2,1,0:T(8,128)}, u32[]{:S(2)}, u32[]{:S(2)}) collective-permute-start(f32[2,512,128]{2,1,0:T(8,128)} %get-tuple-element.92), channel_id=1, source_target_pairs={{0,1},{1,2},{2,3},{3,4},{4,5},{5,6},{6,7},{8,9},{9,10},{10,11},{11... | collective-permute-start | bytes 1572872 | tf_op jit(solution)/shard_map/ppermute | solution.py:604
  93.6 2.5 %collective-permute-start.14 = (f32[2,512,128]{2,1,0:T(8,128)}, f32[2,512,128]{2,1,0:T(8,128)}, u32[]{:S(2)}, u32[]{:S(2)}) collective-permute-start(f32[2,512,128]{2,1,0:T(8,128)} %get-tuple-element.93), channel_id=1, source_target_pairs={{1,0},{2,1},{3,2},{4,3},{5,4},{6,5},{7,6},{9,8},{10,9},{11,10},{12... | collective-permute-start | bytes 1572872 | tf_op jit(solution)/shard_map/ppermute | solution.py:604
  96.2 8.0 %step_joined.1 = (f32[2,4,512,128]{3,2,1,0:T(8,128)S(1)}, f32[2,2,512,128]{3,2,1,0:T(8,128)S(1)}, f32[2,2,512,128]{3,2,1,0:T(8,128)S(1)}) custom-call(f32[27]{0:T(128)S(1)} %concatenate.3.prm.refs_0_.refs_1_, f32[4,512,128]{2,1,0:T(8,128)} %get-tuple-element.80.refs_1_, f32[4,512,128]{2,1,0:T(8,128)} %get-tuple-element.81.refs_2_, ...), custom_call_target="tpu_custom_call" | custom-call | flops 1000 | bytes 1000 | tf_op jit(solution)/shard_map/step_joined/pallas_call | solution.py:573
  104.3 4.4 %replay.1 = (f32[2,4,512,128]{3,2,1,0:T(8,128)S(1)}, f32[2,2,512,128]{3,2,1,0:T(8,128)S(1)}, f32[2,4,512,128]{3,2,1,0:T(8,128)}) custom-call(s32[1]{0:T(128)} %bitcast.2.refs_0_, f32[27]{0:T(128)S(1)} %concatenate.3.prm.refs_0_.refs_1_, f32[4,512,128]{2,1,0:T(8,128)} %collective-permute-done.6.refs_2_, f32[4,512,128]{2,1,0:T(8,128)} %collective-permute-done.7.refs_3_, ...), custom_call_target="tpu_custom_call" | custom-call | flops 1000 | bytes 1000 | tf_op jit(solution)/shard_map/replay/pallas_call | solution.py:573
  108.7 2.2 %collective-permute-start.12 = (f32[2,4,512,128]{3,2,1,0:T(8,128)}, f32[2,4,512,128]{3,2,1,0:T(8,128)}, u32[]{:S(2)}, u32[]{:S(2)}) collective-permute-start(f32[2,4,512,128]{3,2,1,0:T(8,128)} %get-tuple-element.88.refs_5_.refs_6_), channel_id=1, source_target_pairs={{8,16},{9,17},{10,18},{11,19},{12,20},{13,21},{14,22},{15,23}} | collective-permute-start | bytes 6291464 | tf_op jit(solution)/shard_map/ppermute | solution.py:604
  110.8 5.1 %collective-permute-done.13.refs_2_ = f32[2,512,128]{2,1,0:T(8,128)} collective-permute-done((f32[2,512,128]{2,1,0:T(8,128)}, f32[2,512,128]{2,1,0:T(8,128)}, u32[]{:S(2)}, u32[]{:S(2)}) %collective-permute-start.13) | collective-permute-done | bytes 524320 | tf_op jit(solution)/shard_map/ppermute | solution.py:604
  116.0 2.2 %collective-permute-done.14.refs_3_ = f32[2,512,128]{2,1,0:T(8,128)} collective-permute-done((f32[2,512,128]{2,1,0:T(8,128)}, f32[2,512,128]{2,1,0:T(8,128)}, u32[]{:S(2)}, u32[]{:S(2)}) %collective-permute-start.14) | collective-permute-done | bytes 524320 | tf_op jit(solution)/shard_map/ppermute | solution.py:604
  118.2 2.2 %edges_apart.1 = (f32[2,2,512,128]{3,2,1,0:T(8,128)S(1)}, f32[2,512,128]{2,1,0:T(8,128)S(1)}, f32[2,512,128]{2,1,0:T(8,128)S(1)}, f32[2,512,128]{2,1,0:T(8,128)S(1)}, f32[2,512,128]{2,1,0:T(8,128)S(1)}) custom-call(f32[27]{0:T(128)S(1)} %concatenate.3.prm.refs_0_.refs_1_, f32[2,2,512,128]{3,2,1,0:T(8,128)S(1)} %get-tuple-element.91.refs_1_, ...), custom_call_target="tpu_custom_call" | custom-call | flops 1000 | bytes 1000 | tf_op jit(solution)/shard_map/edges_apart/pallas_call | solution.py:573
  125.6 2.0 coarse_edges.1
  132.8 3.7 %coarse_mid.1.refs_10_ = f32[2,4,512,128]{3,2,1,0:T(8,128)} custom-call(s32[1]{0:T(128)} %bitcast.1.refs_0_, f32[27]{0:T(128)S(1)} %concatenate.3.prm.refs_0_.refs_1_, f32[2,4,512,128]{3,2,1,0:T(8,128)} %collective-permute-done.12.refs_2_, f32[2,2,512,128]{3,2,1,0:T(8,128)S(1)} %collective-permute-done.17.refs_3_, f32[2,4,512,128]{3,2,1,0:T(8,128)S(1)} %copy-done.1, ...), custom_call_target="tpu_custom_call" | custom-call | flops 1000 | bytes 1000 | tf_op jit(solution)/shard_map/coarse_mid/pallas_call | solution.py:573
  137.8 37.1 %collective-permute-done.23.refs_14_.refs_2_.refs_3_ = f32[2,4,512,128]{3,2,1,0:T(8,128)S(1)} collective-permute-done((f32[2,4,512,128]{3,2,1,0:T(8,128)}, f32[2,4,512,128]{3,2,1,0:T(8,128)S(1)}, u32[]{:S(2)}, u32[]{:S(2)}) %collective-permute-start.23) | collective-permute-done | bytes 2097184 | tf_op jit(solution)/shard_map/ppermute | solution.py:604
  176.3 4.3 %coarse_outer.1 = (f32[2,4,512,128]{3,2,1,0:T(8,128)}, f32[2,512,128]{2,1,0:T(8,128)}, f32[2,512,128]{2,1,0:T(8,128)}) custom-call(s32[1]{0:T(128)} %bitcast.1.refs_0_, f32[27]{0:T(128)S(1)} %concatenate.3.prm.refs_0_.refs_1_, f32[2,4,512,128]{3,2,1,0:T(8,128)} %collective-permute-done.12.refs_2_, f32[2,2,512,128]{3,2,1,0:T(8,128)S(1)} %collective-permute-done.17.refs_3_, ...), custom_call_target="tpu_custom_call" | custom-call | flops 1000 | bytes 1000 | tf_op jit(solution)/shard_map/coarse_outer/pallas_call | solution.py:784
  184.5 6.9 %collective-permute-done.26.refs_4_ = f32[2,4,512,128]{3,2,1,0:T(8,128)} collective-permute-done((f32[2,4,512,128]{3,2,1,0:T(8,128)}, f32[2,4,512,128]{3,2,1,0:T(8,128)}, u32[]{:S(2)}, u32[]{:S(2)}) %collective-permute-start.26) | collective-permute-done | bytes 2097184 | tf_op jit(solution)/shard_map/ppermute | solution.py:604
  191.4 12.1 %last_rows.1 = (f32[1,8,512,128]{3,2,1,0:T(8,128)}, f32[1,8,512,128]{3,2,1,0:T(8,128)}) custom-call(s32[1]{0:T(128)} %bitcast.refs_0_.own, f32[27]{0:T(128)S(1)} %concatenate.3.prm.refs_0_.refs_1_, f32[2,4,512,128]{3,2,1,0:T(8,128)} %copy-done.12, f32[2,4,512,128]{3,2,1,0:T(8,128)} %copy-done.12, f32[2,4,512,128]{3,2,1,0:T(8,128)} %collective-permute-done.26.refs_4_, ...), custom_call_target="tpu_custom_call" | custom-call | flops 1000 | bytes 1000 | tf_op jit(solution)/shard_map/last_rows/pallas_call | solution.py:804
  203.6 2.5 %last_edges.1 = (f32[1,8,512,128]{3,2,1,0:T(8,128)}, f32[1,8,512,128]{3,2,1,0:T(8,128)}) custom-call(s32[1]{0:T(128)} %bitcast.refs_0_.own, f32[27]{0:T(128)S(1)} %concatenate.3.prm.refs_0_.refs_1_, f32[2,512,128]{2,1,0:T(8,128)S(1)} %collective-permute-done.24.low, ...), custom_call_target="tpu_custom_call", output_to_operand_aliasing={{0}: (5, {}), {1}: (6, {})} | custom-call | flops 1000 | bytes 1000 | tf_op jit(solution)/shard_map/last_edges/pallas_call | solution.py:619
  (68 shorter events, 30.0 us)
Async XLA Ops:
  3.9 17.7 %collective-permute-start = (f32[2,512,128]{2,1,0:T(8,128)S(1)}, f32[2,512,128]{2,1,0:T(8,128)S(1)}, u32[]{:S(2)}, u32[]{:S(2)}) collective-permute-start(f32[2,512,128]{2,1,0:T(8,128)S(1)} %get-tuple-element.62), channel_id=1, source_target_pairs={{0,1},{1,2},{2,3},{3,4},{4,5},{5,6},{6,7},{16,17},{17,18},{18,19},... | collective-permute-start | bytes 1572872 | tf_op jit(solution)/shard_map/ppermute | solution.py:604
  4.6 17.0 %collective-permute-start.1 = (f32[2,512,128]{2,1,0:T(8,128)S(1)}, f32[2,512,128]{2,1,0:T(8,128)S(1)}, u32[]{:S(2)}, u32[]{:S(2)}) collective-permute-start(f32[2,512,128]{2,1,0:T(8,128)S(1)} %get-tuple-element.63), channel_id=1, source_target_pairs={{1,0},{2,1},{3,2},{4,3},{5,4},{6,5},{7,6},{17,16},{18,17},{19,18},... | collective-permute-start | bytes 1572872 | tf_op jit(solution)/shard_map/ppermute | solution.py:604
  15.4 70.4 %copy-start.7 = (s32[2,512,128]{2,1,0:T(8,128)}, s32[2,512,128]{2,1,0:T(8,128)S(1)}, u32[]{:S(2)}) copy-start(s32[2,512,128]{2,1,0:T(8,128)S(1)} %get-tuple-element.68.refs_6_.refs_4_.refs_5_.ide) | copy-start | bytes 1572868
  15.4 15.7 %collective-permute-start.2 = (f32[2,512,128]{2,1,0:T(8,128)S(1)}, f32[2,512,128]{2,1,0:T(8,128)S(1)}, u32[]{:S(2)}, u32[]{:S(2)}) collective-permute-start(f32[2,512,128]{2,1,0:T(8,128)S(1)} %get-tuple-element.66), channel_id=1, source_target_pairs={{8,9},{9,10},{10,11},{11,12},{12,13},{13,14},{14,15},{24,25},{25,2... | collective-permute-start | bytes 1572872 | tf_op jit(solution)/shard_map/ppermute | solution.py:604
  18.6 14.1 %collective-permute-start.3 = (f32[2,512,128]{2,1,0:T(8,128)S(1)}, f32[2,512,128]{2,1,0:T(8,128)S(1)}, u32[]{:S(2)}, u32[]{:S(2)}) collective-permute-start(f32[2,512,128]{2,1,0:T(8,128)S(1)} %get-tuple-element.67), channel_id=1, source_target_pairs={{9,8},{10,9},{11,10},{12,11},{13,12},{14,13},{15,14},{25,24},{26,2... | collective-permute-start | bytes 1572872 | tf_op jit(solution)/shard_map/ppermute | solution.py:604
  34.1 20.8 %collective-permute-start.4 = (f32[2,512,128]{2,1,0:T(8,128)S(1)}, f32[2,512,128]{2,1,0:T(8,128)S(1)}, u32[]{:S(2)}, u32[]{:S(2)}) collective-permute-start(f32[2,512,128]{2,1,0:T(8,128)S(1)} %get-tuple-element.74), channel_id=1, source_target_pairs={{0,1},{1,2},{2,3},{3,4},{4,5},{5,6},{6,7},{8,9},{9,10},{10,11},{11... | collective-permute-start | bytes 1572872 | tf_op jit(solution)/shard_map/ppermute | solution.py:604
  36.4 21.8 %collective-permute-start.5 = (f32[2,512,128]{2,1,0:T(8,128)S(1)}, f32[2,512,128]{2,1,0:T(8,128)S(1)}, u32[]{:S(2)}, u32[]{:S(2)}) collective-permute-start(f32[2,512,128]{2,1,0:T(8,128)S(1)} %get-tuple-element.75), channel_id=1, source_target_pairs={{1,0},{2,1},{3,2},{4,3},{5,4},{6,5},{7,6},{9,8},{10,9},{11,10},{12... | collective-permute-start | bytes 1572872 | tf_op jit(solution)/shard_map/ppermute | solution.py:604
  44.1 41.8 %copy-start = (f32[2,4,512,128]{3,2,1,0:T(8,128)}, f32[2,4,512,128]{3,2,1,0:T(8,128)S(1)}, u32[]{:S(2)}) copy-start(f32[2,4,512,128]{3,2,1,0:T(8,128)S(1)} %get-tuple-element.76.refs_5_.refs_7_.refs_4_) | copy-start | bytes 6291460
  44.1 41.8 %copy-start.3 = (f32[2,2,512,128]{3,2,1,0:T(8,128)}, f32[2,2,512,128]{3,2,1,0:T(8,128)S(1)}, u32[]{:S(2)}) copy-start(f32[2,2,512,128]{3,2,1,0:T(8,128)S(1)} %get-tuple-element.78.refs_7_.refs_8_) | copy-start | bytes 3145732
  44.1 79.1 %copy-start.2 = (f32[2,2,512,128]{3,2,1,0:T(8,128)}, f32[2,2,512,128]{3,2,1,0:T(8,128)S(1)}, u32[]{:S(2)}) copy-start(f32[2,2,512,128]{3,2,1,0:T(8,128)S(1)} %get-tuple-element.77.refs_6_.refs_7_) | copy-start | bytes 3145732
  59.6 26.2 %collective-permute-start.10 = (f32[2,512,128]{2,1,0:T(8,128)S(1)}, f32[2,512,128]{2,1,0:T(8,128)S(1)}, u32[]{:S(2)}, u32[]{:S(2)}) collective-permute-start(f32[2,512,128]{2,1,0:T(8,128)S(1)} %get-tuple-element.85), channel_id=1, source_target_pairs={{1,0},{2,1},{3,2},{4,3},{5,4},{6,5},{7,6},{9,8},{10,9},{11,10},{12... | collective-permute-start | bytes 1572872 | tf_op jit(solution)/shard_map/ppermute | solution.py:604
  61.5 24.3 %collective-permute-start.9 = (f32[2,512,128]{2,1,0:T(8,128)S(1)}, f32[2,512,128]{2,1,0:T(8,128)S(1)}, u32[]{:S(2)}, u32[]{:S(2)}) collective-permute-start(f32[2,512,128]{2,1,0:T(8,128)S(1)} %get-tuple-element.84), channel_id=1, source_target_pairs={{0,1},{1,2},{2,3},{3,4},{4,5},{5,6},{6,7},{8,9},{9,10},{10,11},{11... | collective-permute-start | bytes 1572872 | tf_op jit(solution)/shard_map/ppermute | solution.py:604
  74.8 18.9 %collective-permute-start.6 = (f32[4,512,128]{2,1,0:T(8,128)}, f32[4,512,128]{2,1,0:T(8,128)}, u32[]{:S(2)}, u32[]{:S(2)}) collective-permute-start(f32[4,512,128]{2,1,0:T(8,128)} %get-tuple-element.80.refs_1_), channel_id=1, source_target_pairs={{0,8},{1,9},{2,10},{3,11},{4,12},{5,13},{6,14},{7,15}} | collective-permute-start | bytes 3145736 | tf_op jit(solution)/shard_map/ppermute | solution.py:604
  76.4 27.8 %collective-permute-start.7 = (f32[4,512,128]{2,1,0:T(8,128)}, f32[4,512,128]{2,1,0:T(8,128)}, u32[]{:S(2)}, u32[]{:S(2)}) collective-permute-start(f32[4,512,128]{2,1,0:T(8,128)} %get-tuple-element.81.refs_2_), channel_id=1, source_target_pairs={{0,8},{1,9},{2,10},{3,11},{4,12},{5,13},{6,14},{7,15}} | collective-permute-start | bytes 3145736 | tf_op jit(solution)/shard_map/ppermute | solution.py:604
  78.1 26.2 %collective-permute-start.8 = (f32[2,2,512,128]{3,2,1,0:T(8,128)}, f32[2,2,512,128]{3,2,1,0:T(8,128)}, u32[]{:S(2)}, u32[]{:S(2)}) collective-permute-start(f32[2,2,512,128]{3,2,1,0:T(8,128)} %get-tuple-element.82.refs_3_), channel_id=1, source_target_pairs={{0,8},{1,9},{2,10},{3,11},{4,12},{5,13},{6,14},{7,15}} | collective-permute-start | bytes 3145736 | tf_op jit(solution)/shard_map/ppermute | solution.py:604
  88.4 15.9 %collective-permute-start.11 = (f32[2,2,512,128]{3,2,1,0:T(8,128)}, f32[2,2,512,128]{3,2,1,0:T(8,128)}, u32[]{:S(2)}, u32[]{:S(2)}) collective-permute-start(f32[2,2,512,128]{3,2,1,0:T(8,128)} %get-tuple-element.86.refs_4_), channel_id=1, source_target_pairs={{0,8},{1,9},{2,10},{3,11},{4,12},{5,13},{6,14},{7,15}} | collective-permute-start | bytes 3145736 | tf_op jit(solution)/shard_map/ppermute | solution.py:604
  90.0 26.0 %collective-permute-start.13 = (f32[2,512,128]{2,1,0:T(8,128)}, f32[2,512,128]{2,1,0:T(8,128)}, u32[]{:S(2)}, u32[]{:S(2)}) collective-permute-start(f32[2,512,128]{2,1,0:T(8,128)} %get-tuple-element.92), channel_id=1, source_target_pairs={{0,1},{1,2},{2,3},{3,4},{4,5},{5,6},{6,7},{8,9},{9,10},{10,11},{11... | collective-permute-start | bytes 1572872 | tf_op jit(solution)/shard_map/ppermute | solution.py:604
  93.6 24.5 %collective-permute-start.14 = (f32[2,512,128]{2,1,0:T(8,128)}, f32[2,512,128]{2,1,0:T(8,128)}, u32[]{:S(2)}, u32[]{:S(2)}) collective-permute-start(f32[2,512,128]{2,1,0:T(8,128)} %get-tuple-element.93), channel_id=1, source_target_pairs={{1,0},{2,1},{3,2},{4,3},{5,4},{6,5},{7,6},{9,8},{10,9},{11,10},{12... | collective-permute-start | bytes 1572872 | tf_op jit(solution)/shard_map/ppermute | solution.py:604
  104.2 13.9 %copy-start.8 = (s32[2,512,128]{2,1,0:T(8,128)S(1)}, s32[2,512,128]{2,1,0:T(8,128)}, u32[]{:S(2)}) copy-start(s32[2,512,128]{2,1,0:T(8,128)} %copy-done.7) | copy-start | bytes 1572868
  108.7 22.5 %collective-permute-start.12 = (f32[2,4,512,128]{3,2,1,0:T(8,128)}, f32[2,4,512,128]{3,2,1,0:T(8,128)}, u32[]{:S(2)}, u32[]{:S(2)}) collective-permute-start(f32[2,4,512,128]{3,2,1,0:T(8,128)} %get-tuple-element.88.refs_5_.refs_6_), channel_id=1, source_target_pairs={{8,16},{9,17},{10,18},{11,19},{12,20},{13,21},{14,22},{15,23}} | collective-permute-start | bytes 6291464 | tf_op jit(solution)/shard_map/ppermute | solution.py:604
  120.4 2.8 %collective-permute-start.15 = (f32[2,512,128]{2,1,0:T(8,128)S(1)}, f32[2,512,128]{2,1,0:T(8,128)S(1)}, u32[]{:S(2)}, u32[]{:S(2)}) collective-permute-start(f32[2,512,128]{2,1,0:T(8,128)S(1)} %get-tuple-element.94), channel_id=1, source_target_pairs={{0,8},{1,9},{2,10},{3,11},{4,12},{5,13},{6,14},{7,15}} | collective-permute-start | bytes 1572872 | tf_op jit(solution)/shard_map/ppermute | solution.py:604
  121.1 2.1 %collective-permute-start.16 = (f32[2,512,128]{2,1,0:T(8,128)S(1)}, f32[2,512,128]{2,1,0:T(8,128)S(1)}, u32[]{:S(2)}, u32[]{:S(2)}) collective-permute-start(f32[2,512,128]{2,1,0:T(8,128)S(1)} %get-tuple-element.95), channel_id=1, source_target_pairs={{0,8},{1,9},{2,10},{3,11},{4,12},{5,13},{6,14},{7,15}} | collective-permute-start | bytes 1572872 | tf_op jit(solution)/shard_map/ppermute | solution.py:604
  121.8 3.8 %collective-permute-start.18 = (f32[2,512,128]{2,1,0:T(8,128)S(1)}, f32[2,512,128]{2,1,0:T(8,128)S(1)}, u32[]{:S(2)}, u32[]{:S(2)}) collective-permute-start(f32[2,512,128]{2,1,0:T(8,128)S(1)} %get-tuple-element.100), channel_id=1, source_target_pairs={{0,9},{1,10},{2,11},{3,12},{4,13},{5,14},{6,15}} | collective-permute-start | bytes 1572872 | tf_op jit(solution)/shard_map/ppermute | solution.py:604
  122.5 3.1 %collective-permute-start.19 = (f32[2,512,128]{2,1,0:T(8,128)S(1)}, f32[2,512,128]{2,1,0:T(8,128)S(1)}, u32[]{:S(2)}, u32[]{:S(2)}) collective-permute-start(f32[2,512,128]{2,1,0:T(8,128)S(1)} %get-tuple-element.101), channel_id=1, source_target_pairs={{1,8},{2,9},{3,10},{4,11},{5,12},{6,13},{7,14}} | collective-permute-start | bytes 1572872 | tf_op jit(solution)/shard_map/ppermute | solution.py:604
  124.8 6.3 %collective-permute-start.17 = (f32[2,2,512,128]{3,2,1,0:T(8,128)}, f32[2,2,512,128]{3,2,1,0:T(8,128)S(1)}, u32[]{:S(2)}, u32[]{:S(2)}) collective-permute-start(f32[2,2,512,128]{3,2,1,0:T(8,128)} %get-tuple-element.98.refs_9_), channel_id=1, source_target_pairs={{8,16},{9,17},{10,18},{11,19},{12,20},{13,21},{14,22},{15,23}} | collective-permute-start | bytes 3145736 | tf_op jit(solution)/shard_map/ppermute | solution.py:604
  127.6 10.3 %collective-permute-start.21 = (f32[2,512,128]{2,1,0:T(8,128)}, f32[2,512,128]{2,1,0:T(8,128)}, u32[]{:S(2)}, u32[]{:S(2)}) collective-permute-start(f32[2,512,128]{2,1,0:T(8,128)} %get-tuple-element.103), channel_id=1, source_target_pairs={{8,17},{9,18},{10,19},{11,20},{12,21},{13,22},{14,23}} | collective-permute-start | bytes 1572872 | tf_op jit(solution)/shard_map/ppermute | solution.py:604
  129.0 8.8 %collective-permute-start.22 = (f32[2,512,128]{2,1,0:T(8,128)}, f32[2,512,128]{2,1,0:T(8,128)}, u32[]{:S(2)}, u32[]{:S(2)}) collective-permute-start(f32[2,512,128]{2,1,0:T(8,128)} %get-tuple-element.104), channel_id=1, source_target_pairs={{9,16},{10,17},{11,18},{12,19},{13,20},{14,21},{15,22}} | collective-permute-start | bytes 1572872 | tf_op jit(solution)/shard_map/ppermute | solution.py:604
  130.4 7.4 %collective-permute-start.20 = (f32[2,2,512,128]{3,2,1,0:T(8,128)}, f32[2,2,512,128]{3,2,1,0:T(8,128)S(1)}, u32[]{:S(2)}, u32[]{:S(2)}) collective-permute-start(f32[2,2,512,128]{3,2,1,0:T(8,128)} %get-tuple-element.102.refs_10_), channel_id=1, source_target_pairs={{8,16},{9,17},{10,18},{11,19},{12,20},{13,21},{14,22},{15,23}} | collective-permute-start | bytes 3145736 | tf_op jit(solution)/shard_map/ppermute | solution.py:604
  136.5 38.4 %collective-permute-start.23 = (f32[2,4,512,128]{3,2,1,0:T(8,128)}, f32[2,4,512,128]{3,2,1,0:T(8,128)S(1)}, u32[]{:S(2)}, u32[]{:S(2)}) collective-permute-start(f32[2,4,512,128]{3,2,1,0:T(8,128)} %coarse_mid.1.refs_10_), channel_id=1, source_target_pairs={{16,24},{17,25},{18,26},{19,27},{20,28},{21,29},{22,30},{23,31}} | collective-permute-start | bytes 6291464 | tf_op jit(solution)/shard_map/ppermute | solution.py:604
  180.6 10.8 %collective-permute-start.26 = (f32[2,4,512,128]{3,2,1,0:T(8,128)}, f32[2,4,512,128]{3,2,1,0:T(8,128)}, u32[]{:S(2)}, u32[]{:S(2)}) collective-permute-start(f32[2,4,512,128]{3,2,1,0:T(8,128)} %get-tuple-element.109.refs_11_), channel_id=1, source_target_pairs={{16,24},{17,25},{18,26},{19,27},{20,28},{21,29},{22,30},{23,31}} | collective-permute-start | bytes 6291464 | tf_op jit(solution)/shard_map/ppermute | solution.py:604
  181.9 21.7 %collective-permute-start.24 = (f32[2,512,128]{2,1,0:T(8,128)}, f32[2,512,128]{2,1,0:T(8,128)S(1)}, u32[]{:S(2)}, u32[]{:S(2)}) collective-permute-start(f32[2,512,128]{2,1,0:T(8,128)} %get-tuple-element.107), channel_id=1, source_target_pairs={{16,25},{17,26},{18,27},{19,28},{20,29},{21,30},{22,31}} | collective-permute-start | bytes 1572872 | tf_op jit(solution)/shard_map/ppermute | solution.py:604
  183.2 20.4 %collective-permute-start.25 = (f32[2,512,128]{2,1,0:T(8,128)}, f32[2,512,128]{2,1,0:T(8,128)S(1)}, u32[]{:S(2)}, u32[]{:S(2)}) collective-permute-start(f32[2,512,128]{2,1,0:T(8,128)} %get-tuple-element.108), channel_id=1, source_target_pairs={{17,24},{18,25},{19,26},{20,27},{21,28},{22,29},{23,30}} | collective-permute-start | bytes 1572872 | tf_op jit(solution)/shard_map/ppermute | solution.py:604
  (8 other events, 33.3 us)
